TPU v7x, 32 devices: a whole 2x2x4 slice. The times are simulated.
32 devices in a mesh: groups: 2 (over x), leaf: 16 (over z, y, core).
Axes of the slice: x: 2, y: 2, z: 4, core: 2. Of those that a mesh axis runs over, the one named last changes fastest.
Arguments:
- coords: bfloat16 [64, 32768], P(None, ('groups', 'leaf')), parts along dimension 1, may hold values from -1.1953125 to 1.1953125
- charges: bfloat16 [64, 32768], P(None, ('groups', 'leaf')), parts along dimension 1, may hold values from -6 to 6
- near_lists: int32 [64, 16], P(('groups', 'leaf')), parts along dimension 0, may hold values from -1 to 31, as said below
- far_lists: int32 [64, 32], P(('groups', 'leaf')), parts along dimension 0, may hold values from -1 to 16, as said below
- leaf_interp: bfloat16 [32768, 128], P(('groups', 'leaf')), parts along dimension 0, may hold values from -0.25 to 0.25
- node_interp: bfloat16 [8192, 128], P(('groups', 'leaf')), parts along dimension 0, may hold values from -0.375 to 0.375
- upper_interp: bfloat16 [4096, 128], P(('groups', 'leaf')), parts along dimension 0, may hold values from -0.125 to 0.125
- node_points: bfloat16 [64, 4096], P(None, ('groups', 'leaf')), parts along dimension 1, may hold values from -1.1953125 to 1.1953125
- upper_points: bfloat16 [64, 256], P(None, 'groups'), parts along dimension 1, may hold values from -1.1953125 to 1.1953125
Outputs:
- first: bfloat16 [64, 32768], P(None, ('groups', 'leaf')), parts along dimension 1
- second: bfloat16 [64, 32768], P(None, ('groups', 'leaf')), parts along dimension 1
There are 2 independent parts, one for each index of `groups`. A program takes and returns all parts, laid end to end along the dimension named above; each array names one. Nothing has to cross between parts.
Inputs may be any that keep to these rules, and one draw needn't show every extreme that they name: `near_lists`: used slots come first, then -1 for each unused slot. Slot 0 of leaf b names b itself and slot 1 names another leaf of b's device. Over the near lists of the leaves of one device, at most one distinct leaf of any other device is named, though it may be named several times. `far_lists`: used slots come first, then -1 for each unused slot. An entry under 16 names a device node, the others name upper nodes. No entry names the device node that holds the leaf itself.
All inputs are finite; a program needn't handle non-finite values.
Results may differ from a plain program's by a relative error of at most 0.008.
Values may be sent and summed in bfloat16 or wider, within the bound.
No kernel may reach another device: no remote copies, remote signals or barrier semaphores. Data moves between devices by JAX's collectives and lax.ppermute only.
A program may use at most 64 MiB of HBM per device.

v0:
```python
import jax
import jax.numpy as jnp
from jax import lax
from jax.sharding import PartitionSpec as P

BRANCH = 16


nodes_per_turn = 4


def kernel_block(source_coords, target_coords, target_sq):
    source_sq = jnp.sum(jnp.square(source_coords.astype(jnp.float32)), axis=0)
    products = jnp.einsum(
        "dls,dlt->lst", source_coords, target_coords, preferred_element_type=jnp.float32
    )
    distance = source_sq[:, :, None] + target_sq[:, None, :] - 2.0 * products
    return jnp.exp(-distance).astype(jnp.bfloat16)


def request_list(near_lists, leaves_dev, peer_count, my_index):
    owner_dev = jnp.where(near_lists >= 0, near_lists // leaves_dev, -1)
    local_leaf = near_lists - owner_dev * leaves_dev
    remote = (owner_dev >= 0) & (owner_dev != my_index)
    matches = (owner_dev[:, :, None] == jnp.arange(peer_count)[None, None, :]) & remote[:, :, None]
    wanted = jnp.max(jnp.where(matches, local_leaf[:, :, None], -1), axis=(0, 1))
    source_index = jnp.where(
        owner_dev == my_index, local_leaf, leaves_dev + jnp.maximum(owner_dev, 0)
    )
    source_index = jnp.where(near_lists >= 0, source_index, 0)
    return (wanted, source_index, near_lists >= 0)


def fetch_blocks(stacked, wanted):
    incoming = lax.all_to_all(wanted, "leaf", split_axis=0, concat_axis=0, tiled=True)
    served = jnp.take(stacked, jnp.maximum(incoming, 0), axis=1)
    return (incoming, lax.all_to_all(served, "leaf", split_axis=1, concat_axis=1, tiled=True))


def on_device(
    coords,
    charges,
    near_lists,
    far_lists,
    leaf_interp,
    node_interp,
    upper_interp,
    node_points,
    upper_points,
):
    feature_dim, local_width = coords.shape
    columns = charges.shape[0]
    leaves_dev, near_slots = near_lists.shape
    far_slots = far_lists.shape[1]
    leaf_points = local_width // leaves_dev
    skeleton = leaf_interp.shape[1]
    peer_count = lax.axis_size("leaf")
    my_index = lax.axis_index("leaf")
    point_blocks = coords.reshape(feature_dim, leaves_dev, leaf_points)
    target_sq = jnp.sum(jnp.square(point_blocks.astype(jnp.float32)), axis=0)
    all_points = lax.all_gather(node_points, "leaf", axis=1, tiled=True)
    table_points = jnp.concatenate([all_points, upper_points], axis=1)
    node_count = table_points.shape[1] // skeleton
    table_points = table_points.reshape(feature_dim, node_count, skeleton)
    wanted, source_index, near_valid = request_list(near_lists, leaves_dev, peer_count, my_index)
    leaf_maps = leaf_interp.reshape(leaves_dev, leaf_points, skeleton)

    def kernel_product(charges_now, source_pool):
        charge_blocks = charges_now.reshape(columns, leaves_dev, leaf_points)
        leaf_weights = jnp.einsum(
            "rls,lsk->rlk", charge_blocks, leaf_maps, preferred_element_type=jnp.float32
        ).astype(jnp.bfloat16)
        device_weights = jnp.dot(
            leaf_weights.reshape(columns, leaves_dev * skeleton),
            node_interp,
            preferred_element_type=jnp.float32,
        ).astype(jnp.bfloat16)
        upper_term = jnp.dot(
            device_weights, upper_interp, preferred_element_type=jnp.float32
        ).astype(jnp.bfloat16)
        all_weights, all_terms = (
            lax.all_gather(device_weights, "leaf", axis=1, tiled=True),
            lax.all_gather(upper_term, "leaf", axis=1, tiled=True),
        )
        grouped = all_terms.reshape(columns, peer_count // BRANCH, BRANCH, skeleton).astype(
            jnp.float32
        )
        upper_weights = jnp.sum(grouped, axis=2).astype(jnp.bfloat16)
        table_weights = jnp.concatenate(
            [all_weights.reshape(columns, peer_count, skeleton), upper_weights], axis=1
        )

        def near_step(position, totals):
            chosen = lax.dynamic_index_in_dim(source_index, position, 1, keepdims=False)
            present = lax.dynamic_index_in_dim(near_valid, position, 1, keepdims=False)
            blocks = jnp.take(source_pool, chosen, axis=1)
            source_coords = blocks[:feature_dim]
            source_charges = blocks[feature_dim:] * present.astype(jnp.bfloat16)[None, :, None]
            weights = kernel_block(source_coords, point_blocks, target_sq)
            return totals + jnp.einsum(
                "rls,lst->rlt", source_charges, weights, preferred_element_type=jnp.float32
            )

        def far_step(group_turn, totals):
            node_ids = lax.dynamic_slice_in_dim(
                far_lists, group_turn * nodes_per_turn, nodes_per_turn, 1
            )
            safe_ids = jnp.maximum(node_ids, 0)
            present = (node_ids >= 0).astype(jnp.bfloat16)
            source_coords = jnp.take(table_points, safe_ids, axis=1).reshape(
                feature_dim, leaves_dev, nodes_per_turn * skeleton
            )
            picked = jnp.take(table_weights, safe_ids, axis=1) * present[None, :, :, None]
            source_charges = picked.reshape(columns, leaves_dev, nodes_per_turn * skeleton)
            weights = kernel_block(source_coords, point_blocks, target_sq)
            return totals + jnp.einsum(
                "rls,lst->rlt", source_charges, weights, preferred_element_type=jnp.float32
            )

        initial = jnp.zeros((columns, leaves_dev, leaf_points), jnp.float32)
        totals = lax.fori_loop(0, near_slots, near_step, initial)
        totals = lax.fori_loop(0, far_slots // nodes_per_turn, far_step, totals)
        return totals.reshape(columns, local_width).astype(jnp.bfloat16)

    stacked = jnp.concatenate([coords, charges], axis=0).reshape(
        feature_dim + columns, leaves_dev, leaf_points
    )
    incoming, fetched = fetch_blocks(stacked, wanted)
    first_pass = kernel_product(charges, jnp.concatenate([stacked, fetched], axis=1))
    restacked = jnp.concatenate([coords, first_pass], axis=0).reshape(
        feature_dim + columns, leaves_dev, leaf_points
    )
    unused, fetched_again = fetch_blocks(restacked, wanted)
    second_pass = kernel_product(first_pass, jnp.concatenate([restacked, fetched_again], axis=1))
    return (first_pass, second_pass)


def solution(mesh):
    placed = (
        P(None, ("groups", "leaf")),
        P(None, ("groups", "leaf")),
        P(("groups", "leaf"), None),
        P(("groups", "leaf"), None),
        P(("groups", "leaf"), None),
        P(("groups", "leaf"), None),
        P(("groups", "leaf"), None),
        P(None, ("groups", "leaf")),
        P(None, "groups"),
    )
    return jax.shard_map(
        on_device,
        mesh=mesh,
        in_specs=placed,
        out_specs=(P(None, ("groups", "leaf")), P(None, ("groups", "leaf"))),
        check_vma=False,
    )
```

profile of v0, /device:TPU:0, one launch (start us, length us, event | category | flops | bytes accessed | tf_op | source)
XLA Modules:
  0.0 418.5 jit_solution(18038456888509704263)
XLA Ops:
  2.5 7.4 %all-to-all-start = ((s32[16,1,1]{2,1,0:T(1,128)}), s32[16,1,1]{2,1,0:T(1,128)S(1)}, u32[]{:S(2)}, u32[]{:S(2)}) async-start(s32[16,1,1]{2,1,0:T(1,128)} %copy.196), calls=%async_computation | async-start | bytes 16384 | tf_op jit(solution)/shard_map/all_to_all | solution.py:35
  12.4 3.9 all-to-all-done
  19.0 3.9 all-to-all-start.1
  24.7 53.4 %all_gather.17 = bf16[64,2048]{1,0:T(8,128)(2,1)S(1)} all-gather(bf16[64,128]{1,0:T(8,128)(2,1)S(1)} %convolution_convert_fusion.4), channel_id=1, replica_groups=mesh['groups'=2,'leaf'=16] {'leaf'}, dimensions={1}, use_global_device_ids=true | all-gather | bytes 278528 | tf_op jit(solution)/shard_map/all_gather | solution.py:83
  78.0 24.2 %all_gather.15 = bf16[64,2048]{1,0:T(8,128)(2,1)S(1)} all-gather(bf16[64,128]{1,0:T(8,128)(2,1)} %param.30), channel_id=1, replica_groups=mesh['groups'=2,'leaf'=16] {'leaf'}, dimensions={1}, use_global_device_ids=true | all-gather | bytes 278528 | tf_op jit(solution)/shard_map/all_gather | solution.py:61
  103.0 18.2 %all_gather.16 = bf16[64,2048]{1,0:T(8,128)(2,1)S(1)} all-gather(bf16[64,128]{1,0:T(8,128)(2,1)S(1)} %convolution_convert_fusion.5), channel_id=1, replica_groups=mesh['groups'=2,'leaf'=16] {'leaf'}, dimensions={1}, use_global_device_ids=true | all-gather | bytes 278528 | tf_op jit(solution)/shard_map/all_gather | solution.py:82
  123.0 79.2 %while.56 = (s32[]{:T(128)}, f32[64,2,512]{2,0,1:T(8,128)}, s32[2,16]{0,1:T(8,128)S(1)}, bf16[128,18,512]{2,0,1:T(8,128)(2,1)}, f32[2,512]{1,0:T(2,128)}, /*inde...) while((s32[]{:T(128)}, f32[64,2,512]{2,0,1:T(8,128)}, ...), condition=%wide.region_4.7_spmd.clone, body=%wide.region_2.6_spmd.clone.sunk | while | flops 137560080 | bytes 2113701 | solution.py:121
  140.2 2.5 fusion.111
  155.0 2.5 fusion.111
  199.6 2.5 fusion.111
  202.2 32.9 %while.54 = (s32[]{:T(128)}, f32[64,2,512]{2,0,1:T(8,128)}, s32[2,32]{1,0:T(2,128)S(1)}, bf16[64,17,128]{2,0,1:T(8,128)(2,1)S(1)}, f32[2,512]{1,0:T(2,128)}, /*i...) while((s32[]{:T(128)}, f32[64,2,512]{2,0,1:T(8,128)}, ...), condition=%wide.region_8.12_spmd, body=%wide.region_6.11_spmd.sunk | while | flops 137297952 | bytes 1991103 | solution.py:122
  203.7 2.5 fusion.102
  207.9 2.5 fusion.102
  212.0 2.5 fusion.102
  216.1 2.5 fusion.102
  220.2 2.5 fusion.102
  224.3 2.5 fusion.102
  228.4 2.5 fusion.102
  232.5 2.5 fusion.102
  239.3 3.8 all-to-all-start.2
  244.4 53.9 %all_gather.19 = bf16[64,2048]{1,0:T(8,128)(2,1)S(1)} all-gather(bf16[64,128]{1,0:T(8,128)(2,1)S(1)} %convolution_convert_fusion.2), channel_id=1, replica_groups=mesh['groups'=2,'leaf'=16] {'leaf'}, dimensions={1}, use_global_device_ids=true | all-gather | bytes 278528 | tf_op jit(solution)/shard_map/all_gather | solution.py:83
  298.3 23.9 %all_gather.18 = bf16[64,2048]{1,0:T(8,128)(2,1)S(1)} all-gather(bf16[64,128]{1,0:T(8,128)(2,1)S(1)} %convolution_convert_fusion.3), channel_id=1, replica_groups=mesh['groups'=2,'leaf'=16] {'leaf'}, dimensions={1}, use_global_device_ids=true | all-gather | bytes 278528 | tf_op jit(solution)/shard_map/all_gather | solution.py:82
  324.1 66.9 %while.57 = (s32[]{:T(128)}, f32[64,2,512]{2,0,1:T(8,128)S(1)}, s32[2,16]{0,1:T(8,128)S(1)}, bf16[128,18,512]{2,0,1:T(8,128)(2,1)}, f32[2,512]{1,0:T(2,128)S(1)}...) while((s32[]{:T(128)}, f32[64,2,512]{2,0,1:T(8,128)S(1)}, ...), condition=%wide.region_11.15_spmd.clone, body=%wide.region_9.14_spmd.clone.sunk | while | flops 137560080 | bytes 2113701 | solution.py:121
  391.1 26.7 %while.55 = (s32[]{:T(128)}, f32[64,2,512]{2,0,1:T(8,128)S(1)}, s32[2,32]{1,0:T(2,128)S(1)}, bf16[64,17,128]{2,0,1:T(8,128)(2,1)S(1)}, f32[2,512]{1,0:T(2,128)S(...) while((s32[]{:T(128)}, f32[64,2,512]{2,0,1:T(8,128)S(1)}, ...), condition=%wide.region_15.19_spmd, body=%wide.region_13.18_spmd.sunk | while | flops 137297952 | bytes 1991103 | solution.py:122
  (434 shorter events, 194.9 us)
Async XLA Ops:
  0.6 23.6 %copy-start = (bf16[1024,128]{1,0:T(8,128)(2,1)S(1)}, bf16[1024,128]{1,0:T(8,128)(2,1)}, u32[]{:S(2)}) copy-start(bf16[1024,128]{1,0:T(8,128)(2,1)} %param.27) | copy-start | bytes 786436
  2.5 13.7 %all-to-all-start = ((s32[16,1,1]{2,1,0:T(1,128)}), s32[16,1,1]{2,1,0:T(1,128)S(1)}, u32[]{:S(2)}, u32[]{:S(2)}) async-start(s32[16,1,1]{2,1,0:T(1,128)} %copy.196), calls=%async_computation | async-start | bytes 16384 | tf_op jit(solution)/shard_map/all_to_all | solution.py:35
  16.6 0.7 copy-start.11
  16.7 0.7 copy-start.9
  19.0 3.9 copy-start.3
  19.0 5.2 %copy-start.4 = (bf16[64,1024]{1,0:T(8,128)(2,1)S(1)}, bf16[64,1024]{1,0:T(8,128)(2,1)}, u32[]{:S(2)}) copy-start(bf16[64,1024]{1,0:T(8,128)(2,1)} %param.24) | copy-start | bytes 393220
  19.0 5.4 %copy-start.5 = (bf16[256,128]{1,0:T(8,128)(2,1)S(1)}, bf16[256,128]{1,0:T(8,128)(2,1)}, u32[]{:S(2)}) copy-start(bf16[256,128]{1,0:T(8,128)(2,1)} %param.28) | copy-start | bytes 196612
  19.0 5.5 %copy-start.7 = (bf16[128,128]{1,0:T(8,128)(2,1)S(1)}, bf16[128,128]{1,0:T(8,128)(2,1)}, u32[]{:S(2)}) copy-start(bf16[128,128]{1,0:T(8,128)(2,1)} %param.29) | copy-start | bytes 98308
  19.0 102.4 %all-to-all-start.1 = ((bf16[128,16,512]{2,0,1:T(8,128)(2,1)}), bf16[128,16,512]{2,0,1:T(8,128)(2,1)S(1)}, u32[]{:S(2)}, u32[]{:S(2)}) async-start(bf16[128,16,512]{2,0,1:T(8,128)(2,1)} %select_bitcast_fusion.3), calls=%async_computation.1 | async-start | bytes 4194304 | tf_op jit(solution)/shard_map/all_to_all | solution.py:37
  123.0 79.2 %copy-start.8 = (s32[2,32]{1,0:T(2,128)S(1)}, s32[2,32]{1,0:T(2,128)}, u32[]{:S(2)}) copy-start(s32[2,32]{1,0:T(2,128)} %param.26) | copy-start | bytes 772
  236.0 0.7 copy-start.1
  236.8 0.8 copy-start.12
  239.3 4.7 %copy-start.2 = (bf16[64,2,512]{2,0,1:T(8,128)(2,1)S(1)}, bf16[64,2,512]{2,0,1:T(8,128)(2,1)}, u32[]{:S(2)}) copy-start(bf16[64,2,512]{2,0,1:T(8,128)(2,1)} %copy-done.1) | copy-start | bytes 393220
  239.3 83.2 %all-to-all-start.2 = ((bf16[128,16,512]{2,0,1:T(8,128)(2,1)}), bf16[128,16,512]{2,0,1:T(8,128)(2,1)S(1)}, u32[]{:S(2)}, u32[]{:S(2)}) async-start(bf16[128,16,512]{2,0,1:T(8,128)(2,1)} %select_bitcast_fusion.2), calls=%async_computation.2 | async-start | bytes 4194304 | tf_op jit(solution)/shard_map/all_to_all | solution.py:37
  322.5 1.7 copy-start.6
  322.5 1.7 copy-start.10
where the time goes:
time: 421 us; the launch traced here: 418 us
  blocking collectives  173 us (41%)
  matrix products  103 us (24%)
  local copies, waits for them, and re-layouts  101 us (24%)
  other arithmetic  19.1 us (5%)
  starting transfers between devices  15.1 us (4%)
    all_gather x2, blocking collectives, kernel_product(): lax.all_gather(upper_term, 'leaf', axis=1, tiled=True)  107 us
    gather x32, local copies, waits for them, and re-layouts, near_step(): blocks = jnp.take(source_pool, chosen, axis=1)  71.3 us
    dot_general x32, matrix products, near_step(): jnp.einsum('rls,lst->rlt', source_charges, weights, preferred_element_typ...  67.9 us
    all_gather x2, blocking collectives, kernel_product(): lax.all_gather(device_weights, 'leaf', axis=1, tiled=True)  42.1 us
    dot_general x16, matrix products, far_step(): jnp.einsum('rls,lst->rlt', source_charges, weights, preferred_element_typ...  34 us
    all_gather x1, blocking collectives, on_device(): all_points = lax.all_gather(node_points, 'leaf', axis=1, tiled=True)  24.2 us
    gather x16, local copies, waits for them, and re-layouts, far_step(): jnp.take(table_weights, safe_ids, axis=1) * present[None, :, :, None]  9.15 us
    gather x16, local copies, waits for them, and re-layouts, far_step(): jnp.take(table_points, safe_ids, axis=1)  9.12 us
  transfers between devices with their start and end apart: 3, of which 1 were waited for; matrix products, arithmetic and copies ran while one was open for 2% of the time, Pallas kernels for 0%

commit v1 on v0

v1 whole, which is shorter than its diff:
```python
import functools

import jax
import jax.numpy as jnp
from jax import lax
from jax.experimental import pallas as pl
from jax.experimental.pallas import tpu as pltpu
from jax.sharding import PartitionSpec as P

BRANCH = 16
EXTRA = 16
DEPTH = 128
GROUP = 4

bf16 = jnp.bfloat16
f32 = jnp.float32

CONTRACT_LAST = (((1,), (1,)), ((), ()))


def matmul(left, right):
    return jnp.dot(left, right, preferred_element_type=f32)


def square_parts(points):
    minus = -jnp.sum(points * points, axis=0, keepdims=True)
    high = minus.astype(bf16).astype(f32)
    rest = minus - high
    middle = rest.astype(bf16).astype(f32)
    low = rest - middle
    return high, middle, low


def extra_rows(parts, first, width):
    row = lax.broadcasted_iota(jnp.int32, (EXTRA, width), 0)
    rows = jnp.where(row < 6, 1.0, 0.0).astype(f32)
    for offset, part in enumerate(parts):
        rows = jnp.where(row == first + offset, jnp.broadcast_to(part, (EXTRA, width)), rows)
    return rows


def put_sources(sources_ref, place, points):
    dim, width = points.shape
    columns = pl.ds(place, width)
    sources_ref[0:dim, columns] = points
    parts = square_parts(points.astype(f32))
    sources_ref[dim : dim + EXTRA, columns] = extra_rows(parts, 3, width).astype(bf16)


def put_targets(targets_ref, coords_ref, leaves_dev, leaf_points):
    dim = coords_ref.shape[0]
    for leaf in range(leaves_dev):
        points = coords_ref[:, leaf * leaf_points : (leaf + 1) * leaf_points].astype(f32)
        extra = extra_rows(square_parts(points), 0, leaf_points)
        blank = jnp.zeros((DEPTH - dim - EXTRA, leaf_points), f32)
        stacked = jnp.concatenate([2.0 * points, extra, blank], axis=0)
        targets_ref[leaf] = stacked.T.astype(bf16)


def skeleton_weights(charges, leaf_interp_ref, node_interp_ref, upper_interp_ref, leaves_dev):
    leaf_points = charges.shape[1] // leaves_dev
    parts = []
    for leaf in range(leaves_dev):
        span = slice(leaf * leaf_points, (leaf + 1) * leaf_points)
        parts.append(matmul(charges[:, span], leaf_interp_ref[span, :]).astype(bf16))
    device_weights = matmul(jnp.concatenate(parts, axis=1), node_interp_ref[...]).astype(bf16)
    upper_term = matmul(device_weights, upper_interp_ref[...]).astype(bf16)
    return device_weights, upper_term


def message_kernel(
    leaves_dev,
    coords_ref,
    charges_ref,
    points_ref,
    leaf_interp_ref,
    node_interp_ref,
    upper_interp_ref,
    out_ref,
):
    local = coords_ref.shape[1]
    skeleton = points_ref.shape[1]
    charges = charges_ref[...]
    weights, term = skeleton_weights(
        charges, leaf_interp_ref, node_interp_ref, upper_interp_ref, leaves_dev
    )
    out_ref[:, 0:local] = coords_ref[...]
    out_ref[:, local : 2 * local] = charges
    place = 2 * local
    out_ref[:, place : place + skeleton] = points_ref[...]
    out_ref[:, place + skeleton : place + 2 * skeleton] = weights
    out_ref[:, place + 2 * skeleton : place + 3 * skeleton] = term


def kernel_sum(targets, sources, charges):
    total = targets.shape[0]
    step = min(total, 256)
    out = []
    for begin in range(0, total, step):
        exponent = matmul(targets[begin : begin + step], sources)
        kernel = jnp.exp(exponent).astype(bf16)
        out.append(
            lax.dot_general(kernel, charges, CONTRACT_LAST, preferred_element_type=f32)
        )
    return jnp.concatenate(out, axis=0)


def product_kernel(
    dims,
    near_ref,
    far_ref,
    coords_pool_ref,
    charges_pool_ref,
    coords_ref,
    upper_points_ref,
    *rest,
):
    (leaves_dev, leaf_points, skeleton, peers, charges_at, weights_at, last) = dims
    if last:
        out_ref, targets_ref, sources_ref, far_weights_ref, upper_ref, total_ref, counts_ref = rest
    else:
        (
            leaf_interp_ref,
            node_interp_ref,
            upper_interp_ref,
            out_ref,
            message_ref,
            targets_ref,
            sources_ref,
            far_weights_ref,
            upper_ref,
            total_ref,
            counts_ref,
        ) = rest
    dim = coords_ref.shape[0]
    columns = coords_pool_ref.shape[1]
    near_slots = near_ref.shape[1]
    far_slots = far_ref.shape[1]
    n_sub = peers // BRANCH
    nodes = peers + n_sub
    points_at = 2 * leaves_dev * leaf_points
    terms_at = weights_at + skeleton

    put_targets(targets_ref, coords_ref, leaves_dev, leaf_points)
    sources_ref[...] = jnp.zeros_like(sources_ref)

    for sub in range(n_sub):
        span = slice(terms_at, terms_at + skeleton)
        terms = [
            charges_pool_ref[sub * BRANCH + child, :, span].astype(f32) for child in range(BRANCH)
        ]
        while len(terms) > 1:
            terms = [a + b for a, b in zip(terms[::2], terms[1::2])]
        upper_ref[sub] = terms[0].astype(bf16)

    for leaf in range(leaves_dev):
        for node in range(nodes):
            counts_ref[leaf, node] = 0
        for slot in range(far_slots):
            named = far_ref[leaf, slot]

            @pl.when(named >= 0)
            def _():
                counts_ref[leaf, named] = counts_ref[leaf, named] + 1

    group_width = GROUP * skeleton
    full_groups = -(-nodes // GROUP)

    def far_points(node):
        if isinstance(node, int) and node >= peers:
            begin = (node - peers) * skeleton
            return upper_points_ref[:, begin : begin + skeleton], upper_ref[node - peers]
        return (
            coords_pool_ref[node, :, points_at : points_at + skeleton],
            charges_pool_ref[node, :, weights_at : weights_at + skeleton],
        )

    def far_group(members, fresh):
        width = len(members) * skeleton
        weights_of = []
        for position, node in enumerate(members):
            points, weights = far_points(node)
            put_sources(sources_ref, position * skeleton, points)
            weights_of.append(weights.astype(f32))
        for leaf in range(leaves_dev):
            for position, node in enumerate(members):
                scaled = weights_of[position] * counts_ref[leaf, node].astype(f32)
                high = scaled.astype(bf16)
                low = (scaled - high.astype(f32)).astype(bf16)
                place = pl.ds(position * skeleton, skeleton)
                far_weights_ref[0:columns, place] = high
                far_weights_ref[columns : 2 * columns, place] = low
            both = kernel_sum(
                targets_ref[leaf], sources_ref[:, 0:width], far_weights_ref[:, 0:width]
            )
            added = both[:, 0:columns] + both[:, columns : 2 * columns]
            total_ref[leaf] = added if fresh else total_ref[leaf] + added

    upper_nodes = list(range(peers, nodes))
    for begin in range(0, len(upper_nodes), GROUP):
        far_group(upper_nodes[begin : begin + GROUP], begin == 0)

    def far_step(turn, carry):
        far_group([turn * GROUP + member for member in range(GROUP)], False)
        return carry

    lax.fori_loop(0, peers // GROUP, far_step, 0)

    def used(leaf):
        count = jnp.int32(0)
        for slot in range(near_slots):
            count = count + (near_ref[leaf, slot] >= 0).astype(jnp.int32)
        return count

    for leaf in range(leaves_dev):

        def near_step(slot, carry):
            named = near_ref[leaf, slot]
            device = named // leaves_dev
            begin = pl.multiple_of((named - device * leaves_dev) * leaf_points, leaf_points)
            points = coords_pool_ref[device, :, pl.ds(begin, leaf_points)]
            put_sources(sources_ref, 0, points)
            charges = charges_pool_ref[device, :, pl.ds(charges_at + begin, leaf_points)]
            total_ref[leaf] += kernel_sum(targets_ref[leaf], sources_ref[...], charges)
            return carry

        lax.fori_loop(0, used(leaf), near_step, 0)

    parts = [total_ref[leaf].T.astype(bf16) for leaf in range(leaves_dev)]
    result = jnp.concatenate(parts, axis=1)
    out_ref[...] = result
    if not last:
        local = leaves_dev * leaf_points
        weights, term = skeleton_weights(
            result, leaf_interp_ref, node_interp_ref, upper_interp_ref, leaves_dev
        )
        message_ref[:, 0:local] = result
        message_ref[:, local : local + skeleton] = weights
        message_ref[:, local + skeleton : local + 2 * skeleton] = term


def on_device(
    coords,
    charges,
    near_lists,
    far_lists,
    leaf_interp,
    node_interp,
    upper_interp,
    node_points,
    upper_points,
):
    dim, local = coords.shape
    columns = charges.shape[0]
    leaves_dev = near_lists.shape[0]
    leaf_points = local // leaves_dev
    skeleton = leaf_interp.shape[1]
    peers = lax.axis_size("leaf")
    nodes = peers + peers // BRANCH

    vmem = pl.BlockSpec(memory_space=pltpu.VMEM)
    smem = pl.BlockSpec(memory_space=pltpu.SMEM)
    params = pltpu.CompilerParams(vmem_limit_bytes=48 * 1024 * 1024)

    message = pl.pallas_call(
        functools.partial(message_kernel, leaves_dev),
        out_shape=jax.ShapeDtypeStruct((dim, 2 * local + 3 * skeleton), bf16),
        in_specs=[vmem] * 6,
        out_specs=vmem,
        compiler_params=params,
    )(coords, charges, node_points, leaf_interp, node_interp, upper_interp)
    pool = lax.all_gather(message, "leaf", axis=0)

    scratch = [
        pltpu.VMEM((leaves_dev, leaf_points, DEPTH), bf16),
        pltpu.VMEM((DEPTH, leaf_points), bf16),
        pltpu.VMEM((2 * columns, GROUP * skeleton), bf16),
        pltpu.VMEM((peers // BRANCH, columns, skeleton), bf16),
        pltpu.VMEM((leaves_dev, leaf_points, columns), f32),
        pltpu.SMEM((leaves_dev, nodes), jnp.int32),
    ]
    flat = jax.ShapeDtypeStruct((columns, local), bf16)
    sent = jax.ShapeDtypeStruct((columns, local + 2 * skeleton), bf16)

    dims = (leaves_dev, leaf_points, skeleton, peers)
    first, message = pl.pallas_call(
        functools.partial(product_kernel, dims + (local, 2 * local + skeleton, False)),
        out_shape=(flat, sent),
        in_specs=[smem] * 2 + [vmem] * 7,
        out_specs=(vmem, vmem),
        scratch_shapes=scratch,
        compiler_params=params,
    )(
        near_lists,
        far_lists,
        pool,
        pool,
        coords,
        upper_points,
        leaf_interp,
        node_interp,
        upper_interp,
    )
    again = lax.all_gather(message, "leaf", axis=0)
    second = pl.pallas_call(
        functools.partial(product_kernel, dims + (0, local, True)),
        out_shape=flat,
        in_specs=[smem] * 2 + [vmem] * 4,
        out_specs=vmem,
        scratch_shapes=scratch,
        compiler_params=params,
    )(near_lists, far_lists, pool, again, coords, upper_points)
    return (first, second)


def solution(mesh):
    placed = (
        P(None, ("groups", "leaf")),
        P(None, ("groups", "leaf")),
        P(("groups", "leaf"), None),
        P(("groups", "leaf"), None),
        P(("groups", "leaf"), None),
        P(("groups", "leaf"), None),
        P(("groups", "leaf"), None),
        P(None, ("groups", "leaf")),
        P(None, "groups"),
    )
    return jax.shard_map(
        on_device,
        mesh=mesh,
        in_specs=placed,
        out_specs=(P(None, ("groups", "leaf")), P(None, ("groups", "leaf"))),
        check_vma=False,
    )
```

time: 421 us -> 181 us (0.43)
  blocking collectives: 173 us -> 0 us
  matrix products: 103 us -> 0 us
  waiting for transfers between devices: 3.87 us -> 101 us
  local copies, waits for them, and re-layouts: 101 us -> 14.7 us
  Pallas kernels: 0 us -> 50.5 us
  other arithmetic: 19.1 us -> 0 us
  starting transfers between devices: 15.1 us -> 0.08 us
  between operations: 0.99 us -> 14.1 us
    all_gather x5 -> x0, blocking collectives: 173 us -> none  [the longest x2 107 us: kernel_product(): lax.all_gather(upper_term, 'leaf', axis=1, tiled=True)]
    dot_general x54 -> x0, matrix products: 103 us -> none  [the longest x32 67.9 us: near_step(): jnp.einsum('rls,lst->rlt', source_charges, weights, preferred_element_typ...]
    all_gather x0 -> x2, waiting for transfers between devices: none -> 101 us  [the longest x1 57.6 us: on_device(): pool = lax.all_gather(message, 'leaf', axis=0)]
    gather x66 -> x0, local copies, waits for them, and re-layouts: 91.1 us -> none  [the longest x32 71.3 us: near_step(): blocks = jnp.take(source_pool, chosen, axis=1)]
    pallas_call x0 -> x3, Pallas kernels: none -> 50.5 us  [the longest x1 25.5 us: on_device(): pl.pallas_call(functools.partial(product_kernel, dims + (0, local, True))...]
    all_to_all x3 -> x0, starting transfers between devices: 15.1 us -> none  [the longest x2 7.71 us: fetch_blocks(): lax.all_to_all(served, 'leaf', split_axis=1, concat_axis=1, tiled=True)]
    unnamed x32 -> x38, local copies, waits for them, and re-layouts: 4.17 us -> 14.7 us
    select_n x35 -> x0, other arithmetic: 6.19 us -> none  [the longest x3 3.19 us: fetch_blocks(): served = jnp.take(stacked, jnp.maximum(incoming, 0), axis=1)]
  transfers between devices with their start and end apart: 3 -> 2, of which waited for: 1 -> 2; matrix products, arithmetic and copies ran while one was open for 2% -> 0% of each run, Pallas kernels for 0% -> 0%
where the time goes in v1:
time: 181 us; the launch traced here: 180 us
  waiting for transfers between devices  101 us (56%)
  Pallas kernels  50.5 us (28%)
  local copies, waits for them, and re-layouts  14.7 us (8%)
  between operations  14.1 us (8%)
    all_gather x1, waiting for transfers between devices, on_device(): pool = lax.all_gather(message, 'leaf', axis=0)  57.6 us
    all_gather x1, waiting for transfers between devices, on_device(): again = lax.all_gather(message, 'leaf', axis=0)  43.1 us
    pallas_call x1, Pallas kernels, on_device(): pl.pallas_call(functools.partial(product_kernel, dims + (0, local, True))...  25.5 us
    pallas_call x1, Pallas kernels, on_device(): pl.pallas_call(functools.partial(product_kernel, dims + (local, 2 * local...  23.9 us
    unnamed x38, local copies, waits for them, and re-layouts  14.7 us
  transfers between devices with their start and end apart: 2, of which 2 were waited for; matrix products, arithmetic and copies ran while one was open for 0% of the time, Pallas kernels for 0%

profile of v1, /device:TPU:0, one launch (start us, length us, event | category | flops | bytes accessed | tf_op | source)
XLA Modules:
  0.0 180.2 jit_solution(7865247898116451395)
XLA Ops:
  7.2 0.0 all-gather.5.cloned.1.call-start
  7.2 0.9 copy-done.2
  8.1 0.9 copy-done.5
  9.1 0.8 copy-done.7
  9.9 0.8 copy-done.9
  10.7 0.9 copy-done.11
  11.6 0.7 copy-done.14
  12.3 1.1 shard_map.104
  13.4 0.0 all-gather.5.cloned.1.call-update
  13.5 0.0 all-gather.7.cloned.1.call-start
  13.5 57.6 %all-gather.5.cloned.1.call-done = bf16[1024,2432]{1,0:T(8,128)(2,1)} async-done(((bf16[64,2432]{1,0:T(8,128)(2,1)}), bf16[1024,2432]{1,0:T(8,128)(2,1)}) %all-gather.5.cloned.1.call-update) | async-done | bytes 4980752 | tf_op jit(solution)/shard_map/all_gather | solution.py:272
  71.1 2.4 %copy-done = bf16[1024,2432]{1,0:T(8,128)(2,1)S(1)} copy-done((bf16[1024,2432]{1,0:T(8,128)(2,1)S(1)}, bf16[1024,2432]{1,0:T(8,128)(2,1)}, u32[]{:S(2)}) %copy-start) | copy-done | bytes 4980760
  73.5 0.9 copy-done.3
  74.4 0.9 copy-done.6
  75.3 0.8 copy-done.8
  76.2 0.8 copy-done.10
  76.9 0.7 copy-done.12
  77.7 0.7 copy-done.15
  78.3 0.7 copy-done.17
  79.0 23.9 %shard_map.105 = (bf16[64,1024]{1,0:T(8,128)(2,1)}, bf16[64,1280]{1,0:T(8,128)(2,1)}) custom-call(s32[2,16]{1,0:T(2,128)S(1)} %copy-done.15, s32[2,32]{1,0:T(2,128)S(1)} %copy-done.17, bf16[16,64,2432]{2,1,0:T(8,128)(2,1)S(1)} %bitcast.3, bf16[16,64,2432]{2,1,0:T(8,128)(2,1)S(1)} %bitcast.4, bf16[64,1024]{1,0:T(8,128)(2,1)S(1)} %copy-done.3, ...), custom_call_target="tpu_custom_call" | custom-call | tf_op jit(solution)/shard_map/pallas_call | solution.py:286
  103.0 0.0 all-gather.7.cloned.1.call-update
  103.0 43.1 %all-gather.7.cloned.1.call-done = bf16[1024,1280]{1,0:T(8,128)(2,1)} async-done(((bf16[64,1280]{1,0:T(8,128)(2,1)}), bf16[1024,1280]{1,0:T(8,128)(2,1)}) %all-gather.7.cloned.1.call-update) | async-done | bytes 2621456 | tf_op jit(solution)/shard_map/all_gather | solution.py:304
  146.1 1.7 copy-done.1
  147.9 25.5 %shard_map.106 = bf16[64,1024]{1,0:T(8,128)(2,1)} custom-call(s32[2,16]{1,0:T(2,128)S(1)} %copy-done.16, s32[2,32]{1,0:T(2,128)S(1)} %copy-done.18, bf16[16,64,2432]{2,1,0:T(8,128)(2,1)} %bitcast.2, bf16[16,64,1280]{2,1,0:T(8,128)(2,1)S(1)} %bitcast.5, bf16[64,1024]{1,0:T(8,128)(2,1)S(1)} %copy-done.4, bf16[64,128]{1,0:T(8,128)(2,1)S(1)} %copy-done.13), custom_call_target="tpu_custom_call" | custom-call | tf_op jit(solution)/shard_map/pallas_call | solution.py:305
  (23 shorter events, 0.0 us)
Async XLA Ops:
  7.2 63.9 %all-gather.5.cloned.1.call-start = ((), (), s32[]{:S(2)}) async-start(), calls=%async_computation | async-start | bytes 5292032 | tf_op jit(solution)/shard_map/all_gather | solution.py:272
  7.2 0.9 copy-start.2
  8.1 0.9 copy-start.5
  9.1 0.8 copy-start.7
  9.9 0.8 copy-start.9
  10.7 0.9 copy-start.11
  11.6 0.7 copy-start.14
  13.5 132.7 %all-gather.7.cloned.1.call-start = ((), (), s32[]{:S(2)}) async-start(), calls=%async_computation.1 | async-start | bytes 2785280 | tf_op jit(solution)/shard_map/all_gather | solution.py:304
  71.1 2.4 %copy-start = (bf16[1024,2432]{1,0:T(8,128)(2,1)S(1)}, bf16[1024,2432]{1,0:T(8,128)(2,1)}, u32[]{:S(2)}) copy-start(bf16[1024,2432]{1,0:T(8,128)(2,1)} %all-gather.5.cloned.1.call-done) | copy-start | bytes 14942212
  73.5 0.9 copy-start.3
  74.4 0.9 copy-start.6
  75.3 0.8 copy-start.8
  76.2 0.8 copy-start.10
  76.9 0.7 copy-start.12
  77.7 0.7 copy-start.15
  78.3 0.7 copy-start.17
  79.0 67.1 %copy-start.4 = (bf16[64,1024]{1,0:T(8,128)(2,1)S(1)}, bf16[64,1024]{1,0:T(8,128)(2,1)}, u32[]{:S(2)}) copy-start(bf16[64,1024]{1,0:T(8,128)(2,1)} %coords_ref.5) | copy-start | bytes 393220
  79.0 67.1 %copy-start.13 = (bf16[64,128]{1,0:T(8,128)(2,1)S(1)}, bf16[64,128]{1,0:T(8,128)(2,1)}, u32[]{:S(2)}) copy-start(bf16[64,128]{1,0:T(8,128)(2,1)} %upper_points_ref.3) | copy-start | bytes 49156
  79.0 67.1 %copy-start.16 = (s32[2,16]{1,0:T(2,128)S(1)}, s32[2,16]{1,0:T(2,128)}, u32[]{:S(2)}) copy-start(s32[2,16]{1,0:T(2,128)} %near_ref.3) | copy-start | bytes 388
  79.0 67.1 %copy-start.18 = (s32[2,32]{1,0:T(2,128)S(1)}, s32[2,32]{1,0:T(2,128)}, u32[]{:S(2)}) copy-start(s32[2,32]{1,0:T(2,128)} %far_ref.3) | copy-start | bytes 772
  146.1 1.7 copy-start.1
Sparse Core Ops, SparseCore 0:
  13.6 57.4 all-gather.4
  103.1 42.9 all-gather.6

commit v2 on v0

v2 whole, which is shorter than its diff:
```python
import functools

import jax
import jax.numpy as jnp
import numpy as np
from jax import lax
from jax.experimental import pallas as pl
from jax.experimental.pallas import tpu as pltpu
from jax.sharding import PartitionSpec as P

BRANCH = 16
EXTRA = 16
DEPTH = 128
CORES = 2

bf16 = jnp.bfloat16
f32 = jnp.float32
i32 = jnp.int32

CONTRACT_LAST = (((1,), (1,)), ((), ()))


def matmul(left, right):
    return jnp.dot(left, right, preferred_element_type=f32)


def square_parts(points):
    minus = -jnp.sum(points * points, axis=0, keepdims=True)
    high = minus.astype(bf16).astype(f32)
    rest = minus - high
    middle = rest.astype(bf16).astype(f32)
    low = rest - middle
    return high, middle, low


def extra_rows(parts, first, width):
    row = lax.broadcasted_iota(i32, (EXTRA, width), 0)
    rows = jnp.where(row < 6, 1.0, 0.0).astype(f32)
    for offset, part in enumerate(parts):
        rows = jnp.where(row == first + offset, jnp.broadcast_to(part, (EXTRA, width)), rows)
    return rows


def put_sources(sources_ref, points):
    dim, width = points.shape
    sources_ref[0:dim, :] = points
    parts = square_parts(points.astype(f32))
    sources_ref[dim : dim + EXTRA, :] = extra_rows(parts, 3, width).astype(bf16)
    sources_ref[dim + EXTRA :, :] = jnp.zeros((DEPTH - dim - EXTRA, width), bf16)


def target_rows(points):
    dim, width = points.shape
    points = points.astype(f32)
    extra = extra_rows(square_parts(points), 0, width)
    blank = jnp.zeros((DEPTH - dim - EXTRA, width), f32)
    return jnp.concatenate([2.0 * points, extra, blank], axis=0).T.astype(bf16)


def split(values):
    high = values.astype(bf16)
    return high, (values - high.astype(f32)).astype(bf16)


def kernel_sum(targets, sources, charges):
    total = targets.shape[0]
    step = min(total, 256)
    out = []
    for begin in range(0, total, step):
        exponent = matmul(targets[begin : begin + step], sources)
        kernel = jnp.exp(exponent).astype(bf16)
        out.append(lax.dot_general(kernel, charges, CONTRACT_LAST, preferred_element_type=f32))
    return jnp.concatenate(out, axis=0)


def skeleton_weights(charges, leaf_interp_ref, node_interp_ref, upper_interp_ref):
    leaf_points = charges[0].shape[1]
    parts = []
    for leaf, block in enumerate(charges):
        span = slice(leaf * leaf_points, (leaf + 1) * leaf_points)
        parts.append(matmul(block, leaf_interp_ref[span, :]).astype(bf16))
    device_weights = matmul(jnp.concatenate(parts, axis=1), node_interp_ref[...]).astype(bf16)
    upper_term = matmul(device_weights, upper_interp_ref[...]).astype(bf16)
    return device_weights, upper_term


def message_kernel(
    coords_ref, charges_ref, points_ref, leaf_ref, node_ref, upper_ref, part0_ref, part1_ref
):
    half = coords_ref.shape[1] // 2
    skeleton = points_ref.shape[1]
    charges = [charges_ref[:, 0:half], charges_ref[:, half:]]
    weights, term = skeleton_weights(charges, leaf_ref, node_ref, upper_ref)
    part0_ref[:, 0:half] = charges[0]
    part0_ref[:, half : half + skeleton] = weights
    part0_ref[:, half + skeleton : 2 * half + skeleton] = coords_ref[:, 0:half]
    part0_ref[:, 2 * half + skeleton :] = points_ref[...]
    part1_ref[:, 0:half] = charges[1]
    part1_ref[:, half : half + skeleton] = term
    part1_ref[:, half + skeleton :] = coords_ref[:, half:]


def joined_kernel(mine_ref, other_ref, leaf_ref, node_ref, upper_ref, out_ref, part0_ref, part1_ref):
    half = mine_ref.shape[1] // 2
    skeleton = node_ref.shape[1]
    result = (mine_ref[...] + other_ref[...]).astype(bf16)
    out_ref[...] = result
    charges = [result[:, 0:half], result[:, half:]]
    weights, term = skeleton_weights(charges, leaf_ref, node_ref, upper_ref)
    part0_ref[:, 0:half] = charges[0]
    part0_ref[:, half : half + skeleton] = weights
    part1_ref[:, 0:half] = charges[1]
    part1_ref[:, half : half + skeleton] = term


def added_kernel(mine_ref, other_ref, out_ref):
    out_ref[...] = (mine_ref[...] + other_ref[...]).astype(bf16)


def stage_kernel(stage, *refs):
    spots, n_spots, n_sub, leaf_points, skeleton, first, last, with_targets = stage
    refs = list(refs)
    table_ref = refs.pop(0)
    pairs = [(refs.pop(0), refs.pop(0)) for _ in spots]
    charge_pairs = [(refs.pop(0), refs.pop(0)) for _ in spots]
    if with_targets:
        coords_refs = (refs.pop(0), refs.pop(0))
    else:
        targets_ref = refs.pop(0)
    if not first:
        total_in_ref, sums_in_ref = refs.pop(0), refs.pop(0)
    if last:
        upper_points_ref = refs.pop(0)
    if with_targets:
        targets_ref = refs.pop(0)
    if last:
        mine_ref, other_ref, total_ref, sums_ref = (refs.pop(0) for _ in range(4))
    else:
        total_ref, sums_ref = refs.pop(0), refs.pop(0)
    near_ref, far_ref, far_charges_ref, charges_ref = refs

    columns = charge_pairs[0][0].shape[0]
    points_at = leaf_points + skeleton
    skeletons_at = points_at + leaf_points
    targets = 2 * CORES

    if with_targets:
        for core in range(CORES):
            for leaf in range(2):
                span = slice(leaf * leaf_points, (leaf + 1) * leaf_points)
                targets_ref[core * 2 + leaf] = target_rows(coords_refs[core][:, span])
    if first:
        total_ref[...] = jnp.zeros_like(total_ref)
        sums_ref[...] = jnp.zeros_like(sums_ref)
    else:
        total_ref[...] = total_in_ref[...]
        sums_ref[...] = sums_in_ref[...]

    def far_part(points, weights, entries):
        width = len(points) * skeleton
        put_sources(far_ref.at[:, 0:width], jnp.concatenate(points, axis=1))
        for target in range(targets):
            for position, (block, entry) in enumerate(zip(weights, entries)):
                high, low = split(block * table_ref[target, entry].astype(f32))
                span = slice(position * skeleton, (position + 1) * skeleton)
                far_charges_ref[0:columns, span] = high
                far_charges_ref[columns:, span] = low
            total_ref[target] += kernel_sum(
                targets_ref[target], far_ref[:, 0:width], far_charges_ref[:, 0:width]
            )

    for position, spot in enumerate(spots):
        part0_ref, part1_ref = charge_pairs[position]
        term = part1_ref[:, leaf_points : leaf_points + skeleton].astype(f32)
        sums_ref[table_ref[targets, spot]] += term
        for leaf in range(2):
            place = position * 2 + leaf
            put_sources(
                near_ref.at[place], pairs[position][leaf][:, points_at : points_at + leaf_points]
            )
            charges_ref[place] = charge_pairs[position][leaf][:, 0:leaf_points]

    far_part(
        [pair[0][:, skeletons_at : skeletons_at + skeleton] for pair in pairs],
        [
            pair[0][:, leaf_points : leaf_points + skeleton].astype(f32)
            for pair in charge_pairs
        ],
        [2 * n_spots + spot for spot in spots],
    )
    if last:
        for begin in range(0, n_sub, 2):
            subs = range(begin, min(begin + 2, n_sub))
            far_part(
                [upper_points_ref[:, sub * skeleton : (sub + 1) * skeleton] for sub in subs],
                [sums_ref[sub] for sub in subs],
                [3 * n_spots + sub for sub in subs],
            )

    def near_step(turn, carry):
        place, target = turn // targets, turn % targets
        times = table_ref[target, spots[0] * 2 + place]

        def once(_, carry):
            total_ref[target, :, 0:columns] += kernel_sum(
                targets_ref[target], near_ref[place], charges_ref[place]
            )
            return carry

        return lax.fori_loop(0, times, once, carry)

    lax.fori_loop(0, 2 * len(spots) * targets, near_step, 0)

    if last:
        for core, ref in enumerate((mine_ref, other_ref)):
            for leaf in range(2):
                total = total_ref[core * 2 + leaf].T
                span = slice(leaf * leaf_points, (leaf + 1) * leaf_points)
                ref[:, span] = total[0:columns] + total[columns:]


def whole_block(shape):
    return pl.BlockSpec(shape, lambda i: (0,) * len(shape))


def call(body, args, out_shapes, scratch=(), flops=0):
    specs = [
        pl.BlockSpec(memory_space=pltpu.SMEM) if arg.dtype == i32 else whole_block(arg.shape)
        for arg in args
    ]
    moved = sum(arg.size * arg.dtype.itemsize for arg in args)
    return pl.pallas_call(
        body,
        grid=(1,),
        out_shape=out_shapes,
        in_specs=specs,
        out_specs=[whole_block(out.shape) for out in out_shapes],
        scratch_shapes=list(scratch),
        compiler_params=pltpu.CompilerParams(vmem_limit_bytes=56 * 1024 * 1024),
        cost_estimate=pl.CostEstimate(flops=flops, bytes_accessed=moved, transcendentals=0),
    )(*args)


def ring_order(chips):
    if chips == 8:
        return [0, 2, 4, 6, 7, 5, 3, 1]
    return list(range(chips))


def spots_of(peers):
    ring = ring_order(peers // CORES)
    chips = len(ring)
    found = np.zeros((peers, chips), np.int32)
    for place, chip in enumerate(ring):
        met = [chip]
        for hop in range(1, chips // 2):
            met += [ring[(place - hop) % chips], ring[(place + hop) % chips]]
        met.append(ring[(place + chips // 2) % chips])
        for core in range(CORES):
            found[chip * CORES + core] = [other * CORES + core for other in met]
    return found


def on_device(
    coords,
    charges,
    near_lists,
    far_lists,
    leaf_interp,
    node_interp,
    upper_interp,
    node_points,
    upper_points,
):
    dim, local = coords.shape
    columns = charges.shape[0]
    leaf_points = local // 2
    skeleton = leaf_interp.shape[1]
    peers = lax.axis_size("leaf")
    me = lax.axis_index("leaf")
    n_sub = peers // BRANCH
    ring = ring_order(peers // CORES)
    chips = len(ring)
    near_slots = near_lists.shape[1]

    def along(step):
        return [
            (ring[place] * CORES + core, ring[(place + step) % chips] * CORES + core)
            for place in range(chips)
            for core in range(CORES)
        ]

    to_right = functools.partial(lax.ppermute, axis_name="leaf", perm=along(1))
    to_left = functools.partial(lax.ppermute, axis_name="leaf", perm=along(-1))
    to_sibling = functools.partial(
        lax.ppermute, axis_name="leaf", perm=[(device, device ^ 1) for device in range(peers)]
    )

    def shape(*extent, dtype=bf16):
        return jax.ShapeDtypeStruct(extent, dtype)

    maps = [leaf_interp, node_interp, upper_interp]
    parts = call(
        message_kernel,
        [coords, charges, node_points] + maps,
        [
            shape(dim, 2 * leaf_points + 2 * skeleton),
            shape(dim, 2 * leaf_points + skeleton),
        ],
    )

    lists = jnp.concatenate([near_lists, far_lists], axis=1)
    lists = jnp.concatenate([lists, to_sibling(lists)], axis=0)
    sibling_coords = to_sibling(coords)
    spots = lax.dynamic_index_in_dim(jnp.asarray(spots_of(peers)), me, 0, keepdims=False)
    near_ids = (spots[:, None] * 2 + jnp.arange(2)[None, :]).reshape(-1)
    far_ids = jnp.concatenate([spots, peers + jnp.arange(n_sub)])
    counts = jnp.concatenate(
        [
            jnp.sum((lists[:, :near_slots, None] == near_ids).astype(i32), axis=1),
            jnp.sum((lists[:, near_slots:, None] == far_ids).astype(i32), axis=1),
        ],
        axis=1,
    )
    branch = jnp.pad(spots // BRANCH, (0, counts.shape[1] - chips))
    table = jnp.concatenate([counts, branch[None, :]], axis=0)

    total_shape = shape(2 * CORES, leaf_points, 2 * columns, dtype=f32)
    sums_shape = shape(n_sub, columns, skeleton, dtype=f32)
    flat_shape = shape(columns, local, dtype=f32)
    targets_shape = shape(2 * CORES, leaf_points, DEPTH)

    def stage(places, points, weights, targets, carried, last):
        first = carried is None
        with_targets = targets is None
        args = [table]
        args += [part for pair in points for part in pair]
        args += [part for pair in weights for part in pair]
        args += [coords, sibling_coords] if with_targets else [targets]
        args += [] if first else list(carried)
        args += [upper_points] if last else []
        scratch = [
            pltpu.VMEM((2 * len(places), DEPTH, leaf_points), bf16),
            pltpu.VMEM((DEPTH, 2 * skeleton), bf16),
            pltpu.VMEM((2 * columns, 2 * skeleton), bf16),
            pltpu.VMEM((2 * len(places), columns, leaf_points), bf16),
        ]
        outs = [targets_shape] if with_targets else []
        if last:
            outs += [flat_shape, flat_shape]
            scratch = [pltpu.VMEM(total_shape.shape, f32), pltpu.VMEM(sums_shape.shape, f32)] + scratch
        else:
            outs += [total_shape, sums_shape]
        static = (places, chips, n_sub, leaf_points, skeleton, first, last, with_targets)
        return call(
            functools.partial(stage_kernel, static), args, outs, scratch, flops=len(places) * 2 * 10**9
        )

    def around(parts, points, targets):
        met = [[parts]]
        right = left = parts
        for hop in range(1, chips // 2):
            right = [to_right(part) for part in right]
            left = [to_left(part) for part in left]
            met.append([right, left])
        met.append([[to_right(right[0]), to_left(left[1])]])
        points = met if points is None else points
        carried = None
        place = 0
        for turn, messages in enumerate(met):
            places = tuple(range(place, place + len(messages)))
            place += len(messages)
            last = turn == len(met) - 1
            carried = stage(places, points[turn], messages, targets, carried, last)
            if targets is None:
                targets, *carried = carried
        return met, targets, carried

    points, targets, (mine, other) = around(parts, None, None)
    first, *parts = call(
        joined_kernel,
        [mine, to_sibling(other)] + maps,
        [shape(columns, local)] + [shape(columns, leaf_points + skeleton)] * 2,
    )
    _, _, (mine, other) = around(parts, points, targets)
    (second,) = call(added_kernel, [mine, to_sibling(other)], [shape(columns, local)])
    return (first, second)


def solution(mesh):
    placed = (
        P(None, ("groups", "leaf")),
        P(None, ("groups", "leaf")),
        P(("groups", "leaf"), None),
        P(("groups", "leaf"), None),
        P(("groups", "leaf"), None),
        P(("groups", "leaf"), None),
        P(("groups", "leaf"), None),
        P(None, ("groups", "leaf")),
        P(None, "groups"),
    )
    return jax.shard_map(
        on_device,
        mesh=mesh,
        in_specs=placed,
        out_specs=(P(None, ("groups", "leaf")), P(None, ("groups", "leaf"))),
        check_vma=False,
    )
```

time: 421 us -> 122 us (0.29)
  blocking collectives: 173 us -> 0 us
  matrix products: 103 us -> 0 us
  local copies, waits for them, and re-layouts: 101 us -> 6.64 us
  Pallas kernels: 0 us -> 74.3 us
  other arithmetic: 19.1 us -> 2.07 us
  starting transfers between devices: 15.1 us -> 31.9 us
    all_gather x5 -> x0, blocking collectives: 173 us -> none  [the longest x2 107 us: kernel_product(): lax.all_gather(upper_term, 'leaf', axis=1, tiled=True)]
    dot_general x54 -> x0, matrix products: 103 us -> none  [the longest x32 67.9 us: near_step(): jnp.einsum('rls,lst->rlt', source_charges, weights, preferred_element_typ...]
    gather x66 -> x0, local copies, waits for them, and re-layouts: 91.1 us -> none  [the longest x32 71.3 us: near_step(): blocks = jnp.take(source_pool, chosen, axis=1)]
    pallas_call x0 -> x13, Pallas kernels: none -> 74.3 us  [call(): pl.pallas_call(body, grid=(1,), out_shape=out_shapes, in_specs=specs, out...]
    ppermute x0 -> x32, starting transfers between devices: none -> 31.9 us  [the longest x12 16.1 us: around(): right = [to_right(part) for part in right]]
    all_to_all x3 -> x0, starting transfers between devices: 15.1 us -> none  [the longest x2 7.71 us: fetch_blocks(): lax.all_to_all(served, 'leaf', split_axis=1, concat_axis=1, tiled=True)]
    select_n x35 -> x0, other arithmetic: 6.19 us -> none  [the longest x3 3.19 us: fetch_blocks(): served = jnp.take(stacked, jnp.maximum(incoming, 0), axis=1)]
    reduce_sum x51 -> x2, other arithmetic: 4.65 us -> 0.4 us  [the longest x1 0.31 us: on_device(): jnp.sum((lists[:, near_slots:, None] == far_ids).astype(i32), axis=1)]
  transfers between devices with their start and end apart: 3 -> 32, of which waited for: 1 -> 2; matrix products, arithmetic and copies ran while one was open for 2% -> 3% of each run, Pallas kernels for 0% -> 49%
where the time goes in v2:
time: 122 us; the launch traced here: 119 us
  Pallas kernels  74.3 us (61%)
  starting transfers between devices  31.9 us (26%)
  local copies, waits for them, and re-layouts  6.64 us (5%)
  waiting for transfers between devices  3.57 us (3%)
  other arithmetic  2.07 us (2%)
    pallas_call x13, Pallas kernels, call(): pl.pallas_call(body, grid=(1,), out_shape=out_shapes, in_specs=specs, out...  74.3 us
    ppermute x12, starting transfers between devices, around(): right = [to_right(part) for part in right]  16.1 us
    ppermute x12, starting transfers between devices, around(): left = [to_left(part) for part in left]  10.8 us
    unnamed x66, local copies, waits for them, and re-layouts  5.7 us
    ppermute x4, starting transfers between devices, around(): met.append([[to_right(right[0]), to_left(left[1])]])  4.16 us
    ppermute x2, waiting for transfers between devices, on_device(): to_sibling(other)  3.49 us
  transfers between devices with their start and end apart: 32, of which 2 were waited for; matrix products, arithmetic and copies ran while one was open for 3% of the time, Pallas kernels for 49%

profile of v2, /device:TPU:0, one launch (start us, length us, event | category | flops | bytes accessed | tf_op | source)
XLA Modules:
  0.0 119.3 jit_solution(8245198713200563118)
XLA Ops:
  1.2 2.1 %shard_map.113 = (bf16[64,1280]{1,0:T(8,128)(2,1)}, bf16[64,1152]{1,0:T(8,128)(2,1)}) custom-call(bf16[64,1024]{1,0:T(8,128)(2,1)} %refs_5_.1, bf16[64,1024]{1,0:T(8,128)(2,1)} %charges_ref.1, bf16[64,128]{1,0:T(8,128)(2,1)} %points_ref.1, bf16[1024,128]{1,0:T(8,128)(2,1)} %leaf_ref.3, bf16[256,128]{1,0:T(8,128)(2,1)} %node_ref.3, bf16[128,128]{1,0:T(8,128)(2,1)} %upper_ref.3), custom_call_target="tpu_custom_call" | custom-call | bytes 638976 | tf_op jit(solution)/shard_map/pallas_call | solution.py:232
  3.3 2.6 %collective-permute-start.1 = (bf16[64,1280]{1,0:T(8,128)(2,1)}, bf16[64,1280]{1,0:T(8,128)(2,1)S(1)}, u32[]{:S(2)}, u32[]{:S(2)}) collective-permute-start(bf16[64,1280]{1,0:T(8,128)(2,1)} %get-tuple-element.28.refs_1_.refs_3_), channel_id=1, source_target_pairs={{0,4},{1,5},{4,8},{5,9},{8,12},{9,13},{12,14},{13,15},{14,10},{15,... | collective-permute-start | bytes 491528 | tf_op jit(solution)/shard_map/ppermute | solution.py:363
  6.2 1.9 %collective-permute-start.10 = (bf16[64,1152]{1,0:T(8,128)(2,1)}, bf16[64,1152]{1,0:T(8,128)(2,1)S(1)}, u32[]{:S(2)}, u32[]{:S(2)}) collective-permute-start(bf16[64,1152]{1,0:T(8,128)(2,1)} %get-tuple-element.29.refs_2_.refs_4_), channel_id=1, source_target_pairs={{0,4},{1,5},{4,8},{5,9},{8,12},{9,13},{12,14},{13,15},{14,10},{15,... | collective-permute-start | bytes 442376 | tf_op jit(solution)/shard_map/ppermute | solution.py:363
  11.9 6.1 %shard_map.114 = (bf16[4,512,128]{2,1,0:T(8,128)(2,1)}, f32[4,512,128]{2,1,0:T(8,128)}, f32[1,64,128]{2,1,0:T(8,128)}) custom-call(s32[5,25]{1,0:T(8,128)} %pad_add_fusion.refs_0_, bf16[64,1280]{1,0:T(8,128)(2,1)} %get-tuple-element.28.refs_1_.refs_3_, bf16[64,1152]{1,0:T(8,128)(2,1)} %get-tuple-element.29.refs_2_.refs_4_, ...), custom_call_target="tpu_custom_call" | custom-call | flops 2000000000 | bytes 885236 | tf_op jit(solution)/shard_map/pallas_call | solution.py:232
  18.0 2.5 %collective-permute-start.11 = (bf16[64,1152]{1,0:T(8,128)(2,1)S(1)}, bf16[64,1152]{1,0:T(8,128)(2,1)S(1)}, u32[]{:S(2)}, u32[]{:S(2)}) collective-permute-start(bf16[64,1152]{1,0:T(8,128)(2,1)S(1)} %collective-permute-done.10.refs_2_.refs_6_), channel_id=1, source_target_pairs={{0,4},{1,5},{4,8},{5,9},{8,12},{9,13},{12,14},{13,15},{14,10},{15,... | collective-permute-start | bytes 442376 | tf_op jit(solution)/shard_map/ppermute | solution.py:363
  20.5 1.9 %collective-permute-start.14 = (bf16[64,1280]{1,0:T(8,128)(2,1)S(1)}, bf16[64,1280]{1,0:T(8,128)(2,1)S(1)}, u32[]{:S(2)}, u32[]{:S(2)}) collective-permute-start(bf16[64,1280]{1,0:T(8,128)(2,1)S(1)} %collective-permute-done.13.refs_3_.refs_7_), channel_id=1, source_target_pairs={{0,2},{1,3},{4,0},{5,1},{8,4},{9,5},{12,8},{13,9},{14,12},{15,13},... | collective-permute-start | bytes 491528 | tf_op jit(solution)/shard_map/ppermute | solution.py:364
  23.1 8.6 %shard_map.115 = (f32[4,512,128]{2,1,0:T(8,128)}, f32[1,64,128]{2,1,0:T(8,128)}) custom-call(s32[5,25]{1,0:T(8,128)} %pad_add_fusion.refs_0_, bf16[64,1280]{1,0:T(8,128)(2,1)} %copy-done.4, bf16[64,1152]{1,0:T(8,128)(2,1)} %copy-done.11, bf16[64,1280]{1,0:T(8,128)(2,1)} %copy-done.5, bf16[64,1152]{1,0:T(8,128)(2,1)} %copy-done.16, ...), custom_call_target="tpu_custom_call" | custom-call | flops 4000000000 | bytes 2851316 | tf_op jit(solution)/shard_map/pallas_call | solution.py:232
  35.9 7.5 %shard_map.116 = (f32[4,512,128]{2,1,0:T(8,128)}, f32[1,64,128]{2,1,0:T(8,128)}) custom-call(s32[5,25]{1,0:T(8,128)} %pad_add_fusion.refs_0_, bf16[64,1280]{1,0:T(8,128)(2,1)} %copy-done.8, bf16[64,1152]{1,0:T(8,128)(2,1)} %copy-done.12, bf16[64,1280]{1,0:T(8,128)(2,1)} %copy-done.6, bf16[64,1152]{1,0:T(8,128)(2,1)} %copy-done.14, ...), custom_call_target="tpu_custom_call" | custom-call | flops 4000000000 | bytes 2851316 | tf_op jit(solution)/shard_map/pallas_call | solution.py:232
  43.3 1.6 %collective-permute-start.8 = (bf16[64,1152]{1,0:T(8,128)(2,1)S(1)}, bf16[64,1152]{1,0:T(8,128)(2,1)S(1)}, u32[]{:S(2)}, u32[]{:S(2)}) collective-permute-start(bf16[64,1152]{1,0:T(8,128)(2,1)S(1)} %collective-permute-done.7.refs_4_.refs_8_), channel_id=1, source_target_pairs={{0,2},{1,3},{4,0},{5,1},{8,4},{9,5},{12,8},{13,9},{14,12},{15,13},... | collective-permute-start | bytes 442376 | tf_op jit(solution)/shard_map/ppermute | solution.py:366
  46.1 6.3 %shard_map.117 = (f32[4,512,128]{2,1,0:T(8,128)}, f32[1,64,128]{2,1,0:T(8,128)}) custom-call(s32[5,25]{1,0:T(8,128)} %pad_add_fusion.refs_0_, bf16[64,1280]{1,0:T(8,128)(2,1)} %copy-done.7, bf16[64,1152]{1,0:T(8,128)(2,1)} %copy-done.15, bf16[64,1280]{1,0:T(8,128)(2,1)} %copy-done.9, bf16[64,1152]{1,0:T(8,128)(2,1)} %copy-done.13, ...), custom_call_target="tpu_custom_call" | custom-call | flops 4000000000 | bytes 2851316 | tf_op jit(solution)/shard_map/pallas_call | solution.py:232
  53.2 6.0 %shard_map.118 = (f32[64,1024]{1,0:T(8,128)}, f32[64,1024]{1,0:T(8,128)}) custom-call(s32[5,25]{1,0:T(8,128)} %pad_add_fusion.refs_0_, bf16[64,1280]{1,0:T(8,128)(2,1)} %copy-done.10, bf16[64,1152]{1,0:T(8,128)(2,1)} %copy-done.17, bf16[64,1280]{1,0:T(8,128)(2,1)} %copy-done.10, bf16[64,1152]{1,0:T(8,128)(2,1)} %copy-done.17, ...), custom_call_target="tpu_custom_call" | custom-call | flops 2000000000 | bytes 2245108 | tf_op jit(solution)/shard_map/pallas_call | solution.py:232
  59.1 1.7 %collective-permute-done.16.other_ref = f32[64,1024]{1,0:T(8,128)S(1)} collective-permute-done((f32[64,1024]{1,0:T(8,128)}, f32[64,1024]{1,0:T(8,128)S(1)}, u32[]{:S(2)}, u32[]{:S(2)}) %collective-permute-start.16) | collective-permute-done | bytes 262176 | tf_op jit(solution)/shard_map/ppermute | solution.py:382
  61.6 2.2 %shard_map.119 = (bf16[64,1024]{1,0:T(8,128)(2,1)}, bf16[64,640]{1,0:T(8,128)(2,1)}, bf16[64,640]{1,0:T(8,128)(2,1)}) custom-call(f32[64,1024]{1,0:T(8,128)} %get-tuple-element.39.mine_ref, f32[64,1024]{1,0:T(8,128)} %copy-done, bf16[1024,128]{1,0:T(8,128)(2,1)} %leaf_ref.3, bf16[256,128]{1,0:T(8,128)(2,1)} %node_ref.3, bf16[128,128]{1,0:T(8,128)(2,1)} %upper_ref.3), custom_call_target="tpu_custom_call" | custom-call | bytes 884736 | tf_op jit(solution)/shard_map/pallas_call | solution.py:232
  63.8 2.7 %collective-permute-start.21 = (bf16[64,640]{1,0:T(8,128)(2,1)}, bf16[64,640]{1,0:T(8,128)(2,1)S(1)}, u32[]{:S(2)}, u32[]{:S(2)}) collective-permute-start(bf16[64,640]{1,0:T(8,128)(2,1)} %get-tuple-element.43.refs_4_), channel_id=1, source_target_pairs={{0,2},{1,3},{4,0},{5,1},{8,4},{9,5},{12,8},{13,9},{14,12},{15,13},... | collective-permute-start | bytes 245768 | tf_op jit(solution)/shard_map/ppermute | solution.py:364
  68.6 5.9 %shard_map.120 = (f32[4,512,128]{2,1,0:T(8,128)}, f32[1,64,128]{2,1,0:T(8,128)}) custom-call(s32[5,25]{1,0:T(8,128)} %pad_add_fusion.refs_0_, bf16[64,1280]{1,0:T(8,128)(2,1)} %get-tuple-element.28.refs_1_.refs_3_, bf16[64,1152]{1,0:T(8,128)(2,1)} %get-tuple-element.29.refs_2_.refs_4_, bf16[64,640]{1,0:T(8,128)(2,1)} %get-tuple-element.42.refs_3_, ...), custom_call_target="tpu_custom_call" | custom-call | flops 2000000000 | bytes 999924 | tf_op jit(solution)/shard_map/pallas_call | solution.py:232
  74.4 2.3 %collective-permute-start.18 = (bf16[64,640]{1,0:T(8,128)(2,1)S(1)}, bf16[64,640]{1,0:T(8,128)(2,1)S(1)}, u32[]{:S(2)}, u32[]{:S(2)}) collective-permute-start(bf16[64,640]{1,0:T(8,128)(2,1)S(1)} %collective-permute-done.17.refs_5_), channel_id=1, source_target_pairs={{0,4},{1,5},{4,8},{5,9},{8,12},{9,13},{12,14},{13,15},{14,10},{15,... | collective-permute-start | bytes 245768 | tf_op jit(solution)/shard_map/ppermute | solution.py:363
  77.2 1.7 %collective-permute-start.26 = (bf16[64,640]{1,0:T(8,128)(2,1)S(1)}, bf16[64,640]{1,0:T(8,128)(2,1)S(1)}, u32[]{:S(2)}, u32[]{:S(2)}) collective-permute-start(bf16[64,640]{1,0:T(8,128)(2,1)S(1)} %collective-permute-done.25.refs_6_), channel_id=1, source_target_pairs={{0,4},{1,5},{4,8},{5,9},{8,12},{9,13},{12,14},{13,15},{14,10},{15,... | collective-permute-start | bytes 245768 | tf_op jit(solution)/shard_map/ppermute | solution.py:363
  79.5 8.5 %shard_map.121 = (f32[4,512,128]{2,1,0:T(8,128)}, f32[1,64,128]{2,1,0:T(8,128)}) custom-call(s32[5,25]{1,0:T(8,128)} %pad_add_fusion.refs_0_, bf16[64,1280]{1,0:T(8,128)(2,1)} %copy-done.4, bf16[64,1152]{1,0:T(8,128)(2,1)} %copy-done.11, bf16[64,1280]{1,0:T(8,128)(2,1)} %copy-done.5, bf16[64,1152]{1,0:T(8,128)(2,1)} %copy-done.16, ...), custom_call_target="tpu_custom_call" | custom-call | flops 4000000000 | bytes 2556404 | tf_op jit(solution)/shard_map/pallas_call | solution.py:232
  92.2 7.4 %shard_map.122 = (f32[4,512,128]{2,1,0:T(8,128)}, f32[1,64,128]{2,1,0:T(8,128)}) custom-call(s32[5,25]{1,0:T(8,128)} %pad_add_fusion.refs_0_, bf16[64,1280]{1,0:T(8,128)(2,1)} %copy-done.8, bf16[64,1152]{1,0:T(8,128)(2,1)} %copy-done.12, bf16[64,1280]{1,0:T(8,128)(2,1)} %copy-done.6, bf16[64,1152]{1,0:T(8,128)(2,1)} %copy-done.14, ...), custom_call_target="tpu_custom_call" | custom-call | flops 4000000000 | bytes 2556404 | tf_op jit(solution)/shard_map/pallas_call | solution.py:232
  99.6 2.0 %collective-permute-start.20 = (bf16[64,640]{1,0:T(8,128)(2,1)S(1)}, bf16[64,640]{1,0:T(8,128)(2,1)S(1)}, u32[]{:S(2)}, u32[]{:S(2)}) collective-permute-start(bf16[64,640]{1,0:T(8,128)(2,1)S(1)} %collective-permute-done.19.refs_5_), channel_id=1, source_target_pairs={{0,4},{1,5},{4,8},{5,9},{8,12},{9,13},{12,14},{13,15},{14,10},{15,... | collective-permute-start | bytes 245768 | tf_op jit(solution)/shard_map/ppermute | solution.py:366
  102.3 6.2 %shard_map.123 = (f32[4,512,128]{2,1,0:T(8,128)}, f32[1,64,128]{2,1,0:T(8,128)}) custom-call(s32[5,25]{1,0:T(8,128)} %pad_add_fusion.refs_0_, bf16[64,1280]{1,0:T(8,128)(2,1)} %copy-done.7, bf16[64,1152]{1,0:T(8,128)(2,1)} %copy-done.15, bf16[64,1280]{1,0:T(8,128)(2,1)} %copy-done.9, bf16[64,1152]{1,0:T(8,128)(2,1)} %copy-done.13, ...), custom_call_target="tpu_custom_call" | custom-call | flops 4000000000 | bytes 2556404 | tf_op jit(solution)/shard_map/pallas_call | solution.py:232
  109.2 5.9 %shard_map.124 = (f32[64,1024]{1,0:T(8,128)}, f32[64,1024]{1,0:T(8,128)}) custom-call(s32[5,25]{1,0:T(8,128)} %pad_add_fusion.refs_0_, bf16[64,1280]{1,0:T(8,128)(2,1)} %copy-done.10, bf16[64,1152]{1,0:T(8,128)(2,1)} %copy-done.17, bf16[64,640]{1,0:T(8,128)(2,1)} %copy-done.30, bf16[64,640]{1,0:T(8,128)(2,1)} %copy-done.32, ...), custom_call_target="tpu_custom_call" | custom-call | flops 2000000000 | bytes 2097652 | tf_op jit(solution)/shard_map/pallas_call | solution.py:232
  115.1 1.7 %collective-permute-done.31.other_ref = f32[64,1024]{1,0:T(8,128)S(1)} collective-permute-done((f32[64,1024]{1,0:T(8,128)}, f32[64,1024]{1,0:T(8,128)S(1)}, u32[]{:S(2)}, u32[]{:S(2)}) %collective-permute-start.31) | collective-permute-done | bytes 262176 | tf_op jit(solution)/shard_map/ppermute | solution.py:386
  117.6 1.7 %shard_map.125 = bf16[64,1024]{1,0:T(8,128)(2,1)} custom-call(f32[64,1024]{1,0:T(8,128)} %get-tuple-element.52.mine_ref, f32[64,1024]{1,0:T(8,128)} %copy-done.1), custom_call_target="tpu_custom_call" | custom-call | bytes 524288 | tf_op jit(solution)/shard_map/pallas_call | solution.py:232
  (132 shorter events, 21.4 us)
Async XLA Ops:
  0.6 10.6 %collective-permute-start.9 = (bf16[64,1024]{1,0:T(8,128)(2,1)}, bf16[64,1024]{1,0:T(8,128)(2,1)S(1)}, u32[]{:S(2)}, u32[]{:S(2)}) collective-permute-start(bf16[64,1024]{1,0:T(8,128)(2,1)} %refs_5_.1), channel_id=1, source_target_pairs={{0,1},{1,0},{2,3},{3,2},{4,5},{5,4},{6,7},{7,6},{8,9},{9,8},{10,11... | collective-permute-start | bytes 393224 | tf_op jit(solution)/shard_map/ppermute | solution.py:314
  3.3 19.2 %collective-permute-start.1 = (bf16[64,1280]{1,0:T(8,128)(2,1)}, bf16[64,1280]{1,0:T(8,128)(2,1)S(1)}, u32[]{:S(2)}, u32[]{:S(2)}) collective-permute-start(bf16[64,1280]{1,0:T(8,128)(2,1)} %get-tuple-element.28.refs_1_.refs_3_), channel_id=1, source_target_pairs={{0,4},{1,5},{4,8},{5,9},{8,12},{9,13},{12,14},{13,15},{14,10},{15,... | collective-permute-start | bytes 491528 | tf_op jit(solution)/shard_map/ppermute | solution.py:363
  5.9 14.6 %collective-permute-start.13 = (bf16[64,1280]{1,0:T(8,128)(2,1)}, bf16[64,1280]{1,0:T(8,128)(2,1)S(1)}, u32[]{:S(2)}, u32[]{:S(2)}) collective-permute-start(bf16[64,1280]{1,0:T(8,128)(2,1)} %get-tuple-element.28.refs_1_.refs_3_), channel_id=1, source_target_pairs={{0,2},{1,3},{4,0},{5,1},{8,4},{9,5},{12,8},{13,9},{14,12},{15,13},... | collective-permute-start | bytes 491528 | tf_op jit(solution)/shard_map/ppermute | solution.py:364
  6.2 11.8 %collective-permute-start.10 = (bf16[64,1152]{1,0:T(8,128)(2,1)}, bf16[64,1152]{1,0:T(8,128)(2,1)S(1)}, u32[]{:S(2)}, u32[]{:S(2)}) collective-permute-start(bf16[64,1152]{1,0:T(8,128)(2,1)} %get-tuple-element.29.refs_2_.refs_4_), channel_id=1, source_target_pairs={{0,4},{1,5},{4,8},{5,9},{8,12},{9,13},{12,14},{13,15},{14,10},{15,... | collective-permute-start | bytes 442376 | tf_op jit(solution)/shard_map/ppermute | solution.py:363
  9.7 10.8 %collective-permute-start.5 = (bf16[64,1152]{1,0:T(8,128)(2,1)}, bf16[64,1152]{1,0:T(8,128)(2,1)S(1)}, u32[]{:S(2)}, u32[]{:S(2)}) collective-permute-start(bf16[64,1152]{1,0:T(8,128)(2,1)} %get-tuple-element.29.refs_2_.refs_4_), channel_id=1, source_target_pairs={{0,2},{1,3},{4,0},{5,1},{8,4},{9,5},{12,8},{13,9},{14,12},{15,13},... | collective-permute-start | bytes 442376 | tf_op jit(solution)/shard_map/ppermute | solution.py:364
  18.0 15.3 %collective-permute-start.11 = (bf16[64,1152]{1,0:T(8,128)(2,1)S(1)}, bf16[64,1152]{1,0:T(8,128)(2,1)S(1)}, u32[]{:S(2)}, u32[]{:S(2)}) collective-permute-start(bf16[64,1152]{1,0:T(8,128)(2,1)S(1)} %collective-permute-done.10.refs_2_.refs_6_), channel_id=1, source_target_pairs={{0,4},{1,5},{4,8},{5,9},{8,12},{9,13},{12,14},{13,15},{14,10},{15,... | collective-permute-start | bytes 442376 | tf_op jit(solution)/shard_map/ppermute | solution.py:363
  20.5 11.2 %collective-permute-start.6 = (bf16[64,1152]{1,0:T(8,128)(2,1)S(1)}, bf16[64,1152]{1,0:T(8,128)(2,1)S(1)}, u32[]{:S(2)}, u32[]{:S(2)}) collective-permute-start(bf16[64,1152]{1,0:T(8,128)(2,1)S(1)} %collective-permute-done.5.refs_4_.refs_8_), channel_id=1, source_target_pairs={{0,2},{1,3},{4,0},{5,1},{8,4},{9,5},{12,8},{13,9},{14,12},{15,13},... | collective-permute-start | bytes 442376 | tf_op jit(solution)/shard_map/ppermute | solution.py:364
  20.5 14.2 %collective-permute-start.14 = (bf16[64,1280]{1,0:T(8,128)(2,1)S(1)}, bf16[64,1280]{1,0:T(8,128)(2,1)S(1)}, u32[]{:S(2)}, u32[]{:S(2)}) collective-permute-start(bf16[64,1280]{1,0:T(8,128)(2,1)S(1)} %collective-permute-done.13.refs_3_.refs_7_), channel_id=1, source_target_pairs={{0,2},{1,3},{4,0},{5,1},{8,4},{9,5},{12,8},{13,9},{14,12},{15,13},... | collective-permute-start | bytes 491528 | tf_op jit(solution)/shard_map/ppermute | solution.py:364
  22.5 11.3 %collective-permute-start.2 = (bf16[64,1280]{1,0:T(8,128)(2,1)S(1)}, bf16[64,1280]{1,0:T(8,128)(2,1)S(1)}, u32[]{:S(2)}, u32[]{:S(2)}) collective-permute-start(bf16[64,1280]{1,0:T(8,128)(2,1)S(1)} %collective-permute-done.1.refs_1_.refs_5_), channel_id=1, source_target_pairs={{0,4},{1,5},{4,8},{5,9},{8,12},{9,13},{12,14},{13,15},{14,10},{15,... | collective-permute-start | bytes 491528 | tf_op jit(solution)/shard_map/ppermute | solution.py:363
  31.7 11.6 %collective-permute-start.7 = (bf16[64,1152]{1,0:T(8,128)(2,1)S(1)}, bf16[64,1152]{1,0:T(8,128)(2,1)S(1)}, u32[]{:S(2)}, u32[]{:S(2)}) collective-permute-start(bf16[64,1152]{1,0:T(8,128)(2,1)S(1)} %collective-permute-done.6.refs_4_.refs_8_), channel_id=1, source_target_pairs={{0,2},{1,3},{4,0},{5,1},{8,4},{9,5},{12,8},{13,9},{14,12},{15,13},... | collective-permute-start | bytes 442376 | tf_op jit(solution)/shard_map/ppermute | solution.py:364
  33.4 12.1 %collective-permute-start.12 = (bf16[64,1152]{1,0:T(8,128)(2,1)S(1)}, bf16[64,1152]{1,0:T(8,128)(2,1)S(1)}, u32[]{:S(2)}, u32[]{:S(2)}) collective-permute-start(bf16[64,1152]{1,0:T(8,128)(2,1)S(1)} %collective-permute-done.11.refs_2_.refs_6_), channel_id=1, source_target_pairs={{0,4},{1,5},{4,8},{5,9},{8,12},{9,13},{12,14},{13,15},{14,10},{15,... | collective-permute-start | bytes 442376 | tf_op jit(solution)/shard_map/ppermute | solution.py:363
  33.8 11.2 %collective-permute-start.3 = (bf16[64,1280]{1,0:T(8,128)(2,1)S(1)}, bf16[64,1280]{1,0:T(8,128)(2,1)S(1)}, u32[]{:S(2)}, u32[]{:S(2)}) collective-permute-start(bf16[64,1280]{1,0:T(8,128)(2,1)S(1)} %collective-permute-done.2.refs_1_.refs_5_), channel_id=1, source_target_pairs={{0,4},{1,5},{4,8},{5,9},{8,12},{9,13},{12,14},{13,15},{14,10},{15,... | collective-permute-start | bytes 491528 | tf_op jit(solution)/shard_map/ppermute | solution.py:363
  34.7 10.7 %collective-permute-start.15 = (bf16[64,1280]{1,0:T(8,128)(2,1)S(1)}, bf16[64,1280]{1,0:T(8,128)(2,1)S(1)}, u32[]{:S(2)}, u32[]{:S(2)}) collective-permute-start(bf16[64,1280]{1,0:T(8,128)(2,1)S(1)} %collective-permute-done.14.refs_3_.refs_7_), channel_id=1, source_target_pairs={{0,2},{1,3},{4,0},{5,1},{8,4},{9,5},{12,8},{13,9},{14,12},{15,13},... | collective-permute-start | bytes 491528 | tf_op jit(solution)/shard_map/ppermute | solution.py:364
  63.8 13.0 %collective-permute-start.21 = (bf16[64,640]{1,0:T(8,128)(2,1)}, bf16[64,640]{1,0:T(8,128)(2,1)S(1)}, u32[]{:S(2)}, u32[]{:S(2)}) collective-permute-start(bf16[64,640]{1,0:T(8,128)(2,1)} %get-tuple-element.43.refs_4_), channel_id=1, source_target_pairs={{0,2},{1,3},{4,0},{5,1},{8,4},{9,5},{12,8},{13,9},{14,12},{15,13},... | collective-permute-start | bytes 245768 | tf_op jit(solution)/shard_map/ppermute | solution.py:364
  66.5 10.7 %collective-permute-start.25 = (bf16[64,640]{1,0:T(8,128)(2,1)}, bf16[64,640]{1,0:T(8,128)(2,1)S(1)}, u32[]{:S(2)}, u32[]{:S(2)}) collective-permute-start(bf16[64,640]{1,0:T(8,128)(2,1)} %get-tuple-element.43.refs_4_), channel_id=1, source_target_pairs={{0,4},{1,5},{4,8},{5,9},{8,12},{9,13},{12,14},{13,15},{14,10},{15,... | collective-permute-start | bytes 245768 | tf_op jit(solution)/shard_map/ppermute | solution.py:363
  67.3 11.6 %collective-permute-start.28 = (bf16[64,640]{1,0:T(8,128)(2,1)}, bf16[64,640]{1,0:T(8,128)(2,1)S(1)}, u32[]{:S(2)}, u32[]{:S(2)}) collective-permute-start(bf16[64,640]{1,0:T(8,128)(2,1)} %get-tuple-element.42.refs_3_), channel_id=1, source_target_pairs={{0,2},{1,3},{4,0},{5,1},{8,4},{9,5},{12,8},{13,9},{14,12},{15,13},... | collective-permute-start | bytes 245768 | tf_op jit(solution)/shard_map/ppermute | solution.py:364
  74.4 13.5 %collective-permute-start.18 = (bf16[64,640]{1,0:T(8,128)(2,1)S(1)}, bf16[64,640]{1,0:T(8,128)(2,1)S(1)}, u32[]{:S(2)}, u32[]{:S(2)}) collective-permute-start(bf16[64,640]{1,0:T(8,128)(2,1)S(1)} %collective-permute-done.17.refs_5_), channel_id=1, source_target_pairs={{0,4},{1,5},{4,8},{5,9},{8,12},{9,13},{12,14},{13,15},{14,10},{15,... | collective-permute-start | bytes 245768 | tf_op jit(solution)/shard_map/ppermute | solution.py:363
  76.7 12.8 %collective-permute-start.22 = (bf16[64,640]{1,0:T(8,128)(2,1)S(1)}, bf16[64,640]{1,0:T(8,128)(2,1)S(1)}, u32[]{:S(2)}, u32[]{:S(2)}) collective-permute-start(bf16[64,640]{1,0:T(8,128)(2,1)S(1)} %collective-permute-done.21.refs_8_), channel_id=1, source_target_pairs={{0,2},{1,3},{4,0},{5,1},{8,4},{9,5},{12,8},{13,9},{14,12},{15,13},... | collective-permute-start | bytes 245768 | tf_op jit(solution)/shard_map/ppermute | solution.py:364
  77.2 12.9 %collective-permute-start.26 = (bf16[64,640]{1,0:T(8,128)(2,1)S(1)}, bf16[64,640]{1,0:T(8,128)(2,1)S(1)}, u32[]{:S(2)}, u32[]{:S(2)}) collective-permute-start(bf16[64,640]{1,0:T(8,128)(2,1)S(1)} %collective-permute-done.25.refs_6_), channel_id=1, source_target_pairs={{0,4},{1,5},{4,8},{5,9},{8,12},{9,13},{12,14},{13,15},{14,10},{15,... | collective-permute-start | bytes 245768 | tf_op jit(solution)/shard_map/ppermute | solution.py:363
  78.9 12.7 %collective-permute-start.29 = (bf16[64,640]{1,0:T(8,128)(2,1)S(1)}, bf16[64,640]{1,0:T(8,128)(2,1)S(1)}, u32[]{:S(2)}, u32[]{:S(2)}) collective-permute-start(bf16[64,640]{1,0:T(8,128)(2,1)S(1)} %collective-permute-done.28.refs_7_), channel_id=1, source_target_pairs={{0,2},{1,3},{4,0},{5,1},{8,4},{9,5},{12,8},{13,9},{14,12},{15,13},... | collective-permute-start | bytes 245768 | tf_op jit(solution)/shard_map/ppermute | solution.py:364
  88.0 11.6 %collective-permute-start.19 = (bf16[64,640]{1,0:T(8,128)(2,1)S(1)}, bf16[64,640]{1,0:T(8,128)(2,1)S(1)}, u32[]{:S(2)}, u32[]{:S(2)}) collective-permute-start(bf16[64,640]{1,0:T(8,128)(2,1)S(1)} %collective-permute-done.18.refs_5_), channel_id=1, source_target_pairs={{0,4},{1,5},{4,8},{5,9},{8,12},{9,13},{12,14},{13,15},{14,10},{15,... | collective-permute-start | bytes 245768 | tf_op jit(solution)/shard_map/ppermute | solution.py:363
  89.5 12.1 %collective-permute-start.23 = (bf16[64,640]{1,0:T(8,128)(2,1)S(1)}, bf16[64,640]{1,0:T(8,128)(2,1)S(1)}, u32[]{:S(2)}, u32[]{:S(2)}) collective-permute-start(bf16[64,640]{1,0:T(8,128)(2,1)S(1)} %collective-permute-done.22.refs_8_), channel_id=1, source_target_pairs={{0,2},{1,3},{4,0},{5,1},{8,4},{9,5},{12,8},{13,9},{14,12},{15,13},... | collective-permute-start | bytes 245768 | tf_op jit(solution)/shard_map/ppermute | solution.py:364
  90.1 11.6 %collective-permute-start.27 = (bf16[64,640]{1,0:T(8,128)(2,1)S(1)}, bf16[64,640]{1,0:T(8,128)(2,1)S(1)}, u32[]{:S(2)}, u32[]{:S(2)}) collective-permute-start(bf16[64,640]{1,0:T(8,128)(2,1)S(1)} %collective-permute-done.26.refs_6_), channel_id=1, source_target_pairs={{0,4},{1,5},{4,8},{5,9},{8,12},{9,13},{12,14},{13,15},{14,10},{15,... | collective-permute-start | bytes 245768 | tf_op jit(solution)/shard_map/ppermute | solution.py:363
  91.5 10.1 %collective-permute-start.30 = (bf16[64,640]{1,0:T(8,128)(2,1)S(1)}, bf16[64,640]{1,0:T(8,128)(2,1)S(1)}, u32[]{:S(2)}, u32[]{:S(2)}) collective-permute-start(bf16[64,640]{1,0:T(8,128)(2,1)S(1)} %collective-permute-done.29.refs_7_), channel_id=1, source_target_pairs={{0,2},{1,3},{4,0},{5,1},{8,4},{9,5},{12,8},{13,9},{14,12},{15,13},... | collective-permute-start | bytes 245768 | tf_op jit(solution)/shard_map/ppermute | solution.py:364
  (41 other events, 106.5 us)

commit v3 on v2

v3 whole, which is shorter than its diff:
```python
import functools

import jax
import jax.numpy as jnp
import numpy as np
from jax import lax
from jax.experimental import pallas as pl
from jax.experimental.pallas import tpu as pltpu
from jax.sharding import PartitionSpec as P

BRANCH = 16
EXTRA = 16
LANES = 128
CORES = 2
LEAVES = 2
TARGETS = CORES * LEAVES

bf16 = jnp.bfloat16
f32 = jnp.float32
i32 = jnp.int32


def matmul(left, right):
    return jnp.dot(left, right, preferred_element_type=f32)


def square_parts(points):
    minus = -jnp.sum(points * points, axis=0, keepdims=True)
    high = minus.astype(bf16).astype(f32)
    rest = minus - high
    middle = rest.astype(bf16).astype(f32)
    low = rest - middle
    return high, middle, low


def extra_rows(parts, first, width):
    row = lax.broadcasted_iota(i32, (EXTRA, width), 0)
    rows = jnp.where(row < 6, 1.0, 0.0).astype(f32)
    for offset, part in enumerate(parts):
        rows = jnp.where(row == first + offset, jnp.broadcast_to(part, (EXTRA, width)), rows)
    return rows


def put_sources(sources_ref, points):
    dim, width = points.shape
    sources_ref[0:dim, :] = points
    parts = square_parts(points.astype(f32))
    sources_ref[dim : dim + EXTRA, :] = extra_rows(parts, 3, width).astype(bf16)
    sources_ref[dim + EXTRA :, :] = jnp.zeros((LANES - dim - EXTRA, width), bf16)


def target_rows(points):
    dim, width = points.shape
    points = points.astype(f32)
    extra = extra_rows(square_parts(points), 0, width)
    blank = jnp.zeros((LANES - dim - EXTRA, width), f32)
    return jnp.concatenate([2.0 * points, extra, blank], axis=0).T.astype(bf16)


def in_low_half(shape):
    return lax.broadcasted_iota(i32, shape, 1) < LANES // 2


def swapped(values):
    return pltpu.roll(values, LANES // 2, 1)


def kernel_sum(targets, sources, charges):
    total = None
    width = sources.shape[1]
    step = min(width, 256)
    for begin in range(0, width, step):
        kernel = jnp.exp(matmul(targets, sources[:, begin : begin + step])).astype(bf16)
        added = matmul(kernel, charges[begin : begin + step])
        total = added if total is None else total + added
    return total


def skeleton_rows(charges, leaf_ref, node_ref, upper_ref):
    points = charges[0].shape[1]
    parts = []
    for leaf, block in enumerate(charges):
        span = slice(leaf * points, (leaf + 1) * points)
        parts.append(matmul(block, leaf_ref[span, :]).astype(bf16))
    weights = matmul(jnp.concatenate(parts, axis=1), node_ref[...]).astype(bf16)
    term = matmul(weights, upper_ref[...])
    return jnp.concatenate([weights.astype(f32), term], axis=0).T.astype(bf16)


def message_kernel(
    coords_ref, charges_ref, points_ref, leaf_ref, node_ref, upper_ref, message_ref
):
    dim, local = coords_ref.shape
    half = local // LEAVES
    charges = [charges_ref[:, 0:half], charges_ref[:, half:]]
    message_ref[0:half, :] = jnp.concatenate(charges, axis=0).astype(f32).T.astype(bf16)
    message_ref[half : half + LANES, :] = skeleton_rows(charges, leaf_ref, node_ref, upper_ref)
    place = half + LANES
    for block in range(local // LANES):
        message_ref[place : place + dim, :] = coords_ref[:, block * LANES : (block + 1) * LANES]
        place += dim
    message_ref[place : place + dim, :] = points_ref[...]


def joined_kernel(mine_ref, other_ref, leaf_ref, node_ref, upper_ref, out_ref, message_ref):
    half = mine_ref.shape[0]
    columns = LANES // LEAVES
    result = mine_ref[...] + other_ref[...]
    message_ref[0:half, :] = result.astype(bf16)
    flat = result.T.astype(bf16)
    charges = [flat[0:columns], flat[columns:]]
    out_ref[...] = jnp.concatenate(charges, axis=1)
    message_ref[half : half + LANES, :] = skeleton_rows(charges, leaf_ref, node_ref, upper_ref)


def added_kernel(mine_ref, other_ref, out_ref):
    columns = LANES // LEAVES
    flat = (mine_ref[...] + other_ref[...]).T.astype(bf16)
    out_ref[...] = jnp.concatenate([flat[0:columns], flat[columns:]], axis=1)


def stage_kernel(stage, *refs):
    spots, n_spots, n_sub, dim, points, first, last, with_targets = stage
    refs = list(refs)
    table_ref = refs.pop(0)
    place_refs = [refs.pop(0) for _ in spots]
    charge_refs = [refs.pop(0) for _ in spots]
    if with_targets:
        coords_refs = (refs.pop(0), refs.pop(0))
    else:
        targets_ref = refs.pop(0)
    if not first:
        total_in_ref, sums_in_ref = refs.pop(0), refs.pop(0)
    if last:
        upper_points_ref = refs.pop(0)
    if with_targets:
        targets_ref = refs.pop(0)
    if last:
        half_refs = refs.pop(0), refs.pop(0)
    total_ref, sums_ref, near_ref, far_ref, far_charges_ref, charges_ref = refs

    coords_at = points + LANES
    blocks = points // LANES
    low_half = in_low_half((LANES, LANES))

    if with_targets:
        for core in range(CORES):
            for leaf in range(LEAVES):
                span = slice(leaf * points, (leaf + 1) * points)
                targets_ref[core * LEAVES + leaf] = target_rows(coords_refs[core][:, span])
    if first:
        total_ref[...] = jnp.zeros_like(total_ref)
        sums_ref[...] = jnp.zeros_like(sums_ref)
    elif last:
        total_ref[...] = total_in_ref[...]
        sums_ref[...] = sums_in_ref[...]

    def far_part(skeletons, weights, entries):
        width = len(skeletons) * LANES
        put_sources(far_ref.at[:, 0:width], jnp.concatenate(skeletons, axis=1))

        def step(core, carry):
            for leaf in range(LEAVES):
                target = core * LEAVES + leaf
                for position, (block, entry) in enumerate(zip(weights, entries)):
                    scaled = block * table_ref[target, entry].astype(f32)
                    high = scaled.astype(bf16).astype(f32)
                    rows = pl.ds(position * LANES, LANES)
                    far_charges_ref[leaf, rows, :] = jnp.where(
                        low_half, high, scaled - high
                    ).astype(bf16)
                total_ref[target] += kernel_sum(
                    targets_ref[target], far_ref[:, 0:width], far_charges_ref[leaf, 0:width]
                )
            return carry

        lax.fori_loop(0, CORES, step, 0)

    weights = []
    for position, spot in enumerate(spots):
        rows = charge_refs[position][points : points + LANES, :].astype(f32)
        weights.append(jnp.where(low_half, rows, swapped(rows)))
        sums_ref[table_ref[TARGETS, spot]] += rows
        lane = lax.broadcasted_iota(i32, (1, LANES), 1) // (LANES // LEAVES)
        for leaf in range(LEAVES):
            place = position * LEAVES + leaf
            begin = coords_at + leaf * blocks * dim
            own = [
                place_refs[position][begin + block * dim : begin + (block + 1) * dim, :]
                for block in range(blocks)
            ]
            put_sources(near_ref.at[place], jnp.concatenate(own, axis=1))
            chosen = jnp.where(lane == leaf, 1.0, 0.0).astype(bf16)
            charges_ref[place] = charge_refs[position][0:points, :] * chosen

    skeletons_at = coords_at + LEAVES * blocks * dim
    far_part(
        [ref[skeletons_at : skeletons_at + dim, :] for ref in place_refs],
        weights,
        [LEAVES * n_spots + spot for spot in spots],
    )
    if last:
        for begin in range(0, n_sub, 2):
            subs = range(begin, min(begin + 2, n_sub))
            far_part(
                [upper_points_ref[:, sub * LANES : (sub + 1) * LANES] for sub in subs],
                [jnp.where(low_half, swapped(sums_ref[sub]), sums_ref[sub]) for sub in subs],
                [(LEAVES + 1) * n_spots + sub for sub in subs],
            )

    def near_part(position, spot, core, leaf):
        targets = [core * LEAVES + own for own in range(LEAVES)]
        if leaf is None:
            named = sum(table_ref[target, spot * LEAVES + 1] for target in targets)
            leaf = jnp.where(named > 0, 1, 0)
        place = position * LEAVES + leaf
        times = [table_ref[target, spot * LEAVES + leaf] for target in targets]

        @pl.when(sum(times) > 0)
        def _():
            for target, count in zip(targets, times):
                total_ref[target] += count.astype(f32) * kernel_sum(
                    targets_ref[target], near_ref[place], charges_ref[place]
                )

    if first:
        def near_step(turn, carry):
            named = table_ref[LEAVES, 1] + table_ref[LEAVES + 1, 1]
            other = jnp.where(named > 0, 1, 0)
            near_part(0, 0, turn // LEAVES, jnp.where(turn < LEAVES, turn, other))
            return carry

        lax.fori_loop(0, LEAVES + 1, near_step, 0)
    else:

        def near_step(turn, carry):
            position = turn // CORES
            near_part(position, spots[0] + position, turn % CORES, None)
            return carry

        lax.fori_loop(0, len(spots) * CORES, near_step, 0)

    if last:
        for core, ref in enumerate(half_refs):
            both = [total_ref[core * LEAVES + leaf] for leaf in range(LEAVES)]
            both = [total + swapped(total) for total in both]
            ref[...] = jnp.where(in_low_half(both[0].shape), both[0], both[1])


def call(body, args, out_shapes, streamed=(), scratch=(), aliases={}, flops=0, vmem_mib=24):
    vmem = pl.BlockSpec(memory_space=pltpu.VMEM)
    specs = []
    for place, arg in enumerate(args):
        if arg.dtype == i32:
            specs.append(pl.BlockSpec(memory_space=pltpu.SMEM))
        elif place in streamed:
            specs.append(pl.BlockSpec(arg.shape, lambda i: (0,) * 2))
        else:
            specs.append(vmem)
    moved = sum(arg.size * arg.dtype.itemsize for arg in args)
    return pl.pallas_call(
        body,
        grid=(1,),
        out_shape=out_shapes,
        in_specs=specs,
        out_specs=[vmem for _ in out_shapes],
        scratch_shapes=list(scratch),
        input_output_aliases=aliases,
        compiler_params=pltpu.CompilerParams(vmem_limit_bytes=vmem_mib * 1024 * 1024),
        cost_estimate=pl.CostEstimate(flops=flops, bytes_accessed=moved, transcendentals=0),
    )(*args)


def ring_order(chips):
    if chips == 8:
        return [0, 2, 4, 6, 7, 5, 3, 1]
    return list(range(chips))


def spots_of(peers):
    ring = ring_order(peers // CORES)
    chips = len(ring)
    found = np.zeros((peers, chips), np.int32)
    for place, chip in enumerate(ring):
        for core in range(CORES):
            way = 1 - 2 * core
            met = [chip]
            for hop in range(1, chips // 2):
                met += [ring[(place - way * hop) % chips], ring[(place + way * hop) % chips]]
            met.append(ring[(place + chips // 2) % chips])
            found[chip * CORES + core] = [other * CORES + core for other in met]
    return found


def on_device(
    coords,
    charges,
    near_lists,
    far_lists,
    leaf_interp,
    node_interp,
    upper_interp,
    node_points,
    upper_points,
):
    dim, local = coords.shape
    columns = charges.shape[0]
    points = local // LEAVES
    peers = lax.axis_size("leaf")
    me = lax.axis_index("leaf")
    n_sub = peers // BRANCH
    ring = ring_order(peers // CORES)
    chips = len(ring)
    near_slots = near_lists.shape[1]

    def along(step):
        return [
            (ring[place] * CORES + core, ring[(place + step * (1 - 2 * core)) % chips] * CORES + core)
            for place in range(chips)
            for core in range(CORES)
        ]

    one_way = functools.partial(lax.ppermute, axis_name="leaf", perm=along(1))
    other_way = functools.partial(lax.ppermute, axis_name="leaf", perm=along(-1))
    to_sibling = functools.partial(
        lax.ppermute, axis_name="leaf", perm=[(device, device ^ 1) for device in range(peers)]
    )

    def shape(*extent, dtype=bf16):
        return jax.ShapeDtypeStruct(extent, dtype)

    maps = [leaf_interp, node_interp, upper_interp]
    (message,) = call(
        message_kernel,
        [coords, charges, node_points] + maps,
        [shape(points + LANES + LEAVES * points // LANES * dim + dim, LANES)],
        streamed=range(6),
        vmem_mib=60,
    )

    lists = jnp.concatenate([near_lists, far_lists], axis=1)
    lists = jnp.concatenate([lists, to_sibling(lists)], axis=0)
    sibling_coords = to_sibling(coords)
    spots = lax.dynamic_index_in_dim(jnp.asarray(spots_of(peers)), me, 0, keepdims=False)
    near_ids = (spots[:, None] * LEAVES + jnp.arange(LEAVES)[None, :]).reshape(-1)
    far_ids = jnp.concatenate([spots, peers + jnp.arange(n_sub)])
    counts = jnp.concatenate(
        [
            jnp.sum((lists[:, :near_slots, None] == near_ids).astype(i32), axis=1),
            jnp.sum((lists[:, near_slots:, None] == far_ids).astype(i32), axis=1),
        ],
        axis=1,
    )
    branch = jnp.pad(spots // BRANCH, (0, counts.shape[1] - chips))
    table = jnp.concatenate([counts, branch[None, :]], axis=0)

    total_shape = shape(TARGETS, points, LANES, dtype=f32)
    sums_shape = shape(n_sub, LANES, LANES, dtype=f32)
    half_shape = shape(points, LANES, dtype=f32)
    targets_shape = shape(TARGETS, points, LANES)

    def stage(places, placed, charged, targets, carried, last):
        first = carried is None
        with_targets = targets is None
        args = [table] + placed + charged
        streamed = []
        if with_targets:
            streamed = [len(args)]
            args += [coords, sibling_coords]
        else:
            args += [targets]
        carried_at = len(args)
        args += [] if first else list(carried)
        args += [upper_points] if last else []
        scratch = [
            pltpu.VMEM((LEAVES * len(places), LANES, points), bf16),
            pltpu.VMEM((LANES, 2 * LANES), bf16),
            pltpu.VMEM((LEAVES, 2 * LANES, LANES), bf16),
            pltpu.VMEM((LEAVES * len(places), points, LANES), bf16),
        ]
        outs = [targets_shape] if with_targets else []
        aliases = {}
        if last:
            outs += [half_shape, half_shape]
            scratch = [pltpu.VMEM(total_shape.shape, f32), pltpu.VMEM(sums_shape.shape, f32)] + scratch
        else:
            if not first:
                aliases = {carried_at: len(outs), carried_at + 1: len(outs) + 1}
            outs += [total_shape, sums_shape]
        static = (places, chips, n_sub, dim, points, first, last, with_targets)
        return call(
            functools.partial(stage_kernel, static),
            args,
            outs,
            streamed=streamed,
            scratch=scratch,
            aliases=aliases,
            flops=len(places) * 2 * 10**9,
        )

    def around(message, placed, targets):
        met = [[message]]
        one = other = message
        for hop in range(1, chips // 2):
            one, other = one_way(one), other_way(other)
            met.append([one, other])
        met.append([one_way(one)])
        placed = met if placed is None else placed
        carried = None
        place = 0
        for turn, messages in enumerate(met):
            places = tuple(range(place, place + len(messages)))
            place += len(messages)
            last = turn == len(met) - 1
            carried = stage(places, placed[turn], messages, targets, carried, last)
            if targets is None:
                targets, *carried = carried
        return met, targets, carried

    placed, targets, (mine, other) = around(message, None, None)
    first, message = call(
        joined_kernel,
        [mine, to_sibling(other)] + maps,
        [shape(columns, local), shape(points + LANES, LANES)],
    )
    _, _, (mine, other) = around(message, placed, targets)
    (second,) = call(added_kernel, [mine, to_sibling(other)], [shape(columns, local)])
    return (first, second)


def solution(mesh):
    placed = (
        P(None, ("groups", "leaf")),
        P(None, ("groups", "leaf")),
        P(("groups", "leaf"), None),
        P(("groups", "leaf"), None),
        P(("groups", "leaf"), None),
        P(("groups", "leaf"), None),
        P(("groups", "leaf"), None),
        P(None, ("groups", "leaf")),
        P(None, "groups"),
    )
    return jax.shard_map(
        on_device,
        mesh=mesh,
        in_specs=placed,
        out_specs=(P(None, ("groups", "leaf")), P(None, ("groups", "leaf"))),
        check_vma=False,
    )
```

time: 122 us -> 84.9 us (0.70); the launches traced: 119 us -> 85.2 us
  Pallas kernels: 74.3 us -> 53.8 us
  starting transfers between devices: 31.9 us -> 19.3 us
  local copies, waits for them, and re-layouts: 6.64 us -> 1.95 us
  waiting for transfers between devices: 3.57 us -> 7.86 us
    pallas_call x13, Pallas kernels: 74.3 us -> 53.8 us  [call(): pl.pallas_call(body, grid=(1,), out_shape=out_shapes, in_specs=specs, out...]
    ppermute x28 -> x14, starting transfers between devices: 31.1 us -> 18.5 us  [the longest x12 14.9 us: around(): one, other = (one_way(one), other_way(other))]
    ppermute x28 -> x14, waiting for transfers between devices: 0.07 us -> 4.81 us  [the longest x12 4.8 us: around(): one, other = (one_way(one), other_way(other))]
    unnamed x66 -> x18, local copies, waits for them, and re-layouts: 5.7 us -> 1.01 us
  transfers between devices with their start and end apart: 32 -> 18, of which waited for: 2 -> 6; matrix products, arithmetic and copies ran while one was open for 3% -> 3% of each run, Pallas kernels for 49% -> 50%
where the time goes in v3:
time: 84.9 us; the launch traced here: 85.2 us
  Pallas kernels  53.8 us (63%)
  starting transfers between devices  19.3 us (23%)
  waiting for transfers between devices  7.86 us (9%)
  local copies, waits for them, and re-layouts  1.95 us (2%)
  other arithmetic  1.48 us (2%)
  between operations  0.86 us (1%)
    pallas_call x13, Pallas kernels, call(): pl.pallas_call(body, grid=(1,), out_shape=out_shapes, in_specs=specs, out...  53.8 us
    ppermute x12, starting transfers between devices, around(): one, other = (one_way(one), other_way(other))  14.9 us
    ppermute x12, waiting for transfers between devices, around(): one, other = (one_way(one), other_way(other))  4.8 us
    ppermute x2, starting transfers between devices, around(): met.append([one_way(one)])  3.6 us
    ppermute x2, waiting for transfers between devices, on_device(): to_sibling(other)  3.04 us
  transfers between devices with their start and end apart: 18, of which 6 were waited for; matrix products, arithmetic and copies ran while one was open for 3% of the time, Pallas kernels for 50%

profile of v3, /device:TPU:0, one launch (start us, length us, event | category | flops | bytes accessed | tf_op | source)
XLA Modules:
  0.0 85.2 jit_solution(5635780885801910991)
XLA Ops:
  1.2 2.3 %shard_map.113.refs_1_.refs_2_ = bf16[1216,128]{1,0:T(8,128)(2,1)} custom-call(bf16[64,1024]{1,0:T(8,128)(2,1)} %refs_3_.1, bf16[64,1024]{1,0:T(8,128)(2,1)} %charges_ref.1, bf16[64,128]{1,0:T(8,128)(2,1)} %points_ref.1, bf16[1024,128]{1,0:T(8,128)(2,1)} %leaf_ref.3, bf16[256,128]{1,0:T(8,128)(2,1)} %node_ref.3, bf16[128,128]{1,0:T(8,128)(2,1)} %upper_ref.3), custom_call_target="tpu_custom_call" | custom-call | bytes 638976 | tf_op jit(solution)/shard_map/pallas_call | solution.py:261
  3.4 2.6 %collective-permute-start.1 = (bf16[1216,128]{1,0:T(8,128)(2,1)}, bf16[1216,128]{1,0:T(8,128)(2,1)S(1)}, u32[]{:S(2)}, u32[]{:S(2)}) collective-permute-start(bf16[1216,128]{1,0:T(8,128)(2,1)} %shard_map.113.refs_1_.refs_2_), channel_id=1, source_target_pairs={{0,4},{1,3},{4,8},{5,1},{8,12},{9,5},{12,14},{13,9},{14,10},{15,13... | collective-permute-start | bytes 933896 | tf_op jit(solution)/shard_map/ppermute | solution.py:405
  8.7 1.0 %copy-done.1 = bf16[1216,128]{1,0:T(8,128)(2,1)S(1)} copy-done((bf16[1216,128]{1,0:T(8,128)(2,1)S(1)}, bf16[1216,128]{1,0:T(8,128)(2,1)}, u32[]{:S(2)}) %copy-start.1) | copy-done | bytes 311320
  9.7 3.7 %shard_map.114 = (bf16[4,512,128]{2,1,0:T(8,128)(2,1)S(1)}, f32[4,512,128]{2,1,0:T(8,128)S(1)}, f32[1,128,128]{2,1,0:T(8,128)S(1)}) custom-call(s32[5,25]{1,0:T(8,128)S(1)} %pad_add_fusion.refs_0_, bf16[1216,128]{1,0:T(8,128)(2,1)S(1)} %copy-done.1, bf16[1216,128]{1,0:T(8,128)(2,1)S(1)} %copy-done.1, bf16[64,1024]{1,0:T(8,128)(2,1)S(1)} %copy-done.4, ...), custom_call_target="tpu_custom_call" | custom-call | flops 2000000000 | bytes 885236 | tf_op jit(solution)/shard_map/pallas_call | solution.py:261
  13.6 2.6 %collective-permute-start.2 = (bf16[1216,128]{1,0:T(8,128)(2,1)S(1)}, bf16[1216,128]{1,0:T(8,128)(2,1)S(1)}, u32[]{:S(2)}, u32[]{:S(2)}) collective-permute-start(bf16[1216,128]{1,0:T(8,128)(2,1)S(1)} %collective-permute-done.1.refs_1_.refs_3_), channel_id=1, source_target_pairs={{0,4},{1,3},{4,8},{5,1},{8,12},{9,5},{12,14},{13,9},{14,10},{15,13... | collective-permute-start | bytes 933896 | tf_op jit(solution)/shard_map/ppermute | solution.py:405
  16.2 4.9 %shard_map.115 = (f32[4,512,128]{2,1,0:T(8,128)S(1)}, f32[1,128,128]{2,1,0:T(8,128)S(1)}) custom-call(s32[5,25]{1,0:T(8,128)S(1)} %pad_add_fusion.refs_0_, bf16[1216,128]{1,0:T(8,128)(2,1)S(1)} %collective-permute-done.1.refs_1_.refs_3_, bf16[1216,128]{1,0:T(8,128)(2,1)S(1)} %collective-permute-done.6.refs_2_.refs_4_, ...), custom_call_target="tpu_custom_call", output_to_operand_aliasing={{0}: (6, {}), {1}: (7, {})} | custom-call | flops 4000000000 | bytes 2884084 | tf_op jit(solution)/shard_map/pallas_call | solution.py:261
  21.1 2.3 %collective-permute-done.2.refs_1_.refs_3_ = bf16[1216,128]{1,0:T(8,128)(2,1)S(1)} collective-permute-done((bf16[1216,128]{1,0:T(8,128)(2,1)S(1)}, bf16[1216,128]{1,0:T(8,128)(2,1)S(1)}, u32[]{:S(2)}, u32[]{:S(2)}) %collective-permute-start.2) | collective-permute-done | bytes 311328 | tf_op jit(solution)/shard_map/ppermute | solution.py:405
  23.4 2.5 %collective-permute-start.3 = (bf16[1216,128]{1,0:T(8,128)(2,1)S(1)}, bf16[1216,128]{1,0:T(8,128)(2,1)S(1)}, u32[]{:S(2)}, u32[]{:S(2)}) collective-permute-start(bf16[1216,128]{1,0:T(8,128)(2,1)S(1)} %collective-permute-done.2.refs_1_.refs_3_), channel_id=1, source_target_pairs={{0,4},{1,3},{4,8},{5,1},{8,12},{9,5},{12,14},{13,9},{14,10},{15,13... | collective-permute-start | bytes 933896 | tf_op jit(solution)/shard_map/ppermute | solution.py:405
  25.9 5.9 %shard_map.116 = (f32[4,512,128]{2,1,0:T(8,128)S(1)}, f32[1,128,128]{2,1,0:T(8,128)S(1)}) custom-call(s32[5,25]{1,0:T(8,128)S(1)} %pad_add_fusion.refs_0_, bf16[1216,128]{1,0:T(8,128)(2,1)S(1)} %collective-permute-done.2.refs_1_.refs_3_, bf16[1216,128]{1,0:T(8,128)(2,1)S(1)} %collective-permute-done.7.refs_2_.refs_4_, ...), custom_call_target="tpu_custom_call", output_to_operand_aliasing={{0}: (6, {}), {1}: (7, {})} | custom-call | flops 4000000000 | bytes 2884084 | tf_op jit(solution)/shard_map/pallas_call | solution.py:261
  31.8 1.3 %collective-permute-done.3.refs_1_.refs_3_ = bf16[1216,128]{1,0:T(8,128)(2,1)S(1)} collective-permute-done((bf16[1216,128]{1,0:T(8,128)(2,1)S(1)}, bf16[1216,128]{1,0:T(8,128)(2,1)S(1)}, u32[]{:S(2)}, u32[]{:S(2)}) %collective-permute-start.3) | collective-permute-done | bytes 311328 | tf_op jit(solution)/shard_map/ppermute | solution.py:405
  33.1 1.8 %collective-permute-start.4 = (bf16[1216,128]{1,0:T(8,128)(2,1)S(1)}, bf16[1216,128]{1,0:T(8,128)(2,1)S(1)}, u32[]{:S(2)}, u32[]{:S(2)}) collective-permute-start(bf16[1216,128]{1,0:T(8,128)(2,1)S(1)} %collective-permute-done.3.refs_1_.refs_3_), channel_id=1, source_target_pairs={{0,4},{1,3},{4,8},{5,1},{8,12},{9,5},{12,14},{13,9},{14,10},{15,13... | collective-permute-start | bytes 933896 | tf_op jit(solution)/shard_map/ppermute | solution.py:407
  34.9 5.9 %shard_map.117 = (f32[4,512,128]{2,1,0:T(8,128)S(1)}, f32[1,128,128]{2,1,0:T(8,128)S(1)}) custom-call(s32[5,25]{1,0:T(8,128)S(1)} %pad_add_fusion.refs_0_, bf16[1216,128]{1,0:T(8,128)(2,1)S(1)} %collective-permute-done.3.refs_1_.refs_3_, bf16[1216,128]{1,0:T(8,128)(2,1)S(1)} %collective-permute-done.8.refs_2_.refs_4_, ...), custom_call_target="tpu_custom_call", output_to_operand_aliasing={{0}: (6, {}), {1}: (7, {})} | custom-call | flops 4000000000 | bytes 2884084 | tf_op jit(solution)/shard_map/pallas_call | solution.py:261
  40.8 4.7 %shard_map.118 = (f32[512,128]{1,0:T(8,128)S(1)}, f32[512,128]{1,0:T(8,128)S(1)}) custom-call(s32[5,25]{1,0:T(8,128)S(1)} %pad_add_fusion.refs_0_, bf16[1216,128]{1,0:T(8,128)(2,1)S(1)} %collective-permute-done.4.refs_1_.refs_2_, bf16[1216,128]{1,0:T(8,128)(2,1)S(1)} %collective-permute-done.4.refs_1_.refs_2_, ...), custom_call_target="tpu_custom_call" | custom-call | flops 2000000000 | bytes 2277876 | tf_op jit(solution)/shard_map/pallas_call | solution.py:261
  45.6 1.5 %collective-permute-done.9.other_ref = f32[512,128]{1,0:T(8,128)S(1)} collective-permute-done((f32[512,128]{1,0:T(8,128)S(1)}, f32[512,128]{1,0:T(8,128)S(1)}, u32[]{:S(2)}, u32[]{:S(2)}) %collective-permute-start.9) | collective-permute-done | bytes 262176 | tf_op jit(solution)/shard_map/ppermute | solution.py:423
  48.0 1.8 %collective-permute-start.10 = (bf16[640,128]{1,0:T(8,128)(2,1)S(1)}, bf16[640,128]{1,0:T(8,128)(2,1)S(1)}, u32[]{:S(2)}, u32[]{:S(2)}) collective-permute-start(bf16[640,128]{1,0:T(8,128)(2,1)S(1)} %get-tuple-element.37.refs_2_), channel_id=1, source_target_pairs={{0,4},{1,3},{4,8},{5,1},{8,12},{9,5},{12,14},{13,9},{14,10},{15,13... | collective-permute-start | bytes 491528 | tf_op jit(solution)/shard_map/ppermute | solution.py:405
  50.0 3.5 %shard_map.120 = (f32[4,512,128]{2,1,0:T(8,128)S(1)}, f32[1,128,128]{2,1,0:T(8,128)S(1)}) custom-call(s32[5,25]{1,0:T(8,128)S(1)} %pad_add_fusion.refs_0_, bf16[1216,128]{1,0:T(8,128)(2,1)S(1)} %copy-done.2, bf16[640,128]{1,0:T(8,128)(2,1)S(1)} %get-tuple-element.37.refs_2_, bf16[4,512,128]{2,1,0:T(8,128)(2,1)S(1)} %get-tuple-element.25.refs_5_.refs_3_), custom_call_target="tpu_custom_call" | custom-call | flops 2000000000 | bytes 999924 | tf_op jit(solution)/shard_map/pallas_call | solution.py:261
  54.5 1.9 %collective-permute-start.11 = (bf16[640,128]{1,0:T(8,128)(2,1)S(1)}, bf16[640,128]{1,0:T(8,128)(2,1)S(1)}, u32[]{:S(2)}, u32[]{:S(2)}) collective-permute-start(bf16[640,128]{1,0:T(8,128)(2,1)S(1)} %collective-permute-done.10.refs_3_), channel_id=1, source_target_pairs={{0,4},{1,3},{4,8},{5,1},{8,12},{9,5},{12,14},{13,9},{14,10},{15,13... | collective-permute-start | bytes 491528 | tf_op jit(solution)/shard_map/ppermute | solution.py:405
  56.7 4.9 %shard_map.121 = (f32[4,512,128]{2,1,0:T(8,128)S(1)}, f32[1,128,128]{2,1,0:T(8,128)S(1)}) custom-call(s32[5,25]{1,0:T(8,128)S(1)} %pad_add_fusion.refs_0_, bf16[1216,128]{1,0:T(8,128)(2,1)S(1)} %collective-permute-done.1.refs_1_.refs_3_, bf16[1216,128]{1,0:T(8,128)(2,1)S(1)} %collective-permute-done.6.refs_2_.refs_4_, ...), custom_call_target="tpu_custom_call", output_to_operand_aliasing={{0}: (6, {}), {1}: (7, {})} | custom-call | flops 4000000000 | bytes 2589172 | tf_op jit(solution)/shard_map/pallas_call | solution.py:261
  61.6 2.7 %collective-permute-start.12 = (bf16[640,128]{1,0:T(8,128)(2,1)S(1)}, bf16[640,128]{1,0:T(8,128)(2,1)S(1)}, u32[]{:S(2)}, u32[]{:S(2)}) collective-permute-start(bf16[640,128]{1,0:T(8,128)(2,1)S(1)} %collective-permute-done.11.refs_3_), channel_id=1, source_target_pairs={{0,4},{1,3},{4,8},{5,1},{8,12},{9,5},{12,14},{13,9},{14,10},{15,13... | collective-permute-start | bytes 491528 | tf_op jit(solution)/shard_map/ppermute | solution.py:405
  64.6 5.8 %shard_map.122 = (f32[4,512,128]{2,1,0:T(8,128)S(1)}, f32[1,128,128]{2,1,0:T(8,128)S(1)}) custom-call(s32[5,25]{1,0:T(8,128)S(1)} %pad_add_fusion.refs_0_, bf16[1216,128]{1,0:T(8,128)(2,1)S(1)} %collective-permute-done.2.refs_1_.refs_3_, bf16[1216,128]{1,0:T(8,128)(2,1)S(1)} %collective-permute-done.7.refs_2_.refs_4_, ...), custom_call_target="tpu_custom_call", output_to_operand_aliasing={{0}: (6, {}), {1}: (7, {})} | custom-call | flops 4000000000 | bytes 2589172 | tf_op jit(solution)/shard_map/pallas_call | solution.py:261
  70.4 1.8 %collective-permute-start.13 = (bf16[640,128]{1,0:T(8,128)(2,1)S(1)}, bf16[640,128]{1,0:T(8,128)(2,1)S(1)}, u32[]{:S(2)}, u32[]{:S(2)}) collective-permute-start(bf16[640,128]{1,0:T(8,128)(2,1)S(1)} %collective-permute-done.12.refs_3_), channel_id=1, source_target_pairs={{0,4},{1,3},{4,8},{5,1},{8,12},{9,5},{12,14},{13,9},{14,10},{15,13... | collective-permute-start | bytes 491528 | tf_op jit(solution)/shard_map/ppermute | solution.py:407
  72.3 5.8 %shard_map.123 = (f32[4,512,128]{2,1,0:T(8,128)S(1)}, f32[1,128,128]{2,1,0:T(8,128)S(1)}) custom-call(s32[5,25]{1,0:T(8,128)S(1)} %pad_add_fusion.refs_0_, bf16[1216,128]{1,0:T(8,128)(2,1)S(1)} %collective-permute-done.3.refs_1_.refs_3_, bf16[1216,128]{1,0:T(8,128)(2,1)S(1)} %collective-permute-done.8.refs_2_.refs_4_, ...), custom_call_target="tpu_custom_call", output_to_operand_aliasing={{0}: (6, {}), {1}: (7, {})} | custom-call | flops 4000000000 | bytes 2589172 | tf_op jit(solution)/shard_map/pallas_call | solution.py:261
  78.2 4.7 %shard_map.124 = (f32[512,128]{1,0:T(8,128)S(1)}, f32[512,128]{1,0:T(8,128)S(1)}) custom-call(s32[5,25]{1,0:T(8,128)S(1)} %pad_add_fusion.refs_0_, bf16[1216,128]{1,0:T(8,128)(2,1)S(1)} %collective-permute-done.4.refs_1_.refs_2_, bf16[640,128]{1,0:T(8,128)(2,1)S(1)} %collective-permute-done.13.refs_2_, ...), custom_call_target="tpu_custom_call" | custom-call | flops 2000000000 | bytes 2130420 | tf_op jit(solution)/shard_map/pallas_call | solution.py:261
  83.0 1.5 %collective-permute-done.17.other_ref = f32[512,128]{1,0:T(8,128)S(1)} collective-permute-done((f32[512,128]{1,0:T(8,128)S(1)}, f32[512,128]{1,0:T(8,128)S(1)}, u32[]{:S(2)}, u32[]{:S(2)}) %collective-permute-start.17) | collective-permute-done | bytes 262176 | tf_op jit(solution)/shard_map/ppermute | solution.py:427
  (56 shorter events, 6.9 us)
Async XLA Ops:
  0.6 8.0 %copy-start.4 = (bf16[64,1024]{1,0:T(8,128)(2,1)S(1)}, bf16[64,1024]{1,0:T(8,128)(2,1)}, u32[]{:S(2)}) copy-start(bf16[64,1024]{1,0:T(8,128)(2,1)} %refs_3_.1) | copy-start | bytes 393220
  0.6 5.4 %copy-start.8 = (s32[2,16]{1,0:T(2,128)S(1)}, s32[2,16]{1,0:T(2,128)}, u32[]{:S(2)}) copy-start(s32[2,16]{1,0:T(2,128)} %param.12) | copy-start | bytes 388
  0.7 8.0 %collective-permute-start.5 = (bf16[64,1024]{1,0:T(8,128)(2,1)}, bf16[64,1024]{1,0:T(8,128)(2,1)S(1)}, u32[]{:S(2)}, u32[]{:S(2)}) collective-permute-start(bf16[64,1024]{1,0:T(8,128)(2,1)} %refs_3_.1), channel_id=1, source_target_pairs={{0,1},{1,0},{2,3},{3,2},{4,5},{5,4},{6,7},{7,6},{8,9},{9,8},{10,11... | collective-permute-start | bytes 393224 | tf_op jit(solution)/shard_map/ppermute | solution.py:343
  3.4 10.2 %collective-permute-start.1 = (bf16[1216,128]{1,0:T(8,128)(2,1)}, bf16[1216,128]{1,0:T(8,128)(2,1)S(1)}, u32[]{:S(2)}, u32[]{:S(2)}) collective-permute-start(bf16[1216,128]{1,0:T(8,128)(2,1)} %shard_map.113.refs_1_.refs_2_), channel_id=1, source_target_pairs={{0,4},{1,3},{4,8},{5,1},{8,12},{9,5},{12,14},{13,9},{14,10},{15,13... | collective-permute-start | bytes 933896 | tf_op jit(solution)/shard_map/ppermute | solution.py:405
  6.0 10.2 %collective-permute-start.6 = (bf16[1216,128]{1,0:T(8,128)(2,1)}, bf16[1216,128]{1,0:T(8,128)(2,1)S(1)}, u32[]{:S(2)}, u32[]{:S(2)}) collective-permute-start(bf16[1216,128]{1,0:T(8,128)(2,1)} %shard_map.113.refs_1_.refs_2_), channel_id=1, source_target_pairs={{0,2},{1,5},{4,0},{5,9},{8,4},{9,13},{12,8},{13,15},{14,12},{15,11... | collective-permute-start | bytes 933896 | tf_op jit(solution)/shard_map/ppermute | solution.py:405
  6.1 1.8 %collective-permute-start = (s32[2,48]{1,0:T(2,128)S(1)}, s32[2,48]{1,0:T(2,128)S(1)}, u32[]{:S(2)}, u32[]{:S(2)}) collective-permute-start(s32[2,48]{1,0:T(2,128)S(1)} %pad_add_fusion.2), channel_id=1, source_target_pairs={{0,1},{1,0},{2,3},{3,2},{4,5},{5,4},{6,7},{7,6},{8,9},{9,8},{10,11... | collective-permute-start | bytes 1160 | tf_op jit(solution)/shard_map/ppermute | solution.py:342
  13.6 9.8 %collective-permute-start.2 = (bf16[1216,128]{1,0:T(8,128)(2,1)S(1)}, bf16[1216,128]{1,0:T(8,128)(2,1)S(1)}, u32[]{:S(2)}, u32[]{:S(2)}) collective-permute-start(bf16[1216,128]{1,0:T(8,128)(2,1)S(1)} %collective-permute-done.1.refs_1_.refs_3_), channel_id=1, source_target_pairs={{0,4},{1,3},{4,8},{5,1},{8,12},{9,5},{12,14},{13,9},{14,10},{15,13... | collective-permute-start | bytes 933896 | tf_op jit(solution)/shard_map/ppermute | solution.py:405
  16.2 9.7 %collective-permute-start.7 = (bf16[1216,128]{1,0:T(8,128)(2,1)S(1)}, bf16[1216,128]{1,0:T(8,128)(2,1)S(1)}, u32[]{:S(2)}, u32[]{:S(2)}) collective-permute-start(bf16[1216,128]{1,0:T(8,128)(2,1)S(1)} %collective-permute-done.6.refs_2_.refs_4_), channel_id=1, source_target_pairs={{0,2},{1,5},{4,0},{5,9},{8,4},{9,13},{12,8},{13,15},{14,12},{15,11... | collective-permute-start | bytes 933896 | tf_op jit(solution)/shard_map/ppermute | solution.py:405
  23.4 9.7 %collective-permute-start.3 = (bf16[1216,128]{1,0:T(8,128)(2,1)S(1)}, bf16[1216,128]{1,0:T(8,128)(2,1)S(1)}, u32[]{:S(2)}, u32[]{:S(2)}) collective-permute-start(bf16[1216,128]{1,0:T(8,128)(2,1)S(1)} %collective-permute-done.2.refs_1_.refs_3_), channel_id=1, source_target_pairs={{0,4},{1,3},{4,8},{5,1},{8,12},{9,5},{12,14},{13,9},{14,10},{15,13... | collective-permute-start | bytes 933896 | tf_op jit(solution)/shard_map/ppermute | solution.py:405
  25.9 8.9 %collective-permute-start.8 = (bf16[1216,128]{1,0:T(8,128)(2,1)S(1)}, bf16[1216,128]{1,0:T(8,128)(2,1)S(1)}, u32[]{:S(2)}, u32[]{:S(2)}) collective-permute-start(bf16[1216,128]{1,0:T(8,128)(2,1)S(1)} %collective-permute-done.7.refs_2_.refs_4_), channel_id=1, source_target_pairs={{0,2},{1,5},{4,0},{5,9},{8,4},{9,13},{12,8},{13,15},{14,12},{15,11... | collective-permute-start | bytes 933896 | tf_op jit(solution)/shard_map/ppermute | solution.py:405
  33.1 7.6 %collective-permute-start.4 = (bf16[1216,128]{1,0:T(8,128)(2,1)S(1)}, bf16[1216,128]{1,0:T(8,128)(2,1)S(1)}, u32[]{:S(2)}, u32[]{:S(2)}) collective-permute-start(bf16[1216,128]{1,0:T(8,128)(2,1)S(1)} %collective-permute-done.3.refs_1_.refs_3_), channel_id=1, source_target_pairs={{0,4},{1,3},{4,8},{5,1},{8,12},{9,5},{12,14},{13,9},{14,10},{15,13... | collective-permute-start | bytes 933896 | tf_op jit(solution)/shard_map/ppermute | solution.py:407
  34.9 5.9 %copy-start.6 = (bf16[64,128]{1,0:T(8,128)(2,1)S(1)}, bf16[64,128]{1,0:T(8,128)(2,1)}, u32[]{:S(2)}) copy-start(bf16[64,128]{1,0:T(8,128)(2,1)} %refs_6_.3) | copy-start | bytes 49156
  40.7 6.4 %copy-start = (bf16[1024,128]{1,0:T(8,128)(2,1)S(1)}, bf16[1024,128]{1,0:T(8,128)(2,1)}, u32[]{:S(2)}) copy-start(bf16[1024,128]{1,0:T(8,128)(2,1)} %leaf_ref.3) | copy-start | bytes 786436
  40.8 6.3 %copy-start.3 = (bf16[256,128]{1,0:T(8,128)(2,1)S(1)}, bf16[256,128]{1,0:T(8,128)(2,1)}, u32[]{:S(2)}) copy-start(bf16[256,128]{1,0:T(8,128)(2,1)} %node_ref.3) | copy-start | bytes 196612
  40.8 6.3 %copy-start.5 = (bf16[128,128]{1,0:T(8,128)(2,1)S(1)}, bf16[128,128]{1,0:T(8,128)(2,1)}, u32[]{:S(2)}) copy-start(bf16[128,128]{1,0:T(8,128)(2,1)} %upper_ref.3) | copy-start | bytes 98308
  45.5 1.6 %collective-permute-start.9 = (f32[512,128]{1,0:T(8,128)S(1)}, f32[512,128]{1,0:T(8,128)S(1)}, u32[]{:S(2)}, u32[]{:S(2)}) collective-permute-start(f32[512,128]{1,0:T(8,128)S(1)} %get-tuple-element.35), channel_id=1, source_target_pairs={{0,1},{1,0},{2,3},{3,2},{4,5},{5,4},{6,7},{7,6},{8,9},{9,8},{10,11... | collective-permute-start | bytes 786440 | tf_op jit(solution)/shard_map/ppermute | solution.py:423
  48.0 6.5 %collective-permute-start.10 = (bf16[640,128]{1,0:T(8,128)(2,1)S(1)}, bf16[640,128]{1,0:T(8,128)(2,1)S(1)}, u32[]{:S(2)}, u32[]{:S(2)}) collective-permute-start(bf16[640,128]{1,0:T(8,128)(2,1)S(1)} %get-tuple-element.37.refs_2_), channel_id=1, source_target_pairs={{0,4},{1,3},{4,8},{5,1},{8,12},{9,5},{12,14},{13,9},{14,10},{15,13... | collective-permute-start | bytes 491528 | tf_op jit(solution)/shard_map/ppermute | solution.py:405
  49.8 6.6 %collective-permute-start.14 = (bf16[640,128]{1,0:T(8,128)(2,1)S(1)}, bf16[640,128]{1,0:T(8,128)(2,1)S(1)}, u32[]{:S(2)}, u32[]{:S(2)}) collective-permute-start(bf16[640,128]{1,0:T(8,128)(2,1)S(1)} %get-tuple-element.37.refs_2_), channel_id=1, source_target_pairs={{0,2},{1,5},{4,0},{5,9},{8,4},{9,13},{12,8},{13,15},{14,12},{15,11... | collective-permute-start | bytes 491528 | tf_op jit(solution)/shard_map/ppermute | solution.py:405
  54.5 7.1 %collective-permute-start.11 = (bf16[640,128]{1,0:T(8,128)(2,1)S(1)}, bf16[640,128]{1,0:T(8,128)(2,1)S(1)}, u32[]{:S(2)}, u32[]{:S(2)}) collective-permute-start(bf16[640,128]{1,0:T(8,128)(2,1)S(1)} %collective-permute-done.10.refs_3_), channel_id=1, source_target_pairs={{0,4},{1,3},{4,8},{5,1},{8,12},{9,5},{12,14},{13,9},{14,10},{15,13... | collective-permute-start | bytes 491528 | tf_op jit(solution)/shard_map/ppermute | solution.py:405
  56.4 7.9 %collective-permute-start.15 = (bf16[640,128]{1,0:T(8,128)(2,1)S(1)}, bf16[640,128]{1,0:T(8,128)(2,1)S(1)}, u32[]{:S(2)}, u32[]{:S(2)}) collective-permute-start(bf16[640,128]{1,0:T(8,128)(2,1)S(1)} %collective-permute-done.14.refs_4_), channel_id=1, source_target_pairs={{0,2},{1,5},{4,0},{5,9},{8,4},{9,13},{12,8},{13,15},{14,12},{15,11... | collective-permute-start | bytes 491528 | tf_op jit(solution)/shard_map/ppermute | solution.py:405
  61.6 8.8 %collective-permute-start.12 = (bf16[640,128]{1,0:T(8,128)(2,1)S(1)}, bf16[640,128]{1,0:T(8,128)(2,1)S(1)}, u32[]{:S(2)}, u32[]{:S(2)}) collective-permute-start(bf16[640,128]{1,0:T(8,128)(2,1)S(1)} %collective-permute-done.11.refs_3_), channel_id=1, source_target_pairs={{0,4},{1,3},{4,8},{5,1},{8,12},{9,5},{12,14},{13,9},{14,10},{15,13... | collective-permute-start | bytes 491528 | tf_op jit(solution)/shard_map/ppermute | solution.py:405
  64.3 7.9 %collective-permute-start.16 = (bf16[640,128]{1,0:T(8,128)(2,1)S(1)}, bf16[640,128]{1,0:T(8,128)(2,1)S(1)}, u32[]{:S(2)}, u32[]{:S(2)}) collective-permute-start(bf16[640,128]{1,0:T(8,128)(2,1)S(1)} %collective-permute-done.15.refs_4_), channel_id=1, source_target_pairs={{0,2},{1,5},{4,0},{5,9},{8,4},{9,13},{12,8},{13,15},{14,12},{15,11... | collective-permute-start | bytes 491528 | tf_op jit(solution)/shard_map/ppermute | solution.py:405
  70.4 7.7 %collective-permute-start.13 = (bf16[640,128]{1,0:T(8,128)(2,1)S(1)}, bf16[640,128]{1,0:T(8,128)(2,1)S(1)}, u32[]{:S(2)}, u32[]{:S(2)}) collective-permute-start(bf16[640,128]{1,0:T(8,128)(2,1)S(1)} %collective-permute-done.12.refs_3_), channel_id=1, source_target_pairs={{0,4},{1,3},{4,8},{5,1},{8,12},{9,5},{12,14},{13,9},{14,10},{15,13... | collective-permute-start | bytes 491528 | tf_op jit(solution)/shard_map/ppermute | solution.py:407
  82.9 1.6 %collective-permute-start.17 = (f32[512,128]{1,0:T(8,128)S(1)}, f32[512,128]{1,0:T(8,128)S(1)}, u32[]{:S(2)}, u32[]{:S(2)}) collective-permute-start(f32[512,128]{1,0:T(8,128)S(1)} %get-tuple-element.47), channel_id=1, source_target_pairs={{0,1},{1,0},{2,3},{3,2},{4,5},{5,4},{6,7},{7,6},{8,9},{9,8},{10,11... | collective-permute-start | bytes 786440 | tf_op jit(solution)/shard_map/ppermute | solution.py:427
  (3 other events, 9.3 us)

commit v4 on v3

--- a/solution.py
+++ b/solution.py
@@ -14,6 +14,7 @@
 CORES = 2
 LEAVES = 2
 TARGETS = CORES * LEAVES
+KEPT_MIB = 30
 
 bf16 = jnp.bfloat16
 f32 = jnp.float32
@@ -65,12 +66,14 @@
     return pltpu.roll(values, LANES // 2, 1)
 
 
-def kernel_sum(targets, sources, charges):
+def kernel_sum(targets, sources, charges, kept_ref):
     total = None
     width = sources.shape[1]
     step = min(width, 256)
     for begin in range(0, width, step):
         kernel = jnp.exp(matmul(targets, sources[:, begin : begin + step])).astype(bf16)
+        if kept_ref is not None:
+            kept_ref[:, begin : begin + step] = kernel
         added = matmul(kernel, charges[begin : begin + step])
         total = added if total is None else total + added
     return total
@@ -120,24 +123,34 @@
 
 
 def stage_kernel(stage, *refs):
-    spots, n_spots, n_sub, dim, points, first, last, with_targets = stage
+    spots, n_spots, n_sub, dim, points, first, last, with_targets, mode = stage
     refs = list(refs)
+    use, keep = mode == "use", mode == "keep"
     table_ref = refs.pop(0)
-    place_refs = [refs.pop(0) for _ in spots]
+    place_refs = [] if use else [refs.pop(0) for _ in spots]
     charge_refs = [refs.pop(0) for _ in spots]
-    if with_targets:
+    near_kept_ref = far_kept_ref = upper_kept_ref = targets_ref = None
+    if use:
+        near_kept_ref, far_kept_ref = refs.pop(0), refs.pop(0)
+        upper_kept_ref = refs.pop(0) if last else None
+    elif with_targets:
         coords_refs = (refs.pop(0), refs.pop(0))
     else:
         targets_ref = refs.pop(0)
     if not first:
         total_in_ref, sums_in_ref = refs.pop(0), refs.pop(0)
-    if last:
+    if last and not use:
         upper_points_ref = refs.pop(0)
     if with_targets:
         targets_ref = refs.pop(0)
+    if keep:
+        near_kept_ref, far_kept_ref = refs.pop(0), refs.pop(0)
+        upper_kept_ref = refs.pop(0) if last else None
     if last:
         half_refs = refs.pop(0), refs.pop(0)
-    total_ref, sums_ref, near_ref, far_ref, far_charges_ref, charges_ref = refs
+    total_ref, sums_ref, far_charges_ref, charges_ref = refs[:4]
+    if not use:
+        near_ref, far_ref = refs[4:]
 
     coords_at = points + LANES
     blocks = points // LANES
@@ -155,9 +168,17 @@
         total_ref[...] = total_in_ref[...]
         sums_ref[...] = sums_in_ref[...]
 
-    def far_part(skeletons, weights, entries):
-        width = len(skeletons) * LANES
-        put_sources(far_ref.at[:, 0:width], jnp.concatenate(skeletons, axis=1))
+    def added(target, sources_ref, charges, kept_ref):
+        if use:
+            return matmul(kept_ref[...], charges)
+        return kernel_sum(targets_ref[target], sources_ref[...], charges, kept_ref)
+
+    def far_part(skeletons, weights, entries, kept_ref, kept_at):
+        width = len(weights) * LANES
+        sources_ref = None
+        if not use:
+            sources_ref = far_ref.at[:, 0:width]
+            put_sources(sources_ref, jnp.concatenate(skeletons, axis=1))
 
         def step(core, carry):
             for leaf in range(LEAVES):
@@ -169,8 +190,11 @@
                     far_charges_ref[leaf, rows, :] = jnp.where(
                         low_half, high, scaled - high
                     ).astype(bf16)
-                total_ref[target] += kernel_sum(
-                    targets_ref[target], far_ref[:, 0:width], far_charges_ref[leaf, 0:width]
+                kept = None
+                if kept_ref is not None:
+                    kept = kept_ref.at[target, :, kept_at : kept_at + width]
+                total_ref[target] += added(
+                    target, sources_ref, far_charges_ref[leaf, 0:width], kept
                 )
             return carry
 
@@ -184,12 +208,13 @@
         lane = lax.broadcasted_iota(i32, (1, LANES), 1) // (LANES // LEAVES)
         for leaf in range(LEAVES):
             place = position * LEAVES + leaf
-            begin = coords_at + leaf * blocks * dim
-            own = [
-                place_refs[position][begin + block * dim : begin + (block + 1) * dim, :]
-                for block in range(blocks)
-            ]
-            put_sources(near_ref.at[place], jnp.concatenate(own, axis=1))
+            if not use:
+                begin = coords_at + leaf * blocks * dim
+                own = [
+                    place_refs[position][begin + block * dim : begin + (block + 1) * dim, :]
+                    for block in range(blocks)
+                ]
+                put_sources(near_ref.at[place], jnp.concatenate(own, axis=1))
             chosen = jnp.where(lane == leaf, 1.0, 0.0).astype(bf16)
             charges_ref[place] = charge_refs[position][0:points, :] * chosen
 
@@ -198,17 +223,24 @@
         [ref[skeletons_at : skeletons_at + dim, :] for ref in place_refs],
         weights,
         [LEAVES * n_spots + spot for spot in spots],
+        far_kept_ref,
+        0,
     )
     if last:
         for begin in range(0, n_sub, 2):
             subs = range(begin, min(begin + 2, n_sub))
+            skeletons = []
+            if not use:
+                skeletons = [upper_points_ref[:, sub * LANES : (sub + 1) * LANES] for sub in subs]
             far_part(
-                [upper_points_ref[:, sub * LANES : (sub + 1) * LANES] for sub in subs],
+                skeletons,
                 [jnp.where(low_half, swapped(sums_ref[sub]), sums_ref[sub]) for sub in subs],
                 [(LEAVES + 1) * n_spots + sub for sub in subs],
+                upper_kept_ref,
+                begin * LANES,
             )
 
-    def near_part(position, spot, core, leaf):
+    def near_part(turn, position, spot, core, leaf):
         targets = [core * LEAVES + own for own in range(LEAVES)]
         if leaf is None:
             named = sum(table_ref[target, spot * LEAVES + 1] for target in targets)
@@ -218,16 +250,18 @@
 
         @pl.when(sum(times) > 0)
         def _():
-            for target, count in zip(targets, times):
-                total_ref[target] += count.astype(f32) * kernel_sum(
-                    targets_ref[target], near_ref[place], charges_ref[place]
+            for own, (target, count) in enumerate(zip(targets, times)):
+                kept = None if near_kept_ref is None else near_kept_ref.at[turn * LEAVES + own]
+                sources_ref = None if use else near_ref.at[place]
+                total_ref[target] += count.astype(f32) * added(
+                    target, sources_ref, charges_ref[place], kept
                 )
 
     if first:
         def near_step(turn, carry):
             named = table_ref[LEAVES, 1] + table_ref[LEAVES + 1, 1]
             other = jnp.where(named > 0, 1, 0)
-            near_part(0, 0, turn // LEAVES, jnp.where(turn < LEAVES, turn, other))
+            near_part(turn, 0, 0, turn // LEAVES, jnp.where(turn < LEAVES, turn, other))
             return carry
 
         lax.fori_loop(0, LEAVES + 1, near_step, 0)
@@ -235,7 +269,7 @@
 
         def near_step(turn, carry):
             position = turn // CORES
-            near_part(position, spots[0] + position, turn % CORES, None)
+            near_part(turn, position, spots[0] + position, turn % CORES, None)
             return carry
 
         lax.fori_loop(0, len(spots) * CORES, near_step, 0)
@@ -247,7 +281,7 @@
             ref[...] = jnp.where(in_low_half(both[0].shape), both[0], both[1])
 
 
-def call(body, args, out_shapes, streamed=(), scratch=(), aliases={}, flops=0, vmem_mib=24):
+def call(body, args, out_shapes, streamed=(), scratch=(), aliases={}, flops=0, vmem_mib=16):
     vmem = pl.BlockSpec(memory_space=pltpu.VMEM)
     specs = []
     for place, arg in enumerate(args):
@@ -359,26 +393,45 @@
     half_shape = shape(points, LANES, dtype=f32)
     targets_shape = shape(TARGETS, points, LANES)
 
-    def stage(places, placed, charged, targets, carried, last):
+    steps = LEAVES + 1 + CORES * (chips - 1)
+    kept_bytes = 2 * points * (steps * LEAVES * points + TARGETS * (chips + n_sub) * LANES)
+    keeping = kept_bytes <= KEPT_MIB * 2**20
+
+    def stage(places, placed, charged, targets, carried, last, kept):
         first = carried is None
         with_targets = targets is None
-        args = [table] + placed + charged
+        mode = "use" if kept else "keep" if keeping else "make"
+        args = [table] + ([] if kept else placed) + charged
         streamed = []
-        if with_targets:
+        if kept:
+            args += kept
+        elif with_targets:
             streamed = [len(args)]
             args += [coords, sibling_coords]
         else:
             args += [targets]
         carried_at = len(args)
         args += [] if first else list(carried)
-        args += [upper_points] if last else []
+        args += [upper_points] if last and not kept else []
         scratch = [
-            pltpu.VMEM((LEAVES * len(places), LANES, points), bf16),
-            pltpu.VMEM((LANES, 2 * LANES), bf16),
             pltpu.VMEM((LEAVES, 2 * LANES, LANES), bf16),
             pltpu.VMEM((LEAVES * len(places), points, LANES), bf16),
         ]
+        if not kept:
+            scratch += [
+                pltpu.VMEM((LEAVES * len(places), LANES, points), bf16),
+                pltpu.VMEM((LANES, 2 * LANES), bf16),
+            ]
         outs = [targets_shape] if with_targets else []
+        kept_at = len(outs)
+        if mode == "keep":
+            turns = LEAVES + 1 if first else CORES * len(places)
+            outs += [
+                shape(turns * LEAVES, points, points),
+                shape(TARGETS, points, len(places) * LANES),
+            ]
+            outs += [shape(TARGETS, points, n_sub * LANES)] if last else []
+        kept_to = len(outs)
         aliases = {}
         if last:
             outs += [half_shape, half_shape]
@@ -387,18 +440,21 @@
             if not first:
                 aliases = {carried_at: len(outs), carried_at + 1: len(outs) + 1}
             outs += [total_shape, sums_shape]
-        static = (places, chips, n_sub, dim, points, first, last, with_targets)
-        return call(
+        static = (places, chips, n_sub, dim, points, first, last, with_targets, mode)
+        results = call(
             functools.partial(stage_kernel, static),
             args,
             outs,
             streamed=streamed,
             scratch=scratch,
             aliases=aliases,
-            flops=len(places) * 2 * 10**9,
+            flops=len(places) * (1 if kept else 2) * 10**9,
         )
-
-    def around(message, placed, targets):
+        if with_targets:
+            targets = results[0]
+        return targets, list(results[kept_at:kept_to]), results[kept_to:]
+
+    def around(message, placed, targets, kept):
         met = [[message]]
         one = other = message
         for hop in range(1, chips // 2):
@@ -408,22 +464,25 @@
         placed = met if placed is None else placed
         carried = None
         place = 0
+        made = []
         for turn, messages in enumerate(met):
             places = tuple(range(place, place + len(messages)))
             place += len(messages)
             last = turn == len(met) - 1
-            carried = stage(places, placed[turn], messages, targets, carried, last)
-            if targets is None:
-                targets, *carried = carried
-        return met, targets, carried
-
-    placed, targets, (mine, other) = around(message, None, None)
+            given = kept[turn] if kept else []
+            targets, values, carried = stage(
+                places, placed[turn], messages, targets, carried, last, given
+            )
+            made.append(values)
+        return met, targets, made, carried
+
+    placed, targets, kept, (mine, other) = around(message, None, None, None)
     first, message = call(
         joined_kernel,
         [mine, to_sibling(other)] + maps,
         [shape(columns, local), shape(points + LANES, LANES)],
     )
-    _, _, (mine, other) = around(message, placed, targets)
+    *_, (mine, other) = around(message, placed, targets, kept if keeping else None)
     (second,) = call(added_kernel, [mine, to_sibling(other)], [shape(columns, local)])
     return (first, second)
 

time: 84.9 us -> 80.4 us (0.947)
  Pallas kernels: 53.8 us -> 44.7 us
  waiting for transfers between devices: 7.86 us -> 11.9 us
  starting transfers between devices: 19.3 us -> 17 us
  other arithmetic: 1.48 us -> 2.87 us
  local copies, waits for them, and re-layouts: 1.95 us -> 2.84 us
    pallas_call x13, Pallas kernels: 53.8 us -> 44.7 us  [call(): pl.pallas_call(body, grid=(1,), out_shape=out_shapes, in_specs=specs, out...]
    ppermute x12, waiting for transfers between devices: 4.8 us -> 7.91 us  [around(): one, other = (one_way(one), other_way(other))]
    ppermute x12, starting transfers between devices: 14.9 us -> 13.2 us  [around(): one, other = (one_way(one), other_way(other))]
    ppermute x2, waiting for transfers between devices: 0.01 us -> 0.98 us  [around(): met.append([one_way(one)])]
    unnamed x18 -> x12, local copies, waits for them, and re-layouts: 1.01 us -> 1.9 us
  transfers between devices with their start and end apart: 18 -> 18, of which waited for: 6 -> 8; matrix products, arithmetic and copies ran while one was open for 3% -> 5% of each run, Pallas kernels for 50% -> 44%
where the time goes in v4:
time: 80.4 us; the launch traced here: 80.1 us
  Pallas kernels  44.7 us (56%)
  starting transfers between devices  17 us (21%)
  waiting for transfers between devices  11.9 us (15%)
  other arithmetic  2.87 us (4%)
  local copies, waits for them, and re-layouts  2.84 us (4%)
    pallas_call x13, Pallas kernels, call(): pl.pallas_call(body, grid=(1,), out_shape=out_shapes, in_specs=specs, out...  44.7 us
    ppermute x12, starting transfers between devices, around(): one, other = (one_way(one), other_way(other))  13.2 us
    ppermute x12, waiting for transfers between devices, around(): one, other = (one_way(one), other_way(other))  7.91 us
    ppermute x2, waiting for transfers between devices, on_device(): to_sibling(other)  3.04 us
    ppermute x2, starting transfers between devices, around(): met.append([one_way(one)])  2.92 us
    unnamed x12, local copies, waits for them, and re-layouts  1.9 us
  transfers between devices with their start and end apart: 18, of which 8 were waited for; matrix products, arithmetic and copies ran while one was open for 5% of the time, Pallas kernels for 44%

profile of v4, /device:TPU:0, one launch (start us, length us, event | category | flops | bytes accessed | tf_op | source)
XLA Modules:
  0.0 80.1 jit_solution(16195556543385737376)
XLA Ops:
  1.1 2.3 %shard_map.113.refs_1_.refs_2_ = bf16[1216,128]{1,0:T(8,128)(2,1)} custom-call(bf16[64,1024]{1,0:T(8,128)(2,1)} %refs_3_.1, bf16[64,1024]{1,0:T(8,128)(2,1)} %charges_ref.1, bf16[64,128]{1,0:T(8,128)(2,1)} %points_ref.1, bf16[1024,128]{1,0:T(8,128)(2,1)} %leaf_ref.3, bf16[256,128]{1,0:T(8,128)(2,1)} %node_ref.3, bf16[128,128]{1,0:T(8,128)(2,1)} %upper_ref.3), custom_call_target="tpu_custom_call" | custom-call | bytes 638976 | tf_op jit(solution)/shard_map/pallas_call | solution.py:295
  3.4 2.5 %collective-permute-start.6 = (bf16[1216,128]{1,0:T(8,128)(2,1)}, bf16[1216,128]{1,0:T(8,128)(2,1)S(1)}, u32[]{:S(2)}, u32[]{:S(2)}) collective-permute-start(bf16[1216,128]{1,0:T(8,128)(2,1)} %shard_map.113.refs_1_.refs_2_), channel_id=1, source_target_pairs={{0,2},{1,5},{4,0},{5,9},{8,4},{9,13},{12,8},{13,15},{14,12},{15,11... | collective-permute-start | bytes 933896 | tf_op jit(solution)/shard_map/ppermute | solution.py:461
  11.9 4.6 %shard_map.114 = (bf16[4,512,128]{2,1,0:T(8,128)(2,1)S(1)}, bf16[6,512,512]{2,1,0:T(8,128)(2,1)S(1)}, bf16[4,512,128]{2,1,0:T(8,128)(2,1)S(1)}, f32[4,512,128]{2,1,0:T(8,128)S(1)}, f32[1,128,128]{2,1,0:T(8,128)S(1)}) custom-call(s32[5,25]{1,0:T(8,128)S(1)} %pad_add_fusion.refs_0_, bf16[1216,128]{1,0:T(8,128)(2,1)S(1)} %copy-done.1, ...), custom_call_target="tpu_custom_call" | custom-call | flops 2000000000 | bytes 885236 | tf_op jit(solution)/shard_map/pallas_call | solution.py:295
  16.6 1.8 %collective-permute-start.7 = (bf16[1216,128]{1,0:T(8,128)(2,1)S(1)}, bf16[1216,128]{1,0:T(8,128)(2,1)S(1)}, u32[]{:S(2)}, u32[]{:S(2)}) collective-permute-start(bf16[1216,128]{1,0:T(8,128)(2,1)S(1)} %collective-permute-done.6.refs_2_.refs_4_), channel_id=1, source_target_pairs={{0,2},{1,5},{4,0},{5,9},{8,4},{9,13},{12,8},{13,15},{14,12},{15,11... | collective-permute-start | bytes 933896 | tf_op jit(solution)/shard_map/ppermute | solution.py:461
  18.7 4.9 %shard_map.115 = (bf16[8,512,512]{2,1,0:T(8,128)(2,1)S(1)}, bf16[4,512,256]{2,1,0:T(8,128)(2,1)S(1)}, f32[4,512,128]{2,1,0:T(8,128)S(1)}, f32[1,128,128]{2,1,0:T(8,128)S(1)}) custom-call(s32[5,25]{1,0:T(8,128)S(1)} %pad_add_fusion.refs_0_, ...), custom_call_target="tpu_custom_call", output_to_operand_aliasing={{2}: (6, {}), {3}: (7, {})} | custom-call | flops 4000000000 | bytes 2884084 | tf_op jit(solution)/shard_map/pallas_call | solution.py:295
  23.6 2.2 %collective-permute-done.7.refs_2_.refs_4_ = bf16[1216,128]{1,0:T(8,128)(2,1)S(1)} collective-permute-done((bf16[1216,128]{1,0:T(8,128)(2,1)S(1)}, bf16[1216,128]{1,0:T(8,128)(2,1)S(1)}, u32[]{:S(2)}, u32[]{:S(2)}) %collective-permute-start.7) | collective-permute-done | bytes 311328 | tf_op jit(solution)/shard_map/ppermute | solution.py:461
  25.8 2.5 %collective-permute-start.8 = (bf16[1216,128]{1,0:T(8,128)(2,1)S(1)}, bf16[1216,128]{1,0:T(8,128)(2,1)S(1)}, u32[]{:S(2)}, u32[]{:S(2)}) collective-permute-start(bf16[1216,128]{1,0:T(8,128)(2,1)S(1)} %collective-permute-done.7.refs_2_.refs_4_), channel_id=1, source_target_pairs={{0,2},{1,5},{4,0},{5,9},{8,4},{9,13},{12,8},{13,15},{14,12},{15,11... | collective-permute-start | bytes 933896 | tf_op jit(solution)/shard_map/ppermute | solution.py:461
  28.2 5.9 %shard_map.116 = (bf16[8,512,512]{2,1,0:T(8,128)(2,1)S(1)}, bf16[4,512,256]{2,1,0:T(8,128)(2,1)S(1)}, f32[4,512,128]{2,1,0:T(8,128)S(1)}, f32[1,128,128]{2,1,0:T(8,128)S(1)}) custom-call(s32[5,25]{1,0:T(8,128)S(1)} %pad_add_fusion.refs_0_, ...), custom_call_target="tpu_custom_call", output_to_operand_aliasing={{2}: (6, {}), {3}: (7, {})} | custom-call | flops 4000000000 | bytes 2884084 | tf_op jit(solution)/shard_map/pallas_call | solution.py:295
  35.1 1.8 %collective-permute-start.4 = (bf16[1216,128]{1,0:T(8,128)(2,1)S(1)}, bf16[1216,128]{1,0:T(8,128)(2,1)S(1)}, u32[]{:S(2)}, u32[]{:S(2)}) collective-permute-start(bf16[1216,128]{1,0:T(8,128)(2,1)S(1)} %collective-permute-done.3.refs_1_.refs_3_), channel_id=1, source_target_pairs={{0,4},{1,3},{4,8},{5,1},{8,12},{9,5},{12,14},{13,9},{14,10},{15,13... | collective-permute-start | bytes 933896 | tf_op jit(solution)/shard_map/ppermute | solution.py:463
  37.0 5.9 %shard_map.117 = (bf16[8,512,512]{2,1,0:T(8,128)(2,1)S(1)}, bf16[4,512,256]{2,1,0:T(8,128)(2,1)S(1)}, f32[4,512,128]{2,1,0:T(8,128)S(1)}, f32[1,128,128]{2,1,0:T(8,128)S(1)}) custom-call(s32[5,25]{1,0:T(8,128)S(1)} %pad_add_fusion.refs_0_, ...), custom_call_target="tpu_custom_call", output_to_operand_aliasing={{2}: (6, {}), {3}: (7, {})} | custom-call | flops 4000000000 | bytes 2884084 | tf_op jit(solution)/shard_map/pallas_call | solution.py:295
  42.9 4.7 %shard_map.118 = (bf16[4,512,512]{2,1,0:T(8,128)(2,1)S(1)}, bf16[4,512,128]{2,1,0:T(8,128)(2,1)S(1)}, bf16[4,512,128]{2,1,0:T(8,128)(2,1)S(1)}, f32[512,128]{1,0:T(8,128)S(1)}, f32[512,128]{1,0:T(8,128)S(1)}) custom-call(s32[5,25]{1,0:T(8,128)S(1)} %pad_add_fusion.refs_0_, bf16[1216,128]{1,0:T(8,128)(2,1)S(1)} %collective-permute-done.4.refs_1_.refs_2_, ...), custom_call_target="tpu_custom_call" | custom-call | flops 2000000000 | bytes 2277876 | tf_op jit(solution)/shard_map/pallas_call | solution.py:295
  47.7 1.5 %collective-permute-done.9.other_ref = f32[512,128]{1,0:T(8,128)S(1)} collective-permute-done((f32[512,128]{1,0:T(8,128)S(1)}, f32[512,128]{1,0:T(8,128)S(1)}, u32[]{:S(2)}, u32[]{:S(2)}) %collective-permute-start.9) | collective-permute-done | bytes 262176 | tf_op jit(solution)/shard_map/ppermute | solution.py:482
  50.9 1.2 %collective-permute-start.10 = (bf16[640,128]{1,0:T(8,128)(2,1)S(1)}, bf16[640,128]{1,0:T(8,128)(2,1)S(1)}, u32[]{:S(2)}, u32[]{:S(2)}) collective-permute-start(bf16[640,128]{1,0:T(8,128)(2,1)S(1)} %get-tuple-element.48.refs_1_), channel_id=1, source_target_pairs={{0,4},{1,3},{4,8},{5,1},{8,12},{9,5},{12,14},{13,9},{14,10},{15,13... | collective-permute-start | bytes 491528 | tf_op jit(solution)/shard_map/ppermute | solution.py:461
  52.1 2.6 %shard_map.120 = (f32[4,512,128]{2,1,0:T(8,128)S(1)}, f32[1,128,128]{2,1,0:T(8,128)S(1)}) custom-call(s32[5,25]{1,0:T(8,128)S(1)} %pad_add_fusion.refs_0_, bf16[640,128]{1,0:T(8,128)(2,1)S(1)} %get-tuple-element.48.refs_1_, bf16[6,512,512]{2,1,0:T(8,128)(2,1)S(1)} %get-tuple-element.58.refs_2_, bf16[4,512,128]{2,1,0:T(8,128)(2,1)S(1)} %get-tuple-element.59.refs_3_), custom_call_target="tpu_custom_call" | custom-call | flops 1000000000 | bytes 3834356 | tf_op jit(solution)/shard_map/pallas_call | solution.py:295
  54.7 2.3 %collective-permute-done.14.refs_2_ = bf16[640,128]{1,0:T(8,128)(2,1)S(1)} collective-permute-done((bf16[640,128]{1,0:T(8,128)(2,1)S(1)}, bf16[640,128]{1,0:T(8,128)(2,1)S(1)}, u32[]{:S(2)}, u32[]{:S(2)}) %collective-permute-start.14) | collective-permute-done | bytes 163872 | tf_op jit(solution)/shard_map/ppermute | solution.py:461
  57.9 1.1 %collective-permute-start.11 = (bf16[640,128]{1,0:T(8,128)(2,1)S(1)}, bf16[640,128]{1,0:T(8,128)(2,1)S(1)}, u32[]{:S(2)}, u32[]{:S(2)}) collective-permute-start(bf16[640,128]{1,0:T(8,128)(2,1)S(1)} %collective-permute-done.10.refs_1_), channel_id=1, source_target_pairs={{0,4},{1,3},{4,8},{5,1},{8,12},{9,5},{12,14},{13,9},{14,10},{15,13... | collective-permute-start | bytes 491528 | tf_op jit(solution)/shard_map/ppermute | solution.py:461
  59.0 2.8 %shard_map.121 = (f32[4,512,128]{2,1,0:T(8,128)S(1)}, f32[1,128,128]{2,1,0:T(8,128)S(1)}) custom-call(s32[5,25]{1,0:T(8,128)S(1)} %pad_add_fusion.refs_0_, bf16[640,128]{1,0:T(8,128)(2,1)S(1)} %collective-permute-done.10.refs_1_, bf16[640,128]{1,0:T(8,128)(2,1)S(1)} %collective-permute-done.14.refs_2_, ...), custom_call_target="tpu_custom_call", output_to_operand_aliasing={{0}: (5, {}), {1}: (6, {})} | custom-call | flops 2000000000 | bytes 6685172 | tf_op jit(solution)/shard_map/pallas_call | solution.py:295
  61.8 1.4 %collective-permute-done.15.refs_2_ = bf16[640,128]{1,0:T(8,128)(2,1)S(1)} collective-permute-done((bf16[640,128]{1,0:T(8,128)(2,1)S(1)}, bf16[640,128]{1,0:T(8,128)(2,1)S(1)}, u32[]{:S(2)}, u32[]{:S(2)}) %collective-permute-start.15) | collective-permute-done | bytes 163872 | tf_op jit(solution)/shard_map/ppermute | solution.py:461
  64.1 1.1 %collective-permute-start.12 = (bf16[640,128]{1,0:T(8,128)(2,1)S(1)}, bf16[640,128]{1,0:T(8,128)(2,1)S(1)}, u32[]{:S(2)}, u32[]{:S(2)}) collective-permute-start(bf16[640,128]{1,0:T(8,128)(2,1)S(1)} %collective-permute-done.11.refs_1_), channel_id=1, source_target_pairs={{0,4},{1,3},{4,8},{5,1},{8,12},{9,5},{12,14},{13,9},{14,10},{15,13... | collective-permute-start | bytes 491528 | tf_op jit(solution)/shard_map/ppermute | solution.py:461
  65.2 3.2 %shard_map.122 = (f32[4,512,128]{2,1,0:T(8,128)S(1)}, f32[1,128,128]{2,1,0:T(8,128)S(1)}) custom-call(s32[5,25]{1,0:T(8,128)S(1)} %pad_add_fusion.refs_0_, bf16[640,128]{1,0:T(8,128)(2,1)S(1)} %collective-permute-done.11.refs_1_, bf16[640,128]{1,0:T(8,128)(2,1)S(1)} %collective-permute-done.15.refs_2_, ...), custom_call_target="tpu_custom_call", output_to_operand_aliasing={{0}: (5, {}), {1}: (6, {})} | custom-call | flops 2000000000 | bytes 6685172 | tf_op jit(solution)/shard_map/pallas_call | solution.py:295
  69.5 1.1 %collective-permute-start.13 = (bf16[640,128]{1,0:T(8,128)(2,1)S(1)}, bf16[640,128]{1,0:T(8,128)(2,1)S(1)}, u32[]{:S(2)}, u32[]{:S(2)}) collective-permute-start(bf16[640,128]{1,0:T(8,128)(2,1)S(1)} %collective-permute-done.12.refs_1_), channel_id=1, source_target_pairs={{0,4},{1,3},{4,8},{5,1},{8,12},{9,5},{12,14},{13,9},{14,10},{15,13... | collective-permute-start | bytes 491528 | tf_op jit(solution)/shard_map/ppermute | solution.py:463
  70.6 3.2 %shard_map.123 = (f32[4,512,128]{2,1,0:T(8,128)S(1)}, f32[1,128,128]{2,1,0:T(8,128)S(1)}) custom-call(s32[5,25]{1,0:T(8,128)S(1)} %pad_add_fusion.refs_0_, bf16[640,128]{1,0:T(8,128)(2,1)S(1)} %collective-permute-done.12.refs_1_, bf16[640,128]{1,0:T(8,128)(2,1)S(1)} %collective-permute-done.16.refs_2_, ...), custom_call_target="tpu_custom_call", output_to_operand_aliasing={{0}: (5, {}), {1}: (6, {})} | custom-call | flops 2000000000 | bytes 6685172 | tf_op jit(solution)/shard_map/pallas_call | solution.py:295
  74.8 3.0 %shard_map.124 = (f32[512,128]{1,0:T(8,128)S(1)}, f32[512,128]{1,0:T(8,128)S(1)}) custom-call(s32[5,25]{1,0:T(8,128)S(1)} %pad_add_fusion.refs_0_, bf16[640,128]{1,0:T(8,128)(2,1)S(1)} %collective-permute-done.13.refs_1_, bf16[4,512,512]{2,1,0:T(8,128)(2,1)S(1)} %get-tuple-element.49.refs_2_, bf16[4,512,128]{2,1,0:T(8,128)(2,1)S(1)} %get-tuple-element.50.refs_3_, ...), custom_call_target="tpu_custom_call" | custom-call | flops 1000000000 | bytes 4424180 | tf_op jit(solution)/shard_map/pallas_call | solution.py:295
  77.9 1.5 %collective-permute-done.17.other_ref = f32[512,128]{1,0:T(8,128)S(1)} collective-permute-done((f32[512,128]{1,0:T(8,128)S(1)}, f32[512,128]{1,0:T(8,128)S(1)}, u32[]{:S(2)}, u32[]{:S(2)}) %collective-permute-start.17) | collective-permute-done | bytes 262176 | tf_op jit(solution)/shard_map/ppermute | solution.py:486
  (50 shorter events, 14.2 us)
Async XLA Ops:
  0.6 9.4 %collective-permute-start.5 = (bf16[64,1024]{1,0:T(8,128)(2,1)}, bf16[64,1024]{1,0:T(8,128)(2,1)S(1)}, u32[]{:S(2)}, u32[]{:S(2)}) collective-permute-start(bf16[64,1024]{1,0:T(8,128)(2,1)} %refs_3_.1), channel_id=1, source_target_pairs={{0,1},{1,0},{2,3},{3,2},{4,5},{5,4},{6,7},{7,6},{8,9},{9,8},{10,11... | collective-permute-start | bytes 393224 | tf_op jit(solution)/shard_map/ppermute | solution.py:377
  3.4 13.2 %collective-permute-start.6 = (bf16[1216,128]{1,0:T(8,128)(2,1)}, bf16[1216,128]{1,0:T(8,128)(2,1)S(1)}, u32[]{:S(2)}, u32[]{:S(2)}) collective-permute-start(bf16[1216,128]{1,0:T(8,128)(2,1)} %shard_map.113.refs_1_.refs_2_), channel_id=1, source_target_pairs={{0,2},{1,5},{4,0},{5,9},{8,4},{9,13},{12,8},{13,15},{14,12},{15,11... | collective-permute-start | bytes 933896 | tf_op jit(solution)/shard_map/ppermute | solution.py:461
  5.9 12.5 %collective-permute-start.1 = (bf16[1216,128]{1,0:T(8,128)(2,1)}, bf16[1216,128]{1,0:T(8,128)(2,1)S(1)}, u32[]{:S(2)}, u32[]{:S(2)}) collective-permute-start(bf16[1216,128]{1,0:T(8,128)(2,1)} %shard_map.113.refs_1_.refs_2_), channel_id=1, source_target_pairs={{0,4},{1,3},{4,8},{5,1},{8,12},{9,5},{12,14},{13,9},{14,10},{15,13... | collective-permute-start | bytes 933896 | tf_op jit(solution)/shard_map/ppermute | solution.py:461
  6.8 1.8 %collective-permute-start = (s32[2,48]{1,0:T(2,128)S(1)}, s32[2,48]{1,0:T(2,128)S(1)}, u32[]{:S(2)}, u32[]{:S(2)}) collective-permute-start(s32[2,48]{1,0:T(2,128)S(1)} %pad_add_fusion.2), channel_id=1, source_target_pairs={{0,1},{1,0},{2,3},{3,2},{4,5},{5,4},{6,7},{7,6},{8,9},{9,8},{10,11... | collective-permute-start | bytes 1160 | tf_op jit(solution)/shard_map/ppermute | solution.py:376
  10.0 1.0 %copy-start.1 = (bf16[1216,128]{1,0:T(8,128)(2,1)S(1)}, bf16[1216,128]{1,0:T(8,128)(2,1)}, u32[]{:S(2)}) copy-start(bf16[1216,128]{1,0:T(8,128)(2,1)} %shard_map.113.refs_1_.refs_2_) | copy-start | bytes 933892
  11.0 0.9 %copy-start.3 = (bf16[64,1024]{1,0:T(8,128)(2,1)S(1)}, bf16[64,1024]{1,0:T(8,128)(2,1)}, u32[]{:S(2)}) copy-start(bf16[64,1024]{1,0:T(8,128)(2,1)} %refs_3_.1) | copy-start | bytes 393220
  16.6 9.2 %collective-permute-start.7 = (bf16[1216,128]{1,0:T(8,128)(2,1)S(1)}, bf16[1216,128]{1,0:T(8,128)(2,1)S(1)}, u32[]{:S(2)}, u32[]{:S(2)}) collective-permute-start(bf16[1216,128]{1,0:T(8,128)(2,1)S(1)} %collective-permute-done.6.refs_2_.refs_4_), channel_id=1, source_target_pairs={{0,2},{1,5},{4,0},{5,9},{8,4},{9,13},{12,8},{13,15},{14,12},{15,11... | collective-permute-start | bytes 933896 | tf_op jit(solution)/shard_map/ppermute | solution.py:461
  18.4 9.8 %collective-permute-start.2 = (bf16[1216,128]{1,0:T(8,128)(2,1)S(1)}, bf16[1216,128]{1,0:T(8,128)(2,1)S(1)}, u32[]{:S(2)}, u32[]{:S(2)}) collective-permute-start(bf16[1216,128]{1,0:T(8,128)(2,1)S(1)} %collective-permute-done.1.refs_1_.refs_3_), channel_id=1, source_target_pairs={{0,4},{1,3},{4,8},{5,1},{8,12},{9,5},{12,14},{13,9},{14,10},{15,13... | collective-permute-start | bytes 933896 | tf_op jit(solution)/shard_map/ppermute | solution.py:461
  25.8 11.2 %collective-permute-start.8 = (bf16[1216,128]{1,0:T(8,128)(2,1)S(1)}, bf16[1216,128]{1,0:T(8,128)(2,1)S(1)}, u32[]{:S(2)}, u32[]{:S(2)}) collective-permute-start(bf16[1216,128]{1,0:T(8,128)(2,1)S(1)} %collective-permute-done.7.refs_2_.refs_4_), channel_id=1, source_target_pairs={{0,2},{1,5},{4,0},{5,9},{8,4},{9,13},{12,8},{13,15},{14,12},{15,11... | collective-permute-start | bytes 933896 | tf_op jit(solution)/shard_map/ppermute | solution.py:461
  28.2 6.9 %collective-permute-start.3 = (bf16[1216,128]{1,0:T(8,128)(2,1)S(1)}, bf16[1216,128]{1,0:T(8,128)(2,1)S(1)}, u32[]{:S(2)}, u32[]{:S(2)}) collective-permute-start(bf16[1216,128]{1,0:T(8,128)(2,1)S(1)} %collective-permute-done.2.refs_1_.refs_3_), channel_id=1, source_target_pairs={{0,4},{1,3},{4,8},{5,1},{8,12},{9,5},{12,14},{13,9},{14,10},{15,13... | collective-permute-start | bytes 933896 | tf_op jit(solution)/shard_map/ppermute | solution.py:461
  35.1 7.7 %collective-permute-start.4 = (bf16[1216,128]{1,0:T(8,128)(2,1)S(1)}, bf16[1216,128]{1,0:T(8,128)(2,1)S(1)}, u32[]{:S(2)}, u32[]{:S(2)}) collective-permute-start(bf16[1216,128]{1,0:T(8,128)(2,1)S(1)} %collective-permute-done.3.refs_1_.refs_3_), channel_id=1, source_target_pairs={{0,4},{1,3},{4,8},{5,1},{8,12},{9,5},{12,14},{13,9},{14,10},{15,13... | collective-permute-start | bytes 933896 | tf_op jit(solution)/shard_map/ppermute | solution.py:463
  37.0 5.9 %copy-start.5 = (bf16[64,128]{1,0:T(8,128)(2,1)S(1)}, bf16[64,128]{1,0:T(8,128)(2,1)}, u32[]{:S(2)}) copy-start(bf16[64,128]{1,0:T(8,128)(2,1)} %refs_6_.1) | copy-start | bytes 49156
  42.8 6.4 %copy-start = (bf16[1024,128]{1,0:T(8,128)(2,1)S(1)}, bf16[1024,128]{1,0:T(8,128)(2,1)}, u32[]{:S(2)}) copy-start(bf16[1024,128]{1,0:T(8,128)(2,1)} %leaf_ref.3) | copy-start | bytes 786436
  42.8 6.4 %copy-start.2 = (bf16[256,128]{1,0:T(8,128)(2,1)S(1)}, bf16[256,128]{1,0:T(8,128)(2,1)}, u32[]{:S(2)}) copy-start(bf16[256,128]{1,0:T(8,128)(2,1)} %node_ref.3) | copy-start | bytes 196612
  42.9 6.4 %copy-start.4 = (bf16[128,128]{1,0:T(8,128)(2,1)S(1)}, bf16[128,128]{1,0:T(8,128)(2,1)}, u32[]{:S(2)}) copy-start(bf16[128,128]{1,0:T(8,128)(2,1)} %upper_ref.3) | copy-start | bytes 98308
  47.6 1.6 %collective-permute-start.9 = (f32[512,128]{1,0:T(8,128)S(1)}, f32[512,128]{1,0:T(8,128)S(1)}, u32[]{:S(2)}, u32[]{:S(2)}) collective-permute-start(f32[512,128]{1,0:T(8,128)S(1)} %get-tuple-element.46), channel_id=1, source_target_pairs={{0,1},{1,0},{2,3},{3,2},{4,5},{5,4},{6,7},{7,6},{8,9},{9,8},{10,11... | collective-permute-start | bytes 786440 | tf_op jit(solution)/shard_map/ppermute | solution.py:482
  50.1 6.9 %collective-permute-start.14 = (bf16[640,128]{1,0:T(8,128)(2,1)S(1)}, bf16[640,128]{1,0:T(8,128)(2,1)S(1)}, u32[]{:S(2)}, u32[]{:S(2)}) collective-permute-start(bf16[640,128]{1,0:T(8,128)(2,1)S(1)} %get-tuple-element.48.refs_1_), channel_id=1, source_target_pairs={{0,2},{1,5},{4,0},{5,9},{8,4},{9,13},{12,8},{13,15},{14,12},{15,11... | collective-permute-start | bytes 491528 | tf_op jit(solution)/shard_map/ppermute | solution.py:461
  50.9 7.0 %collective-permute-start.10 = (bf16[640,128]{1,0:T(8,128)(2,1)S(1)}, bf16[640,128]{1,0:T(8,128)(2,1)S(1)}, u32[]{:S(2)}, u32[]{:S(2)}) collective-permute-start(bf16[640,128]{1,0:T(8,128)(2,1)S(1)} %get-tuple-element.48.refs_1_), channel_id=1, source_target_pairs={{0,4},{1,3},{4,8},{5,1},{8,12},{9,5},{12,14},{13,9},{14,10},{15,13... | collective-permute-start | bytes 491528 | tf_op jit(solution)/shard_map/ppermute | solution.py:461
  57.0 6.2 %collective-permute-start.15 = (bf16[640,128]{1,0:T(8,128)(2,1)S(1)}, bf16[640,128]{1,0:T(8,128)(2,1)S(1)}, u32[]{:S(2)}, u32[]{:S(2)}) collective-permute-start(bf16[640,128]{1,0:T(8,128)(2,1)S(1)} %collective-permute-done.14.refs_2_), channel_id=1, source_target_pairs={{0,2},{1,5},{4,0},{5,9},{8,4},{9,13},{12,8},{13,15},{14,12},{15,11... | collective-permute-start | bytes 491528 | tf_op jit(solution)/shard_map/ppermute | solution.py:461
  57.9 6.2 %collective-permute-start.11 = (bf16[640,128]{1,0:T(8,128)(2,1)S(1)}, bf16[640,128]{1,0:T(8,128)(2,1)S(1)}, u32[]{:S(2)}, u32[]{:S(2)}) collective-permute-start(bf16[640,128]{1,0:T(8,128)(2,1)S(1)} %collective-permute-done.10.refs_1_), channel_id=1, source_target_pairs={{0,4},{1,3},{4,8},{5,1},{8,12},{9,5},{12,14},{13,9},{14,10},{15,13... | collective-permute-start | bytes 491528 | tf_op jit(solution)/shard_map/ppermute | solution.py:461
  63.2 7.4 %collective-permute-start.16 = (bf16[640,128]{1,0:T(8,128)(2,1)S(1)}, bf16[640,128]{1,0:T(8,128)(2,1)S(1)}, u32[]{:S(2)}, u32[]{:S(2)}) collective-permute-start(bf16[640,128]{1,0:T(8,128)(2,1)S(1)} %collective-permute-done.15.refs_2_), channel_id=1, source_target_pairs={{0,2},{1,5},{4,0},{5,9},{8,4},{9,13},{12,8},{13,15},{14,12},{15,11... | collective-permute-start | bytes 491528 | tf_op jit(solution)/shard_map/ppermute | solution.py:461
  64.1 5.3 %collective-permute-start.12 = (bf16[640,128]{1,0:T(8,128)(2,1)S(1)}, bf16[640,128]{1,0:T(8,128)(2,1)S(1)}, u32[]{:S(2)}, u32[]{:S(2)}) collective-permute-start(bf16[640,128]{1,0:T(8,128)(2,1)S(1)} %collective-permute-done.11.refs_1_), channel_id=1, source_target_pairs={{0,4},{1,3},{4,8},{5,1},{8,12},{9,5},{12,14},{13,9},{14,10},{15,13... | collective-permute-start | bytes 491528 | tf_op jit(solution)/shard_map/ppermute | solution.py:461
  69.5 5.3 %collective-permute-start.13 = (bf16[640,128]{1,0:T(8,128)(2,1)S(1)}, bf16[640,128]{1,0:T(8,128)(2,1)S(1)}, u32[]{:S(2)}, u32[]{:S(2)}) collective-permute-start(bf16[640,128]{1,0:T(8,128)(2,1)S(1)} %collective-permute-done.12.refs_1_), channel_id=1, source_target_pairs={{0,4},{1,3},{4,8},{5,1},{8,12},{9,5},{12,14},{13,9},{14,10},{15,13... | collective-permute-start | bytes 491528 | tf_op jit(solution)/shard_map/ppermute | solution.py:463
  77.8 1.6 %collective-permute-start.17 = (f32[512,128]{1,0:T(8,128)S(1)}, f32[512,128]{1,0:T(8,128)S(1)}, u32[]{:S(2)}, u32[]{:S(2)}) collective-permute-start(f32[512,128]{1,0:T(8,128)S(1)} %get-tuple-element.69), channel_id=1, source_target_pairs={{0,1},{1,0},{2,3},{3,2},{4,5},{5,4},{6,7},{7,6},{8,9},{9,8},{10,11... | collective-permute-start | bytes 786440 | tf_op jit(solution)/shard_map/ppermute | solution.py:486

commit v5 on v4

--- a/solution.py
+++ b/solution.py
@@ -2,7 +2,6 @@
 
 import jax
 import jax.numpy as jnp
-import numpy as np
 from jax import lax
 from jax.experimental import pallas as pl
 from jax.experimental.pallas import tpu as pltpu
@@ -67,16 +66,10 @@
 
 
 def kernel_sum(targets, sources, charges, kept_ref):
-    total = None
-    width = sources.shape[1]
-    step = min(width, 256)
-    for begin in range(0, width, step):
-        kernel = jnp.exp(matmul(targets, sources[:, begin : begin + step])).astype(bf16)
-        if kept_ref is not None:
-            kept_ref[:, begin : begin + step] = kernel
-        added = matmul(kernel, charges[begin : begin + step])
-        total = added if total is None else total + added
-    return total
+    kernel = jnp.exp(matmul(targets, sources)).astype(bf16)
+    if kept_ref is not None:
+        kept_ref[...] = kernel
+    return matmul(kernel, charges)
 
 
 def skeleton_rows(charges, leaf_ref, node_ref, upper_ref):
@@ -90,8 +83,42 @@
     return jnp.concatenate([weights.astype(f32), term], axis=0).T.astype(bf16)
 
 
+def count_rows(ring, near_ref, far_ref):
+    shape = (8, LANES)
+    row, lane = lax.broadcasted_iota(i32, shape, 0), lax.broadcasted_iota(i32, shape, 1)
+    table = jnp.zeros(shape, i32)
+    for leaf in range(LEAVES):
+        for first, ref in ((0, near_ref), (LEAVES, far_ref)):
+            for slot in range(ref.shape[1]):
+                hit = (row == first + leaf) & (lane == ref[leaf, slot])
+                table = table + jnp.where(hit, 1, 0)
+    chips = len(ring)
+    me = lax.axis_index("leaf")
+    core = me % CORES
+    place = jnp.int32(0)
+    for at, chip in enumerate(ring):
+        place = jnp.where(me // CORES == chip, at, place)
+    hop = (lane + 1) // 2
+    way = jnp.where(lane % 2 == 1, -1, 1) * (1 - 2 * core)
+    met = (place + way * hop + chips) % chips
+    device = jnp.zeros(shape, i32)
+    for at, chip in enumerate(ring):
+        device = jnp.where(met == at, chip * CORES + core, device)
+    return jnp.where(row == 2 * LEAVES, device, table)
+
+
 def message_kernel(
-    coords_ref, charges_ref, points_ref, leaf_ref, node_ref, upper_ref, message_ref
+    ring,
+    near_ref,
+    far_ref,
+    coords_ref,
+    charges_ref,
+    points_ref,
+    leaf_ref,
+    node_ref,
+    upper_ref,
+    message_ref,
+    table_ref,
 ):
     dim, local = coords_ref.shape
     half = local // LEAVES
@@ -103,6 +130,7 @@
         message_ref[place : place + dim, :] = coords_ref[:, block * LANES : (block + 1) * LANES]
         place += dim
     message_ref[place : place + dim, :] = points_ref[...]
+    table_ref[...] = count_rows(ring, near_ref, far_ref)
 
 
 def joined_kernel(mine_ref, other_ref, leaf_ref, node_ref, upper_ref, out_ref, message_ref):
@@ -126,7 +154,7 @@
     spots, n_spots, n_sub, dim, points, first, last, with_targets, mode = stage
     refs = list(refs)
     use, keep = mode == "use", mode == "keep"
-    table_ref = refs.pop(0)
+    table_refs = refs.pop(0), refs.pop(0)
     place_refs = [] if use else [refs.pop(0) for _ in spots]
     charge_refs = [refs.pop(0) for _ in spots]
     near_kept_ref = far_kept_ref = upper_kept_ref = targets_ref = None
@@ -134,7 +162,7 @@
         near_kept_ref, far_kept_ref = refs.pop(0), refs.pop(0)
         upper_kept_ref = refs.pop(0) if last else None
     elif with_targets:
-        coords_refs = (refs.pop(0), refs.pop(0))
+        sibling_ref = refs.pop(0)
     else:
         targets_ref = refs.pop(0)
     if not first:
@@ -156,11 +184,22 @@
     blocks = points // LANES
     low_half = in_low_half((LANES, LANES))
 
+    def count(core, row, entry):
+        mine, other = (ref[row, entry] for ref in table_refs)
+        return jnp.where(core == 0, mine, other)
+
+    def points_of(ref, leaf):
+        begin = coords_at + leaf * blocks * dim
+        own = [ref[begin + block * dim : begin + (block + 1) * dim, :] for block in range(blocks)]
+        return jnp.concatenate(own, axis=1)
+
+    devices = [table_refs[0][2 * LEAVES, spot] for spot in spots]
+
     if with_targets:
-        for core in range(CORES):
-            for leaf in range(LEAVES):
-                span = slice(leaf * points, (leaf + 1) * points)
-                targets_ref[core * LEAVES + leaf] = target_rows(coords_refs[core][:, span])
+        for leaf in range(LEAVES):
+            span = slice(leaf * points, (leaf + 1) * points)
+            targets_ref[leaf] = target_rows(points_of(place_refs[0], leaf))
+            targets_ref[LEAVES + leaf] = target_rows(sibling_ref[:, span])
     if first:
         total_ref[...] = jnp.zeros_like(total_ref)
         sums_ref[...] = jnp.zeros_like(sums_ref)
@@ -173,7 +212,7 @@
             return matmul(kept_ref[...], charges)
         return kernel_sum(targets_ref[target], sources_ref[...], charges, kept_ref)
 
-    def far_part(skeletons, weights, entries, kept_ref, kept_at):
+    def far_part(skeletons, weights, nodes, kept_ref, kept_at):
         width = len(weights) * LANES
         sources_ref = None
         if not use:
@@ -183,8 +222,8 @@
         def step(core, carry):
             for leaf in range(LEAVES):
                 target = core * LEAVES + leaf
-                for position, (block, entry) in enumerate(zip(weights, entries)):
-                    scaled = block * table_ref[target, entry].astype(f32)
+                for position, (block, node) in enumerate(zip(weights, nodes)):
+                    scaled = block * count(core, LEAVES + leaf, node).astype(f32)
                     high = scaled.astype(bf16).astype(f32)
                     rows = pl.ds(position * LANES, LANES)
                     far_charges_ref[leaf, rows, :] = jnp.where(
@@ -201,20 +240,15 @@
         lax.fori_loop(0, CORES, step, 0)
 
     weights = []
-    for position, spot in enumerate(spots):
+    for position in range(len(spots)):
         rows = charge_refs[position][points : points + LANES, :].astype(f32)
         weights.append(jnp.where(low_half, rows, swapped(rows)))
-        sums_ref[table_ref[TARGETS, spot]] += rows
+        sums_ref[devices[position] // BRANCH] += rows
         lane = lax.broadcasted_iota(i32, (1, LANES), 1) // (LANES // LEAVES)
         for leaf in range(LEAVES):
             place = position * LEAVES + leaf
             if not use:
-                begin = coords_at + leaf * blocks * dim
-                own = [
-                    place_refs[position][begin + block * dim : begin + (block + 1) * dim, :]
-                    for block in range(blocks)
-                ]
-                put_sources(near_ref.at[place], jnp.concatenate(own, axis=1))
+                put_sources(near_ref.at[place], points_of(place_refs[position], leaf))
             chosen = jnp.where(lane == leaf, 1.0, 0.0).astype(bf16)
             charges_ref[place] = charge_refs[position][0:points, :] * chosen
 
@@ -222,7 +256,7 @@
     far_part(
         [ref[skeletons_at : skeletons_at + dim, :] for ref in place_refs],
         weights,
-        [LEAVES * n_spots + spot for spot in spots],
+        devices,
         far_kept_ref,
         0,
     )
@@ -235,44 +269,40 @@
             far_part(
                 skeletons,
                 [jnp.where(low_half, swapped(sums_ref[sub]), sums_ref[sub]) for sub in subs],
-                [(LEAVES + 1) * n_spots + sub for sub in subs],
+                [CORES * n_spots + sub for sub in subs],
                 upper_kept_ref,
                 begin * LANES,
             )
 
-    def near_part(turn, position, spot, core, leaf):
-        targets = [core * LEAVES + own for own in range(LEAVES)]
+    def near_part(turn, position, core, leaf):
+        device = table_refs[0][2 * LEAVES, spots[0] + position]
         if leaf is None:
-            named = sum(table_ref[target, spot * LEAVES + 1] for target in targets)
+            named = sum(count(core, own, device * LEAVES + 1) for own in range(LEAVES))
             leaf = jnp.where(named > 0, 1, 0)
         place = position * LEAVES + leaf
-        times = [table_ref[target, spot * LEAVES + leaf] for target in targets]
+        times = [count(core, own, device * LEAVES + leaf) for own in range(LEAVES)]
 
         @pl.when(sum(times) > 0)
         def _():
-            for own, (target, count) in enumerate(zip(targets, times)):
+            for own in range(LEAVES):
+                target = core * LEAVES + own
                 kept = None if near_kept_ref is None else near_kept_ref.at[turn * LEAVES + own]
                 sources_ref = None if use else near_ref.at[place]
-                total_ref[target] += count.astype(f32) * added(
+                total_ref[target] += times[own].astype(f32) * added(
                     target, sources_ref, charges_ref[place], kept
                 )
 
-    if first:
-        def near_step(turn, carry):
-            named = table_ref[LEAVES, 1] + table_ref[LEAVES + 1, 1]
+    def near_step(turn, carry):
+        if first:
+            device = table_refs[0][2 * LEAVES, 0]
+            named = sum(count(1, own, device * LEAVES + 1) for own in range(LEAVES))
             other = jnp.where(named > 0, 1, 0)
-            near_part(turn, 0, 0, turn // LEAVES, jnp.where(turn < LEAVES, turn, other))
-            return carry
-
-        lax.fori_loop(0, LEAVES + 1, near_step, 0)
-    else:
-
-        def near_step(turn, carry):
-            position = turn // CORES
-            near_part(turn, position, spots[0] + position, turn % CORES, None)
-            return carry
-
-        lax.fori_loop(0, len(spots) * CORES, near_step, 0)
+            near_part(turn, 0, turn // LEAVES, jnp.where(turn < LEAVES, turn, other))
+        else:
+            near_part(turn, turn // CORES, turn % CORES, None)
+        return carry
+
+    lax.fori_loop(0, LEAVES + 1 if first else len(spots) * CORES, near_step, 0)
 
     if last:
         for core, ref in enumerate(half_refs):
@@ -311,21 +341,6 @@
     return list(range(chips))
 
 
-def spots_of(peers):
-    ring = ring_order(peers // CORES)
-    chips = len(ring)
-    found = np.zeros((peers, chips), np.int32)
-    for place, chip in enumerate(ring):
-        for core in range(CORES):
-            way = 1 - 2 * core
-            met = [chip]
-            for hop in range(1, chips // 2):
-                met += [ring[(place - way * hop) % chips], ring[(place + way * hop) % chips]]
-            met.append(ring[(place + chips // 2) % chips])
-            found[chip * CORES + core] = [other * CORES + core for other in met]
-    return found
-
-
 def on_device(
     coords,
     charges,
@@ -341,11 +356,9 @@
     columns = charges.shape[0]
     points = local // LEAVES
     peers = lax.axis_size("leaf")
-    me = lax.axis_index("leaf")
     n_sub = peers // BRANCH
     ring = ring_order(peers // CORES)
     chips = len(ring)
-    near_slots = near_lists.shape[1]
 
     def along(step):
         return [
@@ -364,29 +377,18 @@
         return jax.ShapeDtypeStruct(extent, dtype)
 
     maps = [leaf_interp, node_interp, upper_interp]
-    (message,) = call(
-        message_kernel,
-        [coords, charges, node_points] + maps,
-        [shape(points + LANES + LEAVES * points // LANES * dim + dim, LANES)],
-        streamed=range(6),
+    message, table = call(
+        functools.partial(message_kernel, ring),
+        [near_lists, far_lists, coords, charges, node_points] + maps,
+        [
+            shape(points + LANES + LEAVES * points // LANES * dim + dim, LANES),
+            shape(8, LANES, dtype=i32),
+        ],
+        streamed=range(2, 8),
         vmem_mib=60,
     )
-
-    lists = jnp.concatenate([near_lists, far_lists], axis=1)
-    lists = jnp.concatenate([lists, to_sibling(lists)], axis=0)
+    tables = [table, to_sibling(table)]
     sibling_coords = to_sibling(coords)
-    spots = lax.dynamic_index_in_dim(jnp.asarray(spots_of(peers)), me, 0, keepdims=False)
-    near_ids = (spots[:, None] * LEAVES + jnp.arange(LEAVES)[None, :]).reshape(-1)
-    far_ids = jnp.concatenate([spots, peers + jnp.arange(n_sub)])
-    counts = jnp.concatenate(
-        [
-            jnp.sum((lists[:, :near_slots, None] == near_ids).astype(i32), axis=1),
-            jnp.sum((lists[:, near_slots:, None] == far_ids).astype(i32), axis=1),
-        ],
-        axis=1,
-    )
-    branch = jnp.pad(spots // BRANCH, (0, counts.shape[1] - chips))
-    table = jnp.concatenate([counts, branch[None, :]], axis=0)
 
     total_shape = shape(TARGETS, points, LANES, dtype=f32)
     sums_shape = shape(n_sub, LANES, LANES, dtype=f32)
@@ -401,13 +403,11 @@
         first = carried is None
         with_targets = targets is None
         mode = "use" if kept else "keep" if keeping else "make"
-        args = [table] + ([] if kept else placed) + charged
-        streamed = []
+        args = tables + ([] if kept else placed) + charged
         if kept:
             args += kept
         elif with_targets:
-            streamed = [len(args)]
-            args += [coords, sibling_coords]
+            args += [sibling_coords]
         else:
             args += [targets]
         carried_at = len(args)
@@ -445,7 +445,6 @@
             functools.partial(stage_kernel, static),
             args,
             outs,
-            streamed=streamed,
             scratch=scratch,
             aliases=aliases,
             flops=len(places) * (1 if kept else 2) * 10**9,

time: 80.4 us -> 75.9 us (0.944)
  Pallas kernels: 44.7 us -> 41.1 us
  other arithmetic: 2.87 us -> 0 us
  waiting for transfers between devices: 11.9 us -> 14.5 us
  local copies, waits for them, and re-layouts: 2.84 us -> 1.68 us
    pallas_call x13, Pallas kernels: 44.7 us -> 41.1 us  [call(): pl.pallas_call(body, grid=(1,), out_shape=out_shapes, in_specs=specs, out...]
    concatenate x4 -> x0, other arithmetic: 1.7 us -> none  [the longest x1 0.77 us: on_device(): lists = jnp.concatenate([lists, to_sibling(lists)], axis=0)]
    ppermute x12, waiting for transfers between devices: 7.91 us -> 9.35 us  [around(): one, other = (one_way(one), other_way(other))]
    ppermute x1, waiting for transfers between devices: 0.01 us -> 1.21 us  [on_device(): tables = [table, to_sibling(table)]]
    ppermute x2, starting transfers between devices: 2.92 us -> 2.01 us  [around(): met.append([one_way(one)])]
    ppermute x2, starting transfers between devices: 0.14 us -> 0.97 us  [on_device(): to_sibling(other)]
    unnamed x12 -> x14, local copies, waits for them, and re-layouts: 1.9 us -> 1.68 us
  transfers between devices with their start and end apart: 18 -> 18, of which waited for: 8 -> 12; matrix products, arithmetic and copies ran while one was open for 5% -> 0% of each run, Pallas kernels for 44% -> 44%
where the time goes in v5:
time: 75.9 us; the launch traced here: 75.7 us
  Pallas kernels  41.1 us (54%)
  starting transfers between devices  17.6 us (23%)
  waiting for transfers between devices  14.5 us (19%)
  local copies, waits for them, and re-layouts  1.68 us (2%)
  between operations  0.77 us (1%)
    pallas_call x13, Pallas kernels, call(): pl.pallas_call(body, grid=(1,), out_shape=out_shapes, in_specs=specs, out...  41.1 us
    ppermute x12, starting transfers between devices, around(): one, other = (one_way(one), other_way(other))  14 us
    ppermute x12, waiting for transfers between devices, around(): one, other = (one_way(one), other_way(other))  9.35 us
    ppermute x2, waiting for transfers between devices, on_device(): to_sibling(other)  2.68 us
    ppermute x2, starting transfers between devices, around(): met.append([one_way(one)])  2.01 us
    unnamed x14, local copies, waits for them, and re-layouts  1.68 us
  transfers between devices with their start and end apart: 18, of which 12 were waited for; matrix products, arithmetic and copies ran while one was open for 0% of the time, Pallas kernels for 44%

profile of v5, /device:TPU:0, one launch (start us, length us, event | category | flops | bytes accessed | tf_op | source)
XLA Modules:
  0.0 75.7 jit_solution(2922459137786856042)
XLA Ops:
  1.1 2.3 %shard_map.104 = (bf16[1216,128]{1,0:T(8,128)(2,1)}, s32[8,128]{1,0:T(8,128)}) custom-call(s32[2,16]{1,0:T(2,128)} %near_ref.1, s32[2,32]{1,0:T(2,128)} %far_ref.1, bf16[64,1024]{1,0:T(8,128)(2,1)} %coords_ref.1, bf16[64,1024]{1,0:T(8,128)(2,1)} %charges_ref.1, bf16[64,128]{1,0:T(8,128)(2,1)} %points_ref.1, bf16[1024,128]{1,0:T(8,128)(2,1)} %leaf_ref.3, ...), custom_call_target="tpu_custom_call" | custom-call | bytes 639360 | tf_op jit(solution)/shard_map/pallas_call | solution.py:325
  3.4 2.5 %collective-permute-start.6 = (bf16[1216,128]{1,0:T(8,128)(2,1)}, bf16[1216,128]{1,0:T(8,128)(2,1)S(1)}, u32[]{:S(2)}, u32[]{:S(2)}) collective-permute-start(bf16[1216,128]{1,0:T(8,128)(2,1)} %get-tuple-element.39.refs_2_.refs_3_), channel_id=1, source_target_pairs={{0,2},{1,5},{4,0},{5,9},{8,4},{9,13},{12,8},{13,15},{14,12},{15,11... | collective-permute-start | bytes 933896 | tf_op jit(solution)/shard_map/ppermute | solution.py:460
  6.2 1.2 %collective-permute-done.refs_1_ = s32[8,128]{1,0:T(8,128)S(1)} collective-permute-done((s32[8,128]{1,0:T(8,128)}, s32[8,128]{1,0:T(8,128)S(1)}, u32[]{:S(2)}, u32[]{:S(2)}) %collective-permute-start) | collective-permute-done | bytes 4128 | tf_op jit(solution)/shard_map/ppermute | solution.py:390
  9.1 3.5 %shard_map.105 = (bf16[4,512,128]{2,1,0:T(8,128)(2,1)S(1)}, bf16[6,512,512]{2,1,0:T(8,128)(2,1)S(1)}, bf16[4,512,128]{2,1,0:T(8,128)(2,1)S(1)}, f32[4,512,128]{2,1,0:T(8,128)S(1)}, f32[1,128,128]{2,1,0:T(8,128)S(1)}) custom-call(s32[8,128]{1,0:T(8,128)S(1)} %copy-done.3, s32[8,128]{1,0:T(8,128)S(1)} %collective-permute-done.refs_1_, ...), custom_call_target="tpu_custom_call" | custom-call | flops 2000000000 | bytes 761856 | tf_op jit(solution)/shard_map/pallas_call | solution.py:325
  13.7 2.4 %collective-permute-start.7 = (bf16[1216,128]{1,0:T(8,128)(2,1)S(1)}, bf16[1216,128]{1,0:T(8,128)(2,1)S(1)}, u32[]{:S(2)}, u32[]{:S(2)}) collective-permute-start(bf16[1216,128]{1,0:T(8,128)(2,1)S(1)} %collective-permute-done.6.refs_3_.refs_5_), channel_id=1, source_target_pairs={{0,2},{1,5},{4,0},{5,9},{8,4},{9,13},{12,8},{13,15},{14,12},{15,11... | collective-permute-start | bytes 933896 | tf_op jit(solution)/shard_map/ppermute | solution.py:460
  16.0 4.6 %shard_map.106 = (bf16[8,512,512]{2,1,0:T(8,128)(2,1)S(1)}, bf16[4,512,256]{2,1,0:T(8,128)(2,1)S(1)}, f32[4,512,128]{2,1,0:T(8,128)S(1)}, f32[1,128,128]{2,1,0:T(8,128)S(1)}) custom-call(s32[8,128]{1,0:T(8,128)S(1)} %copy-done.4, s32[8,128]{1,0:T(8,128)S(1)} %collective-permute-done.refs_1_, ...), custom_call_target="tpu_custom_call", output_to_operand_aliasing={{2}: (7, {}), {3}: (8, {})} | custom-call | flops 4000000000 | bytes 2891776 | tf_op jit(solution)/shard_map/pallas_call | solution.py:325
  20.7 2.5 %collective-permute-done.7.refs_3_.refs_5_ = bf16[1216,128]{1,0:T(8,128)(2,1)S(1)} collective-permute-done((bf16[1216,128]{1,0:T(8,128)(2,1)S(1)}, bf16[1216,128]{1,0:T(8,128)(2,1)S(1)}, u32[]{:S(2)}, u32[]{:S(2)}) %collective-permute-start.7) | collective-permute-done | bytes 311328 | tf_op jit(solution)/shard_map/ppermute | solution.py:460
  23.1 2.0 %collective-permute-start.8 = (bf16[1216,128]{1,0:T(8,128)(2,1)S(1)}, bf16[1216,128]{1,0:T(8,128)(2,1)S(1)}, u32[]{:S(2)}, u32[]{:S(2)}) collective-permute-start(bf16[1216,128]{1,0:T(8,128)(2,1)S(1)} %collective-permute-done.7.refs_3_.refs_5_), channel_id=1, source_target_pairs={{0,2},{1,5},{4,0},{5,9},{8,4},{9,13},{12,8},{13,15},{14,12},{15,11... | collective-permute-start | bytes 933896 | tf_op jit(solution)/shard_map/ppermute | solution.py:460
  25.6 5.4 %shard_map.107 = (bf16[8,512,512]{2,1,0:T(8,128)(2,1)S(1)}, bf16[4,512,256]{2,1,0:T(8,128)(2,1)S(1)}, f32[4,512,128]{2,1,0:T(8,128)S(1)}, f32[1,128,128]{2,1,0:T(8,128)S(1)}) custom-call(s32[8,128]{1,0:T(8,128)S(1)} %copy-done.4, s32[8,128]{1,0:T(8,128)S(1)} %collective-permute-done.refs_1_, ...), custom_call_target="tpu_custom_call", output_to_operand_aliasing={{2}: (7, {}), {3}: (8, {})} | custom-call | flops 4000000000 | bytes 2891776 | tf_op jit(solution)/shard_map/pallas_call | solution.py:325
  32.0 1.1 %collective-permute-start.4 = (bf16[1216,128]{1,0:T(8,128)(2,1)S(1)}, bf16[1216,128]{1,0:T(8,128)(2,1)S(1)}, u32[]{:S(2)}, u32[]{:S(2)}) collective-permute-start(bf16[1216,128]{1,0:T(8,128)(2,1)S(1)} %collective-permute-done.3.refs_2_.refs_4_), channel_id=1, source_target_pairs={{0,4},{1,3},{4,8},{5,1},{8,12},{9,5},{12,14},{13,9},{14,10},{15,13... | collective-permute-start | bytes 933896 | tf_op jit(solution)/shard_map/ppermute | solution.py:462
  33.2 5.4 %shard_map.108 = (bf16[8,512,512]{2,1,0:T(8,128)(2,1)S(1)}, bf16[4,512,256]{2,1,0:T(8,128)(2,1)S(1)}, f32[4,512,128]{2,1,0:T(8,128)S(1)}, f32[1,128,128]{2,1,0:T(8,128)S(1)}) custom-call(s32[8,128]{1,0:T(8,128)S(1)} %copy-done.4, s32[8,128]{1,0:T(8,128)S(1)} %collective-permute-done.refs_1_, ...), custom_call_target="tpu_custom_call", output_to_operand_aliasing={{2}: (7, {}), {3}: (8, {})} | custom-call | flops 4000000000 | bytes 2891776 | tf_op jit(solution)/shard_map/pallas_call | solution.py:325
  38.9 3.7 %shard_map.109 = (bf16[4,512,512]{2,1,0:T(8,128)(2,1)S(1)}, bf16[4,512,128]{2,1,0:T(8,128)(2,1)S(1)}, bf16[4,512,128]{2,1,0:T(8,128)(2,1)S(1)}, f32[512,128]{1,0:T(8,128)S(1)}, f32[512,128]{1,0:T(8,128)S(1)}) custom-call(s32[8,128]{1,0:T(8,128)S(1)} %copy-done.4, s32[8,128]{1,0:T(8,128)S(1)} %collective-permute-done.refs_1_, ...), custom_call_target="tpu_custom_call" | custom-call | flops 2000000000 | bytes 2285568 | tf_op jit(solution)/shard_map/pallas_call | solution.py:325
  43.5 1.2 %collective-permute-done.9.other_ref = f32[512,128]{1,0:T(8,128)S(1)} collective-permute-done((f32[512,128]{1,0:T(8,128)S(1)}, f32[512,128]{1,0:T(8,128)S(1)}, u32[]{:S(2)}, u32[]{:S(2)}) %collective-permute-start.9) | collective-permute-done | bytes 262176 | tf_op jit(solution)/shard_map/ppermute | solution.py:481
  45.6 1.2 %collective-permute-start.14 = (bf16[640,128]{1,0:T(8,128)(2,1)S(1)}, bf16[640,128]{1,0:T(8,128)(2,1)S(1)}, u32[]{:S(2)}, u32[]{:S(2)}) collective-permute-start(bf16[640,128]{1,0:T(8,128)(2,1)S(1)} %get-tuple-element.52.refs_2_), channel_id=1, source_target_pairs={{0,2},{1,5},{4,0},{5,9},{8,4},{9,13},{12,8},{13,15},{14,12},{15,11... | collective-permute-start | bytes 491528 | tf_op jit(solution)/shard_map/ppermute | solution.py:460
  47.6 2.2 %shard_map.111 = (f32[4,512,128]{2,1,0:T(8,128)S(1)}, f32[1,128,128]{2,1,0:T(8,128)S(1)}) custom-call(s32[8,128]{1,0:T(8,128)S(1)} %copy-done.4, s32[8,128]{1,0:T(8,128)S(1)} %collective-permute-done.refs_1_, bf16[640,128]{1,0:T(8,128)(2,1)S(1)} %get-tuple-element.52.refs_2_, bf16[6,512,512]{2,1,0:T(8,128)(2,1)S(1)} %get-tuple-element.62.refs_3_, ...), custom_call_target="tpu_custom_call" | custom-call | flops 1000000000 | bytes 3842048 | tf_op jit(solution)/shard_map/pallas_call | solution.py:325
  49.8 2.0 %collective-permute-done.14.refs_3_ = bf16[640,128]{1,0:T(8,128)(2,1)S(1)} collective-permute-done((bf16[640,128]{1,0:T(8,128)(2,1)S(1)}, bf16[640,128]{1,0:T(8,128)(2,1)S(1)}, u32[]{:S(2)}, u32[]{:S(2)}) %collective-permute-start.14) | collective-permute-done | bytes 163872 | tf_op jit(solution)/shard_map/ppermute | solution.py:460
  51.8 2.0 %collective-permute-start.15 = (bf16[640,128]{1,0:T(8,128)(2,1)S(1)}, bf16[640,128]{1,0:T(8,128)(2,1)S(1)}, u32[]{:S(2)}, u32[]{:S(2)}) collective-permute-start(bf16[640,128]{1,0:T(8,128)(2,1)S(1)} %collective-permute-done.14.refs_3_), channel_id=1, source_target_pairs={{0,2},{1,5},{4,0},{5,9},{8,4},{9,13},{12,8},{13,15},{14,12},{15,11... | collective-permute-start | bytes 491528 | tf_op jit(solution)/shard_map/ppermute | solution.py:460
  54.3 2.9 %shard_map.112 = (f32[4,512,128]{2,1,0:T(8,128)S(1)}, f32[1,128,128]{2,1,0:T(8,128)S(1)}) custom-call(s32[8,128]{1,0:T(8,128)S(1)} %copy-done.4, s32[8,128]{1,0:T(8,128)S(1)} %collective-permute-done.refs_1_, bf16[640,128]{1,0:T(8,128)(2,1)S(1)} %collective-permute-done.10.refs_2_, ...), custom_call_target="tpu_custom_call", output_to_operand_aliasing={{0}: (6, {}), {1}: (7, {})} | custom-call | flops 2000000000 | bytes 6692864 | tf_op jit(solution)/shard_map/pallas_call | solution.py:325
  57.2 1.7 %collective-permute-done.15.refs_3_ = bf16[640,128]{1,0:T(8,128)(2,1)S(1)} collective-permute-done((bf16[640,128]{1,0:T(8,128)(2,1)S(1)}, bf16[640,128]{1,0:T(8,128)(2,1)S(1)}, u32[]{:S(2)}, u32[]{:S(2)}) %collective-permute-start.15) | collective-permute-done | bytes 163872 | tf_op jit(solution)/shard_map/ppermute | solution.py:460
  58.9 1.1 %collective-permute-start.16 = (bf16[640,128]{1,0:T(8,128)(2,1)S(1)}, bf16[640,128]{1,0:T(8,128)(2,1)S(1)}, u32[]{:S(2)}, u32[]{:S(2)}) collective-permute-start(bf16[640,128]{1,0:T(8,128)(2,1)S(1)} %collective-permute-done.15.refs_3_), channel_id=1, source_target_pairs={{0,2},{1,5},{4,0},{5,9},{8,4},{9,13},{12,8},{13,15},{14,12},{15,11... | collective-permute-start | bytes 491528 | tf_op jit(solution)/shard_map/ppermute | solution.py:460
  60.9 3.3 %shard_map.113 = (f32[4,512,128]{2,1,0:T(8,128)S(1)}, f32[1,128,128]{2,1,0:T(8,128)S(1)}) custom-call(s32[8,128]{1,0:T(8,128)S(1)} %copy-done.4, s32[8,128]{1,0:T(8,128)S(1)} %collective-permute-done.refs_1_, bf16[640,128]{1,0:T(8,128)(2,1)S(1)} %collective-permute-done.11.refs_2_, ...), custom_call_target="tpu_custom_call", output_to_operand_aliasing={{0}: (6, {}), {1}: (7, {})} | custom-call | flops 2000000000 | bytes 6692864 | tf_op jit(solution)/shard_map/pallas_call | solution.py:325
  66.2 3.3 %shard_map.114 = (f32[4,512,128]{2,1,0:T(8,128)S(1)}, f32[1,128,128]{2,1,0:T(8,128)S(1)}) custom-call(s32[8,128]{1,0:T(8,128)S(1)} %copy-done.4, s32[8,128]{1,0:T(8,128)S(1)} %collective-permute-done.refs_1_, bf16[640,128]{1,0:T(8,128)(2,1)S(1)} %collective-permute-done.12.refs_2_, ...), custom_call_target="tpu_custom_call", output_to_operand_aliasing={{0}: (6, {}), {1}: (7, {})} | custom-call | flops 2000000000 | bytes 6692864 | tf_op jit(solution)/shard_map/pallas_call | solution.py:325
  70.7 2.6 %shard_map.115 = (f32[512,128]{1,0:T(8,128)S(1)}, f32[512,128]{1,0:T(8,128)S(1)}) custom-call(s32[8,128]{1,0:T(8,128)S(1)} %copy-done.4, s32[8,128]{1,0:T(8,128)S(1)} %collective-permute-done.refs_1_, bf16[640,128]{1,0:T(8,128)(2,1)S(1)} %collective-permute-done.13.refs_2_, bf16[4,512,512]{2,1,0:T(8,128)(2,1)S(1)} %get-tuple-element.53.refs_3_, ...), custom_call_target="tpu_custom_call" | custom-call | flops 1000000000 | bytes 4431872 | tf_op jit(solution)/shard_map/pallas_call | solution.py:325
  73.4 1.5 %collective-permute-done.17.other_ref = f32[512,128]{1,0:T(8,128)S(1)} collective-permute-done((f32[512,128]{1,0:T(8,128)S(1)}, f32[512,128]{1,0:T(8,128)S(1)}, u32[]{:S(2)}, u32[]{:S(2)}) %collective-permute-start.17) | collective-permute-done | bytes 262176 | tf_op jit(solution)/shard_map/ppermute | solution.py:485
  (39 shorter events, 13.2 us)
Async XLA Ops:
  0.6 6.8 %collective-permute-start.5 = (bf16[64,1024]{1,0:T(8,128)(2,1)}, bf16[64,1024]{1,0:T(8,128)(2,1)S(1)}, u32[]{:S(2)}, u32[]{:S(2)}) collective-permute-start(bf16[64,1024]{1,0:T(8,128)(2,1)} %coords_ref.1), channel_id=1, source_target_pairs={{0,1},{1,0},{2,3},{3,2},{4,5},{5,4},{6,7},{7,6},{8,9},{9,8},{10,11... | collective-permute-start | bytes 393224 | tf_op jit(solution)/shard_map/ppermute | solution.py:391
  3.4 10.2 %collective-permute-start.6 = (bf16[1216,128]{1,0:T(8,128)(2,1)}, bf16[1216,128]{1,0:T(8,128)(2,1)S(1)}, u32[]{:S(2)}, u32[]{:S(2)}) collective-permute-start(bf16[1216,128]{1,0:T(8,128)(2,1)} %get-tuple-element.39.refs_2_.refs_3_), channel_id=1, source_target_pairs={{0,2},{1,5},{4,0},{5,9},{8,4},{9,13},{12,8},{13,15},{14,12},{15,11... | collective-permute-start | bytes 933896 | tf_op jit(solution)/shard_map/ppermute | solution.py:460
  6.0 10.1 %collective-permute-start.1 = (bf16[1216,128]{1,0:T(8,128)(2,1)}, bf16[1216,128]{1,0:T(8,128)(2,1)S(1)}, u32[]{:S(2)}, u32[]{:S(2)}) collective-permute-start(bf16[1216,128]{1,0:T(8,128)(2,1)} %get-tuple-element.39.refs_2_.refs_3_), channel_id=1, source_target_pairs={{0,4},{1,3},{4,8},{5,1},{8,12},{9,5},{12,14},{13,9},{14,10},{15,13... | collective-permute-start | bytes 933896 | tf_op jit(solution)/shard_map/ppermute | solution.py:460
  6.1 1.4 %collective-permute-start = (s32[8,128]{1,0:T(8,128)}, s32[8,128]{1,0:T(8,128)S(1)}, u32[]{:S(2)}, u32[]{:S(2)}) collective-permute-start(s32[8,128]{1,0:T(8,128)} %get-tuple-element.38.refs_0_), channel_id=1, source_target_pairs={{0,1},{1,0},{2,3},{3,2},{4,5},{5,4},{6,7},{7,6},{8,9},{9,8},{10,11... | collective-permute-start | bytes 12296 | tf_op jit(solution)/shard_map/ppermute | solution.py:390
  8.1 1.0 %copy-start.5 = (bf16[1216,128]{1,0:T(8,128)(2,1)S(1)}, bf16[1216,128]{1,0:T(8,128)(2,1)}, u32[]{:S(2)}) copy-start(bf16[1216,128]{1,0:T(8,128)(2,1)} %get-tuple-element.39.refs_2_.refs_3_) | copy-start | bytes 933892
  9.1 6.9 %copy-start.4 = (s32[8,128]{1,0:T(8,128)S(1)}, s32[8,128]{1,0:T(8,128)}, u32[]{:S(2)}) copy-start(s32[8,128]{1,0:T(8,128)} %get-tuple-element.38.refs_0_) | copy-start | bytes 12292
  13.7 9.5 %collective-permute-start.7 = (bf16[1216,128]{1,0:T(8,128)(2,1)S(1)}, bf16[1216,128]{1,0:T(8,128)(2,1)S(1)}, u32[]{:S(2)}, u32[]{:S(2)}) collective-permute-start(bf16[1216,128]{1,0:T(8,128)(2,1)S(1)} %collective-permute-done.6.refs_3_.refs_5_), channel_id=1, source_target_pairs={{0,2},{1,5},{4,0},{5,9},{8,4},{9,13},{12,8},{13,15},{14,12},{15,11... | collective-permute-start | bytes 933896 | tf_op jit(solution)/shard_map/ppermute | solution.py:460
  16.0 9.1 %collective-permute-start.2 = (bf16[1216,128]{1,0:T(8,128)(2,1)S(1)}, bf16[1216,128]{1,0:T(8,128)(2,1)S(1)}, u32[]{:S(2)}, u32[]{:S(2)}) collective-permute-start(bf16[1216,128]{1,0:T(8,128)(2,1)S(1)} %collective-permute-done.1.refs_2_.refs_4_), channel_id=1, source_target_pairs={{0,4},{1,3},{4,8},{5,1},{8,12},{9,5},{12,14},{13,9},{14,10},{15,13... | collective-permute-start | bytes 933896 | tf_op jit(solution)/shard_map/ppermute | solution.py:460
  23.1 10.1 %collective-permute-start.8 = (bf16[1216,128]{1,0:T(8,128)(2,1)S(1)}, bf16[1216,128]{1,0:T(8,128)(2,1)S(1)}, u32[]{:S(2)}, u32[]{:S(2)}) collective-permute-start(bf16[1216,128]{1,0:T(8,128)(2,1)S(1)} %collective-permute-done.7.refs_3_.refs_5_), channel_id=1, source_target_pairs={{0,2},{1,5},{4,0},{5,9},{8,4},{9,13},{12,8},{13,15},{14,12},{15,11... | collective-permute-start | bytes 933896 | tf_op jit(solution)/shard_map/ppermute | solution.py:460
  25.1 6.9 %collective-permute-start.3 = (bf16[1216,128]{1,0:T(8,128)(2,1)S(1)}, bf16[1216,128]{1,0:T(8,128)(2,1)S(1)}, u32[]{:S(2)}, u32[]{:S(2)}) collective-permute-start(bf16[1216,128]{1,0:T(8,128)(2,1)S(1)} %collective-permute-done.2.refs_2_.refs_4_), channel_id=1, source_target_pairs={{0,4},{1,3},{4,8},{5,1},{8,12},{9,5},{12,14},{13,9},{14,10},{15,13... | collective-permute-start | bytes 933896 | tf_op jit(solution)/shard_map/ppermute | solution.py:460
  32.0 6.9 %collective-permute-start.4 = (bf16[1216,128]{1,0:T(8,128)(2,1)S(1)}, bf16[1216,128]{1,0:T(8,128)(2,1)S(1)}, u32[]{:S(2)}, u32[]{:S(2)}) collective-permute-start(bf16[1216,128]{1,0:T(8,128)(2,1)S(1)} %collective-permute-done.3.refs_2_.refs_4_), channel_id=1, source_target_pairs={{0,4},{1,3},{4,8},{5,1},{8,12},{9,5},{12,14},{13,9},{14,10},{15,13... | collective-permute-start | bytes 933896 | tf_op jit(solution)/shard_map/ppermute | solution.py:462
  33.2 5.7 %copy-start.6 = (bf16[64,128]{1,0:T(8,128)(2,1)S(1)}, bf16[64,128]{1,0:T(8,128)(2,1)}, u32[]{:S(2)}) copy-start(bf16[64,128]{1,0:T(8,128)(2,1)} %refs_7_.1) | copy-start | bytes 49156
  38.7 6.0 %copy-start = (bf16[1024,128]{1,0:T(8,128)(2,1)S(1)}, bf16[1024,128]{1,0:T(8,128)(2,1)}, u32[]{:S(2)}) copy-start(bf16[1024,128]{1,0:T(8,128)(2,1)} %leaf_ref.3) | copy-start | bytes 786436
  38.7 6.0 %copy-start.1 = (bf16[256,128]{1,0:T(8,128)(2,1)S(1)}, bf16[256,128]{1,0:T(8,128)(2,1)}, u32[]{:S(2)}) copy-start(bf16[256,128]{1,0:T(8,128)(2,1)} %node_ref.3) | copy-start | bytes 196612
  38.7 6.0 %copy-start.2 = (bf16[128,128]{1,0:T(8,128)(2,1)S(1)}, bf16[128,128]{1,0:T(8,128)(2,1)}, u32[]{:S(2)}) copy-start(bf16[128,128]{1,0:T(8,128)(2,1)} %upper_ref.3) | copy-start | bytes 98308
  42.6 2.1 %collective-permute-start.9 = (f32[512,128]{1,0:T(8,128)S(1)}, f32[512,128]{1,0:T(8,128)S(1)}, u32[]{:S(2)}, u32[]{:S(2)}) collective-permute-start(f32[512,128]{1,0:T(8,128)S(1)} %get-tuple-element.50), channel_id=1, source_target_pairs={{0,1},{1,0},{2,3},{3,2},{4,5},{5,4},{6,7},{7,6},{8,9},{9,8},{10,11... | collective-permute-start | bytes 786440 | tf_op jit(solution)/shard_map/ppermute | solution.py:481
  45.6 6.2 %collective-permute-start.14 = (bf16[640,128]{1,0:T(8,128)(2,1)S(1)}, bf16[640,128]{1,0:T(8,128)(2,1)S(1)}, u32[]{:S(2)}, u32[]{:S(2)}) collective-permute-start(bf16[640,128]{1,0:T(8,128)(2,1)S(1)} %get-tuple-element.52.refs_2_), channel_id=1, source_target_pairs={{0,2},{1,5},{4,0},{5,9},{8,4},{9,13},{12,8},{13,15},{14,12},{15,11... | collective-permute-start | bytes 491528 | tf_op jit(solution)/shard_map/ppermute | solution.py:460
  46.8 7.0 %collective-permute-start.10 = (bf16[640,128]{1,0:T(8,128)(2,1)S(1)}, bf16[640,128]{1,0:T(8,128)(2,1)S(1)}, u32[]{:S(2)}, u32[]{:S(2)}) collective-permute-start(bf16[640,128]{1,0:T(8,128)(2,1)S(1)} %get-tuple-element.52.refs_2_), channel_id=1, source_target_pairs={{0,4},{1,3},{4,8},{5,1},{8,12},{9,5},{12,14},{13,9},{14,10},{15,13... | collective-permute-start | bytes 491528 | tf_op jit(solution)/shard_map/ppermute | solution.py:460
  51.8 7.1 %collective-permute-start.15 = (bf16[640,128]{1,0:T(8,128)(2,1)S(1)}, bf16[640,128]{1,0:T(8,128)(2,1)S(1)}, u32[]{:S(2)}, u32[]{:S(2)}) collective-permute-start(bf16[640,128]{1,0:T(8,128)(2,1)S(1)} %collective-permute-done.14.refs_3_), channel_id=1, source_target_pairs={{0,2},{1,5},{4,0},{5,9},{8,4},{9,13},{12,8},{13,15},{14,12},{15,11... | collective-permute-start | bytes 491528 | tf_op jit(solution)/shard_map/ppermute | solution.py:460
  53.8 6.2 %collective-permute-start.11 = (bf16[640,128]{1,0:T(8,128)(2,1)S(1)}, bf16[640,128]{1,0:T(8,128)(2,1)S(1)}, u32[]{:S(2)}, u32[]{:S(2)}) collective-permute-start(bf16[640,128]{1,0:T(8,128)(2,1)S(1)} %collective-permute-done.10.refs_2_), channel_id=1, source_target_pairs={{0,4},{1,3},{4,8},{5,1},{8,12},{9,5},{12,14},{13,9},{14,10},{15,13... | collective-permute-start | bytes 491528 | tf_op jit(solution)/shard_map/ppermute | solution.py:460
  58.9 7.4 %collective-permute-start.16 = (bf16[640,128]{1,0:T(8,128)(2,1)S(1)}, bf16[640,128]{1,0:T(8,128)(2,1)S(1)}, u32[]{:S(2)}, u32[]{:S(2)}) collective-permute-start(bf16[640,128]{1,0:T(8,128)(2,1)S(1)} %collective-permute-done.15.refs_3_), channel_id=1, source_target_pairs={{0,2},{1,5},{4,0},{5,9},{8,4},{9,13},{12,8},{13,15},{14,12},{15,11... | collective-permute-start | bytes 491528 | tf_op jit(solution)/shard_map/ppermute | solution.py:460
  60.0 5.3 %collective-permute-start.12 = (bf16[640,128]{1,0:T(8,128)(2,1)S(1)}, bf16[640,128]{1,0:T(8,128)(2,1)S(1)}, u32[]{:S(2)}, u32[]{:S(2)}) collective-permute-start(bf16[640,128]{1,0:T(8,128)(2,1)S(1)} %collective-permute-done.11.refs_2_), channel_id=1, source_target_pairs={{0,4},{1,3},{4,8},{5,1},{8,12},{9,5},{12,14},{13,9},{14,10},{15,13... | collective-permute-start | bytes 491528 | tf_op jit(solution)/shard_map/ppermute | solution.py:460
  65.3 5.3 %collective-permute-start.13 = (bf16[640,128]{1,0:T(8,128)(2,1)S(1)}, bf16[640,128]{1,0:T(8,128)(2,1)S(1)}, u32[]{:S(2)}, u32[]{:S(2)}) collective-permute-start(bf16[640,128]{1,0:T(8,128)(2,1)S(1)} %collective-permute-done.12.refs_2_), channel_id=1, source_target_pairs={{0,4},{1,3},{4,8},{5,1},{8,12},{9,5},{12,14},{13,9},{14,10},{15,13... | collective-permute-start | bytes 491528 | tf_op jit(solution)/shard_map/ppermute | solution.py:462
  73.3 1.6 %collective-permute-start.17 = (f32[512,128]{1,0:T(8,128)S(1)}, f32[512,128]{1,0:T(8,128)S(1)}, u32[]{:S(2)}, u32[]{:S(2)}) collective-permute-start(f32[512,128]{1,0:T(8,128)S(1)} %get-tuple-element.73), channel_id=1, source_target_pairs={{0,1},{1,0},{2,3},{3,2},{4,5},{5,4},{6,7},{7,6},{8,9},{9,8},{10,11... | collective-permute-start | bytes 786440 | tf_op jit(solution)/shard_map/ppermute | solution.py:485
  (1 other events, 0.7 us)

commit v6 on v5

--- a/solution.py
+++ b/solution.py
@@ -12,7 +12,6 @@
 LANES = 128
 CORES = 2
 LEAVES = 2
-TARGETS = CORES * LEAVES
 KEPT_MIB = 30
 
 bf16 = jnp.bfloat16
@@ -65,11 +64,8 @@
     return pltpu.roll(values, LANES // 2, 1)
 
 
-def kernel_sum(targets, sources, charges, kept_ref):
-    kernel = jnp.exp(matmul(targets, sources)).astype(bf16)
-    if kept_ref is not None:
-        kept_ref[...] = kernel
-    return matmul(kernel, charges)
+def kernel_values(targets, sources):
+    return jnp.exp(matmul(targets, sources)).astype(bf16)
 
 
 def skeleton_rows(charges, leaf_ref, node_ref, upper_ref):
@@ -198,19 +194,19 @@
     if with_targets:
         for leaf in range(LEAVES):
             span = slice(leaf * points, (leaf + 1) * points)
-            targets_ref[leaf] = target_rows(points_of(place_refs[0], leaf))
-            targets_ref[LEAVES + leaf] = target_rows(sibling_ref[:, span])
+            targets_ref[0, span, :] = target_rows(points_of(place_refs[0], leaf))
+            targets_ref[1, span, :] = target_rows(sibling_ref[:, span])
     if first:
         total_ref[...] = jnp.zeros_like(total_ref)
         sums_ref[...] = jnp.zeros_like(sums_ref)
-    elif last:
-        total_ref[...] = total_in_ref[...]
-        sums_ref[...] = sums_in_ref[...]
-
-    def added(target, sources_ref, charges, kept_ref):
+
+    def values(core, sources_ref, kept_ref):
         if use:
-            return matmul(kept_ref[...], charges)
-        return kernel_sum(targets_ref[target], sources_ref[...], charges, kept_ref)
+            return kept_ref[...]
+        made = kernel_values(targets_ref[core], sources_ref[...])
+        if kept_ref is not None:
+            kept_ref[...] = made
+        return made
 
     def far_part(skeletons, weights, nodes, kept_ref, kept_at):
         width = len(weights) * LANES
@@ -220,8 +216,11 @@
             put_sources(sources_ref, jnp.concatenate(skeletons, axis=1))
 
         def step(core, carry):
+            kept = None
+            if kept_ref is not None:
+                kept = kept_ref.at[core, :, kept_at : kept_at + width]
+            kernel = values(core, sources_ref, kept)
             for leaf in range(LEAVES):
-                target = core * LEAVES + leaf
                 for position, (block, node) in enumerate(zip(weights, nodes)):
                     scaled = block * count(core, LEAVES + leaf, node).astype(f32)
                     high = scaled.astype(bf16).astype(f32)
@@ -229,11 +228,9 @@
                     far_charges_ref[leaf, rows, :] = jnp.where(
                         low_half, high, scaled - high
                     ).astype(bf16)
-                kept = None
-                if kept_ref is not None:
-                    kept = kept_ref.at[target, :, kept_at : kept_at + width]
-                total_ref[target] += added(
-                    target, sources_ref, far_charges_ref[leaf, 0:width], kept
+                span = slice(leaf * points, (leaf + 1) * points)
+                total_ref[core, span, :] += matmul(
+                    kernel[span], far_charges_ref[leaf, 0:width]
                 )
             return carry
 
@@ -284,13 +281,12 @@
 
         @pl.when(sum(times) > 0)
         def _():
+            kept = None if near_kept_ref is None else near_kept_ref.at[turn]
+            kernel = values(core, None if use else near_ref.at[place], kept)
+            added = matmul(kernel, charges_ref[place])
             for own in range(LEAVES):
-                target = core * LEAVES + own
-                kept = None if near_kept_ref is None else near_kept_ref.at[turn * LEAVES + own]
-                sources_ref = None if use else near_ref.at[place]
-                total_ref[target] += times[own].astype(f32) * added(
-                    target, sources_ref, charges_ref[place], kept
-                )
+                span = slice(own * points, (own + 1) * points)
+                total_ref[core, span, :] += times[own].astype(f32) * added[span]
 
     def near_step(turn, carry):
         if first:
@@ -306,7 +302,9 @@
 
     if last:
         for core, ref in enumerate(half_refs):
-            both = [total_ref[core * LEAVES + leaf] for leaf in range(LEAVES)]
+            both = [
+                total_ref[core, leaf * points : (leaf + 1) * points, :] for leaf in range(LEAVES)
+            ]
             both = [total + swapped(total) for total in both]
             ref[...] = jnp.where(in_low_half(both[0].shape), both[0], both[1])
 
@@ -390,13 +388,13 @@
     tables = [table, to_sibling(table)]
     sibling_coords = to_sibling(coords)
 
-    total_shape = shape(TARGETS, points, LANES, dtype=f32)
+    total_shape = shape(CORES, local, LANES, dtype=f32)
     sums_shape = shape(n_sub, LANES, LANES, dtype=f32)
     half_shape = shape(points, LANES, dtype=f32)
-    targets_shape = shape(TARGETS, points, LANES)
+    targets_shape = shape(CORES, local, LANES)
 
     steps = LEAVES + 1 + CORES * (chips - 1)
-    kept_bytes = 2 * points * (steps * LEAVES * points + TARGETS * (chips + n_sub) * LANES)
+    kept_bytes = 2 * points * (steps * local + CORES * LEAVES * (chips + n_sub) * LANES)
     keeping = kept_bytes <= KEPT_MIB * 2**20
 
     def stage(places, placed, charged, targets, carried, last, kept):
@@ -427,19 +425,14 @@
         if mode == "keep":
             turns = LEAVES + 1 if first else CORES * len(places)
             outs += [
-                shape(turns * LEAVES, points, points),
-                shape(TARGETS, points, len(places) * LANES),
+                shape(turns, local, points),
+                shape(CORES, local, len(places) * LANES),
             ]
-            outs += [shape(TARGETS, points, n_sub * LANES)] if last else []
+            outs += [shape(CORES, local, n_sub * LANES)] if last else []
         kept_to = len(outs)
-        aliases = {}
-        if last:
-            outs += [half_shape, half_shape]
-            scratch = [pltpu.VMEM(total_shape.shape, f32), pltpu.VMEM(sums_shape.shape, f32)] + scratch
-        else:
-            if not first:
-                aliases = {carried_at: len(outs), carried_at + 1: len(outs) + 1}
-            outs += [total_shape, sums_shape]
+        outs += [half_shape, half_shape] if last else []
+        aliases = {} if first else {carried_at + k: len(outs) + k for k in range(2)}
+        outs += [total_shape, sums_shape]
         static = (places, chips, n_sub, dim, points, first, last, with_targets, mode)
         results = call(
             functools.partial(stage_kernel, static),
@@ -451,7 +444,7 @@
         )
         if with_targets:
             targets = results[0]
-        return targets, list(results[kept_at:kept_to]), results[kept_to:]
+        return targets, list(results[kept_at:kept_to]), results[kept_to : kept_to + 2]
 
     def around(message, placed, targets, kept):
         met = [[message]]

time: 75.9 us -> 75.7 us (level)
  waiting for transfers between devices: 14.5 us -> 15.4 us
  Pallas kernels: 41.1 us -> 40.3 us
    ppermute x12, waiting for transfers between devices: 9.35 us -> 10.3 us  [around(): one, other = (one_way(one), other_way(other))]
    ppermute x2, starting transfers between devices: 0.97 us -> 0.14 us  [on_device(): to_sibling(other)]
    pallas_call x13, Pallas kernels: 41.1 us -> 40.3 us  [call(): pl.pallas_call(body, grid=(1,), out_shape=out_shapes, in_specs=specs, out...]
  transfers between devices with their start and end apart: 18 -> 18, of which waited for: 12 -> 12; matrix products, arithmetic and copies ran while one was open for 0% -> 0% of each run, Pallas kernels for 44% -> 42%
where the time goes in v6:
time: 75.7 us; the launch traced here: 75.3 us
  Pallas kernels  40.3 us (53%)
  starting transfers between devices  17.1 us (23%)
  waiting for transfers between devices  15.4 us (20%)
  local copies, waits for them, and re-layouts  1.68 us (2%)
  between operations  0.77 us (1%)
    pallas_call x13, Pallas kernels, call(): pl.pallas_call(body, grid=(1,), out_shape=out_shapes, in_specs=specs, out...  40.3 us
    ppermute x12, starting transfers between devices, around(): one, other = (one_way(one), other_way(other))  13.8 us
    ppermute x12, waiting for transfers between devices, around(): one, other = (one_way(one), other_way(other))  10.3 us
    ppermute x2, waiting for transfers between devices, on_device(): to_sibling(other)  3.04 us
    ppermute x2, starting transfers between devices, around(): met.append([one_way(one)])  2.51 us
    unnamed x14, local copies, waits for them, and re-layouts  1.68 us
  transfers between devices with their start and end apart: 18, of which 12 were waited for; matrix products, arithmetic and copies ran while one was open for 0% of the time, Pallas kernels for 42%

profile of v6, /device:TPU:0, one launch (start us, length us, event | category | flops | bytes accessed | tf_op | source)
XLA Modules:
  0.0 75.3 jit_solution(628518617066775482)
XLA Ops:
  1.1 2.3 %shard_map.104 = (bf16[1216,128]{1,0:T(8,128)(2,1)}, s32[8,128]{1,0:T(8,128)}) custom-call(s32[2,16]{1,0:T(2,128)} %near_ref.1, s32[2,32]{1,0:T(2,128)} %far_ref.1, bf16[64,1024]{1,0:T(8,128)(2,1)} %coords_ref.1, bf16[64,1024]{1,0:T(8,128)(2,1)} %charges_ref.1, bf16[64,128]{1,0:T(8,128)(2,1)} %points_ref.1, bf16[1024,128]{1,0:T(8,128)(2,1)} %leaf_ref.3, ...), custom_call_target="tpu_custom_call" | custom-call | bytes 639360 | tf_op jit(solution)/shard_map/pallas_call | solution.py:323
  3.4 2.5 %collective-permute-start.6 = (bf16[1216,128]{1,0:T(8,128)(2,1)}, bf16[1216,128]{1,0:T(8,128)(2,1)S(1)}, u32[]{:S(2)}, u32[]{:S(2)}) collective-permute-start(bf16[1216,128]{1,0:T(8,128)(2,1)} %get-tuple-element.39.refs_2_.refs_3_), channel_id=1, source_target_pairs={{0,2},{1,5},{4,0},{5,9},{8,4},{9,13},{12,8},{13,15},{14,12},{15,11... | collective-permute-start | bytes 933896 | tf_op jit(solution)/shard_map/ppermute | solution.py:453
  9.1 3.3 %shard_map.105 = (bf16[2,1024,128]{2,1,0:T(8,128)(2,1)S(1)}, bf16[3,1024,512]{2,1,0:T(8,128)(2,1)S(1)}, bf16[2,1024,128]{2,1,0:T(8,128)(2,1)S(1)}, f32[2,1024,128]{2,1,0:T(8,128)S(1)}, f32[1,128,128]{2,1,0:T(8,128)S(1)}) custom-call(s32[8,128]{1,0:T(8,128)S(1)} %copy-done.3, s32[8,128]{1,0:T(8,128)S(1)} %collective-permute-done.refs_1_, ...), custom_call_target="tpu_custom_call" | custom-call | flops 2000000000 | bytes 761856 | tf_op jit(solution)/shard_map/pallas_call | solution.py:323
  12.4 1.3 %collective-permute-done.6.refs_3_.refs_5_ = bf16[1216,128]{1,0:T(8,128)(2,1)S(1)} collective-permute-done((bf16[1216,128]{1,0:T(8,128)(2,1)}, bf16[1216,128]{1,0:T(8,128)(2,1)S(1)}, u32[]{:S(2)}, u32[]{:S(2)}) %collective-permute-start.6) | collective-permute-done | bytes 311328 | tf_op jit(solution)/shard_map/ppermute | solution.py:453
  13.7 2.4 %collective-permute-start.7 = (bf16[1216,128]{1,0:T(8,128)(2,1)S(1)}, bf16[1216,128]{1,0:T(8,128)(2,1)S(1)}, u32[]{:S(2)}, u32[]{:S(2)}) collective-permute-start(bf16[1216,128]{1,0:T(8,128)(2,1)S(1)} %collective-permute-done.6.refs_3_.refs_5_), channel_id=1, source_target_pairs={{0,2},{1,5},{4,0},{5,9},{8,4},{9,13},{12,8},{13,15},{14,12},{15,11... | collective-permute-start | bytes 933896 | tf_op jit(solution)/shard_map/ppermute | solution.py:453
  16.0 4.9 %shard_map.106 = (bf16[4,1024,512]{2,1,0:T(8,128)(2,1)S(1)}, bf16[2,1024,256]{2,1,0:T(8,128)(2,1)S(1)}, f32[2,1024,128]{2,1,0:T(8,128)S(1)}, f32[1,128,128]{2,1,0:T(8,128)S(1)}) custom-call(s32[8,128]{1,0:T(8,128)S(1)} %copy-done.4, s32[8,128]{1,0:T(8,128)S(1)} %collective-permute-done.refs_1_, ...), custom_call_target="tpu_custom_call", output_to_operand_aliasing={{2}: (7, {}), {3}: (8, {})} | custom-call | flops 4000000000 | bytes 2891776 | tf_op jit(solution)/shard_map/pallas_call | solution.py:323
  21.0 2.2 %collective-permute-done.7.refs_3_.refs_5_ = bf16[1216,128]{1,0:T(8,128)(2,1)S(1)} collective-permute-done((bf16[1216,128]{1,0:T(8,128)(2,1)S(1)}, bf16[1216,128]{1,0:T(8,128)(2,1)S(1)}, u32[]{:S(2)}, u32[]{:S(2)}) %collective-permute-start.7) | collective-permute-done | bytes 311328 | tf_op jit(solution)/shard_map/ppermute | solution.py:453
  23.2 1.9 %collective-permute-start.8 = (bf16[1216,128]{1,0:T(8,128)(2,1)S(1)}, bf16[1216,128]{1,0:T(8,128)(2,1)S(1)}, u32[]{:S(2)}, u32[]{:S(2)}) collective-permute-start(bf16[1216,128]{1,0:T(8,128)(2,1)S(1)} %collective-permute-done.7.refs_3_.refs_5_), channel_id=1, source_target_pairs={{0,2},{1,5},{4,0},{5,9},{8,4},{9,13},{12,8},{13,15},{14,12},{15,11... | collective-permute-start | bytes 933896 | tf_op jit(solution)/shard_map/ppermute | solution.py:453
  25.9 4.2 %shard_map.107 = (bf16[4,1024,512]{2,1,0:T(8,128)(2,1)S(1)}, bf16[2,1024,256]{2,1,0:T(8,128)(2,1)S(1)}, f32[2,1024,128]{2,1,0:T(8,128)S(1)}, f32[1,128,128]{2,1,0:T(8,128)S(1)}) custom-call(s32[8,128]{1,0:T(8,128)S(1)} %copy-done.4, s32[8,128]{1,0:T(8,128)S(1)} %collective-permute-done.refs_1_, ...), custom_call_target="tpu_custom_call", output_to_operand_aliasing={{2}: (7, {}), {3}: (8, {})} | custom-call | flops 4000000000 | bytes 2891776 | tf_op jit(solution)/shard_map/pallas_call | solution.py:323
  30.1 1.9 %collective-permute-done.3.refs_2_.refs_4_ = bf16[1216,128]{1,0:T(8,128)(2,1)S(1)} collective-permute-done((bf16[1216,128]{1,0:T(8,128)(2,1)S(1)}, bf16[1216,128]{1,0:T(8,128)(2,1)S(1)}, u32[]{:S(2)}, u32[]{:S(2)}) %collective-permute-start.3) | collective-permute-done | bytes 311328 | tf_op jit(solution)/shard_map/ppermute | solution.py:453
  33.4 4.9 %shard_map.108 = (bf16[4,1024,512]{2,1,0:T(8,128)(2,1)S(1)}, bf16[2,1024,256]{2,1,0:T(8,128)(2,1)S(1)}, f32[2,1024,128]{2,1,0:T(8,128)S(1)}, f32[1,128,128]{2,1,0:T(8,128)S(1)}) custom-call(s32[8,128]{1,0:T(8,128)S(1)} %copy-done.4, s32[8,128]{1,0:T(8,128)S(1)} %collective-permute-done.refs_1_, ...), custom_call_target="tpu_custom_call", output_to_operand_aliasing={{2}: (7, {}), {3}: (8, {})} | custom-call | flops 4000000000 | bytes 2891776 | tf_op jit(solution)/shard_map/pallas_call | solution.py:323
  38.9 4.2 %shard_map.109 = (bf16[2,1024,512]{2,1,0:T(8,128)(2,1)S(1)}, bf16[2,1024,128]{2,1,0:T(8,128)(2,1)S(1)}, bf16[2,1024,128]{2,1,0:T(8,128)(2,1)S(1)}, f32[512,128]{...) custom-call(s32[8,128]{1,0:T(8,128)S(1)} %copy-done.4, ...), custom_call_target="tpu_custom_call", output_to_operand_aliasing={{5}: (5, {}), {6}: (6, {})} | custom-call | flops 2000000000 | bytes 2285568 | tf_op jit(solution)/shard_map/pallas_call | solution.py:323
  43.2 1.5 %collective-permute-done.9.other_ref = f32[512,128]{1,0:T(8,128)S(1)} collective-permute-done((f32[512,128]{1,0:T(8,128)S(1)}, f32[512,128]{1,0:T(8,128)S(1)}, u32[]{:S(2)}, u32[]{:S(2)}) %collective-permute-start.9) | collective-permute-done | bytes 262176 | tf_op jit(solution)/shard_map/ppermute | solution.py:474
  45.9 1.8 %collective-permute-start.10 = (bf16[640,128]{1,0:T(8,128)(2,1)S(1)}, bf16[640,128]{1,0:T(8,128)(2,1)S(1)}, u32[]{:S(2)}, u32[]{:S(2)}) collective-permute-start(bf16[640,128]{1,0:T(8,128)(2,1)S(1)} %get-tuple-element.52.refs_2_), channel_id=1, source_target_pairs={{0,4},{1,3},{4,8},{5,1},{8,12},{9,5},{12,14},{13,9},{14,10},{15,13... | collective-permute-start | bytes 491528 | tf_op jit(solution)/shard_map/ppermute | solution.py:453
  47.7 2.2 %shard_map.111 = (f32[2,1024,128]{2,1,0:T(8,128)S(1)}, f32[1,128,128]{2,1,0:T(8,128)S(1)}) custom-call(s32[8,128]{1,0:T(8,128)S(1)} %copy-done.4, s32[8,128]{1,0:T(8,128)S(1)} %collective-permute-done.refs_1_, bf16[640,128]{1,0:T(8,128)(2,1)S(1)} %get-tuple-element.52.refs_2_, bf16[3,1024,512]{2,1,0:T(8,128)(2,1)S(1)} %get-tuple-element.62.refs_3_, ...), custom_call_target="tpu_custom_call" | custom-call | flops 1000000000 | bytes 3842048 | tf_op jit(solution)/shard_map/pallas_call | solution.py:323
  49.9 2.7 %collective-permute-done.14.refs_3_ = bf16[640,128]{1,0:T(8,128)(2,1)S(1)} collective-permute-done((bf16[640,128]{1,0:T(8,128)(2,1)S(1)}, bf16[640,128]{1,0:T(8,128)(2,1)S(1)}, u32[]{:S(2)}, u32[]{:S(2)}) %collective-permute-start.14) | collective-permute-done | bytes 163872 | tf_op jit(solution)/shard_map/ppermute | solution.py:453
  52.6 2.0 %collective-permute-start.11 = (bf16[640,128]{1,0:T(8,128)(2,1)S(1)}, bf16[640,128]{1,0:T(8,128)(2,1)S(1)}, u32[]{:S(2)}, u32[]{:S(2)}) collective-permute-start(bf16[640,128]{1,0:T(8,128)(2,1)S(1)} %collective-permute-done.10.refs_2_), channel_id=1, source_target_pairs={{0,4},{1,3},{4,8},{5,1},{8,12},{9,5},{12,14},{13,9},{14,10},{15,13... | collective-permute-start | bytes 491528 | tf_op jit(solution)/shard_map/ppermute | solution.py:453
  54.6 3.3 %shard_map.112 = (f32[2,1024,128]{2,1,0:T(8,128)S(1)}, f32[1,128,128]{2,1,0:T(8,128)S(1)}) custom-call(s32[8,128]{1,0:T(8,128)S(1)} %copy-done.4, s32[8,128]{1,0:T(8,128)S(1)} %collective-permute-done.refs_1_, bf16[640,128]{1,0:T(8,128)(2,1)S(1)} %collective-permute-done.10.refs_2_, ...), custom_call_target="tpu_custom_call", output_to_operand_aliasing={{0}: (6, {}), {1}: (7, {})} | custom-call | flops 2000000000 | bytes 6692864 | tf_op jit(solution)/shard_map/pallas_call | solution.py:323
  59.2 1.6 %collective-permute-start.12 = (bf16[640,128]{1,0:T(8,128)(2,1)S(1)}, bf16[640,128]{1,0:T(8,128)(2,1)S(1)}, u32[]{:S(2)}, u32[]{:S(2)}) collective-permute-start(bf16[640,128]{1,0:T(8,128)(2,1)S(1)} %collective-permute-done.11.refs_2_), channel_id=1, source_target_pairs={{0,4},{1,3},{4,8},{5,1},{8,12},{9,5},{12,14},{13,9},{14,10},{15,13... | collective-permute-start | bytes 491528 | tf_op jit(solution)/shard_map/ppermute | solution.py:453
  60.9 2.9 %shard_map.113 = (f32[2,1024,128]{2,1,0:T(8,128)S(1)}, f32[1,128,128]{2,1,0:T(8,128)S(1)}) custom-call(s32[8,128]{1,0:T(8,128)S(1)} %copy-done.4, s32[8,128]{1,0:T(8,128)S(1)} %collective-permute-done.refs_1_, bf16[640,128]{1,0:T(8,128)(2,1)S(1)} %collective-permute-done.11.refs_2_, ...), custom_call_target="tpu_custom_call", output_to_operand_aliasing={{0}: (6, {}), {1}: (7, {})} | custom-call | flops 2000000000 | bytes 6692864 | tf_op jit(solution)/shard_map/pallas_call | solution.py:323
  64.5 1.6 %collective-permute-start.13 = (bf16[640,128]{1,0:T(8,128)(2,1)S(1)}, bf16[640,128]{1,0:T(8,128)(2,1)S(1)}, u32[]{:S(2)}, u32[]{:S(2)}) collective-permute-start(bf16[640,128]{1,0:T(8,128)(2,1)S(1)} %collective-permute-done.12.refs_2_), channel_id=1, source_target_pairs={{0,4},{1,3},{4,8},{5,1},{8,12},{9,5},{12,14},{13,9},{14,10},{15,13... | collective-permute-start | bytes 491528 | tf_op jit(solution)/shard_map/ppermute | solution.py:455
  66.2 3.3 %shard_map.114 = (f32[2,1024,128]{2,1,0:T(8,128)S(1)}, f32[1,128,128]{2,1,0:T(8,128)S(1)}) custom-call(s32[8,128]{1,0:T(8,128)S(1)} %copy-done.4, s32[8,128]{1,0:T(8,128)S(1)} %collective-permute-done.refs_1_, bf16[640,128]{1,0:T(8,128)(2,1)S(1)} %collective-permute-done.12.refs_2_, ...), custom_call_target="tpu_custom_call", output_to_operand_aliasing={{0}: (6, {}), {1}: (7, {})} | custom-call | flops 2000000000 | bytes 6692864 | tf_op jit(solution)/shard_map/pallas_call | solution.py:323
  69.9 3.0 %shard_map.115 = (f32[512,128]{1,0:T(8,128)S(1)}, f32[512,128]{1,0:T(8,128)S(1)}, f32[2,1024,128]{2,1,0:T(8,128)S(1)}, f32[1,128,128]{2,1,0:T(8,128)S(1)}) custom-call(s32[8,128]{1,0:T(8,128)S(1)} %copy-done.4, s32[8,128]{1,0:T(8,128)S(1)} %collective-permute-done.refs_1_, ...), custom_call_target="tpu_custom_call", output_to_operand_aliasing={{2}: (6, {}), {3}: (7, {})} | custom-call | flops 1000000000 | bytes 4431872 | tf_op jit(solution)/shard_map/pallas_call | solution.py:323
  73.0 1.5 %collective-permute-done.17.other_ref = f32[512,128]{1,0:T(8,128)S(1)} collective-permute-done((f32[512,128]{1,0:T(8,128)S(1)}, f32[512,128]{1,0:T(8,128)S(1)}, u32[]{:S(2)}, u32[]{:S(2)}) %collective-permute-start.17) | collective-permute-done | bytes 262176 | tf_op jit(solution)/shard_map/ppermute | solution.py:478
  (39 shorter events, 10.9 us)
Async XLA Ops:
  0.6 6.8 %collective-permute-start.5 = (bf16[64,1024]{1,0:T(8,128)(2,1)}, bf16[64,1024]{1,0:T(8,128)(2,1)S(1)}, u32[]{:S(2)}, u32[]{:S(2)}) collective-permute-start(bf16[64,1024]{1,0:T(8,128)(2,1)} %coords_ref.1), channel_id=1, source_target_pairs={{0,1},{1,0},{2,3},{3,2},{4,5},{5,4},{6,7},{7,6},{8,9},{9,8},{10,11... | collective-permute-start | bytes 393224 | tf_op jit(solution)/shard_map/ppermute | solution.py:389
  3.4 10.2 %collective-permute-start.6 = (bf16[1216,128]{1,0:T(8,128)(2,1)}, bf16[1216,128]{1,0:T(8,128)(2,1)S(1)}, u32[]{:S(2)}, u32[]{:S(2)}) collective-permute-start(bf16[1216,128]{1,0:T(8,128)(2,1)} %get-tuple-element.39.refs_2_.refs_3_), channel_id=1, source_target_pairs={{0,2},{1,5},{4,0},{5,9},{8,4},{9,13},{12,8},{13,15},{14,12},{15,11... | collective-permute-start | bytes 933896 | tf_op jit(solution)/shard_map/ppermute | solution.py:453
  6.0 10.1 %collective-permute-start.1 = (bf16[1216,128]{1,0:T(8,128)(2,1)}, bf16[1216,128]{1,0:T(8,128)(2,1)S(1)}, u32[]{:S(2)}, u32[]{:S(2)}) collective-permute-start(bf16[1216,128]{1,0:T(8,128)(2,1)} %get-tuple-element.39.refs_2_.refs_3_), channel_id=1, source_target_pairs={{0,4},{1,3},{4,8},{5,1},{8,12},{9,5},{12,14},{13,9},{14,10},{15,13... | collective-permute-start | bytes 933896 | tf_op jit(solution)/shard_map/ppermute | solution.py:453
  6.1 1.4 %collective-permute-start = (s32[8,128]{1,0:T(8,128)}, s32[8,128]{1,0:T(8,128)S(1)}, u32[]{:S(2)}, u32[]{:S(2)}) collective-permute-start(s32[8,128]{1,0:T(8,128)} %get-tuple-element.38.refs_0_), channel_id=1, source_target_pairs={{0,1},{1,0},{2,3},{3,2},{4,5},{5,4},{6,7},{7,6},{8,9},{9,8},{10,11... | collective-permute-start | bytes 12296 | tf_op jit(solution)/shard_map/ppermute | solution.py:388
  8.1 1.0 %copy-start.5 = (bf16[1216,128]{1,0:T(8,128)(2,1)S(1)}, bf16[1216,128]{1,0:T(8,128)(2,1)}, u32[]{:S(2)}) copy-start(bf16[1216,128]{1,0:T(8,128)(2,1)} %get-tuple-element.39.refs_2_.refs_3_) | copy-start | bytes 933892
  9.1 6.9 %copy-start.4 = (s32[8,128]{1,0:T(8,128)S(1)}, s32[8,128]{1,0:T(8,128)}, u32[]{:S(2)}) copy-start(s32[8,128]{1,0:T(8,128)} %get-tuple-element.38.refs_0_) | copy-start | bytes 12292
  13.7 9.5 %collective-permute-start.7 = (bf16[1216,128]{1,0:T(8,128)(2,1)S(1)}, bf16[1216,128]{1,0:T(8,128)(2,1)S(1)}, u32[]{:S(2)}, u32[]{:S(2)}) collective-permute-start(bf16[1216,128]{1,0:T(8,128)(2,1)S(1)} %collective-permute-done.6.refs_3_.refs_5_), channel_id=1, source_target_pairs={{0,2},{1,5},{4,0},{5,9},{8,4},{9,13},{12,8},{13,15},{14,12},{15,11... | collective-permute-start | bytes 933896 | tf_op jit(solution)/shard_map/ppermute | solution.py:453
  16.0 9.1 %collective-permute-start.2 = (bf16[1216,128]{1,0:T(8,128)(2,1)S(1)}, bf16[1216,128]{1,0:T(8,128)(2,1)S(1)}, u32[]{:S(2)}, u32[]{:S(2)}) collective-permute-start(bf16[1216,128]{1,0:T(8,128)(2,1)S(1)} %collective-permute-done.1.refs_2_.refs_4_), channel_id=1, source_target_pairs={{0,4},{1,3},{4,8},{5,1},{8,12},{9,5},{12,14},{13,9},{14,10},{15,13... | collective-permute-start | bytes 933896 | tf_op jit(solution)/shard_map/ppermute | solution.py:453
  23.2 10.2 %collective-permute-start.8 = (bf16[1216,128]{1,0:T(8,128)(2,1)S(1)}, bf16[1216,128]{1,0:T(8,128)(2,1)S(1)}, u32[]{:S(2)}, u32[]{:S(2)}) collective-permute-start(bf16[1216,128]{1,0:T(8,128)(2,1)S(1)} %collective-permute-done.7.refs_3_.refs_5_), channel_id=1, source_target_pairs={{0,2},{1,5},{4,0},{5,9},{8,4},{9,13},{12,8},{13,15},{14,12},{15,11... | collective-permute-start | bytes 933896 | tf_op jit(solution)/shard_map/ppermute | solution.py:453
  25.1 6.9 %collective-permute-start.3 = (bf16[1216,128]{1,0:T(8,128)(2,1)S(1)}, bf16[1216,128]{1,0:T(8,128)(2,1)S(1)}, u32[]{:S(2)}, u32[]{:S(2)}) collective-permute-start(bf16[1216,128]{1,0:T(8,128)(2,1)S(1)} %collective-permute-done.2.refs_2_.refs_4_), channel_id=1, source_target_pairs={{0,4},{1,3},{4,8},{5,1},{8,12},{9,5},{12,14},{13,9},{14,10},{15,13... | collective-permute-start | bytes 933896 | tf_op jit(solution)/shard_map/ppermute | solution.py:453
  32.0 6.9 %collective-permute-start.4 = (bf16[1216,128]{1,0:T(8,128)(2,1)S(1)}, bf16[1216,128]{1,0:T(8,128)(2,1)S(1)}, u32[]{:S(2)}, u32[]{:S(2)}) collective-permute-start(bf16[1216,128]{1,0:T(8,128)(2,1)S(1)} %collective-permute-done.3.refs_2_.refs_4_), channel_id=1, source_target_pairs={{0,4},{1,3},{4,8},{5,1},{8,12},{9,5},{12,14},{13,9},{14,10},{15,13... | collective-permute-start | bytes 933896 | tf_op jit(solution)/shard_map/ppermute | solution.py:455
  33.4 5.5 %copy-start.6 = (bf16[64,128]{1,0:T(8,128)(2,1)S(1)}, bf16[64,128]{1,0:T(8,128)(2,1)}, u32[]{:S(2)}) copy-start(bf16[64,128]{1,0:T(8,128)(2,1)} %refs_7_.1) | copy-start | bytes 49156
  38.4 6.4 %copy-start = (bf16[1024,128]{1,0:T(8,128)(2,1)S(1)}, bf16[1024,128]{1,0:T(8,128)(2,1)}, u32[]{:S(2)}) copy-start(bf16[1024,128]{1,0:T(8,128)(2,1)} %leaf_ref.3) | copy-start | bytes 786436
  38.4 6.4 %copy-start.1 = (bf16[256,128]{1,0:T(8,128)(2,1)S(1)}, bf16[256,128]{1,0:T(8,128)(2,1)}, u32[]{:S(2)}) copy-start(bf16[256,128]{1,0:T(8,128)(2,1)} %node_ref.3) | copy-start | bytes 196612
  38.4 6.4 %copy-start.2 = (bf16[128,128]{1,0:T(8,128)(2,1)S(1)}, bf16[128,128]{1,0:T(8,128)(2,1)}, u32[]{:S(2)}) copy-start(bf16[128,128]{1,0:T(8,128)(2,1)} %upper_ref.3) | copy-start | bytes 98308
  43.2 1.6 %collective-permute-start.9 = (f32[512,128]{1,0:T(8,128)S(1)}, f32[512,128]{1,0:T(8,128)S(1)}, u32[]{:S(2)}, u32[]{:S(2)}) collective-permute-start(f32[512,128]{1,0:T(8,128)S(1)} %get-tuple-element.50), channel_id=1, source_target_pairs={{0,1},{1,0},{2,3},{3,2},{4,5},{5,4},{6,7},{7,6},{8,9},{9,8},{10,11... | collective-permute-start | bytes 786440 | tf_op jit(solution)/shard_map/ppermute | solution.py:474
  45.7 6.9 %collective-permute-start.14 = (bf16[640,128]{1,0:T(8,128)(2,1)S(1)}, bf16[640,128]{1,0:T(8,128)(2,1)S(1)}, u32[]{:S(2)}, u32[]{:S(2)}) collective-permute-start(bf16[640,128]{1,0:T(8,128)(2,1)S(1)} %get-tuple-element.52.refs_2_), channel_id=1, source_target_pairs={{0,2},{1,5},{4,0},{5,9},{8,4},{9,13},{12,8},{13,15},{14,12},{15,11... | collective-permute-start | bytes 491528 | tf_op jit(solution)/shard_map/ppermute | solution.py:453
  45.9 6.7 %collective-permute-start.10 = (bf16[640,128]{1,0:T(8,128)(2,1)S(1)}, bf16[640,128]{1,0:T(8,128)(2,1)S(1)}, u32[]{:S(2)}, u32[]{:S(2)}) collective-permute-start(bf16[640,128]{1,0:T(8,128)(2,1)S(1)} %get-tuple-element.52.refs_2_), channel_id=1, source_target_pairs={{0,4},{1,3},{4,8},{5,1},{8,12},{9,5},{12,14},{13,9},{14,10},{15,13... | collective-permute-start | bytes 491528 | tf_op jit(solution)/shard_map/ppermute | solution.py:453
  52.6 6.2 %collective-permute-start.15 = (bf16[640,128]{1,0:T(8,128)(2,1)S(1)}, bf16[640,128]{1,0:T(8,128)(2,1)S(1)}, u32[]{:S(2)}, u32[]{:S(2)}) collective-permute-start(bf16[640,128]{1,0:T(8,128)(2,1)S(1)} %collective-permute-done.14.refs_3_), channel_id=1, source_target_pairs={{0,2},{1,5},{4,0},{5,9},{8,4},{9,13},{12,8},{13,15},{14,12},{15,11... | collective-permute-start | bytes 491528 | tf_op jit(solution)/shard_map/ppermute | solution.py:453
  52.6 6.6 %collective-permute-start.11 = (bf16[640,128]{1,0:T(8,128)(2,1)S(1)}, bf16[640,128]{1,0:T(8,128)(2,1)S(1)}, u32[]{:S(2)}, u32[]{:S(2)}) collective-permute-start(bf16[640,128]{1,0:T(8,128)(2,1)S(1)} %collective-permute-done.10.refs_2_), channel_id=1, source_target_pairs={{0,4},{1,3},{4,8},{5,1},{8,12},{9,5},{12,14},{13,9},{14,10},{15,13... | collective-permute-start | bytes 491528 | tf_op jit(solution)/shard_map/ppermute | solution.py:453
  58.8 7.4 %collective-permute-start.16 = (bf16[640,128]{1,0:T(8,128)(2,1)S(1)}, bf16[640,128]{1,0:T(8,128)(2,1)S(1)}, u32[]{:S(2)}, u32[]{:S(2)}) collective-permute-start(bf16[640,128]{1,0:T(8,128)(2,1)S(1)} %collective-permute-done.15.refs_3_), channel_id=1, source_target_pairs={{0,2},{1,5},{4,0},{5,9},{8,4},{9,13},{12,8},{13,15},{14,12},{15,11... | collective-permute-start | bytes 491528 | tf_op jit(solution)/shard_map/ppermute | solution.py:453
  59.2 5.3 %collective-permute-start.12 = (bf16[640,128]{1,0:T(8,128)(2,1)S(1)}, bf16[640,128]{1,0:T(8,128)(2,1)S(1)}, u32[]{:S(2)}, u32[]{:S(2)}) collective-permute-start(bf16[640,128]{1,0:T(8,128)(2,1)S(1)} %collective-permute-done.11.refs_2_), channel_id=1, source_target_pairs={{0,4},{1,3},{4,8},{5,1},{8,12},{9,5},{12,14},{13,9},{14,10},{15,13... | collective-permute-start | bytes 491528 | tf_op jit(solution)/shard_map/ppermute | solution.py:453
  64.5 5.3 %collective-permute-start.13 = (bf16[640,128]{1,0:T(8,128)(2,1)S(1)}, bf16[640,128]{1,0:T(8,128)(2,1)S(1)}, u32[]{:S(2)}, u32[]{:S(2)}) collective-permute-start(bf16[640,128]{1,0:T(8,128)(2,1)S(1)} %collective-permute-done.12.refs_2_), channel_id=1, source_target_pairs={{0,4},{1,3},{4,8},{5,1},{8,12},{9,5},{12,14},{13,9},{14,10},{15,13... | collective-permute-start | bytes 491528 | tf_op jit(solution)/shard_map/ppermute | solution.py:455
  72.9 1.6 %collective-permute-start.17 = (f32[512,128]{1,0:T(8,128)S(1)}, f32[512,128]{1,0:T(8,128)S(1)}, u32[]{:S(2)}, u32[]{:S(2)}) collective-permute-start(f32[512,128]{1,0:T(8,128)S(1)} %get-tuple-element.73), channel_id=1, source_target_pairs={{0,1},{1,0},{2,3},{3,2},{4,5},{5,4},{6,7},{7,6},{8,9},{9,8},{10,11... | collective-permute-start | bytes 786440 | tf_op jit(solution)/shard_map/ppermute | solution.py:478
  (1 other events, 0.7 us)

commit v7 on v6

v7 whole, which is shorter than its diff:
```python
import functools

import jax
import jax.numpy as jnp
from jax import lax
from jax.experimental import pallas as pl
from jax.experimental.pallas import tpu as pltpu
from jax.sharding import PartitionSpec as P

BRANCH = 16
EXTRA = 16
LANES = 128
CORES = 2
LEAVES = 2
KEPT_MIB = 30

bf16 = jnp.bfloat16
f32 = jnp.float32
i32 = jnp.int32


def matmul(left, right):
    return jnp.dot(left, right, preferred_element_type=f32)


def square_parts(points):
    minus = -jnp.sum(points * points, axis=0, keepdims=True)
    high = minus.astype(bf16).astype(f32)
    rest = minus - high
    middle = rest.astype(bf16).astype(f32)
    low = rest - middle
    return high, middle, low


def extra_rows(parts, first, width):
    row = lax.broadcasted_iota(i32, (EXTRA, width), 0)
    rows = jnp.where(row < 6, 1.0, 0.0).astype(f32)
    for offset, part in enumerate(parts):
        rows = jnp.where(row == first + offset, jnp.broadcast_to(part, (EXTRA, width)), rows)
    return rows


def put_sources(sources_ref, points):
    dim, width = points.shape
    sources_ref[0:dim, :] = points
    parts = square_parts(points.astype(f32))
    sources_ref[dim : dim + EXTRA, :] = extra_rows(parts, 3, width).astype(bf16)
    sources_ref[dim + EXTRA :, :] = jnp.zeros((LANES - dim - EXTRA, width), bf16)


def target_rows(points):
    dim, width = points.shape
    points = points.astype(f32)
    extra = extra_rows(square_parts(points), 0, width)
    blank = jnp.zeros((LANES - dim - EXTRA, width), f32)
    return jnp.concatenate([2.0 * points, extra, blank], axis=0).T.astype(bf16)


def in_low_half(shape):
    return lax.broadcasted_iota(i32, shape, 1) < LANES // 2


def swapped(values):
    return pltpu.roll(values, LANES // 2, 1)


def kernel_values(targets, sources):
    return jnp.exp(matmul(targets, sources)).astype(bf16)


def skeleton_rows(charges, leaf_ref, node_ref, upper_ref):
    points = charges[0].shape[1]
    parts = []
    for leaf, block in enumerate(charges):
        span = slice(leaf * points, (leaf + 1) * points)
        parts.append(matmul(block, leaf_ref[span, :]).astype(bf16))
    weights = matmul(jnp.concatenate(parts, axis=1), node_ref[...]).astype(bf16)
    term = matmul(weights, upper_ref[...])
    return jnp.concatenate([weights.astype(f32), term], axis=0).T.astype(bf16)


def ring_offset(lane):
    pair = (lane - 2) // 2
    far = pair + 1 + lane % 2
    return jnp.where(lane < 2, lane, jnp.where(pair % 2 == 0, -far, far))


def count_rows(ring, near_ref, far_ref):
    shape = (8, LANES)
    row, lane = lax.broadcasted_iota(i32, shape, 0), lax.broadcasted_iota(i32, shape, 1)
    table = jnp.zeros(shape, i32)
    for leaf in range(LEAVES):
        for first, ref in ((0, near_ref), (LEAVES, far_ref)):
            for slot in range(ref.shape[1]):
                hit = (row == first + leaf) & (lane == ref[leaf, slot])
                table = table + jnp.where(hit, 1, 0)
    chips = len(ring)
    me = lax.axis_index("leaf")
    core = me % CORES
    place = jnp.int32(0)
    for at, chip in enumerate(ring):
        place = jnp.where(me // CORES == chip, at, place)
    sense = jnp.where(place % 2 == core, 1, -1)
    met = (place + sense * ring_offset(lane) + 2 * LANES * chips) % chips
    device = jnp.zeros(shape, i32)
    for at, chip in enumerate(ring):
        device = jnp.where(met == at, chip * CORES + core, device)
    return jnp.where(row == 2 * LEAVES, device, table)


def message_kernel(
    ring,
    near_ref,
    far_ref,
    coords_ref,
    charges_ref,
    points_ref,
    leaf_ref,
    node_ref,
    upper_ref,
    place_ref,
    message_ref,
    table_ref,
    charges_buf,
    leaf_buf,
    node_buf,
    upper_buf,
    sems,
):
    dim, local = charges_ref.shape
    half = local // LEAVES
    copies = [
        pltpu.make_async_copy(source, target, sems.at[k])
        for k, (source, target) in enumerate(
            [
                (charges_ref, charges_buf),
                (leaf_ref, leaf_buf),
                (node_ref, node_buf),
                (upper_ref, upper_buf),
                (coords_ref, place_ref.at[0]),
                (points_ref, message_ref.at[0, half + LANES : half + LANES + dim, :]),
            ]
        )
    ]
    for copy in copies:
        copy.start()
    table_ref[...] = count_rows(ring, near_ref, far_ref)
    copies[0].wait()
    charges = [charges_buf[:, 0:half], charges_buf[:, half:]]
    message_ref[0, 0:half, :] = jnp.concatenate(charges, axis=0).astype(f32).T.astype(bf16)
    for copy in copies[1:4]:
        copy.wait()
    message_ref[0, half : half + LANES, :] = skeleton_rows(charges, leaf_buf, node_buf, upper_buf)
    for copy in copies[4:]:
        copy.wait()


def joined_kernel(mine_ref, other_ref, leaf_ref, node_ref, upper_ref, out_ref, message_ref):
    half = mine_ref.shape[0]
    columns = LANES // LEAVES
    result = mine_ref[...] + other_ref[...]
    message_ref[0, 0:half, :] = result.astype(bf16)
    flat = result.T.astype(bf16)
    charges = [flat[0:columns], flat[columns:]]
    out_ref[...] = jnp.concatenate(charges, axis=1)
    message_ref[0, half : half + LANES, :] = skeleton_rows(charges, leaf_ref, node_ref, upper_ref)


def added_kernel(mine_ref, other_ref, out_ref):
    columns = LANES // LEAVES
    flat = (mine_ref[...] + other_ref[...]).T.astype(bf16)
    out_ref[...] = jnp.concatenate([flat[0:columns], flat[columns:]], axis=1)


def stage_kernel(stage, *refs):
    spots, n_spots, n_sub, dim, points, first, last, near, far = stage
    refs = list(refs)
    makes_near, makes_far = near != "use", far in ("make", "keep")
    table_refs = refs.pop(0), refs.pop(0)
    place_ref = refs.pop(0) if makes_near else None
    skeleton_ref = refs.pop(0) if makes_far else None
    charge_ref = refs.pop(0) if near != "only" else None
    near_kept_ref = far_kept_ref = upper_kept_ref = targets_ref = None
    if near == "use":
        near_kept_ref = refs.pop(0)
    if far == "use":
        far_kept_ref = refs.pop(0)
        upper_kept_ref = refs.pop(0) if last else None
    sibling_ref = refs.pop(0) if first and makes_near else None
    if (makes_near or makes_far) and not first:
        targets_ref = refs.pop(0)
    if not first and near != "only":
        refs.pop(0), refs.pop(0)
    upper_points_ref = refs.pop(0) if last and makes_far else None
    if sibling_ref is not None:
        targets_ref = refs.pop(0)
    if near in ("keep", "only"):
        near_kept_ref = refs.pop(0)
    if far == "keep":
        far_kept_ref = refs.pop(0)
        upper_kept_ref = refs.pop(0) if last else None
    if last and near != "only":
        half_refs = refs.pop(0), refs.pop(0)
    if near != "only":
        total_ref, sums_ref, far_charges_ref, charges_ref = (refs.pop(0) for _ in range(4))
    near_ref = refs.pop(0) if makes_near else None
    far_ref = refs.pop(0) if makes_far else None

    low_half = in_low_half((LANES, LANES))
    devices = [table_refs[0][2 * LEAVES, spot] for spot in spots]

    def count(core, row, entry):
        mine, other = (ref[row, entry] for ref in table_refs)
        return jnp.where(core == 0, mine, other)

    def span_of(leaf):
        return slice(leaf * points, (leaf + 1) * points)

    if sibling_ref is not None:
        for leaf in range(LEAVES):
            targets_ref[0, span_of(leaf), :] = target_rows(place_ref[0, :, span_of(leaf)])
            targets_ref[1, span_of(leaf), :] = target_rows(sibling_ref[:, span_of(leaf)])
    if first:
        total_ref[...] = jnp.zeros_like(total_ref)
        sums_ref[...] = jnp.zeros_like(sums_ref)

    def values(makes, core, sources_ref, kept_ref):
        if not makes:
            return kept_ref[...]
        made = kernel_values(targets_ref[core], sources_ref[...])
        if kept_ref is not None:
            kept_ref[...] = made
        return made

    def far_part(skeletons, weights, nodes, kept_ref, kept_at):
        width = len(weights) * LANES
        sources_ref = None
        if makes_far:
            sources_ref = far_ref.at[:, 0:width]
            put_sources(sources_ref, jnp.concatenate(skeletons, axis=1))

        def step(core, carry):
            kept = None
            if kept_ref is not None:
                kept = kept_ref.at[core, :, kept_at : kept_at + width]
            kernel = values(makes_far, core, sources_ref, kept)
            for leaf in range(LEAVES):
                for position, (block, node) in enumerate(zip(weights, nodes)):
                    scaled = block * count(core, LEAVES + leaf, node).astype(f32)
                    high = scaled.astype(bf16).astype(f32)
                    rows = pl.ds(position * LANES, LANES)
                    far_charges_ref[leaf, rows, :] = jnp.where(
                        low_half, high, scaled - high
                    ).astype(bf16)
                total_ref[core, span_of(leaf), :] += matmul(
                    kernel[span_of(leaf)], far_charges_ref[leaf, 0:width]
                )
            return carry

        lax.fori_loop(0, CORES, step, 0)

    def skeletons_of(position):
        begin = points + LANES
        return skeleton_ref[position, begin : begin + dim, :]

    weights = []
    for position in range(len(spots)):
        if near != "only":
            rows = charge_ref[position, points : points + LANES, :].astype(f32)
            weights.append(jnp.where(low_half, rows, swapped(rows)))
            sums_ref[devices[position] // BRANCH] += rows
        lane = lax.broadcasted_iota(i32, (1, LANES), 1) // (LANES // LEAVES)
        for leaf in range(LEAVES):
            place = position * LEAVES + leaf
            if makes_near:
                put_sources(near_ref.at[place], place_ref[position, :, span_of(leaf)])
            if near != "only":
                chosen = jnp.where(lane == leaf, 1.0, 0.0).astype(bf16)
                charges_ref[place] = charge_ref[position, 0:points, :] * chosen

    if near != "only":
        far_part(
            [skeletons_of(position) for position in range(len(spots))] if makes_far else [],
            weights,
            devices,
            far_kept_ref,
            0,
        )
    if last and near != "only":
        for begin in range(0, n_sub, 2):
            subs = range(begin, min(begin + 2, n_sub))
            skeletons = []
            if makes_far:
                skeletons = [upper_points_ref[:, sub * LANES : (sub + 1) * LANES] for sub in subs]
            far_part(
                skeletons,
                [jnp.where(low_half, swapped(sums_ref[sub]), sums_ref[sub]) for sub in subs],
                [CORES * n_spots + sub for sub in subs],
                upper_kept_ref,
                begin * LANES,
            )

    def near_part(turn, position, core, leaf):
        device = table_refs[0][2 * LEAVES, spots[0] + position]
        if leaf is None:
            named = sum(count(core, own, device * LEAVES + 1) for own in range(LEAVES))
            leaf = jnp.where(named > 0, 1, 0)
        place = position * LEAVES + leaf
        times = [count(core, own, device * LEAVES + leaf) for own in range(LEAVES)]

        @pl.when(sum(times) > 0)
        def _():
            kept = None if near_kept_ref is None else near_kept_ref.at[turn]
            kernel = values(makes_near, core, near_ref.at[place] if makes_near else None, kept)
            if near != "only":
                added = matmul(kernel, charges_ref[place])
                for own in range(LEAVES):
                    total_ref[core, span_of(own), :] += times[own].astype(f32) * added[span_of(own)]

    def near_step(turn, carry):
        if first:
            device = table_refs[0][2 * LEAVES, 0]
            named = sum(count(1, own, device * LEAVES + 1) for own in range(LEAVES))
            other = jnp.where(named > 0, 1, 0)
            near_part(turn, 0, turn // LEAVES, jnp.where(turn < LEAVES, turn, other))
        else:
            near_part(turn, turn // CORES, turn % CORES, None)
        return carry

    lax.fori_loop(0, LEAVES + 1 if first else len(spots) * CORES, near_step, 0)

    if last and near != "only":
        for core, ref in enumerate(half_refs):
            both = [total_ref[core, span_of(leaf), :] for leaf in range(LEAVES)]
            both = [total + swapped(total) for total in both]
            ref[...] = jnp.where(in_low_half(both[0].shape), both[0], both[1])


def call(body, args, out_shapes, scratch=(), aliases={}, flops=0, in_hbm=False):
    vmem = pl.BlockSpec(memory_space=pltpu.VMEM)
    hbm = pl.BlockSpec(memory_space=pltpu.HBM)
    smem = pl.BlockSpec(memory_space=pltpu.SMEM)
    moved = sum(arg.size * arg.dtype.itemsize for arg in args)
    return pl.pallas_call(
        body,
        out_shape=out_shapes,
        in_specs=[smem if arg.dtype == i32 else hbm if in_hbm else vmem for arg in args],
        out_specs=[vmem for _ in out_shapes],
        scratch_shapes=list(scratch),
        input_output_aliases=aliases,
        compiler_params=pltpu.CompilerParams(vmem_limit_bytes=16 * 1024 * 1024),
        cost_estimate=pl.CostEstimate(flops=flops, bytes_accessed=moved, transcendentals=0),
    )(*args)


def ring_order(chips):
    if chips == 8:
        return [0, 2, 4, 6, 7, 5, 3, 1]
    return list(range(chips))


def on_device(
    coords,
    charges,
    near_lists,
    far_lists,
    leaf_interp,
    node_interp,
    upper_interp,
    node_points,
    upper_points,
):
    dim, local = coords.shape
    columns = charges.shape[0]
    points = local // LEAVES
    peers = lax.axis_size("leaf")
    n_sub = peers // BRANCH
    ring = ring_order(peers // CORES)
    chips = len(ring)

    def swap(turn):
        pairs = []
        for place, chip in enumerate(ring):
            for core in range(CORES):
                step = 1 if (place + core + turn) % 2 == 0 else -1
                pairs.append((chip * CORES + core, ring[(place + step) % chips] * CORES + core))
        return functools.partial(lax.ppermute, axis_name="leaf", perm=pairs)

    def gathered(message):
        met = [message, swap(0)(message)]
        sent = jnp.concatenate(met, axis=0)
        for turn in range(1, chips // 2):
            sent = swap(turn)(sent)
            met.append(sent)
        return met

    to_sibling = functools.partial(
        lax.ppermute, axis_name="leaf", perm=[(device, device ^ 1) for device in range(peers)]
    )

    def shape(*extent, dtype=bf16):
        return jax.ShapeDtypeStruct(extent, dtype)

    maps = [leaf_interp, node_interp, upper_interp]
    place, message, table = call(
        functools.partial(message_kernel, ring),
        [near_lists, far_lists, coords, charges, node_points] + maps,
        [
            shape(1, dim, local),
            shape(1, points + LANES + dim, LANES),
            shape(8, LANES, dtype=i32),
        ],
        scratch=[pltpu.VMEM(arg.shape, bf16) for arg in [charges] + maps]
        + [pltpu.SemaphoreType.DMA((6,))],
        in_hbm=True,
    )
    sibling_coords = to_sibling(coords)
    partner = swap(0)(coords)[None]
    tables = [table, to_sibling(table)]

    total_shape = shape(CORES, local, LANES, dtype=f32)
    sums_shape = shape(n_sub, LANES, LANES, dtype=f32)
    half_shape = shape(points, LANES, dtype=f32)
    targets_shape = shape(CORES, local, LANES)

    steps = LEAVES + 1 + CORES * (chips - 1)
    kept_bytes = 2 * points * (steps * local + CORES * LEAVES * (chips + n_sub) * LANES)
    keeping = kept_bytes <= KEPT_MIB * 2**20

    def stage(spots, near, far, places, skeletons, charged, targets, carried, last, kept):
        first = spots[0] == 0
        adds = near != "only"
        makes_near, makes_far = near != "use", far in ("make", "keep")
        makes_targets = first and makes_near
        args = list(tables)
        args += [places] if makes_near else []
        args += [skeletons] if makes_far else []
        args += [charged] if adds else []
        args += kept
        args += [sibling_coords] if makes_targets else []
        args += [targets] if (makes_near or makes_far) and not first else []
        carried_at = len(args)
        args += carried if not first and adds else []
        args += [upper_points] if last and makes_far else []
        scratch = []
        if adds:
            scratch += [
                pltpu.VMEM((LEAVES, 2 * LANES, LANES), bf16),
                pltpu.VMEM((LEAVES * len(spots), points, LANES), bf16),
            ]
        scratch += [pltpu.VMEM((LEAVES * len(spots), LANES, points), bf16)] if makes_near else []
        scratch += [pltpu.VMEM((LANES, 2 * LANES), bf16)] if makes_far else []
        outs = [targets_shape] if makes_targets else []
        near_at = len(outs)
        if near in ("keep", "only"):
            outs.append(shape(LEAVES + 1 if first else CORES * len(spots), local, points))
        far_at = len(outs)
        if far == "keep":
            outs.append(shape(CORES, local, len(spots) * LANES))
            outs += [shape(CORES, local, n_sub * LANES)] if last else []
        carried_to = len(outs)
        aliases = {}
        if adds:
            outs += [half_shape, half_shape] if last else []
            aliases = {} if first else {carried_at + k: len(outs) + k for k in range(2)}
            outs += [total_shape, sums_shape]
        static = (spots, chips, n_sub, dim, points, first, last, near, far)
        results = call(
            functools.partial(stage_kernel, static),
            args,
            outs,
            scratch=scratch,
            aliases=aliases,
            flops=len(spots) * (2 if makes_near else 1) * 10**9,
        )
        targets = results[0] if makes_targets else targets
        carried = results[carried_to : carried_to + 2]
        return targets, results[near_at:far_at], results[far_at:carried_to], carried

    def around(places, skeletons, charged, targets, kept):
        carried = []
        made = []
        spots = (0,)
        for turn, messages in enumerate(charged):
            last = turn == len(charged) - 1
            given = list(kept[turn][0]) + list(kept[turn][1]) if kept else []
            near = far = "use" if kept else "keep" if keeping else "make"
            near_values = []
            if last and near == "keep":
                _, near_values, _, _ = stage(
                    spots, "only", "none", places[turn], None, None, targets, carried, last, []
                )
                near, given = "use", list(near_values)
            targets, more_near, far_values, carried = stage(
                spots, near, far, places[turn], skeletons[turn], messages, targets, carried, last, given
            )
            made.append((list(near_values) + list(more_near), far_values))
            count = min(2, spots[-1] + 1)
            spots = tuple(range(spots[-1] + 1, spots[-1] + 1 + count))
        return targets, made, carried

    places = [place, partner]
    sent = jnp.concatenate(places, axis=0)
    for turn in range(1, chips // 2):
        sent = swap(turn)(sent)
        places.append(sent)
    charged = gathered(message)
    targets, kept, (mine, other) = around(places, charged, charged, None, None)
    first, message = call(
        joined_kernel,
        [mine, to_sibling(other)] + maps,
        [shape(columns, local), shape(1, points + LANES, LANES)],
    )
    again = gathered(message)
    *_, (mine, other) = around(places, charged, again, targets, kept if keeping else None)
    (second,) = call(added_kernel, [mine, to_sibling(other)], [shape(columns, local)])
    return (first, second)


def solution(mesh):
    placed = (
        P(None, ("groups", "leaf")),
        P(None, ("groups", "leaf")),
        P(("groups", "leaf"), None),
        P(("groups", "leaf"), None),
        P(("groups", "leaf"), None),
        P(("groups", "leaf"), None),
        P(("groups", "leaf"), None),
        P(None, ("groups", "leaf")),
        P(None, "groups"),
    )
    return jax.shard_map(
        on_device,
        mesh=mesh,
        in_specs=placed,
        out_specs=(P(None, ("groups", "leaf")), P(None, ("groups", "leaf"))),
        check_vma=False,
    )
```

time: 75.7 us -> 91.9 us (1.21)
  waiting for transfers between devices: 15.4 us -> 27.4 us
  local copies, waits for them, and re-layouts: 1.68 us -> 6.45 us
  starting transfers between devices: 17.1 us -> 14.1 us
  Pallas kernels: 40.3 us -> 42.1 us
    ppermute x14 -> x12, waiting for transfers between devices: 11.2 us -> 24.4 us  [the longest x6 15.2 us: gathered(): sent = swap(turn)(sent)]
    unnamed x14 -> x24, local copies, waits for them, and re-layouts: 1.68 us -> 6.45 us
    ppermute x14 -> x12, starting transfers between devices: 16.3 us -> 13.4 us  [the longest x6 4.73 us: gathered(): sent = swap(turn)(sent)]
    pallas_call x13 -> x14, Pallas kernels: 40.3 us -> 42.1 us  [call(): pl.pallas_call(body, out_shape=out_shapes, in_specs=[smem if arg.dtype ==...]
    ppermute x1, waiting for transfers between devices: 1.21 us -> 0.01 us  [on_device(): tables = [table, to_sibling(table)]]
  transfers between devices with their start and end apart: 18 -> 16, of which waited for: 12 -> 9; matrix products, arithmetic and copies ran while one was open for 0% -> 0% of each run, Pallas kernels for 42% -> 34%
where the time goes in v7:
time: 91.9 us; the launch traced here: 91 us
  Pallas kernels  42.1 us (46%)
  waiting for transfers between devices  27.4 us (30%)
  starting transfers between devices  14.1 us (15%)
  local copies, waits for them, and re-layouts  6.45 us (7%)
    pallas_call x14, Pallas kernels, call(): pl.pallas_call(body, out_shape=out_shapes, in_specs=[smem if arg.dtype ==...  42.1 us
    ppermute x6, waiting for transfers between devices, gathered(): sent = swap(turn)(sent)  15.2 us
    ppermute x2, waiting for transfers between devices, gathered(): met = [message, swap(0)(message)]  8.36 us
    unnamed x24, local copies, waits for them, and re-layouts  6.45 us
    ppermute x6, starting transfers between devices, gathered(): sent = swap(turn)(sent)  4.73 us
    ppermute x3, starting transfers between devices, on_device(): sent = swap(turn)(sent)  3.67 us
    ppermute x1, starting transfers between devices, on_device(): partner = swap(0)(coords)[None]  3.09 us
    ppermute x2, waiting for transfers between devices, on_device(): to_sibling(other)  3.04 us
  transfers between devices with their start and end apart: 16, of which 9 were waited for; matrix products, arithmetic and copies ran while one was open for 0% of the time, Pallas kernels for 34%

profile of v7, /device:TPU:0, one launch (start us, length us, event | category | flops | bytes accessed | tf_op | source)
XLA Modules:
  0.0 91.0 jit_solution(4551041765188663929)
XLA Ops:
  0.6 3.1 %collective-permute-start.5 = (bf16[64,1024]{1,0:T(8,128)(2,1)}, bf16[64,1024]{1,0:T(8,128)(2,1)S(1)}, u32[]{:S(2)}, u32[]{:S(2)}) collective-permute-start(bf16[64,1024]{1,0:T(8,128)(2,1)} %coords_ref.1), channel_id=1, source_target_pairs={{0,4},{1,3},{4,0},{5,9},{8,12},{9,5},{12,8},{13,15},{14,10},{15,13... | collective-permute-start | bytes 393224 | tf_op jit(solution)/shard_map/ppermute | solution.py:418
  10.2 1.8 %shard_map.104 = (bf16[1,64,1024]{2,1,0:T(8,128)(2,1)S(1)}, bf16[1,704,128]{2,1,0:T(8,128)(2,1)S(1)}, s32[8,128]{1,0:T(8,128)S(1)}) custom-call(s32[2,16]{1,0:T(2,128)S(1)} %copy-done.9, s32[2,32]{1,0:T(2,128)S(1)} %copy-done.10, bf16[64,1024]{1,0:T(8,128)(2,1)S(1)} %copy-done.7, bf16[64,1024]{1,0:T(8,128)(2,1)S(1)} %copy-done.6, ...), custom_call_target="tpu_custom_call" | custom-call | bytes 639360 | tf_op jit(solution)/shard_map/pallas_call | solution.py:344
  12.7 2.0 %collective-permute-start.6 = (bf16[2,64,1024]{2,1,0:T(8,128)(2,1)S(1)}, bf16[2,64,1024]{2,1,0:T(8,128)(2,1)S(1)}, u32[]{:S(2)}, u32[]{:S(2)}) collective-permute-start(bf16[2,64,1024]{2,1,0:T(8,128)(2,1)S(1)} %pad_maximum_fusion.2), channel_id=1, source_target_pairs={{0,2},{1,5},{4,8},{5,1},{8,4},{9,13},{12,14},{13,9},{14,12},{15,11... | collective-permute-start | bytes 786440 | tf_op jit(solution)/shard_map/ppermute | solution.py:505
  14.6 4.8 %collective-permute-done.1.refs_3_.refs_4_ = bf16[1,704,128]{2,1,0:T(8,128)(2,1)S(1)} collective-permute-done((bf16[1,704,128]{2,1,0:T(8,128)(2,1)S(1)}, bf16[1,704,128]{2,1,0:T(8,128)(2,1)S(1)}, u32[]{:S(2)}, u32[]{:S(2)}) %collective-permute-start.1) | collective-permute-done | bytes 180256 | tf_op jit(solution)/shard_map/ppermute | solution.py:390
  19.5 1.5 %collective-permute-start.2 = (bf16[2,704,128]{2,1,0:T(8,128)(2,1)S(1)}, bf16[2,704,128]{2,1,0:T(8,128)(2,1)S(1)}, u32[]{:S(2)}, u32[]{:S(2)}) collective-permute-start(bf16[2,704,128]{2,1,0:T(8,128)(2,1)S(1)} %pad_maximum_fusion), channel_id=1, source_target_pairs={{0,2},{1,5},{4,8},{5,1},{8,4},{9,13},{12,14},{13,9},{14,12},{15,11... | collective-permute-start | bytes 1081352 | tf_op jit(solution)/shard_map/ppermute | solution.py:393
  21.0 3.9 %shard_map.105 = (bf16[2,1024,128]{2,1,0:T(8,128)(2,1)S(1)}, bf16[3,1024,512]{2,1,0:T(8,128)(2,1)S(1)}, bf16[2,1024,128]{2,1,0:T(8,128)(2,1)S(1)}, f32[2,1024,128]{2,1,0:T(8,128)S(1)}, f32[1,128,128]{2,1,0:T(8,128)S(1)}) custom-call(s32[8,128]{1,0:T(8,128)S(1)} %get-tuple-element.38.refs_0_, s32[8,128]{1,0:T(8,128)S(1)} %collective-permute-done.refs_1_, ...), custom_call_target="tpu_custom_call" | custom-call | flops 2000000000 | bytes 630784 | tf_op jit(solution)/shard_map/pallas_call | solution.py:344
  24.9 3.0 %shard_map.107 = (bf16[2,1024,512]{2,1,0:T(8,128)(2,1)S(1)}, bf16[2,1024,128]{2,1,0:T(8,128)(2,1)S(1)}, f32[2,1024,128]{2,1,0:T(8,128)S(1)}, f32[1,128,128]{2,1,0:T(8,128)S(1)}) custom-call(s32[8,128]{1,0:T(8,128)S(1)} %get-tuple-element.38.refs_0_, s32[8,128]{1,0:T(8,128)S(1)} %collective-permute-done.refs_1_, ...), custom_call_target="tpu_custom_call", output_to_operand_aliasing={{2}: (6, {}), {3}: (7, {})} | custom-call | flops 2000000000 | bytes 2138112 | tf_op jit(solution)/shard_map/pallas_call | solution.py:344
  28.0 1.7 %collective-permute-start.7 = (bf16[2,64,1024]{2,1,0:T(8,128)(2,1)S(1)}, bf16[2,64,1024]{2,1,0:T(8,128)(2,1)S(1)}, u32[]{:S(2)}, u32[]{:S(2)}) collective-permute-start(bf16[2,64,1024]{2,1,0:T(8,128)(2,1)S(1)} %collective-permute-done.6.refs_2_), channel_id=1, source_target_pairs={{0,4},{1,3},{4,0},{5,9},{8,12},{9,5},{12,8},{13,15},{14,10},{15,13... | collective-permute-start | bytes 786440 | tf_op jit(solution)/shard_map/ppermute | solution.py:505
  30.1 4.2 %shard_map.108 = (bf16[4,1024,512]{2,1,0:T(8,128)(2,1)S(1)}, bf16[2,1024,256]{2,1,0:T(8,128)(2,1)S(1)}, f32[2,1024,128]{2,1,0:T(8,128)S(1)}, f32[1,128,128]{2,1,0:T(8,128)S(1)}) custom-call(s32[8,128]{1,0:T(8,128)S(1)} %get-tuple-element.38.refs_0_, s32[8,128]{1,0:T(8,128)S(1)} %collective-permute-done.refs_1_, ...), custom_call_target="tpu_custom_call", output_to_operand_aliasing={{2}: (6, {}), {3}: (7, {})} | custom-call | flops 4000000000 | bytes 2629632 | tf_op jit(solution)/shard_map/pallas_call | solution.py:344
  35.1 7.7 %collective-permute-done.3.refs_3_.refs_4_ = bf16[2,704,128]{2,1,0:T(8,128)(2,1)S(1)} collective-permute-done((bf16[2,704,128]{2,1,0:T(8,128)(2,1)S(1)}, bf16[2,704,128]{2,1,0:T(8,128)(2,1)S(1)}, u32[]{:S(2)}, u32[]{:S(2)}) %collective-permute-start.3) | collective-permute-done | bytes 360480 | tf_op jit(solution)/shard_map/ppermute | solution.py:393
  42.8 4.9 %shard_map.109 = (bf16[4,1024,512]{2,1,0:T(8,128)(2,1)S(1)}, bf16[2,1024,256]{2,1,0:T(8,128)(2,1)S(1)}, f32[2,1024,128]{2,1,0:T(8,128)S(1)}, f32[1,128,128]{2,1,0:T(8,128)S(1)}) custom-call(s32[8,128]{1,0:T(8,128)S(1)} %get-tuple-element.38.refs_0_, s32[8,128]{1,0:T(8,128)S(1)} %collective-permute-done.refs_1_, ...), custom_call_target="tpu_custom_call", output_to_operand_aliasing={{2}: (6, {}), {3}: (7, {})} | custom-call | flops 4000000000 | bytes 2629632 | tf_op jit(solution)/shard_map/pallas_call | solution.py:344
  47.7 2.6 %shard_map.106.refs_4_.refs_3_ = bf16[4,1024,512]{2,1,0:T(8,128)(2,1)S(1)} custom-call(s32[8,128]{1,0:T(8,128)S(1)} %get-tuple-element.38.refs_0_, s32[8,128]{1,0:T(8,128)S(1)} %collective-permute-done.refs_1_, bf16[2,64,1024]{2,1,0:T(8,128)(2,1)S(1)} %collective-permute-done.8.refs_2_, bf16[2,1024,128]{2,1,0:T(8,128)(2,1)S(1)} %get-tuple-element.41.refs_3_.refs_5_), custom_call_target="tpu_custom_call" | custom-call | flops 4000000000 | bytes 794624 | tf_op jit(solution)/shard_map/pallas_call | solution.py:344
  50.3 5.0 %shard_map.110 = (bf16[2,1024,256]{2,1,0:T(8,128)(2,1)S(1)}, bf16[2,1024,128]{2,1,0:T(8,128)(2,1)S(1)}, f32[512,128]{1,0:T(8,128)S(1)}, f32[512,128]{1,0:T(8,128...) custom-call(s32[8,128]{1,0:T(8,128)S(1)} %get-tuple-element.38.refs_, ...), custom_call_target="tpu_custom_call", output_to_operand_aliasing={{4}: (6, {}), {5}: (7, {})} | custom-call | flops 2000000000 | bytes 6578176 | tf_op jit(solution)/shard_map/pallas_call | solution.py:344
  55.4 1.5 %collective-permute-done.10.other_ref = f32[512,128]{1,0:T(8,128)S(1)} collective-permute-done((f32[512,128]{1,0:T(8,128)S(1)}, f32[512,128]{1,0:T(8,128)S(1)}, u32[]{:S(2)}, u32[]{:S(2)}) %collective-permute-start.10) | collective-permute-done | bytes 262176 | tf_op jit(solution)/shard_map/ppermute | solution.py:511
  57.8 1.8 %collective-permute-start.11 = (bf16[1,640,128]{2,1,0:T(8,128)(2,1)S(1)}, bf16[1,640,128]{2,1,0:T(8,128)(2,1)S(1)}, u32[]{:S(2)}, u32[]{:S(2)}) collective-permute-start(bf16[1,640,128]{2,1,0:T(8,128)(2,1)S(1)} %get-tuple-element.53.refs_2_), channel_id=1, source_target_pairs={{0,4},{1,3},{4,0},{5,9},{8,12},{9,5},{12,8},{13,15},{14,10},{15,13... | collective-permute-start | bytes 491528 | tf_op jit(solution)/shard_map/ppermute | solution.py:390
  59.6 3.5 %collective-permute-done.11.refs_2_ = bf16[1,640,128]{2,1,0:T(8,128)(2,1)S(1)} collective-permute-done((bf16[1,640,128]{2,1,0:T(8,128)(2,1)S(1)}, bf16[1,640,128]{2,1,0:T(8,128)(2,1)S(1)}, u32[]{:S(2)}, u32[]{:S(2)}) %collective-permute-start.11) | collective-permute-done | bytes 163872 | tf_op jit(solution)/shard_map/ppermute | solution.py:390
  63.7 6.6 %collective-permute-done.12.refs_2_ = bf16[2,640,128]{2,1,0:T(8,128)(2,1)S(1)} collective-permute-done((bf16[2,640,128]{2,1,0:T(8,128)(2,1)S(1)}, bf16[2,640,128]{2,1,0:T(8,128)(2,1)S(1)}, u32[]{:S(2)}, u32[]{:S(2)}) %collective-permute-start.12) | collective-permute-done | bytes 327712 | tf_op jit(solution)/shard_map/ppermute | solution.py:393
  70.3 1.8 %collective-permute-start.13 = (bf16[2,640,128]{2,1,0:T(8,128)(2,1)S(1)}, bf16[2,640,128]{2,1,0:T(8,128)(2,1)S(1)}, u32[]{:S(2)}, u32[]{:S(2)}) collective-permute-start(bf16[2,640,128]{2,1,0:T(8,128)(2,1)S(1)} %collective-permute-done.12.refs_2_), channel_id=1, source_target_pairs={{0,4},{1,3},{4,0},{5,9},{8,12},{9,5},{12,8},{13,15},{14,10},{15,13... | collective-permute-start | bytes 983048 | tf_op jit(solution)/shard_map/ppermute | solution.py:393
  72.1 2.6 %shard_map.112 = (f32[2,1024,128]{2,1,0:T(8,128)S(1)}, f32[1,128,128]{2,1,0:T(8,128)S(1)}) custom-call(s32[8,128]{1,0:T(8,128)S(1)} %get-tuple-element.38.refs_0_, s32[8,128]{1,0:T(8,128)S(1)} %collective-permute-done.refs_1_, bf16[1,640,128]{2,1,0:T(8,128)(2,1)S(1)} %get-tuple-element.53.refs_2_, bf16[3,1024,512]{2,1,0:T(8,128)(2,1)S(1)} %get-tuple-element.62.refs_3_, ...), custom_call_target="tpu_custom_call" | custom-call | flops 1000000000 | bytes 3842048 | tf_op jit(solution)/shard_map/pallas_call | solution.py:344
  74.7 2.1 %shard_map.113 = (f32[2,1024,128]{2,1,0:T(8,128)S(1)}, f32[1,128,128]{2,1,0:T(8,128)S(1)}) custom-call(s32[8,128]{1,0:T(8,128)S(1)} %get-tuple-element.38.refs_0_, s32[8,128]{1,0:T(8,128)S(1)} %collective-permute-done.refs_1_, bf16[1,640,128]{2,1,0:T(8,128)(2,1)S(1)} %collective-permute-done.11.refs_2_, ...), custom_call_target="tpu_custom_call", output_to_operand_aliasing={{0}: (5, {}), {1}: (6, {})} | custom-call | flops 1000000000 | bytes 3907584 | tf_op jit(solution)/shard_map/pallas_call | solution.py:344
  77.8 2.9 %shard_map.114 = (f32[2,1024,128]{2,1,0:T(8,128)S(1)}, f32[1,128,128]{2,1,0:T(8,128)S(1)}) custom-call(s32[8,128]{1,0:T(8,128)S(1)} %get-tuple-element.38.refs_0_, s32[8,128]{1,0:T(8,128)S(1)} %collective-permute-done.refs_1_, bf16[2,640,128]{2,1,0:T(8,128)(2,1)S(1)} %collective-permute-done.12.refs_2_, ...), custom_call_target="tpu_custom_call", output_to_operand_aliasing={{0}: (5, {}), {1}: (6, {})} | custom-call | flops 2000000000 | bytes 6692864 | tf_op jit(solution)/shard_map/pallas_call | solution.py:344
  80.7 3.3 %shard_map.115 = (f32[2,1024,128]{2,1,0:T(8,128)S(1)}, f32[1,128,128]{2,1,0:T(8,128)S(1)}) custom-call(s32[8,128]{1,0:T(8,128)S(1)} %get-tuple-element.38.refs_0_, s32[8,128]{1,0:T(8,128)S(1)} %collective-permute-done.refs_1_, bf16[2,640,128]{2,1,0:T(8,128)(2,1)S(1)} %collective-permute-done.13.refs_2_, ...), custom_call_target="tpu_custom_call", output_to_operand_aliasing={{0}: (5, {}), {1}: (6, {})} | custom-call | flops 2000000000 | bytes 6692864 | tf_op jit(solution)/shard_map/pallas_call | solution.py:344
  84.4 4.2 %shard_map.116 = (f32[512,128]{1,0:T(8,128)S(1)}, f32[512,128]{1,0:T(8,128)S(1)}, f32[2,1024,128]{2,1,0:T(8,128)S(1)}, f32[1,128,128]{2,1,0:T(8,128)S(1)}) custom-call(s32[8,128]{1,0:T(8,128)S(1)} %get-tuple-element.38.refs_0_, s32[8,128]{1,0:T(8,128)S(1)} %collective-permute-done.refs_1_, ...), custom_call_target="tpu_custom_call", output_to_operand_aliasing={{2}: (6, {}), {3}: (7, {})} | custom-call | flops 2000000000 | bytes 7217152 | tf_op jit(solution)/shard_map/pallas_call | solution.py:344
  88.7 1.5 %collective-permute-done.15.other_ref = f32[512,128]{1,0:T(8,128)S(1)} collective-permute-done((f32[512,128]{1,0:T(8,128)S(1)}, f32[512,128]{1,0:T(8,128)S(1)}, u32[]{:S(2)}, u32[]{:S(2)}) %collective-permute-start.15) | collective-permute-done | bytes 262176 | tf_op jit(solution)/shard_map/ppermute | solution.py:516
  (49 shorter events, 12.2 us)
Async XLA Ops:
  0.6 12.0 %collective-permute-start.5 = (bf16[64,1024]{1,0:T(8,128)(2,1)}, bf16[64,1024]{1,0:T(8,128)(2,1)S(1)}, u32[]{:S(2)}, u32[]{:S(2)}) collective-permute-start(bf16[64,1024]{1,0:T(8,128)(2,1)} %coords_ref.1), channel_id=1, source_target_pairs={{0,4},{1,3},{4,0},{5,9},{8,12},{9,5},{12,8},{13,15},{14,10},{15,13... | collective-permute-start | bytes 393224 | tf_op jit(solution)/shard_map/ppermute | solution.py:418
  3.7 0.9 %copy-start = (bf16[1024,128]{1,0:T(8,128)(2,1)S(1)}, bf16[1024,128]{1,0:T(8,128)(2,1)}, u32[]{:S(2)}) copy-start(bf16[1024,128]{1,0:T(8,128)(2,1)} %leaf_ref.3) | copy-start | bytes 786436
  4.7 0.8 copy-start.2
  6.3 0.9 copy-start.6
  7.2 0.9 copy-start.7
  12.0 7.5 %collective-permute-start.1 = (bf16[1,704,128]{2,1,0:T(8,128)(2,1)S(1)}, bf16[1,704,128]{2,1,0:T(8,128)(2,1)S(1)}, u32[]{:S(2)}, u32[]{:S(2)}) collective-permute-start(bf16[1,704,128]{2,1,0:T(8,128)(2,1)S(1)} %get-tuple-element.39.refs_3_.refs_4_), channel_id=1, source_target_pairs={{0,4},{1,3},{4,0},{5,9},{8,12},{9,5},{12,8},{13,15},{14,10},{15,13... | collective-permute-start | bytes 540680 | tf_op jit(solution)/shard_map/ppermute | solution.py:390
  12.1 8.9 %collective-permute-start.9 = (bf16[64,1024]{1,0:T(8,128)(2,1)S(1)}, bf16[64,1024]{1,0:T(8,128)(2,1)S(1)}, u32[]{:S(2)}, u32[]{:S(2)}) collective-permute-start(bf16[64,1024]{1,0:T(8,128)(2,1)S(1)} %copy-done.7), channel_id=1, source_target_pairs={{0,1},{1,0},{2,3},{3,2},{4,5},{5,4},{6,7},{7,6},{8,9},{9,8},{10,11... | collective-permute-start | bytes 393224 | tf_op jit(solution)/shard_map/ppermute | solution.py:417
  12.1 8.9 %collective-permute-start = (s32[8,128]{1,0:T(8,128)S(1)}, s32[8,128]{1,0:T(8,128)S(1)}, u32[]{:S(2)}, u32[]{:S(2)}) collective-permute-start(s32[8,128]{1,0:T(8,128)S(1)} %get-tuple-element.38.refs_0_), channel_id=1, source_target_pairs={{0,1},{1,0},{2,3},{3,2},{4,5},{5,4},{6,7},{7,6},{8,9},{9,8},{10,11... | collective-permute-start | bytes 12296 | tf_op jit(solution)/shard_map/ppermute | solution.py:419
  12.7 15.3 %collective-permute-start.6 = (bf16[2,64,1024]{2,1,0:T(8,128)(2,1)S(1)}, bf16[2,64,1024]{2,1,0:T(8,128)(2,1)S(1)}, u32[]{:S(2)}, u32[]{:S(2)}) collective-permute-start(bf16[2,64,1024]{2,1,0:T(8,128)(2,1)S(1)} %pad_maximum_fusion.2), channel_id=1, source_target_pairs={{0,2},{1,5},{4,8},{5,1},{8,4},{9,13},{12,14},{13,9},{14,12},{15,11... | collective-permute-start | bytes 786440 | tf_op jit(solution)/shard_map/ppermute | solution.py:505
  19.5 10.2 %collective-permute-start.2 = (bf16[2,704,128]{2,1,0:T(8,128)(2,1)S(1)}, bf16[2,704,128]{2,1,0:T(8,128)(2,1)S(1)}, u32[]{:S(2)}, u32[]{:S(2)}) collective-permute-start(bf16[2,704,128]{2,1,0:T(8,128)(2,1)S(1)} %pad_maximum_fusion), channel_id=1, source_target_pairs={{0,2},{1,5},{4,8},{5,1},{8,4},{9,13},{12,14},{13,9},{14,12},{15,11... | collective-permute-start | bytes 1081352 | tf_op jit(solution)/shard_map/ppermute | solution.py:393
  28.0 7.1 %collective-permute-start.7 = (bf16[2,64,1024]{2,1,0:T(8,128)(2,1)S(1)}, bf16[2,64,1024]{2,1,0:T(8,128)(2,1)S(1)}, u32[]{:S(2)}, u32[]{:S(2)}) collective-permute-start(bf16[2,64,1024]{2,1,0:T(8,128)(2,1)S(1)} %collective-permute-done.6.refs_2_), channel_id=1, source_target_pairs={{0,4},{1,3},{4,0},{5,9},{8,12},{9,5},{12,8},{13,15},{14,10},{15,13... | collective-permute-start | bytes 786440 | tf_op jit(solution)/shard_map/ppermute | solution.py:505
  29.7 13.1 %collective-permute-start.3 = (bf16[2,704,128]{2,1,0:T(8,128)(2,1)S(1)}, bf16[2,704,128]{2,1,0:T(8,128)(2,1)S(1)}, u32[]{:S(2)}, u32[]{:S(2)}) collective-permute-start(bf16[2,704,128]{2,1,0:T(8,128)(2,1)S(1)} %collective-permute-done.2.refs_3_.refs_4_), channel_id=1, source_target_pairs={{0,4},{1,3},{4,0},{5,9},{8,12},{9,5},{12,8},{13,15},{14,10},{15,13... | collective-permute-start | bytes 1081352 | tf_op jit(solution)/shard_map/ppermute | solution.py:393
  35.1 12.6 %collective-permute-start.8 = (bf16[2,64,1024]{2,1,0:T(8,128)(2,1)S(1)}, bf16[2,64,1024]{2,1,0:T(8,128)(2,1)S(1)}, u32[]{:S(2)}, u32[]{:S(2)}) collective-permute-start(bf16[2,64,1024]{2,1,0:T(8,128)(2,1)S(1)} %collective-permute-done.7.refs_2_), channel_id=1, source_target_pairs={{0,2},{1,5},{4,8},{5,1},{8,4},{9,13},{12,14},{13,9},{14,12},{15,11... | collective-permute-start | bytes 786440 | tf_op jit(solution)/shard_map/ppermute | solution.py:505
  42.8 7.5 %collective-permute-start.4 = (bf16[2,704,128]{2,1,0:T(8,128)(2,1)S(1)}, bf16[2,704,128]{2,1,0:T(8,128)(2,1)S(1)}, u32[]{:S(2)}, u32[]{:S(2)}) collective-permute-start(bf16[2,704,128]{2,1,0:T(8,128)(2,1)S(1)} %collective-permute-done.3.refs_3_.refs_4_), channel_id=1, source_target_pairs={{0,2},{1,5},{4,8},{5,1},{8,4},{9,13},{12,14},{13,9},{14,12},{15,11... | collective-permute-start | bytes 1081352 | tf_op jit(solution)/shard_map/ppermute | solution.py:393
  47.7 2.6 %copy-start.11 = (bf16[64,128]{1,0:T(8,128)(2,1)S(1)}, bf16[64,128]{1,0:T(8,128)(2,1)}, u32[]{:S(2)}) copy-start(bf16[64,128]{1,0:T(8,128)(2,1)} %refs_8_.1) | copy-start | bytes 49156
  50.3 6.6 %copy-start.1 = (bf16[1024,128]{1,0:T(8,128)(2,1)S(1)}, bf16[1024,128]{1,0:T(8,128)(2,1)}, u32[]{:S(2)}) copy-start(bf16[1024,128]{1,0:T(8,128)(2,1)} %leaf_ref.3) | copy-start | bytes 786436
  50.3 6.6 %copy-start.3 = (bf16[256,128]{1,0:T(8,128)(2,1)S(1)}, bf16[256,128]{1,0:T(8,128)(2,1)}, u32[]{:S(2)}) copy-start(bf16[256,128]{1,0:T(8,128)(2,1)} %node_ref.3) | copy-start | bytes 196612
  50.3 6.6 %copy-start.5 = (bf16[128,128]{1,0:T(8,128)(2,1)S(1)}, bf16[128,128]{1,0:T(8,128)(2,1)}, u32[]{:S(2)}) copy-start(bf16[128,128]{1,0:T(8,128)(2,1)} %upper_ref.3) | copy-start | bytes 98308
  55.3 1.6 %collective-permute-start.10 = (f32[512,128]{1,0:T(8,128)S(1)}, f32[512,128]{1,0:T(8,128)S(1)}, u32[]{:S(2)}, u32[]{:S(2)}) collective-permute-start(f32[512,128]{1,0:T(8,128)S(1)} %get-tuple-element.51), channel_id=1, source_target_pairs={{0,1},{1,0},{2,3},{3,2},{4,5},{5,4},{6,7},{7,6},{8,9},{9,8},{10,11... | collective-permute-start | bytes 786440 | tf_op jit(solution)/shard_map/ppermute | solution.py:511
  57.8 5.3 %collective-permute-start.11 = (bf16[1,640,128]{2,1,0:T(8,128)(2,1)S(1)}, bf16[1,640,128]{2,1,0:T(8,128)(2,1)S(1)}, u32[]{:S(2)}, u32[]{:S(2)}) collective-permute-start(bf16[1,640,128]{2,1,0:T(8,128)(2,1)S(1)} %get-tuple-element.53.refs_2_), channel_id=1, source_target_pairs={{0,4},{1,3},{4,0},{5,9},{8,12},{9,5},{12,8},{13,15},{14,10},{15,13... | collective-permute-start | bytes 491528 | tf_op jit(solution)/shard_map/ppermute | solution.py:390
  63.1 7.1 %collective-permute-start.12 = (bf16[2,640,128]{2,1,0:T(8,128)(2,1)S(1)}, bf16[2,640,128]{2,1,0:T(8,128)(2,1)S(1)}, u32[]{:S(2)}, u32[]{:S(2)}) collective-permute-start(bf16[2,640,128]{2,1,0:T(8,128)(2,1)S(1)} %pad_maximum_fusion.1), channel_id=1, source_target_pairs={{0,2},{1,5},{4,8},{5,1},{8,4},{9,13},{12,14},{13,9},{14,12},{15,11... | collective-permute-start | bytes 983048 | tf_op jit(solution)/shard_map/ppermute | solution.py:393
  70.3 7.1 %collective-permute-start.13 = (bf16[2,640,128]{2,1,0:T(8,128)(2,1)S(1)}, bf16[2,640,128]{2,1,0:T(8,128)(2,1)S(1)}, u32[]{:S(2)}, u32[]{:S(2)}) collective-permute-start(bf16[2,640,128]{2,1,0:T(8,128)(2,1)S(1)} %collective-permute-done.12.refs_2_), channel_id=1, source_target_pairs={{0,4},{1,3},{4,0},{5,9},{8,12},{9,5},{12,8},{13,15},{14,10},{15,13... | collective-permute-start | bytes 983048 | tf_op jit(solution)/shard_map/ppermute | solution.py:393
  77.4 7.1 %collective-permute-start.14 = (bf16[2,640,128]{2,1,0:T(8,128)(2,1)S(1)}, bf16[2,640,128]{2,1,0:T(8,128)(2,1)S(1)}, u32[]{:S(2)}, u32[]{:S(2)}) collective-permute-start(bf16[2,640,128]{2,1,0:T(8,128)(2,1)S(1)} %collective-permute-done.13.refs_2_), channel_id=1, source_target_pairs={{0,2},{1,5},{4,8},{5,1},{8,4},{9,13},{12,14},{13,9},{14,12},{15,11... | collective-permute-start | bytes 983048 | tf_op jit(solution)/shard_map/ppermute | solution.py:393
  88.6 1.6 %collective-permute-start.15 = (f32[512,128]{1,0:T(8,128)S(1)}, f32[512,128]{1,0:T(8,128)S(1)}, u32[]{:S(2)}, u32[]{:S(2)}) collective-permute-start(f32[512,128]{1,0:T(8,128)S(1)} %get-tuple-element.73), channel_id=1, source_target_pairs={{0,1},{1,0},{2,3},{3,2},{4,5},{5,4},{6,7},{7,6},{8,9},{9,8},{10,11... | collective-permute-start | bytes 786440 | tf_op jit(solution)/shard_map/ppermute | solution.py:516
  (4 other events, 2.8 us)

commit v8 on v6

v8 whole, which is shorter than its diff:
```python
import functools

import jax
import jax.numpy as jnp
from jax import lax
from jax.experimental import pallas as pl
from jax.experimental.pallas import tpu as pltpu
from jax.sharding import PartitionSpec as P

BRANCH = 16
EXTRA = 16
LANES = 128
CORES = 2
LEAVES = 2
KEPT_MIB = 30

bf16 = jnp.bfloat16
f32 = jnp.float32
i32 = jnp.int32


def matmul(left, right):
    return jnp.dot(left, right, preferred_element_type=f32)


def square_parts(points):
    minus = -jnp.sum(points * points, axis=0, keepdims=True)
    high = minus.astype(bf16).astype(f32)
    rest = minus - high
    middle = rest.astype(bf16).astype(f32)
    low = rest - middle
    return high, middle, low


def extra_rows(parts, first, width):
    row = lax.broadcasted_iota(i32, (EXTRA, width), 0)
    rows = jnp.where(row < 6, 1.0, 0.0).astype(f32)
    for offset, part in enumerate(parts):
        rows = jnp.where(row == first + offset, jnp.broadcast_to(part, (EXTRA, width)), rows)
    return rows


def put_sources(sources_ref, points):
    dim, width = points.shape
    sources_ref[0:dim, :] = points
    parts = square_parts(points.astype(f32))
    sources_ref[dim : dim + EXTRA, :] = extra_rows(parts, 3, width).astype(bf16)
    sources_ref[dim + EXTRA :, :] = jnp.zeros((LANES - dim - EXTRA, width), bf16)


def target_rows(points):
    dim, width = points.shape
    points = points.astype(f32)
    extra = extra_rows(square_parts(points), 0, width)
    blank = jnp.zeros((LANES - dim - EXTRA, width), f32)
    return jnp.concatenate([2.0 * points, extra, blank], axis=0).T.astype(bf16)


def in_low_half(shape):
    return lax.broadcasted_iota(i32, shape, 1) < LANES // 2


def swapped(values):
    return pltpu.roll(values, LANES // 2, 1)


def kernel_values(targets, sources):
    return jnp.exp(matmul(targets, sources)).astype(bf16)


def skeleton_rows(charges, leaf_ref, node_ref, upper_ref):
    points = charges[0].shape[1]
    parts = []
    for leaf, block in enumerate(charges):
        span = slice(leaf * points, (leaf + 1) * points)
        parts.append(matmul(block, leaf_ref[span, :]).astype(bf16))
    weights = matmul(jnp.concatenate(parts, axis=1), node_ref[...]).astype(bf16)
    term = matmul(weights, upper_ref[...])
    return jnp.concatenate([weights.astype(f32), term], axis=0).T.astype(bf16)


def count_rows(near_ref, far_ref):
    shape = (8, LANES)
    row, lane = lax.broadcasted_iota(i32, shape, 0), lax.broadcasted_iota(i32, shape, 1)
    table = jnp.zeros(shape, f32)
    for leaf in range(LEAVES):
        for first, ref in ((0, near_ref), (LEAVES, far_ref)):
            for slot in range(ref.shape[1]):
                hit = (row == first + leaf) & (lane == ref[leaf, slot])
                table = table + jnp.where(hit, 1.0, 0.0)
    return table


def device_of(ring, spot):
    chips = len(ring)
    me = lax.axis_index("leaf")
    core = me % CORES
    place = jnp.int32(0)
    for at, chip in enumerate(ring):
        place = jnp.where(me // CORES == chip, at, place)
    hop = (spot + 1) // 2
    step = hop if spot % 2 == 0 else -hop
    met = (place + step * (1 - 2 * core) + chips) % chips
    device = jnp.int32(0)
    for at, chip in enumerate(ring):
        device = jnp.where(met == at, chip * CORES + core, device)
    return device


def message_kernel(
    near_ref,
    far_ref,
    coords_ref,
    charges_ref,
    points_ref,
    leaf_ref,
    node_ref,
    upper_ref,
    message_ref,
    table_ref,
):
    dim, local = coords_ref.shape
    half = local // LEAVES
    charges = [charges_ref[:, 0:half], charges_ref[:, half:]]
    message_ref[0:half, :] = jnp.concatenate(charges, axis=0).astype(f32).T.astype(bf16)
    message_ref[half : half + LANES, :] = skeleton_rows(charges, leaf_ref, node_ref, upper_ref)
    place = half + LANES
    for block in range(local // LANES):
        message_ref[place : place + dim, :] = coords_ref[:, block * LANES : (block + 1) * LANES]
        place += dim
    message_ref[place : place + dim, :] = points_ref[...]
    table_ref[...] = count_rows(near_ref, far_ref)


def joined_kernel(mine_ref, other_ref, leaf_ref, node_ref, upper_ref, out_ref, message_ref):
    half = mine_ref.shape[0]
    columns = LANES // LEAVES
    result = mine_ref[...] + other_ref[...]
    message_ref[0:half, :] = result.astype(bf16)
    flat = result.T.astype(bf16)
    charges = [flat[0:columns], flat[columns:]]
    out_ref[...] = jnp.concatenate(charges, axis=1)
    message_ref[half : half + LANES, :] = skeleton_rows(charges, leaf_ref, node_ref, upper_ref)


def added_kernel(mine_ref, other_ref, out_ref):
    columns = LANES // LEAVES
    flat = (mine_ref[...] + other_ref[...]).T.astype(bf16)
    out_ref[...] = jnp.concatenate([flat[0:columns], flat[columns:]], axis=1)


def stage_kernel(stage, *refs):
    ring, spots, far_of, n_sub, dim, points, first, last, mode = stage
    refs = list(refs)
    use, keep = mode == "use", mode == "keep"
    table_refs = refs.pop(0), refs.pop(0)
    place_refs = [] if use else [refs.pop(0) for _ in spots]
    charge_refs = [refs.pop(0) for _ in spots]
    near_kept_ref = far_kept_ref = targets_ref = None
    has_far = bool(far_of)
    if use:
        near_kept_ref = refs.pop(0)
        far_kept_ref = refs.pop(0) if has_far else None
    elif first:
        sibling_ref = refs.pop(0)
    else:
        targets_ref = refs.pop(0)
    if not first:
        refs.pop(0), refs.pop(0)
    upper_points_ref = refs.pop(0) if last and not use else None
    if first and not use:
        targets_ref = refs.pop(0)
    if keep:
        near_kept_ref = refs.pop(0)
        far_kept_ref = refs.pop(0) if has_far else None
    if last:
        half_refs = refs.pop(0), refs.pop(0)
    total_ref, sums_ref, far_charges_ref, charges_ref = refs[:4]
    if not use:
        near_ref, far_ref = refs[4:]

    coords_at = points + LANES
    blocks = points // LANES
    skeletons_at = coords_at + LEAVES * blocks * dim
    low_half = in_low_half((LANES, LANES))
    lane = lax.broadcasted_iota(i32, (8, LANES), 1)

    def span_of(leaf):
        return slice(leaf * points, (leaf + 1) * points)

    def points_of(leaf):
        begin = coords_at + leaf * blocks * dim
        ref = place_refs[-1]
        own = [ref[begin + block * dim : begin + (block + 1) * dim, :] for block in range(blocks)]
        return jnp.concatenate(own, axis=1)

    if first and not use:
        for leaf in range(LEAVES):
            targets_ref[0, span_of(leaf), :] = target_rows(points_of(leaf))
            targets_ref[1, span_of(leaf), :] = target_rows(sibling_ref[:, span_of(leaf)])
    if first:
        total_ref[...] = jnp.zeros_like(total_ref)
        sums_ref[...] = jnp.zeros_like(sums_ref)

    def table_of(core):
        mine, other = (ref[...] for ref in table_refs)
        return jnp.where(core == 0, mine, other)

    def picked(table, entry):
        return jnp.sum(jnp.where(lane == entry, table, 0.0), axis=1, keepdims=True)

    def values(core, sources_ref, kept_ref):
        if use:
            return kept_ref[...]
        made = kernel_values(targets_ref[core], sources_ref[...])
        if kept_ref is not None:
            kept_ref[...] = made
        return made

    device = device_of(ring, spots[-1])

    def near_part(turn, core, leaf):
        table = table_of(core)
        named = [picked(table, device * LEAVES + which)[0:LEAVES] for which in range(LEAVES)]
        if leaf is None:
            second = jnp.where(jnp.sum(named[1], axis=0, keepdims=True) > 0.0, 1.0, 0.0)
        else:
            second = jnp.full((1, 1), float(leaf), f32)
        times = named[0] * (1.0 - second) + named[1] * second
        if not use:
            chosen = points_of(0) * (1.0 - second).astype(bf16) + points_of(1) * second.astype(bf16)
            put_sources(near_ref, chosen)
        half = jnp.where(lane[0:1] < LANES // LEAVES, 1.0 - second, second).astype(bf16)
        charges_ref[...] = charge_refs[-1][0:points, :] * half
        kept = None if near_kept_ref is None else near_kept_ref.at[turn]
        added = matmul(values(core, None if use else near_ref, kept), charges_ref[...])
        return [times[own : own + 1] * added[span_of(own)] for own in range(LEAVES)]

    weights = []
    skeletons = []
    for at in far_of:
        rows = charge_refs[at][points : points + LANES, :].astype(f32)
        node = device_of(ring, spots[at])
        weights.append((jnp.where(low_half, rows, swapped(rows)), node))
        sums_ref[node // BRANCH] += rows
        if not use:
            skeletons.append(place_refs[at][skeletons_at : skeletons_at + dim, :])
    if last:
        for sub in range(n_sub):
            rows = sums_ref[sub]
            weights.append((jnp.where(low_half, swapped(rows), rows), len(ring) * CORES + sub))
            if not use:
                skeletons.append(upper_points_ref[:, sub * LANES : (sub + 1) * LANES])
    if has_far and not use:
        put_sources(far_ref, jnp.concatenate(skeletons, axis=1))

    def far_part(core):
        table = table_of(core)
        kernel = values(
            core,
            None if use else far_ref,
            None if far_kept_ref is None else far_kept_ref.at[core],
        )
        added = []
        for own in range(LEAVES):
            for position, (block, node) in enumerate(weights):
                scaled = block * picked(table, node)[LEAVES + own : LEAVES + own + 1]
                high = scaled.astype(bf16).astype(f32)
                rows = slice(position * LANES, (position + 1) * LANES)
                far_charges_ref[own, rows, :] = jnp.where(low_half, high, scaled - high).astype(bf16)
            added.append(matmul(kernel[span_of(own)], far_charges_ref[own]))
        return added

    def add(core, parts):
        for own in range(LEAVES):
            total = total_ref[core, span_of(own), :]
            for part in parts:
                total = total + part[own]
            total_ref[core, span_of(own), :] = total

    if first:
        for leaf in range(LEAVES):
            add(0, [near_part(leaf, 0, leaf)])
        add(1, [near_part(LEAVES, 1, None), far_part(1)])
    else:

        def step(core, carry):
            parts = [near_part(core, core, None)]
            add(core, parts + ([far_part(core)] if has_far else []))
            return carry

        lax.fori_loop(0, CORES, step, 0)

    if last:
        for core, ref in enumerate(half_refs):
            both = [total_ref[core, span_of(leaf), :] for leaf in range(LEAVES)]
            both = [total + swapped(total) for total in both]
            ref[...] = jnp.where(in_low_half(both[0].shape), both[0], both[1])


def gate_kernel(message_ref, after_ref, out_ref):
    pass


def gated(message, after):
    anywhere = pl.BlockSpec(memory_space=pl.ANY)
    return pl.pallas_call(
        gate_kernel,
        out_shape=jax.ShapeDtypeStruct(message.shape, message.dtype),
        in_specs=[anywhere] * 2,
        out_specs=anywhere,
        input_output_aliases={0: 0},
    )(message, after)


def call(body, args, out_shapes, streamed=(), scratch=(), aliases={}, flops=0, vmem_mib=16):
    vmem = pl.BlockSpec(memory_space=pltpu.VMEM)
    specs = []
    for place, arg in enumerate(args):
        if arg.dtype == i32:
            specs.append(pl.BlockSpec(memory_space=pltpu.SMEM))
        elif place in streamed:
            specs.append(pl.BlockSpec(arg.shape, lambda i: (0,) * 2))
        else:
            specs.append(vmem)
    moved = sum(arg.size * arg.dtype.itemsize for arg in args)
    return pl.pallas_call(
        body,
        grid=(1,),
        out_shape=out_shapes,
        in_specs=specs,
        out_specs=[vmem for _ in out_shapes],
        scratch_shapes=list(scratch),
        input_output_aliases=aliases,
        compiler_params=pltpu.CompilerParams(vmem_limit_bytes=vmem_mib * 1024 * 1024),
        cost_estimate=pl.CostEstimate(flops=flops, bytes_accessed=moved, transcendentals=0),
    )(*args)


def ring_order(chips):
    if chips == 8:
        return [0, 2, 4, 6, 7, 5, 3, 1]
    return list(range(chips))


def on_device(
    coords,
    charges,
    near_lists,
    far_lists,
    leaf_interp,
    node_interp,
    upper_interp,
    node_points,
    upper_points,
):
    dim, local = coords.shape
    columns = charges.shape[0]
    points = local // LEAVES
    peers = lax.axis_size("leaf")
    n_sub = peers // BRANCH
    ring = ring_order(peers // CORES)
    chips = len(ring)

    def along(step):
        return [
            (ring[place] * CORES + core, ring[(place + step * (1 - 2 * core)) % chips] * CORES + core)
            for place in range(chips)
            for core in range(CORES)
        ]

    one_way = functools.partial(lax.ppermute, axis_name="leaf", perm=along(1))
    other_way = functools.partial(lax.ppermute, axis_name="leaf", perm=along(-1))
    to_sibling = functools.partial(
        lax.ppermute, axis_name="leaf", perm=[(device, device ^ 1) for device in range(peers)]
    )

    def shape(*extent, dtype=bf16):
        return jax.ShapeDtypeStruct(extent, dtype)

    maps = [leaf_interp, node_interp, upper_interp]
    message, table = call(
        message_kernel,
        [near_lists, far_lists, coords, charges, node_points] + maps,
        [
            shape(points + LANES + LEAVES * points // LANES * dim + dim, LANES),
            shape(8, LANES, dtype=f32),
        ],
        streamed=range(2, 8),
        vmem_mib=60,
    )
    tables = [table, to_sibling(table)]
    sibling_coords = to_sibling(coords)

    total_shape = shape(CORES, local, LANES, dtype=f32)
    sums_shape = shape(n_sub, LANES, LANES, dtype=f32)
    half_shape = shape(points, LANES, dtype=f32)
    targets_shape = shape(CORES, local, LANES)

    steps = LEAVES + 1 + CORES * (chips - 1)
    kept_bytes = 2 * points * (steps * local + CORES * LEAVES * (chips + n_sub) * LANES)
    keeping = kept_bytes <= KEPT_MIB * 2**20

    def stage(spots, far_of, placed, charged, targets, carried, last, kept):
        first = not carried
        mode = "use" if kept else "keep" if keeping else "make"
        args = tables + ([] if kept else placed) + charged
        if kept:
            args += kept
        else:
            args += [sibling_coords] if first else [targets]
        carried_at = len(args)
        args += carried
        args += [upper_points] if last and not kept else []
        far_width = LANES * (len(far_of) + (n_sub if last else 0))
        scratch = [
            pltpu.VMEM((LEAVES, max(far_width, LANES), LANES), bf16),
            pltpu.VMEM((points, LANES), bf16),
        ]
        if not kept:
            scratch += [
                pltpu.VMEM((LANES, points), bf16),
                pltpu.VMEM((LANES, max(far_width, LANES)), bf16),
            ]
        outs = [targets_shape] if first and not kept else []
        kept_at = len(outs)
        if mode == "keep":
            outs.append(shape(LEAVES + 1 if first else CORES, local, points))
            outs += [shape(CORES, local, far_width)] if far_of else []
        kept_to = len(outs)
        outs += [half_shape, half_shape] if last else []
        aliases = {carried_at + k: len(outs) + k for k in range(len(carried))}
        outs += [total_shape, sums_shape]
        static = (ring, spots, far_of, n_sub, dim, points, first, last, mode)
        results = call(
            functools.partial(stage_kernel, static),
            args,
            outs,
            scratch=scratch,
            aliases=aliases,
            flops=(1 if kept else 2) * 10**9,
        )
        targets = results[0] if first and not kept else targets
        return targets, list(results[kept_at:kept_to]), list(results[kept_to : kept_to + 2])

    def around(message, placed, targets, kept):
        met = []
        made = []
        carried = []

        def arrived(message):
            nonlocal targets, carried
            met.append(message)
            spot = len(met) - 1
            last = spot == chips - 1
            spots = (spot - 1, spot) if spot % 2 == 0 and spot > 0 else (spot,)
            far_of = () if spot % 2 == 1 and not last else tuple(range(len(spots)))
            charged = [met[at] for at in spots]
            targets, values, carried = stage(
                spots,
                far_of,
                [placed[at] for at in spots] if placed else charged,
                charged,
                targets,
                carried,
                last,
                kept[spot] if kept else [],
            )
            made.append(values)

        one, other = one_way(message), other_way(message)
        arrived(message)
        for hop in range(1, chips // 2):
            one_next = one_way(one)
            arrived(one)
            other_next = None
            if hop < chips // 2 - 1:
                other = gated(other, carried[1])
                other_next = other_way(other)
            arrived(other)
            one, other = one_next, other_next
        arrived(one)
        placed = met if placed is None else placed
        return placed, targets, made, carried

    placed, targets, kept, (mine, other) = around(message, None, None, None)
    first, message = call(
        joined_kernel,
        [mine, to_sibling(other)] + maps,
        [shape(columns, local), shape(points + LANES, LANES)],
    )
    *_, (mine, other) = around(message, placed, targets, kept if keeping else None)
    (second,) = call(added_kernel, [mine, to_sibling(other)], [shape(columns, local)])
    return (first, second)


def solution(mesh):
    placed = (
        P(None, ("groups", "leaf")),
        P(None, ("groups", "leaf")),
        P(("groups", "leaf"), None),
        P(("groups", "leaf"), None),
        P(("groups", "leaf"), None),
        P(("groups", "leaf"), None),
        P(("groups", "leaf"), None),
        P(None, ("groups", "leaf")),
        P(None, "groups"),
    )
    return jax.shard_map(
        on_device,
        mesh=mesh,
        in_specs=placed,
        out_specs=(P(None, ("groups", "leaf")), P(None, ("groups", "leaf"))),
        check_vma=False,
    )
```

time: 75.7 us -> 97.3 us (1.29)
  local copies, waits for them, and re-layouts: 1.68 us -> 35.2 us
  waiting for transfers between devices: 15.4 us -> 6.59 us
  Pallas kernels: 40.3 us -> 34.8 us
  starting transfers between devices: 17.1 us -> 18.8 us
    unnamed x14 -> x102, local copies, waits for them, and re-layouts: 1.68 us -> 35.2 us
    ppermute x14, waiting for transfers between devices: 11.2 us -> 3.53 us  [the longest x4 3.5 us: around(): one, other = (one_way(message), other_way(message))]
    pallas_call x13 -> x19, Pallas kernels: 40.3 us -> 34.8 us  [call(): pl.pallas_call(body, grid=(1,), out_shape=out_shapes, in_specs=specs, out...]
    ppermute x14, starting transfers between devices: 16.3 us -> 18.1 us  [the longest x6 10.2 us: around(): one_next = one_way(one)]
    ppermute x1, waiting for transfers between devices: 1.21 us -> 0.01 us  [on_device(): tables = [table, to_sibling(table)]]
  transfers between devices with their start and end apart: 18 -> 18, of which waited for: 12 -> 3; matrix products, arithmetic and copies ran while one was open for 0% -> 0% of each run, Pallas kernels for 42% -> 30%
where the time goes in v8:
time: 97.3 us; the launch traced here: 96.4 us
  local copies, waits for them, and re-layouts  35.2 us (36%)
  Pallas kernels  34.8 us (36%)
  starting transfers between devices  18.8 us (19%)
  waiting for transfers between devices  6.59 us (7%)
  between operations  1 us (1%)
    unnamed x102, local copies, waits for them, and re-layouts  35.2 us
    pallas_call x19, Pallas kernels, call(): pl.pallas_call(body, grid=(1,), out_shape=out_shapes, in_specs=specs, out...  34.8 us
    ppermute x6, starting transfers between devices, around(): one_next = one_way(one)  10.2 us
    ppermute x4, starting transfers between devices, around(): one, other = (one_way(message), other_way(message))  6.19 us
    ppermute x4, waiting for transfers between devices, around(): one, other = (one_way(message), other_way(message))  3.5 us
    ppermute x2, waiting for transfers between devices, on_device(): to_sibling(other)  3.05 us
  transfers between devices with their start and end apart: 18, of which 3 were waited for; matrix products, arithmetic and copies ran while one was open for 0% of the time, Pallas kernels for 30%

profile of v8, /device:TPU:0, one launch (start us, length us, event | category | flops | bytes accessed | tf_op | source)
XLA Modules:
  0.0 96.4 jit_solution(5731570267008328768)
XLA Ops:
  1.1 2.3 %shard_map.104 = (bf16[1216,128]{1,0:T(8,128)(2,1)}, f32[8,128]{1,0:T(8,128)}) custom-call(s32[2,16]{1,0:T(2,128)} %near_ref.1, s32[2,32]{1,0:T(2,128)} %far_ref.1, bf16[64,1024]{1,0:T(8,128)(2,1)} %coords_ref.1, bf16[64,1024]{1,0:T(8,128)(2,1)} %charges_ref.1, bf16[64,128]{1,0:T(8,128)(2,1)} %points_ref.1, bf16[1024,128]{1,0:T(8,128)(2,1)} %leaf_ref.3, ...), custom_call_target="tpu_custom_call" | custom-call | bytes 639360 | tf_op jit(solution)/shard_map/pallas_call | solution.py:327
  3.4 2.6 %collective-permute-start.1 = (bf16[1216,128]{1,0:T(8,128)(2,1)}, bf16[1216,128]{1,0:T(8,128)(2,1)S(1)}, u32[]{:S(2)}, u32[]{:S(2)}) collective-permute-start(bf16[1216,128]{1,0:T(8,128)(2,1)} %get-tuple-element.53.refs_2_.refs_3_), channel_id=1, source_target_pairs={{0,4},{1,3},{4,8},{5,1},{8,12},{9,5},{12,14},{13,9},{14,10},{15,13... | collective-permute-start | bytes 933896 | tf_op jit(solution)/shard_map/ppermute | solution.py:471
  6.2 1.6 %collective-permute-start.6 = (bf16[1216,128]{1,0:T(8,128)(2,1)}, bf16[1216,128]{1,0:T(8,128)(2,1)S(1)}, u32[]{:S(2)}, u32[]{:S(2)}) collective-permute-start(bf16[1216,128]{1,0:T(8,128)(2,1)} %get-tuple-element.53.refs_2_.refs_3_), channel_id=1, source_target_pairs={{0,2},{1,5},{4,0},{5,9},{8,4},{9,13},{12,8},{13,15},{14,12},{15,11... | collective-permute-start | bytes 933896 | tf_op jit(solution)/shard_map/ppermute | solution.py:471
  9.4 2.1 %shard_map.105 = (bf16[2,1024,128]{2,1,0:T(8,128)(2,1)S(1)}, bf16[3,1024,512]{2,1,0:T(8,128)(2,1)S(1)}, bf16[2,1024,128]{2,1,0:T(8,128)(2,1)S(1)}, f32[2,1024,128]{2,1,0:T(8,128)S(1)}, f32[1,128,128]{2,1,0:T(8,128)S(1)}) custom-call(f32[8,128]{1,0:T(8,128)S(1)} %copy-done.39, f32[8,128]{1,0:T(8,128)S(1)} %collective-permute-done.refs_1_, ...), custom_call_target="tpu_custom_call" | custom-call | flops 2000000000 | bytes 761856 | tf_op jit(solution)/shard_map/pallas_call | solution.py:327
  11.5 1.6 %copy-done = bf16[3,1024,512]{2,1,0:T(8,128)(2,1)} copy-done((bf16[3,1024,512]{2,1,0:T(8,128)(2,1)}, bf16[3,1024,512]{2,1,0:T(8,128)(2,1)S(1)}, u32[]{:S(2)}) %copy-start) | copy-done | bytes 3145752
  13.1 2.2 %collective-permute-start.2 = (bf16[1216,128]{1,0:T(8,128)(2,1)S(1)}, bf16[1216,128]{1,0:T(8,128)(2,1)S(1)}, u32[]{:S(2)}, u32[]{:S(2)}) collective-permute-start(bf16[1216,128]{1,0:T(8,128)(2,1)S(1)} %collective-permute-done.1.refs_2_.refs_3_.refs_4_), channel_id=1, source_target_pairs={{0,4},{1,3},{4,8},{5,1},{8,12},{9,5},{12,14},{13,9},{14,10},{15,13... | collective-permute-start | bytes 933896 | tf_op jit(solution)/shard_map/ppermute | solution.py:474
  15.3 1.6 %shard_map.106 = (bf16[2,1024,512]{2,1,0:T(8,128)(2,1)S(1)}, f32[2,1024,128]{2,1,0:T(8,128)S(1)}, f32[1,128,128]{2,1,0:T(8,128)S(1)}) custom-call(f32[8,128]{1,0:T(8,128)S(1)} %copy-done.39, f32[8,128]{1,0:T(8,128)S(1)} %collective-permute-done.refs_1_, ...), custom_call_target="tpu_custom_call", output_to_operand_aliasing={{1}: (5, {}), {2}: (6, {})} | custom-call | flops 2000000000 | bytes 2269184 | tf_op jit(solution)/shard_map/pallas_call | solution.py:327
  21.8 2.3 %shard_map.108 = (bf16[2,1024,512]{2,1,0:T(8,128)(2,1)S(1)}, bf16[2,1024,256]{2,1,0:T(8,128)(2,1)S(1)}, f32[2,1024,128]{2,1,0:T(8,128)S(1)}, f32[1,128,128]{2,1,0:T(8,128)S(1)}) custom-call(f32[8,128]{1,0:T(8,128)S(1)} %copy-done.40, f32[8,128]{1,0:T(8,128)S(1)} %collective-permute-done.refs_1_, ...), custom_call_target="tpu_custom_call", output_to_operand_aliasing={{2}: (7, {}), {3}: (8, {})} | custom-call | flops 2000000000 | bytes 2891776 | tf_op jit(solution)/shard_map/pallas_call | solution.py:327
  25.4 1.7 %collective-permute-start.3 = (bf16[1216,128]{1,0:T(8,128)(2,1)S(1)}, bf16[1216,128]{1,0:T(8,128)(2,1)S(1)}, u32[]{:S(2)}, u32[]{:S(2)}) collective-permute-start(bf16[1216,128]{1,0:T(8,128)(2,1)S(1)} %collective-permute-done.2.refs_2_.refs_3_.refs_4_), channel_id=1, source_target_pairs={{0,4},{1,3},{4,8},{5,1},{8,12},{9,5},{12,14},{13,9},{14,10},{15,13... | collective-permute-start | bytes 933896 | tf_op jit(solution)/shard_map/ppermute | solution.py:474
  27.1 1.6 %shard_map.109 = (bf16[2,1024,512]{2,1,0:T(8,128)(2,1)S(1)}, f32[2,1024,128]{2,1,0:T(8,128)S(1)}, f32[1,128,128]{2,1,0:T(8,128)S(1)}) custom-call(f32[8,128]{1,0:T(8,128)S(1)} %copy-done.40, f32[8,128]{1,0:T(8,128)S(1)} %collective-permute-done.refs_1_, ...), custom_call_target="tpu_custom_call", output_to_operand_aliasing={{1}: (5, {}), {2}: (6, {})} | custom-call | flops 2000000000 | bytes 2269184 | tf_op jit(solution)/shard_map/pallas_call | solution.py:327
  33.7 2.3 %shard_map.111 = (bf16[2,1024,512]{2,1,0:T(8,128)(2,1)S(1)}, bf16[2,1024,256]{2,1,0:T(8,128)(2,1)S(1)}, f32[2,1024,128]{2,1,0:T(8,128)S(1)}, f32[1,128,128]{2,1,0:T(8,128)S(1)}) custom-call(f32[8,128]{1,0:T(8,128)S(1)} %copy-done.40, f32[8,128]{1,0:T(8,128)S(1)} %collective-permute-done.refs_1_, ...), custom_call_target="tpu_custom_call", output_to_operand_aliasing={{2}: (7, {}), {3}: (8, {})} | custom-call | flops 2000000000 | bytes 2891776 | tf_op jit(solution)/shard_map/pallas_call | solution.py:327
  37.3 1.7 %collective-permute-start.4 = (bf16[1216,128]{1,0:T(8,128)(2,1)S(1)}, bf16[1216,128]{1,0:T(8,128)(2,1)S(1)}, u32[]{:S(2)}, u32[]{:S(2)}) collective-permute-start(bf16[1216,128]{1,0:T(8,128)(2,1)S(1)} %collective-permute-done.3.refs_2_.refs_3_.refs_4_), channel_id=1, source_target_pairs={{0,4},{1,3},{4,8},{5,1},{8,12},{9,5},{12,14},{13,9},{14,10},{15,13... | collective-permute-start | bytes 933896 | tf_op jit(solution)/shard_map/ppermute | solution.py:474
  39.0 1.6 %shard_map.112 = (bf16[2,1024,512]{2,1,0:T(8,128)(2,1)S(1)}, f32[2,1024,128]{2,1,0:T(8,128)S(1)}, f32[1,128,128]{2,1,0:T(8,128)S(1)}) custom-call(f32[8,128]{1,0:T(8,128)S(1)} %copy-done.40, f32[8,128]{1,0:T(8,128)S(1)} %collective-permute-done.refs_1_, ...), custom_call_target="tpu_custom_call", output_to_operand_aliasing={{1}: (5, {}), {2}: (6, {})} | custom-call | flops 2000000000 | bytes 2269184 | tf_op jit(solution)/shard_map/pallas_call | solution.py:327
  42.1 2.3 %shard_map.113 = (bf16[2,1024,512]{2,1,0:T(8,128)(2,1)S(1)}, bf16[2,1024,256]{2,1,0:T(8,128)(2,1)S(1)}, f32[2,1024,128]{2,1,0:T(8,128)S(1)}, f32[1,128,128]{2,1,0:T(8,128)S(1)}) custom-call(f32[8,128]{1,0:T(8,128)S(1)} %copy-done.40, f32[8,128]{1,0:T(8,128)S(1)} %collective-permute-done.refs_1_, ...), custom_call_target="tpu_custom_call", output_to_operand_aliasing={{2}: (7, {}), {3}: (8, {})} | custom-call | flops 2000000000 | bytes 2891776 | tf_op jit(solution)/shard_map/pallas_call | solution.py:327
  50.4 2.7 %shard_map.114 = (bf16[2,1024,512]{2,1,0:T(8,128)(2,1)S(1)}, bf16[2,1024,256]{2,1,0:T(8,128)(2,1)S(1)}, f32[512,128]{1,0:T(8,128)S(1)}, f32[512,128]{1,0:T(8,128...) custom-call(f32[8,128]{1,0:T(8,128)S(1)} %copy-done.40, ...), custom_call_target="tpu_custom_call", output_to_operand_aliasing={{4}: (5, {}), {5}: (6, {})} | custom-call | flops 2000000000 | bytes 2285568 | tf_op jit(solution)/shard_map/pallas_call | solution.py:327
  56.5 1.7 %collective-permute-start.10 = (bf16[640,128]{1,0:T(8,128)(2,1)S(1)}, bf16[640,128]{1,0:T(8,128)(2,1)}, u32[]{:S(2)}, u32[]{:S(2)}) collective-permute-start(bf16[640,128]{1,0:T(8,128)(2,1)S(1)} %get-tuple-element.72.refs_2_), channel_id=1, source_target_pairs={{0,4},{1,3},{4,8},{5,1},{8,12},{9,5},{12,14},{13,9},{14,10},{15,13... | collective-permute-start | bytes 491528 | tf_op jit(solution)/shard_map/ppermute | solution.py:471
  59.6 3.5 %collective-permute-done.10.refs_2_ = bf16[640,128]{1,0:T(8,128)(2,1)} collective-permute-done((bf16[640,128]{1,0:T(8,128)(2,1)S(1)}, bf16[640,128]{1,0:T(8,128)(2,1)}, u32[]{:S(2)}, u32[]{:S(2)}) %collective-permute-start.10) | collective-permute-done | bytes 163872 | tf_op jit(solution)/shard_map/ppermute | solution.py:471
  64.6 2.0 %shard_map.117 = (f32[2,1024,128]{2,1,0:T(8,128)S(1)}, f32[1,128,128]{2,1,0:T(8,128)S(1)}) custom-call(f32[8,128]{1,0:T(8,128)S(1)} %copy-done.40, f32[8,128]{1,0:T(8,128)S(1)} %collective-permute-done.refs_1_, bf16[640,128]{1,0:T(8,128)(2,1)} %collective-permute-done.10.refs_2_, ...), custom_call_target="tpu_custom_call", output_to_operand_aliasing={{0}: (4, {}), {1}: (5, {})} | custom-call | flops 1000000000 | bytes 3383296 | tf_op jit(solution)/shard_map/pallas_call | solution.py:327
  69.3 1.6 %copy-done.11 = bf16[2,1024,512]{2,1,0:T(8,128)(2,1)S(1)} copy-done((bf16[2,1024,512]{2,1,0:T(8,128)(2,1)S(1)}, bf16[2,1024,512]{2,1,0:T(8,128)(2,1)}, u32[]{:S(2)}) %copy-start.11) | copy-done | bytes 2097176
  73.1 2.5 %shard_map.119 = (f32[2,1024,128]{2,1,0:T(8,128)S(1)}, f32[1,128,128]{2,1,0:T(8,128)S(1)}) custom-call(f32[8,128]{1,0:T(8,128)S(1)} %copy-done.40, f32[8,128]{1,0:T(8,128)S(1)} %collective-permute-done.refs_1_, bf16[640,128]{1,0:T(8,128)(2,1)} %collective-permute-done.10.refs_2_, ...), custom_call_target="tpu_custom_call", output_to_operand_aliasing={{0}: (6, {}), {1}: (7, {})} | custom-call | flops 1000000000 | bytes 4595712 | tf_op jit(solution)/shard_map/pallas_call | solution.py:327
  80.9 1.6 %copy-done.9 = bf16[2,1024,512]{2,1,0:T(8,128)(2,1)S(1)} copy-done((bf16[2,1024,512]{2,1,0:T(8,128)(2,1)S(1)}, bf16[2,1024,512]{2,1,0:T(8,128)(2,1)}, u32[]{:S(2)}) %copy-start.9) | copy-done | bytes 2097176
  87.7 2.0 %shard_map.123 = (f32[2,1024,128]{2,1,0:T(8,128)S(1)}, f32[1,128,128]{2,1,0:T(8,128)S(1)}) custom-call(f32[8,128]{1,0:T(8,128)S(1)} %copy-done.40, f32[8,128]{1,0:T(8,128)S(1)} %collective-permute-done.refs_1_, bf16[640,128]{1,0:T(8,128)(2,1)} %collective-permute-done.12.refs_2_, ...), custom_call_target="tpu_custom_call", output_to_operand_aliasing={{0}: (4, {}), {1}: (5, {})} | custom-call | flops 1000000000 | bytes 3383296 | tf_op jit(solution)/shard_map/pallas_call | solution.py:327
  89.7 2.5 %shard_map.124 = (f32[2,1024,128]{2,1,0:T(8,128)S(1)}, f32[1,128,128]{2,1,0:T(8,128)S(1)}) custom-call(f32[8,128]{1,0:T(8,128)S(1)} %copy-done.40, f32[8,128]{1,0:T(8,128)S(1)} %collective-permute-done.refs_1_, bf16[640,128]{1,0:T(8,128)(2,1)} %collective-permute-done.12.refs_2_, ...), custom_call_target="tpu_custom_call", output_to_operand_aliasing={{0}: (6, {}), {1}: (7, {})} | custom-call | flops 1000000000 | bytes 4595712 | tf_op jit(solution)/shard_map/pallas_call | solution.py:327
  92.2 1.8 %shard_map.125 = (f32[512,128]{1,0:T(8,128)S(1)}, f32[512,128]{1,0:T(8,128)S(1)}, f32[2,1024,128]{2,1,0:T(8,128)S(1)}, f32[1,128,128]{2,1,0:T(8,128)S(1)}) custom-call(f32[8,128]{1,0:T(8,128)S(1)} %copy-done.40, f32[8,128]{1,0:T(8,128)S(1)} %collective-permute-done.refs_1_, ...), custom_call_target="tpu_custom_call", output_to_operand_aliasing={{2}: (5, {}), {3}: (6, {})} | custom-call | flops 1000000000 | bytes 4431872 | tf_op jit(solution)/shard_map/pallas_call | solution.py:327
  (137 shorter events, 46.0 us)
Async XLA Ops:
  0.6 7.1 %collective-permute-start.5 = (bf16[64,1024]{1,0:T(8,128)(2,1)}, bf16[64,1024]{1,0:T(8,128)(2,1)S(1)}, u32[]{:S(2)}, u32[]{:S(2)}) collective-permute-start(bf16[64,1024]{1,0:T(8,128)(2,1)} %coords_ref.1), channel_id=1, source_target_pairs={{0,1},{1,0},{2,3},{3,2},{4,5},{5,4},{6,7},{7,6},{8,9},{9,8},{10,11... | collective-permute-start | bytes 393224 | tf_op jit(solution)/shard_map/ppermute | solution.py:393
  3.4 9.7 %collective-permute-start.1 = (bf16[1216,128]{1,0:T(8,128)(2,1)}, bf16[1216,128]{1,0:T(8,128)(2,1)S(1)}, u32[]{:S(2)}, u32[]{:S(2)}) collective-permute-start(bf16[1216,128]{1,0:T(8,128)(2,1)} %get-tuple-element.53.refs_2_.refs_3_), channel_id=1, source_target_pairs={{0,4},{1,3},{4,8},{5,1},{8,12},{9,5},{12,14},{13,9},{14,10},{15,13... | collective-permute-start | bytes 933896 | tf_op jit(solution)/shard_map/ppermute | solution.py:471
  6.0 1.7 %collective-permute-start = (f32[8,128]{1,0:T(8,128)}, f32[8,128]{1,0:T(8,128)S(1)}, u32[]{:S(2)}, u32[]{:S(2)}) collective-permute-start(f32[8,128]{1,0:T(8,128)} %get-tuple-element.52.refs_0_), channel_id=1, source_target_pairs={{0,1},{1,0},{2,3},{3,2},{4,5},{5,4},{6,7},{7,6},{8,9},{9,8},{10,11... | collective-permute-start | bytes 12296 | tf_op jit(solution)/shard_map/ppermute | solution.py:392
  6.2 12.8 %collective-permute-start.6 = (bf16[1216,128]{1,0:T(8,128)(2,1)}, bf16[1216,128]{1,0:T(8,128)(2,1)S(1)}, u32[]{:S(2)}, u32[]{:S(2)}) collective-permute-start(bf16[1216,128]{1,0:T(8,128)(2,1)} %get-tuple-element.53.refs_2_.refs_3_), channel_id=1, source_target_pairs={{0,2},{1,5},{4,0},{5,9},{8,4},{9,13},{12,8},{13,15},{14,12},{15,11... | collective-permute-start | bytes 933896 | tf_op jit(solution)/shard_map/ppermute | solution.py:471
  13.1 12.3 %collective-permute-start.2 = (bf16[1216,128]{1,0:T(8,128)(2,1)S(1)}, bf16[1216,128]{1,0:T(8,128)(2,1)S(1)}, u32[]{:S(2)}, u32[]{:S(2)}) collective-permute-start(bf16[1216,128]{1,0:T(8,128)(2,1)S(1)} %collective-permute-done.1.refs_2_.refs_3_.refs_4_), channel_id=1, source_target_pairs={{0,4},{1,3},{4,8},{5,1},{8,12},{9,5},{12,14},{13,9},{14,10},{15,13... | collective-permute-start | bytes 933896 | tf_op jit(solution)/shard_map/ppermute | solution.py:474
  19.7 11.1 %collective-permute-start.7 = (bf16[1216,128]{1,0:T(8,128)(2,1)}, bf16[1216,128]{1,0:T(8,128)(2,1)S(1)}, u32[]{:S(2)}, u32[]{:S(2)}) collective-permute-start(bf16[1216,128]{1,0:T(8,128)(2,1)} %shard_map.107.refs_3_.refs_5_), channel_id=1, source_target_pairs={{0,2},{1,5},{4,0},{5,9},{8,4},{9,13},{12,8},{13,15},{14,12},{15,11... | collective-permute-start | bytes 933896 | tf_op jit(solution)/shard_map/ppermute | solution.py:479
  25.4 11.9 %collective-permute-start.3 = (bf16[1216,128]{1,0:T(8,128)(2,1)S(1)}, bf16[1216,128]{1,0:T(8,128)(2,1)S(1)}, u32[]{:S(2)}, u32[]{:S(2)}) collective-permute-start(bf16[1216,128]{1,0:T(8,128)(2,1)S(1)} %collective-permute-done.2.refs_2_.refs_3_.refs_4_), channel_id=1, source_target_pairs={{0,4},{1,3},{4,8},{5,1},{8,12},{9,5},{12,14},{13,9},{14,10},{15,13... | collective-permute-start | bytes 933896 | tf_op jit(solution)/shard_map/ppermute | solution.py:474
  31.5 10.5 %collective-permute-start.8 = (bf16[1216,128]{1,0:T(8,128)(2,1)}, bf16[1216,128]{1,0:T(8,128)(2,1)S(1)}, u32[]{:S(2)}, u32[]{:S(2)}) collective-permute-start(bf16[1216,128]{1,0:T(8,128)(2,1)} %shard_map.110.refs_3_.refs_5_), channel_id=1, source_target_pairs={{0,2},{1,5},{4,0},{5,9},{8,4},{9,13},{12,8},{13,15},{14,12},{15,11... | collective-permute-start | bytes 933896 | tf_op jit(solution)/shard_map/ppermute | solution.py:479
  37.3 11.1 %collective-permute-start.4 = (bf16[1216,128]{1,0:T(8,128)(2,1)S(1)}, bf16[1216,128]{1,0:T(8,128)(2,1)S(1)}, u32[]{:S(2)}, u32[]{:S(2)}) collective-permute-start(bf16[1216,128]{1,0:T(8,128)(2,1)S(1)} %collective-permute-done.3.refs_2_.refs_3_.refs_4_), channel_id=1, source_target_pairs={{0,4},{1,3},{4,8},{5,1},{8,12},{9,5},{12,14},{13,9},{14,10},{15,13... | collective-permute-start | bytes 933896 | tf_op jit(solution)/shard_map/ppermute | solution.py:474
  42.1 6.3 %copy-start.42 = (bf16[64,128]{1,0:T(8,128)(2,1)S(1)}, bf16[64,128]{1,0:T(8,128)(2,1)}, u32[]{:S(2)}) copy-start(bf16[64,128]{1,0:T(8,128)(2,1)} %refs_7_.1) | copy-start | bytes 49156
  50.4 5.2 %copy-start.31 = (bf16[256,128]{1,0:T(8,128)(2,1)S(1)}, bf16[256,128]{1,0:T(8,128)(2,1)}, u32[]{:S(2)}) copy-start(bf16[256,128]{1,0:T(8,128)(2,1)} %node_ref.3) | copy-start | bytes 196612
  50.4 5.2 %copy-start.38 = (bf16[128,128]{1,0:T(8,128)(2,1)S(1)}, bf16[128,128]{1,0:T(8,128)(2,1)}, u32[]{:S(2)}) copy-start(bf16[128,128]{1,0:T(8,128)(2,1)} %upper_ref.3) | copy-start | bytes 98308
  50.4 8.1 %copy-start.1 = (bf16[3,1024,512]{2,1,0:T(8,128)(2,1)S(1)}, bf16[3,1024,512]{2,1,0:T(8,128)(2,1)}, u32[]{:S(2)}) copy-start(bf16[3,1024,512]{2,1,0:T(8,128)(2,1)} %copy-done) | copy-start | bytes 9437188
  50.4 8.1 %copy-start.26 = (bf16[2,1024,128]{2,1,0:T(8,128)(2,1)S(1)}, bf16[2,1024,128]{2,1,0:T(8,128)(2,1)}, u32[]{:S(2)}) copy-start(bf16[2,1024,128]{2,1,0:T(8,128)(2,1)} %copy-done.25) | copy-start | bytes 1572868
  54.1 1.5 %collective-permute-start.9 = (f32[512,128]{1,0:T(8,128)S(1)}, f32[512,128]{1,0:T(8,128)S(1)}, u32[]{:S(2)}, u32[]{:S(2)}) collective-permute-start(f32[512,128]{1,0:T(8,128)S(1)} %get-tuple-element.70), channel_id=1, source_target_pairs={{0,1},{1,0},{2,3},{3,2},{4,5},{5,4},{6,7},{7,6},{8,9},{9,8},{10,11... | collective-permute-start | bytes 786440 | tf_op jit(solution)/shard_map/ppermute | solution.py:489
  56.5 8.1 %copy-start.48 = (bf16[2,1024,512]{2,1,0:T(8,128)(2,1)S(1)}, bf16[2,1024,512]{2,1,0:T(8,128)(2,1)}, u32[]{:S(2)}) copy-start(bf16[2,1024,512]{2,1,0:T(8,128)(2,1)} %copy-done.47) | copy-start | bytes 6291460
  56.5 6.6 %collective-permute-start.10 = (bf16[640,128]{1,0:T(8,128)(2,1)S(1)}, bf16[640,128]{1,0:T(8,128)(2,1)}, u32[]{:S(2)}, u32[]{:S(2)}) collective-permute-start(bf16[640,128]{1,0:T(8,128)(2,1)S(1)} %get-tuple-element.72.refs_2_), channel_id=1, source_target_pairs={{0,4},{1,3},{4,8},{5,1},{8,12},{9,5},{12,14},{13,9},{14,10},{15,13... | collective-permute-start | bytes 491528 | tf_op jit(solution)/shard_map/ppermute | solution.py:471
  58.3 9.0 %collective-permute-start.14 = (bf16[640,128]{1,0:T(8,128)(2,1)S(1)}, bf16[640,128]{1,0:T(8,128)(2,1)S(1)}, u32[]{:S(2)}, u32[]{:S(2)}) collective-permute-start(bf16[640,128]{1,0:T(8,128)(2,1)S(1)} %get-tuple-element.72.refs_2_), channel_id=1, source_target_pairs={{0,2},{1,5},{4,0},{5,9},{8,4},{9,13},{12,8},{13,15},{14,12},{15,11... | collective-permute-start | bytes 491528 | tf_op jit(solution)/shard_map/ppermute | solution.py:471
  63.1 12.5 %collective-permute-start.11 = (bf16[640,128]{1,0:T(8,128)(2,1)}, bf16[640,128]{1,0:T(8,128)(2,1)S(1)}, u32[]{:S(2)}, u32[]{:S(2)}) collective-permute-start(bf16[640,128]{1,0:T(8,128)(2,1)} %collective-permute-done.10.refs_2_), channel_id=1, source_target_pairs={{0,4},{1,3},{4,8},{5,1},{8,12},{9,5},{12,14},{13,9},{14,10},{15,13... | collective-permute-start | bytes 491528 | tf_op jit(solution)/shard_map/ppermute | solution.py:474
  67.9 10.9 %collective-permute-start.15 = (bf16[640,128]{1,0:T(8,128)(2,1)}, bf16[640,128]{1,0:T(8,128)(2,1)S(1)}, u32[]{:S(2)}, u32[]{:S(2)}) collective-permute-start(bf16[640,128]{1,0:T(8,128)(2,1)} %shard_map.118.refs_3_), channel_id=1, source_target_pairs={{0,2},{1,5},{4,0},{5,9},{8,4},{9,13},{12,8},{13,15},{14,12},{15,11... | collective-permute-start | bytes 491528 | tf_op jit(solution)/shard_map/ppermute | solution.py:479
  75.6 10.6 %collective-permute-start.12 = (bf16[640,128]{1,0:T(8,128)(2,1)S(1)}, bf16[640,128]{1,0:T(8,128)(2,1)}, u32[]{:S(2)}, u32[]{:S(2)}) collective-permute-start(bf16[640,128]{1,0:T(8,128)(2,1)S(1)} %collective-permute-done.11.refs_2_), channel_id=1, source_target_pairs={{0,4},{1,3},{4,8},{5,1},{8,12},{9,5},{12,14},{13,9},{14,10},{15,13... | collective-permute-start | bytes 491528 | tf_op jit(solution)/shard_map/ppermute | solution.py:474
  79.5 10.2 %collective-permute-start.16 = (bf16[640,128]{1,0:T(8,128)(2,1)}, bf16[640,128]{1,0:T(8,128)(2,1)S(1)}, u32[]{:S(2)}, u32[]{:S(2)}) collective-permute-start(bf16[640,128]{1,0:T(8,128)(2,1)} %shard_map.121.refs_3_), channel_id=1, source_target_pairs={{0,2},{1,5},{4,0},{5,9},{8,4},{9,13},{12,8},{13,15},{14,12},{15,11... | collective-permute-start | bytes 491528 | tf_op jit(solution)/shard_map/ppermute | solution.py:479
  86.2 6.1 %collective-permute-start.13 = (bf16[640,128]{1,0:T(8,128)(2,1)}, bf16[640,128]{1,0:T(8,128)(2,1)S(1)}, u32[]{:S(2)}, u32[]{:S(2)}) collective-permute-start(bf16[640,128]{1,0:T(8,128)(2,1)} %collective-permute-done.12.refs_2_), channel_id=1, source_target_pairs={{0,4},{1,3},{4,8},{5,1},{8,12},{9,5},{12,14},{13,9},{14,10},{15,13... | collective-permute-start | bytes 491528 | tf_op jit(solution)/shard_map/ppermute | solution.py:474
  94.1 1.6 %collective-permute-start.17 = (f32[512,128]{1,0:T(8,128)S(1)}, f32[512,128]{1,0:T(8,128)S(1)}, u32[]{:S(2)}, u32[]{:S(2)}) collective-permute-start(f32[512,128]{1,0:T(8,128)S(1)} %get-tuple-element.101), channel_id=1, source_target_pairs={{0,1},{1,0},{2,3},{3,2},{4,5},{5,4},{6,7},{7,6},{8,9},{9,8},{10,11... | collective-permute-start | bytes 786440 | tf_op jit(solution)/shard_map/ppermute | solution.py:493
  (45 other events, 72.4 us)

commit v9 on v8

--- a/solution.py
+++ b/solution.py
@@ -310,6 +310,7 @@
         in_specs=[anywhere] * 2,
         out_specs=anywhere,
         input_output_aliases={0: 0},
+        compiler_params=pltpu.CompilerParams(vmem_limit_bytes=2**20),
     )(message, after)
 
 

time: 97.3 us -> 75.1 us (0.77)
  local copies, waits for them, and re-layouts: 35.2 us -> 1.67 us
  waiting for transfers between devices: 6.59 us -> 23.5 us
  Pallas kernels: 34.8 us -> 31.1 us
  starting transfers between devices: 18.8 us -> 17.8 us
    unnamed x102 -> x14, local copies, waits for them, and re-layouts: 35.2 us -> 1.67 us
    ppermute x6, waiting for transfers between devices: 0.02 us -> 14.9 us  [around(): one_next = one_way(one)]
    pallas_call x19, Pallas kernels: 34.8 us -> 31 us  [call(): pl.pallas_call(body, grid=(1,), out_shape=out_shapes, in_specs=specs, out...]
    ppermute x6, starting transfers between devices: 10.2 us -> 8.81 us  [around(): one_next = one_way(one)]
    ppermute x4, waiting for transfers between devices: 3.5 us -> 4.82 us  [around(): one, other = (one_way(message), other_way(message))]
  transfers between devices with their start and end apart: 18 -> 18, of which waited for: 3 -> 13; matrix products, arithmetic and copies ran while one was open for 0% -> 0% of each run, Pallas kernels for 30% -> 33%
where the time goes in v9:
time: 75.1 us; the launch traced here: 74.9 us
  Pallas kernels  31.1 us (41%)
  waiting for transfers between devices  23.5 us (31%)
  starting transfers between devices  17.8 us (24%)
  local copies, waits for them, and re-layouts  1.67 us (2%)
  between operations  0.84 us (1%)
    pallas_call x19, Pallas kernels, call(): pl.pallas_call(body, grid=(1,), out_shape=out_shapes, in_specs=specs, out...  31 us
    ppermute x6, waiting for transfers between devices, around(): one_next = one_way(one)  14.9 us
    ppermute x6, starting transfers between devices, around(): one_next = one_way(one)  8.81 us
    ppermute x4, starting transfers between devices, around(): one, other = (one_way(message), other_way(message))  6.19 us
    ppermute x4, waiting for transfers between devices, around(): one, other = (one_way(message), other_way(message))  4.82 us
    ppermute x2, waiting for transfers between devices, on_device(): to_sibling(other)  3.04 us
    ppermute x4, starting transfers between devices, around(): other_next = other_way(other)  2.01 us
    unnamed x14, local copies, waits for them, and re-layouts  1.67 us
  transfers between devices with their start and end apart: 18, of which 13 were waited for; matrix products, arithmetic and copies ran while one was open for 0% of the time, Pallas kernels for 33%

profile of v9, /device:TPU:0, one launch (start us, length us, event | category | flops | bytes accessed | tf_op | source)
XLA Modules:
  0.0 74.9 jit_solution(11440251043197340351)
XLA Ops:
  1.1 2.3 %shard_map.104 = (bf16[1216,128]{1,0:T(8,128)(2,1)}, f32[8,128]{1,0:T(8,128)}) custom-call(s32[2,16]{1,0:T(2,128)} %near_ref.1, s32[2,32]{1,0:T(2,128)} %far_ref.1, bf16[64,1024]{1,0:T(8,128)(2,1)} %coords_ref.1, bf16[64,1024]{1,0:T(8,128)(2,1)} %charges_ref.1, bf16[64,128]{1,0:T(8,128)(2,1)} %points_ref.1, bf16[1024,128]{1,0:T(8,128)(2,1)} %leaf_ref.3, ...), custom_call_target="tpu_custom_call" | custom-call | bytes 639360 | tf_op jit(solution)/shard_map/pallas_call | solution.py:328
  3.4 2.6 %collective-permute-start.1 = (bf16[1216,128]{1,0:T(8,128)(2,1)}, bf16[1216,128]{1,0:T(8,128)(2,1)S(1)}, u32[]{:S(2)}, u32[]{:S(2)}) collective-permute-start(bf16[1216,128]{1,0:T(8,128)(2,1)} %get-tuple-element.53.refs_2_.refs_3_), channel_id=1, source_target_pairs={{0,4},{1,3},{4,8},{5,1},{8,12},{9,5},{12,14},{13,9},{14,10},{15,13... | collective-permute-start | bytes 933896 | tf_op jit(solution)/shard_map/ppermute | solution.py:472
  6.2 1.6 %collective-permute-start.6 = (bf16[1216,128]{1,0:T(8,128)(2,1)}, bf16[1216,128]{1,0:T(8,128)(2,1)S(1)}, u32[]{:S(2)}, u32[]{:S(2)}) collective-permute-start(bf16[1216,128]{1,0:T(8,128)(2,1)} %get-tuple-element.53.refs_2_.refs_3_), channel_id=1, source_target_pairs={{0,2},{1,5},{4,0},{5,9},{8,4},{9,13},{12,8},{13,15},{14,12},{15,11... | collective-permute-start | bytes 933896 | tf_op jit(solution)/shard_map/ppermute | solution.py:472
  9.4 2.1 %shard_map.105 = (bf16[2,1024,128]{2,1,0:T(8,128)(2,1)S(1)}, bf16[3,1024,512]{2,1,0:T(8,128)(2,1)S(1)}, bf16[2,1024,128]{2,1,0:T(8,128)(2,1)S(1)}, f32[2,1024,128]{2,1,0:T(8,128)S(1)}, f32[1,128,128]{2,1,0:T(8,128)S(1)}) custom-call(f32[8,128]{1,0:T(8,128)S(1)} %copy-done.3, f32[8,128]{1,0:T(8,128)S(1)} %collective-permute-done.refs_1_, ...), custom_call_target="tpu_custom_call" | custom-call | flops 2000000000 | bytes 761856 | tf_op jit(solution)/shard_map/pallas_call | solution.py:328
  11.5 1.5 %collective-permute-done.1.refs_2_.refs_3_.refs_4_ = bf16[1216,128]{1,0:T(8,128)(2,1)S(1)} collective-permute-done((bf16[1216,128]{1,0:T(8,128)(2,1)}, bf16[1216,128]{1,0:T(8,128)(2,1)S(1)}, u32[]{:S(2)}, u32[]{:S(2)}) %collective-permute-start.1) | collective-permute-done | bytes 311328 | tf_op jit(solution)/shard_map/ppermute | solution.py:472
  13.0 2.4 %collective-permute-start.2 = (bf16[1216,128]{1,0:T(8,128)(2,1)S(1)}, bf16[1216,128]{1,0:T(8,128)(2,1)S(1)}, u32[]{:S(2)}, u32[]{:S(2)}) collective-permute-start(bf16[1216,128]{1,0:T(8,128)(2,1)S(1)} %collective-permute-done.1.refs_2_.refs_3_.refs_4_), channel_id=1, source_target_pairs={{0,4},{1,3},{4,8},{5,1},{8,12},{9,5},{12,14},{13,9},{14,10},{15,13... | collective-permute-start | bytes 933896 | tf_op jit(solution)/shard_map/ppermute | solution.py:475
  15.3 1.7 %shard_map.106 = (bf16[2,1024,512]{2,1,0:T(8,128)(2,1)S(1)}, f32[2,1024,128]{2,1,0:T(8,128)S(1)}, f32[1,128,128]{2,1,0:T(8,128)S(1)}) custom-call(f32[8,128]{1,0:T(8,128)S(1)} %copy-done.4, f32[8,128]{1,0:T(8,128)S(1)} %collective-permute-done.refs_1_, ...), custom_call_target="tpu_custom_call", output_to_operand_aliasing={{1}: (5, {}), {2}: (6, {})} | custom-call | flops 2000000000 | bytes 2269184 | tf_op jit(solution)/shard_map/pallas_call | solution.py:328
  17.4 2.3 %shard_map.108 = (bf16[2,1024,512]{2,1,0:T(8,128)(2,1)S(1)}, bf16[2,1024,256]{2,1,0:T(8,128)(2,1)S(1)}, f32[2,1024,128]{2,1,0:T(8,128)S(1)}, f32[1,128,128]{2,1,0:T(8,128)S(1)}) custom-call(f32[8,128]{1,0:T(8,128)S(1)} %copy-done.4, f32[8,128]{1,0:T(8,128)S(1)} %collective-permute-done.refs_1_, ...), custom_call_target="tpu_custom_call", output_to_operand_aliasing={{2}: (7, {}), {3}: (8, {})} | custom-call | flops 2000000000 | bytes 2891776 | tf_op jit(solution)/shard_map/pallas_call | solution.py:328
  19.7 3.6 %collective-permute-done.2.refs_2_.refs_3_.refs_4_ = bf16[1216,128]{1,0:T(8,128)(2,1)S(1)} collective-permute-done((bf16[1216,128]{1,0:T(8,128)(2,1)S(1)}, bf16[1216,128]{1,0:T(8,128)(2,1)S(1)}, u32[]{:S(2)}, u32[]{:S(2)}) %collective-permute-start.2) | collective-permute-done | bytes 311328 | tf_op jit(solution)/shard_map/ppermute | solution.py:475
  23.2 2.3 %collective-permute-start.3 = (bf16[1216,128]{1,0:T(8,128)(2,1)S(1)}, bf16[1216,128]{1,0:T(8,128)(2,1)S(1)}, u32[]{:S(2)}, u32[]{:S(2)}) collective-permute-start(bf16[1216,128]{1,0:T(8,128)(2,1)S(1)} %collective-permute-done.2.refs_2_.refs_3_.refs_4_), channel_id=1, source_target_pairs={{0,4},{1,3},{4,8},{5,1},{8,12},{9,5},{12,14},{13,9},{14,10},{15,13... | collective-permute-start | bytes 933896 | tf_op jit(solution)/shard_map/ppermute | solution.py:475
  25.6 1.7 %shard_map.109 = (bf16[2,1024,512]{2,1,0:T(8,128)(2,1)S(1)}, f32[2,1024,128]{2,1,0:T(8,128)S(1)}, f32[1,128,128]{2,1,0:T(8,128)S(1)}) custom-call(f32[8,128]{1,0:T(8,128)S(1)} %copy-done.4, f32[8,128]{1,0:T(8,128)S(1)} %collective-permute-done.refs_1_, ...), custom_call_target="tpu_custom_call", output_to_operand_aliasing={{1}: (5, {}), {2}: (6, {})} | custom-call | flops 2000000000 | bytes 2269184 | tf_op jit(solution)/shard_map/pallas_call | solution.py:328
  27.3 2.3 %shard_map.111 = (bf16[2,1024,512]{2,1,0:T(8,128)(2,1)S(1)}, bf16[2,1024,256]{2,1,0:T(8,128)(2,1)S(1)}, f32[2,1024,128]{2,1,0:T(8,128)S(1)}, f32[1,128,128]{2,1,0:T(8,128)S(1)}) custom-call(f32[8,128]{1,0:T(8,128)S(1)} %copy-done.4, f32[8,128]{1,0:T(8,128)S(1)} %collective-permute-done.refs_1_, ...), custom_call_target="tpu_custom_call", output_to_operand_aliasing={{2}: (7, {}), {3}: (8, {})} | custom-call | flops 2000000000 | bytes 2891776 | tf_op jit(solution)/shard_map/pallas_call | solution.py:328
  29.6 3.9 %collective-permute-done.3.refs_2_.refs_3_.refs_4_ = bf16[1216,128]{1,0:T(8,128)(2,1)S(1)} collective-permute-done((bf16[1216,128]{1,0:T(8,128)(2,1)S(1)}, bf16[1216,128]{1,0:T(8,128)(2,1)S(1)}, u32[]{:S(2)}, u32[]{:S(2)}) %collective-permute-start.3) | collective-permute-done | bytes 311328 | tf_op jit(solution)/shard_map/ppermute | solution.py:475
  34.9 1.7 %shard_map.112 = (bf16[2,1024,512]{2,1,0:T(8,128)(2,1)S(1)}, f32[2,1024,128]{2,1,0:T(8,128)S(1)}, f32[1,128,128]{2,1,0:T(8,128)S(1)}) custom-call(f32[8,128]{1,0:T(8,128)S(1)} %copy-done.4, f32[8,128]{1,0:T(8,128)S(1)} %collective-permute-done.refs_1_, ...), custom_call_target="tpu_custom_call", output_to_operand_aliasing={{1}: (5, {}), {2}: (6, {})} | custom-call | flops 2000000000 | bytes 2269184 | tf_op jit(solution)/shard_map/pallas_call | solution.py:328
  37.0 2.3 %shard_map.113 = (bf16[2,1024,512]{2,1,0:T(8,128)(2,1)S(1)}, bf16[2,1024,256]{2,1,0:T(8,128)(2,1)S(1)}, f32[2,1024,128]{2,1,0:T(8,128)S(1)}, f32[1,128,128]{2,1,0:T(8,128)S(1)}) custom-call(f32[8,128]{1,0:T(8,128)S(1)} %copy-done.4, f32[8,128]{1,0:T(8,128)S(1)} %collective-permute-done.refs_1_, ...), custom_call_target="tpu_custom_call", output_to_operand_aliasing={{2}: (7, {}), {3}: (8, {})} | custom-call | flops 2000000000 | bytes 2891776 | tf_op jit(solution)/shard_map/pallas_call | solution.py:328
  40.4 2.7 %shard_map.114 = (bf16[2,1024,512]{2,1,0:T(8,128)(2,1)S(1)}, bf16[2,1024,256]{2,1,0:T(8,128)(2,1)S(1)}, f32[512,128]{1,0:T(8,128)S(1)}, f32[512,128]{1,0:T(8,128...) custom-call(f32[8,128]{1,0:T(8,128)S(1)} %copy-done.4, ...), custom_call_target="tpu_custom_call", output_to_operand_aliasing={{4}: (5, {}), {5}: (6, {})} | custom-call | flops 2000000000 | bytes 2285568 | tf_op jit(solution)/shard_map/pallas_call | solution.py:328
  43.2 1.5 %collective-permute-done.9.other_ref = f32[512,128]{1,0:T(8,128)S(1)} collective-permute-done((f32[512,128]{1,0:T(8,128)S(1)}, f32[512,128]{1,0:T(8,128)S(1)}, u32[]{:S(2)}, u32[]{:S(2)}) %collective-permute-start.9) | collective-permute-done | bytes 262176 | tf_op jit(solution)/shard_map/ppermute | solution.py:490
  48.7 3.4 %collective-permute-done.10.refs_2_ = bf16[640,128]{1,0:T(8,128)(2,1)S(1)} collective-permute-done((bf16[640,128]{1,0:T(8,128)(2,1)S(1)}, bf16[640,128]{1,0:T(8,128)(2,1)S(1)}, u32[]{:S(2)}, u32[]{:S(2)}) %collective-permute-start.10) | collective-permute-done | bytes 163872 | tf_op jit(solution)/shard_map/ppermute | solution.py:472
  52.1 1.5 %collective-permute-start.11 = (bf16[640,128]{1,0:T(8,128)(2,1)S(1)}, bf16[640,128]{1,0:T(8,128)(2,1)S(1)}, u32[]{:S(2)}, u32[]{:S(2)}) collective-permute-start(bf16[640,128]{1,0:T(8,128)(2,1)S(1)} %collective-permute-done.10.refs_2_), channel_id=1, source_target_pairs={{0,4},{1,3},{4,8},{5,1},{8,12},{9,5},{12,14},{13,9},{14,10},{15,13... | collective-permute-start | bytes 491528 | tf_op jit(solution)/shard_map/ppermute | solution.py:475
  56.7 2.2 %collective-permute-done.11.refs_2_ = bf16[640,128]{1,0:T(8,128)(2,1)S(1)} collective-permute-done((bf16[640,128]{1,0:T(8,128)(2,1)S(1)}, bf16[640,128]{1,0:T(8,128)(2,1)S(1)}, u32[]{:S(2)}, u32[]{:S(2)}) %collective-permute-start.11) | collective-permute-done | bytes 163872 | tf_op jit(solution)/shard_map/ppermute | solution.py:475
  63.5 1.8 %collective-permute-done.12.refs_2_ = bf16[640,128]{1,0:T(8,128)(2,1)S(1)} collective-permute-done((bf16[640,128]{1,0:T(8,128)(2,1)S(1)}, bf16[640,128]{1,0:T(8,128)(2,1)S(1)}, u32[]{:S(2)}, u32[]{:S(2)}) %collective-permute-start.12) | collective-permute-done | bytes 163872 | tf_op jit(solution)/shard_map/ppermute | solution.py:475
  68.4 2.3 %collective-permute-done.13.refs_2_ = bf16[640,128]{1,0:T(8,128)(2,1)S(1)} collective-permute-done((bf16[640,128]{1,0:T(8,128)(2,1)S(1)}, bf16[640,128]{1,0:T(8,128)(2,1)S(1)}, u32[]{:S(2)}, u32[]{:S(2)}) %collective-permute-start.13) | collective-permute-done | bytes 163872 | tf_op jit(solution)/shard_map/ppermute | solution.py:475
  70.7 1.8 %shard_map.125 = (f32[512,128]{1,0:T(8,128)S(1)}, f32[512,128]{1,0:T(8,128)S(1)}, f32[2,1024,128]{2,1,0:T(8,128)S(1)}, f32[1,128,128]{2,1,0:T(8,128)S(1)}) custom-call(f32[8,128]{1,0:T(8,128)S(1)} %copy-done.4, f32[8,128]{1,0:T(8,128)S(1)} %collective-permute-done.refs_1_, ...), custom_call_target="tpu_custom_call", output_to_operand_aliasing={{2}: (5, {}), {3}: (6, {})} | custom-call | flops 1000000000 | bytes 4431872 | tf_op jit(solution)/shard_map/pallas_call | solution.py:328
  72.6 1.5 %collective-permute-done.17.other_ref = f32[512,128]{1,0:T(8,128)S(1)} collective-permute-done((f32[512,128]{1,0:T(8,128)S(1)}, f32[512,128]{1,0:T(8,128)S(1)}, u32[]{:S(2)}, u32[]{:S(2)}) %collective-permute-start.17) | collective-permute-done | bytes 262176 | tf_op jit(solution)/shard_map/ppermute | solution.py:494
  (49 shorter events, 21.4 us)
Async XLA Ops:
  0.6 7.1 %collective-permute-start.5 = (bf16[64,1024]{1,0:T(8,128)(2,1)}, bf16[64,1024]{1,0:T(8,128)(2,1)S(1)}, u32[]{:S(2)}, u32[]{:S(2)}) collective-permute-start(bf16[64,1024]{1,0:T(8,128)(2,1)} %coords_ref.1), channel_id=1, source_target_pairs={{0,1},{1,0},{2,3},{3,2},{4,5},{5,4},{6,7},{7,6},{8,9},{9,8},{10,11... | collective-permute-start | bytes 393224 | tf_op jit(solution)/shard_map/ppermute | solution.py:394
  3.4 9.5 %collective-permute-start.1 = (bf16[1216,128]{1,0:T(8,128)(2,1)}, bf16[1216,128]{1,0:T(8,128)(2,1)S(1)}, u32[]{:S(2)}, u32[]{:S(2)}) collective-permute-start(bf16[1216,128]{1,0:T(8,128)(2,1)} %get-tuple-element.53.refs_2_.refs_3_), channel_id=1, source_target_pairs={{0,4},{1,3},{4,8},{5,1},{8,12},{9,5},{12,14},{13,9},{14,10},{15,13... | collective-permute-start | bytes 933896 | tf_op jit(solution)/shard_map/ppermute | solution.py:472
  6.0 1.7 %collective-permute-start = (f32[8,128]{1,0:T(8,128)}, f32[8,128]{1,0:T(8,128)S(1)}, u32[]{:S(2)}, u32[]{:S(2)}) collective-permute-start(f32[8,128]{1,0:T(8,128)} %get-tuple-element.52.refs_0_), channel_id=1, source_target_pairs={{0,1},{1,0},{2,3},{3,2},{4,5},{5,4},{6,7},{7,6},{8,9},{9,8},{10,11... | collective-permute-start | bytes 12296 | tf_op jit(solution)/shard_map/ppermute | solution.py:393
  6.2 10.8 %collective-permute-start.6 = (bf16[1216,128]{1,0:T(8,128)(2,1)}, bf16[1216,128]{1,0:T(8,128)(2,1)S(1)}, u32[]{:S(2)}, u32[]{:S(2)}) collective-permute-start(bf16[1216,128]{1,0:T(8,128)(2,1)} %get-tuple-element.53.refs_2_.refs_3_), channel_id=1, source_target_pairs={{0,2},{1,5},{4,0},{5,9},{8,4},{9,13},{12,8},{13,15},{14,12},{15,11... | collective-permute-start | bytes 933896 | tf_op jit(solution)/shard_map/ppermute | solution.py:472
  8.5 1.0 %copy-start.5 = (bf16[1216,128]{1,0:T(8,128)(2,1)S(1)}, bf16[1216,128]{1,0:T(8,128)(2,1)}, u32[]{:S(2)}) copy-start(bf16[1216,128]{1,0:T(8,128)(2,1)} %get-tuple-element.53.refs_2_.refs_3_) | copy-start | bytes 933892
  9.4 5.9 %copy-start.4 = (f32[8,128]{1,0:T(8,128)S(1)}, f32[8,128]{1,0:T(8,128)}, u32[]{:S(2)}) copy-start(f32[8,128]{1,0:T(8,128)} %get-tuple-element.52.refs_0_) | copy-start | bytes 12292
  13.0 10.3 %collective-permute-start.2 = (bf16[1216,128]{1,0:T(8,128)(2,1)S(1)}, bf16[1216,128]{1,0:T(8,128)(2,1)S(1)}, u32[]{:S(2)}, u32[]{:S(2)}) collective-permute-start(bf16[1216,128]{1,0:T(8,128)(2,1)S(1)} %collective-permute-done.1.refs_2_.refs_3_.refs_4_), channel_id=1, source_target_pairs={{0,4},{1,3},{4,8},{5,1},{8,12},{9,5},{12,14},{13,9},{14,10},{15,13... | collective-permute-start | bytes 933896 | tf_op jit(solution)/shard_map/ppermute | solution.py:475
  17.0 10.2 %collective-permute-start.7 = (bf16[1216,128]{1,0:T(8,128)(2,1)S(1)}, bf16[1216,128]{1,0:T(8,128)(2,1)S(1)}, u32[]{:S(2)}, u32[]{:S(2)}) collective-permute-start(bf16[1216,128]{1,0:T(8,128)(2,1)S(1)} %shard_map.107.refs_3_.refs_5_), channel_id=1, source_target_pairs={{0,2},{1,5},{4,0},{5,9},{8,4},{9,13},{12,8},{13,15},{14,12},{15,11... | collective-permute-start | bytes 933896 | tf_op jit(solution)/shard_map/ppermute | solution.py:480
  23.2 10.2 %collective-permute-start.3 = (bf16[1216,128]{1,0:T(8,128)(2,1)S(1)}, bf16[1216,128]{1,0:T(8,128)(2,1)S(1)}, u32[]{:S(2)}, u32[]{:S(2)}) collective-permute-start(bf16[1216,128]{1,0:T(8,128)(2,1)S(1)} %collective-permute-done.2.refs_2_.refs_3_.refs_4_), channel_id=1, source_target_pairs={{0,4},{1,3},{4,8},{5,1},{8,12},{9,5},{12,14},{13,9},{14,10},{15,13... | collective-permute-start | bytes 933896 | tf_op jit(solution)/shard_map/ppermute | solution.py:475
  27.2 9.8 %collective-permute-start.8 = (bf16[1216,128]{1,0:T(8,128)(2,1)S(1)}, bf16[1216,128]{1,0:T(8,128)(2,1)S(1)}, u32[]{:S(2)}, u32[]{:S(2)}) collective-permute-start(bf16[1216,128]{1,0:T(8,128)(2,1)S(1)} %shard_map.110.refs_3_.refs_5_), channel_id=1, source_target_pairs={{0,2},{1,5},{4,0},{5,9},{8,4},{9,13},{12,8},{13,15},{14,12},{15,11... | collective-permute-start | bytes 933896 | tf_op jit(solution)/shard_map/ppermute | solution.py:480
  33.5 6.9 %collective-permute-start.4 = (bf16[1216,128]{1,0:T(8,128)(2,1)S(1)}, bf16[1216,128]{1,0:T(8,128)(2,1)S(1)}, u32[]{:S(2)}, u32[]{:S(2)}) collective-permute-start(bf16[1216,128]{1,0:T(8,128)(2,1)S(1)} %collective-permute-done.3.refs_2_.refs_3_.refs_4_), channel_id=1, source_target_pairs={{0,4},{1,3},{4,8},{5,1},{8,12},{9,5},{12,14},{13,9},{14,10},{15,13... | collective-permute-start | bytes 933896 | tf_op jit(solution)/shard_map/ppermute | solution.py:475
  37.0 3.4 %copy-start.6 = (bf16[64,128]{1,0:T(8,128)(2,1)S(1)}, bf16[64,128]{1,0:T(8,128)(2,1)}, u32[]{:S(2)}) copy-start(bf16[64,128]{1,0:T(8,128)(2,1)} %refs_7_.1) | copy-start | bytes 49156
  40.4 4.3 %copy-start = (bf16[1024,128]{1,0:T(8,128)(2,1)S(1)}, bf16[1024,128]{1,0:T(8,128)(2,1)}, u32[]{:S(2)}) copy-start(bf16[1024,128]{1,0:T(8,128)(2,1)} %leaf_ref.3) | copy-start | bytes 786436
  40.4 4.3 %copy-start.1 = (bf16[256,128]{1,0:T(8,128)(2,1)S(1)}, bf16[256,128]{1,0:T(8,128)(2,1)}, u32[]{:S(2)}) copy-start(bf16[256,128]{1,0:T(8,128)(2,1)} %node_ref.3) | copy-start | bytes 196612
  40.4 4.3 %copy-start.2 = (bf16[128,128]{1,0:T(8,128)(2,1)S(1)}, bf16[128,128]{1,0:T(8,128)(2,1)}, u32[]{:S(2)}) copy-start(bf16[128,128]{1,0:T(8,128)(2,1)} %upper_ref.3) | copy-start | bytes 98308
  43.1 1.6 %collective-permute-start.9 = (f32[512,128]{1,0:T(8,128)S(1)}, f32[512,128]{1,0:T(8,128)S(1)}, u32[]{:S(2)}, u32[]{:S(2)}) collective-permute-start(f32[512,128]{1,0:T(8,128)S(1)} %get-tuple-element.70), channel_id=1, source_target_pairs={{0,1},{1,0},{2,3},{3,2},{4,5},{5,4},{6,7},{7,6},{8,9},{9,8},{10,11... | collective-permute-start | bytes 786440 | tf_op jit(solution)/shard_map/ppermute | solution.py:490
  45.6 6.5 %collective-permute-start.10 = (bf16[640,128]{1,0:T(8,128)(2,1)S(1)}, bf16[640,128]{1,0:T(8,128)(2,1)S(1)}, u32[]{:S(2)}, u32[]{:S(2)}) collective-permute-start(bf16[640,128]{1,0:T(8,128)(2,1)S(1)} %get-tuple-element.72.refs_2_), channel_id=1, source_target_pairs={{0,4},{1,3},{4,8},{5,1},{8,12},{9,5},{12,14},{13,9},{14,10},{15,13... | collective-permute-start | bytes 491528 | tf_op jit(solution)/shard_map/ppermute | solution.py:472
  47.0 7.6 %collective-permute-start.14 = (bf16[640,128]{1,0:T(8,128)(2,1)S(1)}, bf16[640,128]{1,0:T(8,128)(2,1)S(1)}, u32[]{:S(2)}, u32[]{:S(2)}) collective-permute-start(bf16[640,128]{1,0:T(8,128)(2,1)S(1)} %get-tuple-element.72.refs_2_), channel_id=1, source_target_pairs={{0,2},{1,5},{4,0},{5,9},{8,4},{9,13},{12,8},{13,15},{14,12},{15,11... | collective-permute-start | bytes 491528 | tf_op jit(solution)/shard_map/ppermute | solution.py:472
  52.1 6.8 %collective-permute-start.11 = (bf16[640,128]{1,0:T(8,128)(2,1)S(1)}, bf16[640,128]{1,0:T(8,128)(2,1)S(1)}, u32[]{:S(2)}, u32[]{:S(2)}) collective-permute-start(bf16[640,128]{1,0:T(8,128)(2,1)S(1)} %collective-permute-done.10.refs_2_), channel_id=1, source_target_pairs={{0,4},{1,3},{4,8},{5,1},{8,12},{9,5},{12,14},{13,9},{14,10},{15,13... | collective-permute-start | bytes 491528 | tf_op jit(solution)/shard_map/ppermute | solution.py:475
  54.7 6.4 %collective-permute-start.15 = (bf16[640,128]{1,0:T(8,128)(2,1)S(1)}, bf16[640,128]{1,0:T(8,128)(2,1)S(1)}, u32[]{:S(2)}, u32[]{:S(2)}) collective-permute-start(bf16[640,128]{1,0:T(8,128)(2,1)S(1)} %shard_map.118.refs_3_), channel_id=1, source_target_pairs={{0,2},{1,5},{4,0},{5,9},{8,4},{9,13},{12,8},{13,15},{14,12},{15,11... | collective-permute-start | bytes 491528 | tf_op jit(solution)/shard_map/ppermute | solution.py:480
  58.9 6.5 %collective-permute-start.12 = (bf16[640,128]{1,0:T(8,128)(2,1)S(1)}, bf16[640,128]{1,0:T(8,128)(2,1)S(1)}, u32[]{:S(2)}, u32[]{:S(2)}) collective-permute-start(bf16[640,128]{1,0:T(8,128)(2,1)S(1)} %collective-permute-done.11.refs_2_), channel_id=1, source_target_pairs={{0,4},{1,3},{4,8},{5,1},{8,12},{9,5},{12,14},{13,9},{14,10},{15,13... | collective-permute-start | bytes 491528 | tf_op jit(solution)/shard_map/ppermute | solution.py:475
  61.1 5.8 %collective-permute-start.16 = (bf16[640,128]{1,0:T(8,128)(2,1)S(1)}, bf16[640,128]{1,0:T(8,128)(2,1)S(1)}, u32[]{:S(2)}, u32[]{:S(2)}) collective-permute-start(bf16[640,128]{1,0:T(8,128)(2,1)S(1)} %shard_map.121.refs_3_), channel_id=1, source_target_pairs={{0,2},{1,5},{4,0},{5,9},{8,4},{9,13},{12,8},{13,15},{14,12},{15,11... | collective-permute-start | bytes 491528 | tf_op jit(solution)/shard_map/ppermute | solution.py:480
  65.4 5.3 %collective-permute-start.13 = (bf16[640,128]{1,0:T(8,128)(2,1)S(1)}, bf16[640,128]{1,0:T(8,128)(2,1)S(1)}, u32[]{:S(2)}, u32[]{:S(2)}) collective-permute-start(bf16[640,128]{1,0:T(8,128)(2,1)S(1)} %collective-permute-done.12.refs_2_), channel_id=1, source_target_pairs={{0,4},{1,3},{4,8},{5,1},{8,12},{9,5},{12,14},{13,9},{14,10},{15,13... | collective-permute-start | bytes 491528 | tf_op jit(solution)/shard_map/ppermute | solution.py:475
  72.5 1.6 %collective-permute-start.17 = (f32[512,128]{1,0:T(8,128)S(1)}, f32[512,128]{1,0:T(8,128)S(1)}, u32[]{:S(2)}, u32[]{:S(2)}) collective-permute-start(f32[512,128]{1,0:T(8,128)S(1)} %get-tuple-element.101), channel_id=1, source_target_pairs={{0,1},{1,0},{2,3},{3,2},{4,5},{5,4},{6,7},{7,6},{8,9},{9,8},{10,11... | collective-permute-start | bytes 786440 | tf_op jit(solution)/shard_map/ppermute | solution.py:494
  (1 other events, 0.7 us)

commit v10 on v9

--- a/solution.py
+++ b/solution.py
@@ -117,19 +117,29 @@
     node_ref,
     upper_ref,
     message_ref,
+    local_ref,
     table_ref,
 ):
     dim, local = coords_ref.shape
     half = local // LEAVES
     charges = [charges_ref[:, 0:half], charges_ref[:, half:]]
-    message_ref[0:half, :] = jnp.concatenate(charges, axis=0).astype(f32).T.astype(bf16)
-    message_ref[half : half + LANES, :] = skeleton_rows(charges, leaf_ref, node_ref, upper_ref)
-    place = half + LANES
+    sent = [
+        jnp.concatenate(charges, axis=0).astype(f32).T.astype(bf16),
+        skeleton_rows(charges, leaf_ref, node_ref, upper_ref),
+        points_ref[...],
+    ]
+    place = 0
+    for part in sent:
+        rows = slice(place, place + part.shape[0])
+        message_ref[rows, :] = part
+        local_ref[rows, :] = part
+        place += part.shape[0]
     for block in range(local // LANES):
-        message_ref[place : place + dim, :] = coords_ref[:, block * LANES : (block + 1) * LANES]
+        local_ref[place : place + dim, :] = coords_ref[:, block * LANES : (block + 1) * LANES]
         place += dim
-    message_ref[place : place + dim, :] = points_ref[...]
-    table_ref[...] = count_rows(near_ref, far_ref)
+    table = count_rows(near_ref, far_ref)
+    table_ref[...] = table
+    local_ref[place : place + 16, :] = jnp.concatenate([table, table], axis=0).astype(bf16)
 
 
 def joined_kernel(mine_ref, other_ref, leaf_ref, node_ref, upper_ref, out_ref, message_ref):
@@ -150,53 +160,63 @@
 
 
 def stage_kernel(stage, *refs):
-    ring, spots, far_of, n_sub, dim, points, first, last, mode = stage
+    ring, near_spots, far_spots, n_sub, dim, points, begins, first, last, mode = stage
     refs = list(refs)
     use, keep = mode == "use", mode == "keep"
-    table_refs = refs.pop(0), refs.pop(0)
-    place_refs = [] if use else [refs.pop(0) for _ in spots]
-    charge_refs = [refs.pop(0) for _ in spots]
-    near_kept_ref = far_kept_ref = targets_ref = None
-    has_far = bool(far_of)
+    spots = sorted(set(near_spots) | set(far_spots))
+    makes = not use
+    table_refs = [refs.pop(0) for _ in range(1 if begins else CORES)]
+    if begins:
+        local_ref = refs.pop(0)
+        charge_refs = skeleton_refs = {spots[0]: local_ref}
+    else:
+        place_refs = {spot: refs.pop(0) for spot in near_spots} if makes else {}
+        skeleton_refs = {spot: refs.pop(0) for spot in far_spots} if makes else {}
+        charge_refs = {spot: refs.pop(0) for spot in spots}
+    kept_refs = {}
+    far_kept_ref = None
     if use:
-        near_kept_ref = refs.pop(0)
-        far_kept_ref = refs.pop(0) if has_far else None
-    elif first:
+        kept_refs = {spot: refs.pop(0) for spot in near_spots}
+        far_kept_ref = refs.pop(0) if far_spots else None
+    if begins:
         sibling_ref = refs.pop(0)
-    else:
+    elif makes:
         targets_ref = refs.pop(0)
     if not first:
         refs.pop(0), refs.pop(0)
-    upper_points_ref = refs.pop(0) if last and not use else None
-    if first and not use:
-        targets_ref = refs.pop(0)
+    upper_points_ref = refs.pop(0) if last and makes else None
+    if begins:
+        targets_ref, table_ref = refs.pop(0), refs.pop(0)
     if keep:
-        near_kept_ref = refs.pop(0)
-        far_kept_ref = refs.pop(0) if has_far else None
+        kept_refs = {spot: refs.pop(0) for spot in near_spots}
+        far_kept_ref = refs.pop(0) if far_spots else None
     if last:
         half_refs = refs.pop(0), refs.pop(0)
     total_ref, sums_ref, far_charges_ref, charges_ref = refs[:4]
-    if not use:
+    if makes:
         near_ref, far_ref = refs[4:]
 
-    coords_at = points + LANES
+    skeletons_at = points + LANES
     blocks = points // LANES
-    skeletons_at = coords_at + LEAVES * blocks * dim
     low_half = in_low_half((LANES, LANES))
     lane = lax.broadcasted_iota(i32, (8, LANES), 1)
 
     def span_of(leaf):
         return slice(leaf * points, (leaf + 1) * points)
 
-    def points_of(leaf):
-        begin = coords_at + leaf * blocks * dim
-        ref = place_refs[-1]
-        own = [ref[begin + block * dim : begin + (block + 1) * dim, :] for block in range(blocks)]
-        return jnp.concatenate(own, axis=1)
-
-    if first and not use:
+    def points_of(spot, leaf):
+        if not begins:
+            return place_refs[spot][:, span_of(leaf)]
+        begin = skeletons_at + dim + leaf * blocks * dim
+        rows = [begin + block * dim for block in range(blocks)]
+        return jnp.concatenate([local_ref[row : row + dim, :] for row in rows], axis=1)
+
+    if begins:
+        begin = skeletons_at + dim + LEAVES * blocks * dim
+        table_ref[...] = local_ref[begin : begin + 16, :].astype(f32)[0:8]
+        table_refs = [table_ref] + table_refs
         for leaf in range(LEAVES):
-            targets_ref[0, span_of(leaf), :] = target_rows(points_of(leaf))
+            targets_ref[0, span_of(leaf), :] = target_rows(points_of(0, leaf))
             targets_ref[1, span_of(leaf), :] = target_rows(sibling_ref[:, span_of(leaf)])
     if first:
         total_ref[...] = jnp.zeros_like(total_ref)
@@ -217,48 +237,51 @@
             kept_ref[...] = made
         return made
 
-    device = device_of(ring, spots[-1])
-
-    def near_part(turn, core, leaf):
+    devices = {spot: device_of(ring, spot) for spot in spots}
+
+    def near_part(turn, spot, core, leaf):
+        at = near_spots.index(spot)
         table = table_of(core)
-        named = [picked(table, device * LEAVES + which)[0:LEAVES] for which in range(LEAVES)]
+        named = [
+            picked(table, devices[spot] * LEAVES + which)[0:LEAVES] for which in range(LEAVES)
+        ]
         if leaf is None:
             second = jnp.where(jnp.sum(named[1], axis=0, keepdims=True) > 0.0, 1.0, 0.0)
         else:
             second = jnp.full((1, 1), float(leaf), f32)
         times = named[0] * (1.0 - second) + named[1] * second
-        if not use:
-            chosen = points_of(0) * (1.0 - second).astype(bf16) + points_of(1) * second.astype(bf16)
-            put_sources(near_ref, chosen)
+        if makes:
+            low, high = (points_of(spot, which) for which in range(LEAVES))
+            chosen = low * (1.0 - second).astype(bf16) + high * second.astype(bf16)
+            put_sources(near_ref.at[at], chosen)
         half = jnp.where(lane[0:1] < LANES // LEAVES, 1.0 - second, second).astype(bf16)
-        charges_ref[...] = charge_refs[-1][0:points, :] * half
-        kept = None if near_kept_ref is None else near_kept_ref.at[turn]
-        added = matmul(values(core, None if use else near_ref, kept), charges_ref[...])
+        charges_ref[at] = charge_refs[spot][0:points, :] * half
+        kept = kept_refs[spot].at[turn] if kept_refs else None
+        added = matmul(values(core, near_ref.at[at] if makes else None, kept), charges_ref[at])
         return [times[own : own + 1] * added[span_of(own)] for own in range(LEAVES)]
 
     weights = []
     skeletons = []
-    for at in far_of:
-        rows = charge_refs[at][points : points + LANES, :].astype(f32)
-        node = device_of(ring, spots[at])
-        weights.append((jnp.where(low_half, rows, swapped(rows)), node))
-        sums_ref[node // BRANCH] += rows
-        if not use:
-            skeletons.append(place_refs[at][skeletons_at : skeletons_at + dim, :])
+    for spot in far_spots:
+        rows = charge_refs[spot][points : points + LANES, :].astype(f32)
+        weights.append((jnp.where(low_half, rows, swapped(rows)), devices[spot]))
+        sums_ref[devices[spot] // BRANCH] += rows
+        if makes:
+            skeletons.append(skeleton_refs[spot][skeletons_at : skeletons_at + dim, :])
     if last:
         for sub in range(n_sub):
             rows = sums_ref[sub]
             weights.append((jnp.where(low_half, swapped(rows), rows), len(ring) * CORES + sub))
-            if not use:
+            if makes:
                 skeletons.append(upper_points_ref[:, sub * LANES : (sub + 1) * LANES])
-    if has_far and not use:
+    if far_spots and makes:
         put_sources(far_ref, jnp.concatenate(skeletons, axis=1))
 
     def far_part(core):
         table = table_of(core)
         kernel = values(
             core,
-            None if use else far_ref,
+            far_ref if makes else None,
             None if far_kept_ref is None else far_kept_ref.at[core],
         )
         added = []
@@ -280,13 +303,13 @@
 
     if first:
         for leaf in range(LEAVES):
-            add(0, [near_part(leaf, 0, leaf)])
-        add(1, [near_part(LEAVES, 1, None), far_part(1)])
+            add(0, [near_part(leaf, 0, 0, leaf)])
+        add(1, [near_part(LEAVES, 0, 1, None), far_part(1)])
     else:
 
         def step(core, carry):
-            parts = [near_part(core, core, None)]
-            add(core, parts + ([far_part(core)] if has_far else []))
+            parts = [near_part(core, spot, core, None) for spot in near_spots]
+            add(core, parts + ([far_part(core)] if far_spots else []))
             return carry
 
         lax.fori_loop(0, CORES, step, 0)
@@ -380,18 +403,20 @@
         return jax.ShapeDtypeStruct(extent, dtype)
 
     maps = [leaf_interp, node_interp, upper_interp]
-    message, table = call(
+    sibling_coords = to_sibling(coords)
+    coords_next = one_way(coords), other_way(coords)
+    message, own, table = call(
         message_kernel,
         [near_lists, far_lists, coords, charges, node_points] + maps,
         [
-            shape(points + LANES + LEAVES * points // LANES * dim + dim, LANES),
+            shape(points + LANES + dim, LANES),
+            shape(points + LANES + dim + LEAVES * points // LANES * dim + 16, LANES),
             shape(8, LANES, dtype=f32),
         ],
         streamed=range(2, 8),
         vmem_mib=60,
     )
-    tables = [table, to_sibling(table)]
-    sibling_coords = to_sibling(coords)
+    sibling_table = to_sibling(table)
 
     total_shape = shape(CORES, local, LANES, dtype=f32)
     sums_shape = shape(n_sub, LANES, LANES, dtype=f32)
@@ -402,96 +427,128 @@
     kept_bytes = 2 * points * (steps * local + CORES * LEAVES * (chips + n_sub) * LANES)
     keeping = kept_bytes <= KEPT_MIB * 2**20
 
-    def stage(spots, far_of, placed, charged, targets, carried, last, kept):
+    def stage(near_spots, far_spots, given, carried, last, mode, begins=False):
         first = not carried
-        mode = "use" if kept else "keep" if keeping else "make"
-        args = tables + ([] if kept else placed) + charged
-        if kept:
-            args += kept
+        makes = mode != "use"
+        spots = sorted(set(near_spots) | set(far_spots))
+        if begins:
+            args = [sibling_table, own, sibling_coords]
         else:
-            args += [sibling_coords] if first else [targets]
+            args = list(given["tables"])
+            if makes:
+                args += [given["places"][spot] for spot in near_spots]
+                args += [given["skeletons"][spot] for spot in far_spots]
+            args += [given["charges"][spot] for spot in spots]
+            if makes:
+                args += [given["targets"]]
+            else:
+                args += [given["near"][spot] for spot in near_spots]
+                args += [given["far"][far_spots]] if far_spots else []
         carried_at = len(args)
         args += carried
-        args += [upper_points] if last and not kept else []
-        far_width = LANES * (len(far_of) + (n_sub if last else 0))
+        args += [upper_points] if last and makes else []
+        far_width = max(LANES, LANES * (len(far_spots) + (n_sub if last else 0)))
         scratch = [
-            pltpu.VMEM((LEAVES, max(far_width, LANES), LANES), bf16),
-            pltpu.VMEM((points, LANES), bf16),
+            pltpu.VMEM((LEAVES, far_width, LANES), bf16),
+            pltpu.VMEM((len(near_spots), points, LANES), bf16),
         ]
-        if not kept:
+        if makes:
             scratch += [
-                pltpu.VMEM((LANES, points), bf16),
-                pltpu.VMEM((LANES, max(far_width, LANES)), bf16),
+                pltpu.VMEM((len(near_spots), LANES, points), bf16),
+                pltpu.VMEM((LANES, far_width), bf16),
             ]
-        outs = [targets_shape] if first and not kept else []
-        kept_at = len(outs)
+        names, outs = [], []
+        if begins:
+            names += ["targets", "table"]
+            outs += [targets_shape, shape(8, LANES, dtype=f32)]
         if mode == "keep":
-            outs.append(shape(LEAVES + 1 if first else CORES, local, points))
-            outs += [shape(CORES, local, far_width)] if far_of else []
-        kept_to = len(outs)
-        outs += [half_shape, half_shape] if last else []
+            names += [("near", spot) for spot in near_spots]
+            outs += [shape(LEAVES + 1 if first else CORES, local, points) for _ in near_spots]
+            names += [("far", far_spots)] if far_spots else []
+            outs += [shape(CORES, local, far_width)] if far_spots else []
+        if last:
+            names += ["mine", "other"]
+            outs += [half_shape, half_shape]
         aliases = {carried_at + k: len(outs) + k for k in range(len(carried))}
+        names += ["total", "sums"]
         outs += [total_shape, sums_shape]
-        static = (ring, spots, far_of, n_sub, dim, points, first, last, mode)
+        static = (
+            ring, near_spots, far_spots, n_sub, dim, points, begins, first, last, mode
+        )
         results = call(
             functools.partial(stage_kernel, static),
             args,
             outs,
             scratch=scratch,
             aliases=aliases,
-            flops=(1 if kept else 2) * 10**9,
+            flops=len(near_spots) * (2 if makes else 1) * 10**9,
         )
-        targets = results[0] if first and not kept else targets
-        return targets, list(results[kept_at:kept_to]), list(results[kept_to : kept_to + 2])
-
-    def around(message, placed, targets, kept):
-        met = []
-        made = []
-        carried = []
-
-        def arrived(message):
-            nonlocal targets, carried
-            met.append(message)
-            spot = len(met) - 1
-            last = spot == chips - 1
-            spots = (spot - 1, spot) if spot % 2 == 0 and spot > 0 else (spot,)
-            far_of = () if spot % 2 == 1 and not last else tuple(range(len(spots)))
-            charged = [met[at] for at in spots]
-            targets, values, carried = stage(
-                spots,
-                far_of,
-                [placed[at] for at in spots] if placed else charged,
-                charged,
-                targets,
-                carried,
-                last,
-                kept[spot] if kept else [],
-            )
-            made.append(values)
-
-        one, other = one_way(message), other_way(message)
-        arrived(message)
-        for hop in range(1, chips // 2):
-            one_next = one_way(one)
-            arrived(one)
-            other_next = None
-            if hop < chips // 2 - 1:
-                other = gated(other, carried[1])
-                other_next = other_way(other)
-            arrived(other)
-            one, other = one_next, other_next
-        arrived(one)
-        placed = met if placed is None else placed
-        return placed, targets, made, carried
-
-    placed, targets, kept, (mine, other) = around(message, None, None, None)
+        return dict(zip(names, results))
+
+    def far_spots_of(spot):
+        return (spot - 1, spot) if spot % 2 == 0 and spot > 0 else (spot,)
+
+    mode = "keep" if keeping else "make"
+    given = {"near": {}, "far": {}, "places": {0: coords}, "skeletons": {0: message}}
+    given["charges"] = given["skeletons"]
+
+    def keep_results(results):
+        for name, value in results.items():
+            if isinstance(name, tuple):
+                given[name[0]][name[1]] = value
+        return [results["total"], results["sums"]]
+
+    sent = one_way(message), other_way(message)
+    results = stage((0,), (0,), given, [], False, mode, begins=True)
+    given["targets"], given["tables"] = results["targets"], [results["table"], sibling_table]
+    carried = keep_results(results)
+    for hop in range(1, chips // 2):
+        final = hop == chips // 2 - 1
+        spots = (2 * hop - 1, 2 * hop)
+        for at, spot in enumerate(spots):
+            given["places"][spot] = coords_next[at]
+            given["skeletons"][spot] = sent[at]
+        coords_next = one_way(coords_next[0]), None if final else other_way(coords_next[1])
+        sent = one_way(sent[0]), None if final else other_way(sent[1])
+        carried = keep_results(stage(spots, spots, given, carried, False, mode))
+    across = (chips - 1,)
+    given["places"][across[0]], given["skeletons"][across[0]] = coords_next[0], sent[0]
+    results = stage(across, across, given, carried, True, mode)
+    keep_results(results)
     first, message = call(
         joined_kernel,
-        [mine, to_sibling(other)] + maps,
+        [results["mine"], to_sibling(results["other"])] + maps,
         [shape(columns, local), shape(points + LANES, LANES)],
     )
-    *_, (mine, other) = around(message, placed, targets, kept if keeping else None)
-    (second,) = call(added_kernel, [mine, to_sibling(other)], [shape(columns, local)])
+
+    mode = "use" if keeping else "make"
+    given["charges"] = {}
+    carried = []
+
+    def arrived(spot, message):
+        nonlocal carried
+        given["charges"][spot] = message
+        last = spot == chips - 1
+        far_spots = () if spot % 2 == 1 and not last else far_spots_of(spot)
+        results = stage((spot,), far_spots, given, carried, last, mode)
+        carried = [results["total"], results["sums"]]
+        return results
+
+    one, other = one_way(message), other_way(message)
+    arrived(0, message)
+    for hop in range(1, chips // 2):
+        one_next = one_way(one)
+        arrived(2 * hop - 1, one)
+        other_next = None
+        if hop < chips // 2 - 1:
+            other = gated(other, carried[1])
+            other_next = other_way(other)
+        arrived(2 * hop, other)
+        one, other = one_next, other_next
+    results = arrived(chips - 1, one)
+    (second,) = call(
+        added_kernel, [results["mine"], to_sibling(results["other"])], [shape(columns, local)]
+    )
     return (first, second)
 
 

time: 75.1 us -> 69 us (0.919)
  waiting for transfers between devices: 23.5 us -> 13.2 us
  starting transfers between devices: 17.8 us -> 24.3 us
  Pallas kernels: 31.1 us -> 29.4 us
    ppermute x17 -> x24, waiting for transfers between devices: 23.5 us -> 13.2 us  [the longest x3 5.76 us: on_device(): one_next = one_way(one)]
    ppermute x17 -> x24, starting transfers between devices: 17.3 us -> 24.3 us  [the longest x5 5.69 us: on_device(): sent = (one_way(sent[0]), None if final else other_way(sent[1]))]
    pallas_call x19 -> x16, Pallas kernels: 31 us -> 29.4 us  [call(): pl.pallas_call(body, grid=(1,), out_shape=out_shapes, in_specs=specs, out...]
    unnamed x14 -> x10, local copies, waits for them, and re-layouts: 1.67 us -> 0.98 us
  transfers between devices with their start and end apart: 18 -> 25, of which waited for: 13 -> 8; matrix products, arithmetic and copies ran while one was open for 0% -> 0% of each run, Pallas kernels for 33% -> 34%
where the time goes in v10:
time: 69 us; the launch traced here: 68.8 us
  Pallas kernels  29.4 us (43%)
  starting transfers between devices  24.3 us (35%)
  waiting for transfers between devices  13.2 us (19%)
  local copies, waits for them, and re-layouts  0.98 us (1%)
  between operations  0.82 us (1%)
    pallas_call x16, Pallas kernels, call(): pl.pallas_call(body, grid=(1,), out_shape=out_shapes, in_specs=specs, out...  29.4 us
    ppermute x3, waiting for transfers between devices, on_device(): one_next = one_way(one)  5.76 us
    ppermute x5, starting transfers between devices, on_device(): sent = (one_way(sent[0]), None if final else other_way(sent[1]))  5.69 us
    ppermute x2, waiting for transfers between devices, on_device(): one, other = (one_way(message), other_way(message))  3.74 us
    ppermute x3, starting transfers between devices, on_device(): one_way(coords_next[0])  3.66 us
    ppermute x2, starting transfers between devices, on_device(): coords_next = (one_way(coords), other_way(coords))  3.14 us
    ppermute x2, waiting for transfers between devices, on_device(): to_sibling(results['other'])  3.04 us
    ppermute x2, starting transfers between devices, on_device(): sent = (one_way(message), other_way(message))  2.99 us
  transfers between devices with their start and end apart: 25, of which 8 were waited for; matrix products, arithmetic and copies ran while one was open for 0% of the time, Pallas kernels for 34%

profile of v10, /device:TPU:0, one launch (start us, length us, event | category | flops | bytes accessed | tf_op | source)
XLA Modules:
  0.0 68.8 jit_solution(17267567745949021926)
XLA Ops:
  0.6 3.0 %collective-permute-start.10 = (bf16[64,1024]{1,0:T(8,128)(2,1)}, bf16[64,1024]{1,0:T(8,128)(2,1)S(1)}, u32[]{:S(2)}, u32[]{:S(2)}) collective-permute-start(bf16[64,1024]{1,0:T(8,128)(2,1)} %coords_ref.1), channel_id=1, source_target_pairs={{0,2},{1,5},{4,0},{5,9},{8,4},{9,13},{12,8},{13,15},{14,12},{15,11... | collective-permute-start | bytes 393224 | tf_op jit(solution)/shard_map/ppermute | solution.py:407
  3.8 2.3 %shard_map.104 = (bf16[704,128]{1,0:T(8,128)(2,1)}, bf16[1232,128]{1,0:T(8,128)(2,1)}, f32[8,128]{1,0:T(8,128)}) custom-call(s32[2,16]{1,0:T(2,128)} %near_ref.1, s32[2,32]{1,0:T(2,128)} %far_ref.1, bf16[64,1024]{1,0:T(8,128)(2,1)} %coords_ref.1, bf16[64,1024]{1,0:T(8,128)(2,1)} %charges_ref.1, bf16[64,128]{1,0:T(8,128)(2,1)} %points_ref.1, ...), custom_call_target="tpu_custom_call" | custom-call | bytes 639360 | tf_op jit(solution)/shard_map/pallas_call | solution.py:351
  6.6 1.9 %collective-permute-start.13 = (bf16[704,128]{1,0:T(8,128)(2,1)}, bf16[704,128]{1,0:T(8,128)(2,1)S(1)}, u32[]{:S(2)}, u32[]{:S(2)}) collective-permute-start(bf16[704,128]{1,0:T(8,128)(2,1)} %get-tuple-element.51), channel_id=1, source_target_pairs={{0,2},{1,5},{4,0},{5,9},{8,4},{9,13},{12,8},{13,15},{14,12},{15,11... | collective-permute-start | bytes 540680 | tf_op jit(solution)/shard_map/ppermute | solution.py:501
  12.6 2.1 %shard_map.105 = (bf16[2,1024,128]{2,1,0:T(8,128)(2,1)S(1)}, f32[8,128]{1,0:T(8,128)S(1)}, bf16[3,1024,512]{2,1,0:T(8,128)(2,1)S(1)}, bf16[2,1024,128]{2,1,0:T(8...) custom-call(f32[8,128]{1,0:T(8,128)S(1)} %collective-permute-done.refs_0_.refs_1_, ...), custom_call_target="tpu_custom_call" | custom-call | flops 2000000000 | bytes 450560 | tf_op jit(solution)/shard_map/pallas_call | solution.py:351
  14.7 1.1 %collective-permute-start.14 = (bf16[704,128]{1,0:T(8,128)(2,1)S(1)}, bf16[704,128]{1,0:T(8,128)(2,1)S(1)}, u32[]{:S(2)}, u32[]{:S(2)}) collective-permute-start(bf16[704,128]{1,0:T(8,128)(2,1)S(1)} %collective-permute-done.13.refs_5_.refs_7_), channel_id=1, source_target_pairs={{0,2},{1,5},{4,0},{5,9},{8,4},{9,13},{12,8},{13,15},{14,12},{15,11... | collective-permute-start | bytes 540680 | tf_op jit(solution)/shard_map/ppermute | solution.py:512
  16.8 3.4 %shard_map.106 = (bf16[2,1024,512]{2,1,0:T(8,128)(2,1)S(1)}, bf16[2,1024,512]{2,1,0:T(8,128)(2,1)S(1)}, bf16[2,1024,256]{2,1,0:T(8,128)(2,1)S(1)}, f32[2,1024,128]{2,1,0:T(8,128)S(1)}, f32[1,128,128]{2,1,0:T(8,128)S(1)}) custom-call(f32[8,128]{1,0:T(8,128)S(1)} %get-tuple-element.50.refs_0_, ...), custom_call_target="tpu_custom_call", output_to_operand_aliasing={{3}: (9, {}), {4}: (10, {})} | custom-call | flops 4000000000 | bytes 2629632 | tf_op jit(solution)/shard_map/pallas_call | solution.py:351
  20.2 1.1 %collective-permute-start.12 = (bf16[64,1024]{1,0:T(8,128)(2,1)S(1)}, bf16[64,1024]{1,0:T(8,128)(2,1)S(1)}, u32[]{:S(2)}, u32[]{:S(2)}) collective-permute-start(bf16[64,1024]{1,0:T(8,128)(2,1)S(1)} %collective-permute-done.11.refs_3_), channel_id=1, source_target_pairs={{0,2},{1,5},{4,0},{5,9},{8,4},{9,13},{12,8},{13,15},{14,12},{15,11... | collective-permute-start | bytes 393224 | tf_op jit(solution)/shard_map/ppermute | solution.py:511
  24.3 3.4 %shard_map.107 = (bf16[2,1024,512]{2,1,0:T(8,128)(2,1)S(1)}, bf16[2,1024,512]{2,1,0:T(8,128)(2,1)S(1)}, bf16[2,1024,256]{2,1,0:T(8,128)(2,1)S(1)}, f32[2,1024,128]{2,1,0:T(8,128)S(1)}, f32[1,128,128]{2,1,0:T(8,128)S(1)}) custom-call(f32[8,128]{1,0:T(8,128)S(1)} %get-tuple-element.50.refs_0_, ...), custom_call_target="tpu_custom_call", output_to_operand_aliasing={{3}: (9, {}), {4}: (10, {})} | custom-call | flops 4000000000 | bytes 2629632 | tf_op jit(solution)/shard_map/pallas_call | solution.py:351
  27.7 1.6 %collective-permute-start.5 = (bf16[64,1024]{1,0:T(8,128)(2,1)S(1)}, bf16[64,1024]{1,0:T(8,128)(2,1)S(1)}, u32[]{:S(2)}, u32[]{:S(2)}) collective-permute-start(bf16[64,1024]{1,0:T(8,128)(2,1)S(1)} %collective-permute-done.4.refs_2_), channel_id=1, source_target_pairs={{0,4},{1,3},{4,8},{5,1},{8,12},{9,5},{12,14},{13,9},{14,10},{15,13... | collective-permute-start | bytes 393224 | tf_op jit(solution)/shard_map/ppermute | solution.py:511
  29.4 1.6 %collective-permute-start.9 = (bf16[704,128]{1,0:T(8,128)(2,1)S(1)}, bf16[704,128]{1,0:T(8,128)(2,1)S(1)}, u32[]{:S(2)}, u32[]{:S(2)}) collective-permute-start(bf16[704,128]{1,0:T(8,128)(2,1)S(1)} %collective-permute-done.8.refs_4_.refs_6_), channel_id=1, source_target_pairs={{0,4},{1,3},{4,8},{5,1},{8,12},{9,5},{12,14},{13,9},{14,10},{15,13... | collective-permute-start | bytes 540680 | tf_op jit(solution)/shard_map/ppermute | solution.py:512
  31.0 3.4 %shard_map.108 = (bf16[2,1024,512]{2,1,0:T(8,128)(2,1)S(1)}, bf16[2,1024,512]{2,1,0:T(8,128)(2,1)S(1)}, bf16[2,1024,256]{2,1,0:T(8,128)(2,1)S(1)}, f32[2,1024,128]{2,1,0:T(8,128)S(1)}, f32[1,128,128]{2,1,0:T(8,128)S(1)}) custom-call(f32[8,128]{1,0:T(8,128)S(1)} %get-tuple-element.50.refs_0_, ...), custom_call_target="tpu_custom_call", output_to_operand_aliasing={{3}: (9, {}), {4}: (10, {})} | custom-call | flops 4000000000 | bytes 2629632 | tf_op jit(solution)/shard_map/pallas_call | solution.py:351
  34.9 2.7 %shard_map.109 = (bf16[2,1024,512]{2,1,0:T(8,128)(2,1)S(1)}, bf16[2,1024,256]{2,1,0:T(8,128)(2,1)S(1)}, f32[512,128]{1,0:T(8,128)S(1)}, f32[512,128]{1,0:T(8,128...) custom-call(f32[8,128]{1,0:T(8,128)S(1)} %get-tuple-element.50.refs_, ...), custom_call_target="tpu_custom_call", output_to_operand_aliasing={{4}: (6, {}), {5}: (7, {})} | custom-call | flops 2000000000 | bytes 2154496 | tf_op jit(solution)/shard_map/pallas_call | solution.py:351
  37.6 1.5 %collective-permute-done.16.other_ref = f32[512,128]{1,0:T(8,128)S(1)} collective-permute-done((f32[512,128]{1,0:T(8,128)S(1)}, f32[512,128]{1,0:T(8,128)S(1)}, u32[]{:S(2)}, u32[]{:S(2)}) %collective-permute-start.16) | collective-permute-done | bytes 262176 | tf_op jit(solution)/shard_map/ppermute | solution.py:520
  40.1 1.6 %collective-permute-start.17 = (bf16[640,128]{1,0:T(8,128)(2,1)S(1)}, bf16[640,128]{1,0:T(8,128)(2,1)S(1)}, u32[]{:S(2)}, u32[]{:S(2)}) collective-permute-start(bf16[640,128]{1,0:T(8,128)(2,1)S(1)} %get-tuple-element.64.refs_2_), channel_id=1, source_target_pairs={{0,4},{1,3},{4,8},{5,1},{8,12},{9,5},{12,14},{13,9},{14,10},{15,13... | collective-permute-start | bytes 491528 | tf_op jit(solution)/shard_map/ppermute | solution.py:537
  43.2 3.7 %collective-permute-done.17.refs_2_ = bf16[640,128]{1,0:T(8,128)(2,1)S(1)} collective-permute-done((bf16[640,128]{1,0:T(8,128)(2,1)S(1)}, bf16[640,128]{1,0:T(8,128)(2,1)S(1)}, u32[]{:S(2)}, u32[]{:S(2)}) %collective-permute-start.17) | collective-permute-done | bytes 163872 | tf_op jit(solution)/shard_map/ppermute | solution.py:537
  50.1 1.5 %shard_map.114 = (f32[2,1024,128]{2,1,0:T(8,128)S(1)}, f32[1,128,128]{2,1,0:T(8,128)S(1)}) custom-call(f32[8,128]{1,0:T(8,128)S(1)} %get-tuple-element.50.refs_0_, f32[8,128]{1,0:T(8,128)S(1)} %collective-permute-done.refs_0_.refs_1_, bf16[640,128]{1,0:T(8,128)(2,1)S(1)} %collective-permute-done.17.refs_2_, ...), custom_call_target="tpu_custom_call", output_to_operand_aliasing={{0}: (6, {}), {1}: (7, {})} | custom-call | flops 1000000000 | bytes 4595712 | tf_op jit(solution)/shard_map/pallas_call | solution.py:351
  51.6 1.7 %collective-permute-done.18.refs_2_ = bf16[640,128]{1,0:T(8,128)(2,1)S(1)} collective-permute-done((bf16[640,128]{1,0:T(8,128)(2,1)S(1)}, bf16[640,128]{1,0:T(8,128)(2,1)S(1)}, u32[]{:S(2)}, u32[]{:S(2)}) %collective-permute-start.18) | collective-permute-done | bytes 163872 | tf_op jit(solution)/shard_map/ppermute | solution.py:540
  54.9 1.6 %collective-permute-start.23 = (bf16[640,128]{1,0:T(8,128)(2,1)S(1)}, bf16[640,128]{1,0:T(8,128)(2,1)S(1)}, u32[]{:S(2)}, u32[]{:S(2)}) collective-permute-start(bf16[640,128]{1,0:T(8,128)(2,1)S(1)} %shard_map.116.refs_3_), channel_id=1, source_target_pairs={{0,2},{1,5},{4,0},{5,9},{8,4},{9,13},{12,8},{13,15},{14,12},{15,11... | collective-permute-start | bytes 491528 | tf_op jit(solution)/shard_map/ppermute | solution.py:545
  56.5 1.5 %shard_map.117 = (f32[2,1024,128]{2,1,0:T(8,128)S(1)}, f32[1,128,128]{2,1,0:T(8,128)S(1)}) custom-call(f32[8,128]{1,0:T(8,128)S(1)} %get-tuple-element.50.refs_0_, f32[8,128]{1,0:T(8,128)S(1)} %collective-permute-done.refs_0_.refs_1_, bf16[640,128]{1,0:T(8,128)(2,1)S(1)} %collective-permute-done.18.refs_2_, ...), custom_call_target="tpu_custom_call", output_to_operand_aliasing={{0}: (6, {}), {1}: (7, {})} | custom-call | flops 1000000000 | bytes 4595712 | tf_op jit(solution)/shard_map/pallas_call | solution.py:351
  58.0 1.3 %collective-permute-done.19.refs_2_ = bf16[640,128]{1,0:T(8,128)(2,1)S(1)} collective-permute-done((bf16[640,128]{1,0:T(8,128)(2,1)S(1)}, bf16[640,128]{1,0:T(8,128)(2,1)S(1)}, u32[]{:S(2)}, u32[]{:S(2)}) %collective-permute-start.19) | collective-permute-done | bytes 163872 | tf_op jit(solution)/shard_map/ppermute | solution.py:540
  60.4 1.5 %shard_map.119 = (f32[2,1024,128]{2,1,0:T(8,128)S(1)}, f32[1,128,128]{2,1,0:T(8,128)S(1)}) custom-call(f32[8,128]{1,0:T(8,128)S(1)} %get-tuple-element.50.refs_0_, f32[8,128]{1,0:T(8,128)S(1)} %collective-permute-done.refs_0_.refs_1_, bf16[640,128]{1,0:T(8,128)(2,1)S(1)} %collective-permute-done.19.refs_2_, ...), custom_call_target="tpu_custom_call", output_to_operand_aliasing={{0}: (6, {}), {1}: (7, {})} | custom-call | flops 1000000000 | bytes 4595712 | tf_op jit(solution)/shard_map/pallas_call | solution.py:351
  61.9 2.8 %collective-permute-done.20.refs_2_ = bf16[640,128]{1,0:T(8,128)(2,1)S(1)} collective-permute-done((bf16[640,128]{1,0:T(8,128)(2,1)S(1)}, bf16[640,128]{1,0:T(8,128)(2,1)S(1)}, u32[]{:S(2)}, u32[]{:S(2)}) %collective-permute-start.20) | collective-permute-done | bytes 163872 | tf_op jit(solution)/shard_map/ppermute | solution.py:540
  64.6 1.8 %shard_map.120 = (f32[512,128]{1,0:T(8,128)S(1)}, f32[512,128]{1,0:T(8,128)S(1)}, f32[2,1024,128]{2,1,0:T(8,128)S(1)}, f32[1,128,128]{2,1,0:T(8,128)S(1)}) custom-call(f32[8,128]{1,0:T(8,128)S(1)} %get-tuple-element.50.refs_0_, f32[8,128]{1,0:T(8,128)S(1)} %collective-permute-done.refs_0_.refs_1_, ...), custom_call_target="tpu_custom_call", output_to_operand_aliasing={{2}: (5, {}), {3}: (6, {})} | custom-call | flops 1000000000 | bytes 4431872 | tf_op jit(solution)/shard_map/pallas_call | solution.py:351
  66.5 1.5 %collective-permute-done.24.other_ref = f32[512,128]{1,0:T(8,128)S(1)} collective-permute-done((f32[512,128]{1,0:T(8,128)S(1)}, f32[512,128]{1,0:T(8,128)S(1)}, u32[]{:S(2)}, u32[]{:S(2)}) %collective-permute-start.24) | collective-permute-done | bytes 262176 | tf_op jit(solution)/shard_map/ppermute | solution.py:550
  (54 shorter events, 18.4 us)
Async XLA Ops:
  0.6 9.0 %collective-permute-start.10 = (bf16[64,1024]{1,0:T(8,128)(2,1)}, bf16[64,1024]{1,0:T(8,128)(2,1)S(1)}, u32[]{:S(2)}, u32[]{:S(2)}) collective-permute-start(bf16[64,1024]{1,0:T(8,128)(2,1)} %coords_ref.1), channel_id=1, source_target_pairs={{0,2},{1,5},{4,0},{5,9},{8,4},{9,13},{12,8},{13,15},{14,12},{15,11... | collective-permute-start | bytes 393224 | tf_op jit(solution)/shard_map/ppermute | solution.py:407
  3.6 6.9 %collective-permute-start.2 = (bf16[64,1024]{1,0:T(8,128)(2,1)}, bf16[64,1024]{1,0:T(8,128)(2,1)S(1)}, u32[]{:S(2)}, u32[]{:S(2)}) collective-permute-start(bf16[64,1024]{1,0:T(8,128)(2,1)} %coords_ref.1), channel_id=1, source_target_pairs={{0,4},{1,3},{4,8},{5,1},{8,12},{9,5},{12,14},{13,9},{14,10},{15,13... | collective-permute-start | bytes 393224 | tf_op jit(solution)/shard_map/ppermute | solution.py:407
  3.8 7.9 %collective-permute-start.1 = (bf16[64,1024]{1,0:T(8,128)(2,1)}, bf16[64,1024]{1,0:T(8,128)(2,1)S(1)}, u32[]{:S(2)}, u32[]{:S(2)}) collective-permute-start(bf16[64,1024]{1,0:T(8,128)(2,1)} %coords_ref.1), channel_id=1, source_target_pairs={{0,1},{1,0},{2,3},{3,2},{4,5},{5,4},{6,7},{7,6},{8,9},{9,8},{10,11... | collective-permute-start | bytes 393224 | tf_op jit(solution)/shard_map/ppermute | solution.py:406
  6.1 2.4 %collective-permute-start = (f32[8,128]{1,0:T(8,128)}, f32[8,128]{1,0:T(8,128)S(1)}, u32[]{:S(2)}, u32[]{:S(2)}) collective-permute-start(f32[8,128]{1,0:T(8,128)} %get-tuple-element.48), channel_id=1, source_target_pairs={{0,1},{1,0},{2,3},{3,2},{4,5},{5,4},{6,7},{7,6},{8,9},{9,8},{10,11... | collective-permute-start | bytes 12296 | tf_op jit(solution)/shard_map/ppermute | solution.py:419
  6.6 8.1 %collective-permute-start.13 = (bf16[704,128]{1,0:T(8,128)(2,1)}, bf16[704,128]{1,0:T(8,128)(2,1)S(1)}, u32[]{:S(2)}, u32[]{:S(2)}) collective-permute-start(bf16[704,128]{1,0:T(8,128)(2,1)} %get-tuple-element.51), channel_id=1, source_target_pairs={{0,2},{1,5},{4,0},{5,9},{8,4},{9,13},{12,8},{13,15},{14,12},{15,11... | collective-permute-start | bytes 540680 | tf_op jit(solution)/shard_map/ppermute | solution.py:501
  8.5 7.3 %collective-permute-start.6 = (bf16[704,128]{1,0:T(8,128)(2,1)}, bf16[704,128]{1,0:T(8,128)(2,1)S(1)}, u32[]{:S(2)}, u32[]{:S(2)}) collective-permute-start(bf16[704,128]{1,0:T(8,128)(2,1)} %get-tuple-element.51), channel_id=1, source_target_pairs={{0,4},{1,3},{4,8},{5,1},{8,12},{9,5},{12,14},{13,9},{14,10},{15,13... | collective-permute-start | bytes 540680 | tf_op jit(solution)/shard_map/ppermute | solution.py:501
  9.6 10.6 %collective-permute-start.11 = (bf16[64,1024]{1,0:T(8,128)(2,1)S(1)}, bf16[64,1024]{1,0:T(8,128)(2,1)S(1)}, u32[]{:S(2)}, u32[]{:S(2)}) collective-permute-start(bf16[64,1024]{1,0:T(8,128)(2,1)S(1)} %collective-permute-done.10.refs_3_), channel_id=1, source_target_pairs={{0,2},{1,5},{4,0},{5,9},{8,4},{9,13},{12,8},{13,15},{14,12},{15,11... | collective-permute-start | bytes 393224 | tf_op jit(solution)/shard_map/ppermute | solution.py:511
  10.6 10.8 %collective-permute-start.3 = (bf16[64,1024]{1,0:T(8,128)(2,1)S(1)}, bf16[64,1024]{1,0:T(8,128)(2,1)S(1)}, u32[]{:S(2)}, u32[]{:S(2)}) collective-permute-start(bf16[64,1024]{1,0:T(8,128)(2,1)S(1)} %collective-permute-done.2.refs_2_), channel_id=1, source_target_pairs={{0,4},{1,3},{4,8},{5,1},{8,12},{9,5},{12,14},{13,9},{14,10},{15,13... | collective-permute-start | bytes 393224 | tf_op jit(solution)/shard_map/ppermute | solution.py:511
  14.7 7.6 %collective-permute-start.14 = (bf16[704,128]{1,0:T(8,128)(2,1)S(1)}, bf16[704,128]{1,0:T(8,128)(2,1)S(1)}, u32[]{:S(2)}, u32[]{:S(2)}) collective-permute-start(bf16[704,128]{1,0:T(8,128)(2,1)S(1)} %collective-permute-done.13.refs_5_.refs_7_), channel_id=1, source_target_pairs={{0,2},{1,5},{4,0},{5,9},{8,4},{9,13},{12,8},{13,15},{14,12},{15,11... | collective-permute-start | bytes 540680 | tf_op jit(solution)/shard_map/ppermute | solution.py:512
  15.8 7.5 %collective-permute-start.7 = (bf16[704,128]{1,0:T(8,128)(2,1)S(1)}, bf16[704,128]{1,0:T(8,128)(2,1)S(1)}, u32[]{:S(2)}, u32[]{:S(2)}) collective-permute-start(bf16[704,128]{1,0:T(8,128)(2,1)S(1)} %collective-permute-done.6.refs_4_.refs_6_), channel_id=1, source_target_pairs={{0,4},{1,3},{4,8},{5,1},{8,12},{9,5},{12,14},{13,9},{14,10},{15,13... | collective-permute-start | bytes 540680 | tf_op jit(solution)/shard_map/ppermute | solution.py:512
  20.2 10.8 %collective-permute-start.12 = (bf16[64,1024]{1,0:T(8,128)(2,1)S(1)}, bf16[64,1024]{1,0:T(8,128)(2,1)S(1)}, u32[]{:S(2)}, u32[]{:S(2)}) collective-permute-start(bf16[64,1024]{1,0:T(8,128)(2,1)S(1)} %collective-permute-done.11.refs_3_), channel_id=1, source_target_pairs={{0,2},{1,5},{4,0},{5,9},{8,4},{9,13},{12,8},{13,15},{14,12},{15,11... | collective-permute-start | bytes 393224 | tf_op jit(solution)/shard_map/ppermute | solution.py:511
  21.3 6.4 %collective-permute-start.4 = (bf16[64,1024]{1,0:T(8,128)(2,1)S(1)}, bf16[64,1024]{1,0:T(8,128)(2,1)S(1)}, u32[]{:S(2)}, u32[]{:S(2)}) collective-permute-start(bf16[64,1024]{1,0:T(8,128)(2,1)S(1)} %collective-permute-done.3.refs_2_), channel_id=1, source_target_pairs={{0,4},{1,3},{4,8},{5,1},{8,12},{9,5},{12,14},{13,9},{14,10},{15,13... | collective-permute-start | bytes 393224 | tf_op jit(solution)/shard_map/ppermute | solution.py:511
  22.3 8.7 %collective-permute-start.15 = (bf16[704,128]{1,0:T(8,128)(2,1)S(1)}, bf16[704,128]{1,0:T(8,128)(2,1)S(1)}, u32[]{:S(2)}, u32[]{:S(2)}) collective-permute-start(bf16[704,128]{1,0:T(8,128)(2,1)S(1)} %collective-permute-done.14.refs_5_.refs_7_), channel_id=1, source_target_pairs={{0,2},{1,5},{4,0},{5,9},{8,4},{9,13},{12,8},{13,15},{14,12},{15,11... | collective-permute-start | bytes 540680 | tf_op jit(solution)/shard_map/ppermute | solution.py:512
  23.4 6.0 %collective-permute-start.8 = (bf16[704,128]{1,0:T(8,128)(2,1)S(1)}, bf16[704,128]{1,0:T(8,128)(2,1)S(1)}, u32[]{:S(2)}, u32[]{:S(2)}) collective-permute-start(bf16[704,128]{1,0:T(8,128)(2,1)S(1)} %collective-permute-done.7.refs_4_.refs_6_), channel_id=1, source_target_pairs={{0,4},{1,3},{4,8},{5,1},{8,12},{9,5},{12,14},{13,9},{14,10},{15,13... | collective-permute-start | bytes 540680 | tf_op jit(solution)/shard_map/ppermute | solution.py:512
  27.7 6.7 %collective-permute-start.5 = (bf16[64,1024]{1,0:T(8,128)(2,1)S(1)}, bf16[64,1024]{1,0:T(8,128)(2,1)S(1)}, u32[]{:S(2)}, u32[]{:S(2)}) collective-permute-start(bf16[64,1024]{1,0:T(8,128)(2,1)S(1)} %collective-permute-done.4.refs_2_), channel_id=1, source_target_pairs={{0,4},{1,3},{4,8},{5,1},{8,12},{9,5},{12,14},{13,9},{14,10},{15,13... | collective-permute-start | bytes 393224 | tf_op jit(solution)/shard_map/ppermute | solution.py:511
  29.4 5.5 %collective-permute-start.9 = (bf16[704,128]{1,0:T(8,128)(2,1)S(1)}, bf16[704,128]{1,0:T(8,128)(2,1)S(1)}, u32[]{:S(2)}, u32[]{:S(2)}) collective-permute-start(bf16[704,128]{1,0:T(8,128)(2,1)S(1)} %collective-permute-done.8.refs_4_.refs_6_), channel_id=1, source_target_pairs={{0,4},{1,3},{4,8},{5,1},{8,12},{9,5},{12,14},{13,9},{14,10},{15,13... | collective-permute-start | bytes 540680 | tf_op jit(solution)/shard_map/ppermute | solution.py:512
  40.1 6.9 %collective-permute-start.17 = (bf16[640,128]{1,0:T(8,128)(2,1)S(1)}, bf16[640,128]{1,0:T(8,128)(2,1)S(1)}, u32[]{:S(2)}, u32[]{:S(2)}) collective-permute-start(bf16[640,128]{1,0:T(8,128)(2,1)S(1)} %get-tuple-element.64.refs_2_), channel_id=1, source_target_pairs={{0,4},{1,3},{4,8},{5,1},{8,12},{9,5},{12,14},{13,9},{14,10},{15,13... | collective-permute-start | bytes 491528 | tf_op jit(solution)/shard_map/ppermute | solution.py:537
  41.6 7.5 %collective-permute-start.21 = (bf16[640,128]{1,0:T(8,128)(2,1)S(1)}, bf16[640,128]{1,0:T(8,128)(2,1)S(1)}, u32[]{:S(2)}, u32[]{:S(2)}) collective-permute-start(bf16[640,128]{1,0:T(8,128)(2,1)S(1)} %get-tuple-element.64.refs_2_), channel_id=1, source_target_pairs={{0,2},{1,5},{4,0},{5,9},{8,4},{9,13},{12,8},{13,15},{14,12},{15,11... | collective-permute-start | bytes 491528 | tf_op jit(solution)/shard_map/ppermute | solution.py:537
  46.9 6.3 %collective-permute-start.18 = (bf16[640,128]{1,0:T(8,128)(2,1)S(1)}, bf16[640,128]{1,0:T(8,128)(2,1)S(1)}, u32[]{:S(2)}, u32[]{:S(2)}) collective-permute-start(bf16[640,128]{1,0:T(8,128)(2,1)S(1)} %collective-permute-done.17.refs_2_), channel_id=1, source_target_pairs={{0,4},{1,3},{4,8},{5,1},{8,12},{9,5},{12,14},{13,9},{14,10},{15,13... | collective-permute-start | bytes 491528 | tf_op jit(solution)/shard_map/ppermute | solution.py:540
  49.1 5.8 %collective-permute-start.22 = (bf16[640,128]{1,0:T(8,128)(2,1)S(1)}, bf16[640,128]{1,0:T(8,128)(2,1)S(1)}, u32[]{:S(2)}, u32[]{:S(2)}) collective-permute-start(bf16[640,128]{1,0:T(8,128)(2,1)S(1)} %shard_map.113.refs_3_), channel_id=1, source_target_pairs={{0,2},{1,5},{4,0},{5,9},{8,4},{9,13},{12,8},{13,15},{14,12},{15,11... | collective-permute-start | bytes 491528 | tf_op jit(solution)/shard_map/ppermute | solution.py:545
  53.2 6.0 %collective-permute-start.19 = (bf16[640,128]{1,0:T(8,128)(2,1)S(1)}, bf16[640,128]{1,0:T(8,128)(2,1)S(1)}, u32[]{:S(2)}, u32[]{:S(2)}) collective-permute-start(bf16[640,128]{1,0:T(8,128)(2,1)S(1)} %collective-permute-done.18.refs_2_), channel_id=1, source_target_pairs={{0,4},{1,3},{4,8},{5,1},{8,12},{9,5},{12,14},{13,9},{14,10},{15,13... | collective-permute-start | bytes 491528 | tf_op jit(solution)/shard_map/ppermute | solution.py:540
  54.9 5.4 %collective-permute-start.23 = (bf16[640,128]{1,0:T(8,128)(2,1)S(1)}, bf16[640,128]{1,0:T(8,128)(2,1)S(1)}, u32[]{:S(2)}, u32[]{:S(2)}) collective-permute-start(bf16[640,128]{1,0:T(8,128)(2,1)S(1)} %shard_map.116.refs_3_), channel_id=1, source_target_pairs={{0,2},{1,5},{4,0},{5,9},{8,4},{9,13},{12,8},{13,15},{14,12},{15,11... | collective-permute-start | bytes 491528 | tf_op jit(solution)/shard_map/ppermute | solution.py:545
  59.3 5.3 %collective-permute-start.20 = (bf16[640,128]{1,0:T(8,128)(2,1)S(1)}, bf16[640,128]{1,0:T(8,128)(2,1)S(1)}, u32[]{:S(2)}, u32[]{:S(2)}) collective-permute-start(bf16[640,128]{1,0:T(8,128)(2,1)S(1)} %collective-permute-done.19.refs_2_), channel_id=1, source_target_pairs={{0,4},{1,3},{4,8},{5,1},{8,12},{9,5},{12,14},{13,9},{14,10},{15,13... | collective-permute-start | bytes 491528 | tf_op jit(solution)/shard_map/ppermute | solution.py:540
  66.4 1.6 %collective-permute-start.24 = (f32[512,128]{1,0:T(8,128)S(1)}, f32[512,128]{1,0:T(8,128)S(1)}, u32[]{:S(2)}, u32[]{:S(2)}) collective-permute-start(f32[512,128]{1,0:T(8,128)S(1)} %get-tuple-element.93), channel_id=1, source_target_pairs={{0,1},{1,0},{2,3},{3,2},{4,5},{5,4},{6,7},{7,6},{8,9},{9,8},{10,11... | collective-permute-start | bytes 786440 | tf_op jit(solution)/shard_map/ppermute | solution.py:550
  (6 other events, 19.4 us)

commit v11 on v10

--- a/solution.py
+++ b/solution.py
@@ -142,15 +142,17 @@
     local_ref[place : place + 16, :] = jnp.concatenate([table, table], axis=0).astype(bf16)
 
 
-def joined_kernel(mine_ref, other_ref, leaf_ref, node_ref, upper_ref, out_ref, message_ref):
+def joined_kernel(mine_ref, other_ref, leaf_ref, node_ref, upper_ref, out_ref, *message_refs):
     half = mine_ref.shape[0]
     columns = LANES // LEAVES
     result = mine_ref[...] + other_ref[...]
-    message_ref[0:half, :] = result.astype(bf16)
     flat = result.T.astype(bf16)
     charges = [flat[0:columns], flat[columns:]]
     out_ref[...] = jnp.concatenate(charges, axis=1)
-    message_ref[half : half + LANES, :] = skeleton_rows(charges, leaf_ref, node_ref, upper_ref)
+    rows = skeleton_rows(charges, leaf_ref, node_ref, upper_ref)
+    for message_ref in message_refs:
+        message_ref[0:half, :] = result.astype(bf16)
+        message_ref[half : half + LANES, :] = rows
 
 
 def added_kernel(mine_ref, other_ref, out_ref):
@@ -515,10 +517,10 @@
     given["places"][across[0]], given["skeletons"][across[0]] = coords_next[0], sent[0]
     results = stage(across, across, given, carried, True, mode)
     keep_results(results)
-    first, message = call(
+    first, message, again = call(
         joined_kernel,
         [results["mine"], to_sibling(results["other"])] + maps,
-        [shape(columns, local), shape(points + LANES, LANES)],
+        [shape(columns, local)] + [shape(points + LANES, LANES)] * 2,
     )
 
     mode = "use" if keeping else "make"
@@ -534,8 +536,9 @@
         carried = [results["total"], results["sums"]]
         return results
 
-    one, other = one_way(message), other_way(message)
+    one = one_way(message)
     arrived(0, message)
+    other = other_way(gated(again, carried[1]))
     for hop in range(1, chips // 2):
         one_next = one_way(one)
         arrived(2 * hop - 1, one)

time: 69 us -> 68.5 us (level)
  waiting for transfers between devices: 13.2 us -> 9.59 us
  starting transfers between devices: 24.3 us -> 27.5 us
    ppermute x3, starting transfers between devices: 1.55 us -> 6.88 us  [on_device(): one_next = one_way(one)]
    ppermute x3, waiting for transfers between devices: 5.76 us -> 3.05 us  [on_device(): one_next = one_way(one)]
    ppermute x2, starting transfers between devices: 2.55 us -> 0.33 us  [on_device(): other_next = other_way(other)]
    ppermute x2, waiting for transfers between devices: 3.74 us -> 2.58 us  [the longest x1 2.58 us: on_device(): one = one_way(message)]
  transfers between devices with their start and end apart: 25 -> 25, of which waited for: 8 -> 9; matrix products, arithmetic and copies ran while one was open for 0% -> 0% of each run, Pallas kernels for 34% -> 34%
where the time goes in v11:
time: 68.5 us; the launch traced here: 68.3 us
  Pallas kernels  29.4 us (43%)
  starting transfers between devices  27.5 us (40%)
  waiting for transfers between devices  9.59 us (14%)
  local copies, waits for them, and re-layouts  0.98 us (1%)
  between operations  0.83 us (1%)
    pallas_call x16, Pallas kernels, call(): pl.pallas_call(body, grid=(1,), out_shape=out_shapes, in_specs=specs, out...  29.4 us
    ppermute x3, starting transfers between devices, on_device(): one_next = one_way(one)  6.88 us
    ppermute x5, starting transfers between devices, on_device(): sent = (one_way(sent[0]), None if final else other_way(sent[1]))  5.69 us
    ppermute x3, starting transfers between devices, on_device(): one_way(coords_next[0])  3.66 us
    ppermute x2, starting transfers between devices, on_device(): coords_next = (one_way(coords), other_way(coords))  3.14 us
    ppermute x3, waiting for transfers between devices, on_device(): one_next = one_way(one)  3.05 us
    ppermute x2, waiting for transfers between devices, on_device(): to_sibling(results['other'])  3.04 us
    ppermute x2, starting transfers between devices, on_device(): sent = (one_way(message), other_way(message))  2.99 us
  transfers between devices with their start and end apart: 25, of which 9 were waited for; matrix products, arithmetic and copies ran while one was open for 0% of the time, Pallas kernels for 34%

profile of v11, /device:TPU:0, one launch (start us, length us, event | category | flops | bytes accessed | tf_op | source)
XLA Modules:
  0.0 68.3 jit_solution(16732870960883305716)
XLA Ops:
  0.6 3.0 %collective-permute-start.10 = (bf16[64,1024]{1,0:T(8,128)(2,1)}, bf16[64,1024]{1,0:T(8,128)(2,1)S(1)}, u32[]{:S(2)}, u32[]{:S(2)}) collective-permute-start(bf16[64,1024]{1,0:T(8,128)(2,1)} %coords_ref.1), channel_id=1, source_target_pairs={{0,2},{1,5},{4,0},{5,9},{8,4},{9,13},{12,8},{13,15},{14,12},{15,11... | collective-permute-start | bytes 393224 | tf_op jit(solution)/shard_map/ppermute | solution.py:409
  3.8 2.3 %shard_map.104 = (bf16[704,128]{1,0:T(8,128)(2,1)}, bf16[1232,128]{1,0:T(8,128)(2,1)}, f32[8,128]{1,0:T(8,128)}) custom-call(s32[2,16]{1,0:T(2,128)} %near_ref.1, s32[2,32]{1,0:T(2,128)} %far_ref.1, bf16[64,1024]{1,0:T(8,128)(2,1)} %coords_ref.1, bf16[64,1024]{1,0:T(8,128)(2,1)} %charges_ref.1, bf16[64,128]{1,0:T(8,128)(2,1)} %points_ref.1, ...), custom_call_target="tpu_custom_call" | custom-call | bytes 639360 | tf_op jit(solution)/shard_map/pallas_call | solution.py:353
  6.6 1.9 %collective-permute-start.13 = (bf16[704,128]{1,0:T(8,128)(2,1)}, bf16[704,128]{1,0:T(8,128)(2,1)S(1)}, u32[]{:S(2)}, u32[]{:S(2)}) collective-permute-start(bf16[704,128]{1,0:T(8,128)(2,1)} %get-tuple-element.52), channel_id=1, source_target_pairs={{0,2},{1,5},{4,0},{5,9},{8,4},{9,13},{12,8},{13,15},{14,12},{15,11... | collective-permute-start | bytes 540680 | tf_op jit(solution)/shard_map/ppermute | solution.py:503
  12.6 2.1 %shard_map.105 = (bf16[2,1024,128]{2,1,0:T(8,128)(2,1)S(1)}, f32[8,128]{1,0:T(8,128)S(1)}, bf16[3,1024,512]{2,1,0:T(8,128)(2,1)S(1)}, bf16[2,1024,128]{2,1,0:T(8...) custom-call(f32[8,128]{1,0:T(8,128)S(1)} %collective-permute-done.refs_0_.refs_1_, ...), custom_call_target="tpu_custom_call" | custom-call | flops 2000000000 | bytes 450560 | tf_op jit(solution)/shard_map/pallas_call | solution.py:353
  14.7 1.1 %collective-permute-start.14 = (bf16[704,128]{1,0:T(8,128)(2,1)S(1)}, bf16[704,128]{1,0:T(8,128)(2,1)S(1)}, u32[]{:S(2)}, u32[]{:S(2)}) collective-permute-start(bf16[704,128]{1,0:T(8,128)(2,1)S(1)} %collective-permute-done.13.refs_5_.refs_7_), channel_id=1, source_target_pairs={{0,2},{1,5},{4,0},{5,9},{8,4},{9,13},{12,8},{13,15},{14,12},{15,11... | collective-permute-start | bytes 540680 | tf_op jit(solution)/shard_map/ppermute | solution.py:514
  16.8 3.4 %shard_map.106 = (bf16[2,1024,512]{2,1,0:T(8,128)(2,1)S(1)}, bf16[2,1024,512]{2,1,0:T(8,128)(2,1)S(1)}, bf16[2,1024,256]{2,1,0:T(8,128)(2,1)S(1)}, f32[2,1024,128]{2,1,0:T(8,128)S(1)}, f32[1,128,128]{2,1,0:T(8,128)S(1)}) custom-call(f32[8,128]{1,0:T(8,128)S(1)} %get-tuple-element.51.refs_0_, ...), custom_call_target="tpu_custom_call", output_to_operand_aliasing={{3}: (9, {}), {4}: (10, {})} | custom-call | flops 4000000000 | bytes 2629632 | tf_op jit(solution)/shard_map/pallas_call | solution.py:353
  20.2 1.1 %collective-permute-start.12 = (bf16[64,1024]{1,0:T(8,128)(2,1)S(1)}, bf16[64,1024]{1,0:T(8,128)(2,1)S(1)}, u32[]{:S(2)}, u32[]{:S(2)}) collective-permute-start(bf16[64,1024]{1,0:T(8,128)(2,1)S(1)} %collective-permute-done.11.refs_3_), channel_id=1, source_target_pairs={{0,2},{1,5},{4,0},{5,9},{8,4},{9,13},{12,8},{13,15},{14,12},{15,11... | collective-permute-start | bytes 393224 | tf_op jit(solution)/shard_map/ppermute | solution.py:513
  24.3 3.4 %shard_map.107 = (bf16[2,1024,512]{2,1,0:T(8,128)(2,1)S(1)}, bf16[2,1024,512]{2,1,0:T(8,128)(2,1)S(1)}, bf16[2,1024,256]{2,1,0:T(8,128)(2,1)S(1)}, f32[2,1024,128]{2,1,0:T(8,128)S(1)}, f32[1,128,128]{2,1,0:T(8,128)S(1)}) custom-call(f32[8,128]{1,0:T(8,128)S(1)} %get-tuple-element.51.refs_0_, ...), custom_call_target="tpu_custom_call", output_to_operand_aliasing={{3}: (9, {}), {4}: (10, {})} | custom-call | flops 4000000000 | bytes 2629632 | tf_op jit(solution)/shard_map/pallas_call | solution.py:353
  27.7 1.6 %collective-permute-start.5 = (bf16[64,1024]{1,0:T(8,128)(2,1)S(1)}, bf16[64,1024]{1,0:T(8,128)(2,1)S(1)}, u32[]{:S(2)}, u32[]{:S(2)}) collective-permute-start(bf16[64,1024]{1,0:T(8,128)(2,1)S(1)} %collective-permute-done.4.refs_2_), channel_id=1, source_target_pairs={{0,4},{1,3},{4,8},{5,1},{8,12},{9,5},{12,14},{13,9},{14,10},{15,13... | collective-permute-start | bytes 393224 | tf_op jit(solution)/shard_map/ppermute | solution.py:513
  29.4 1.6 %collective-permute-start.9 = (bf16[704,128]{1,0:T(8,128)(2,1)S(1)}, bf16[704,128]{1,0:T(8,128)(2,1)S(1)}, u32[]{:S(2)}, u32[]{:S(2)}) collective-permute-start(bf16[704,128]{1,0:T(8,128)(2,1)S(1)} %collective-permute-done.8.refs_4_.refs_6_), channel_id=1, source_target_pairs={{0,4},{1,3},{4,8},{5,1},{8,12},{9,5},{12,14},{13,9},{14,10},{15,13... | collective-permute-start | bytes 540680 | tf_op jit(solution)/shard_map/ppermute | solution.py:514
  31.0 3.4 %shard_map.108 = (bf16[2,1024,512]{2,1,0:T(8,128)(2,1)S(1)}, bf16[2,1024,512]{2,1,0:T(8,128)(2,1)S(1)}, bf16[2,1024,256]{2,1,0:T(8,128)(2,1)S(1)}, f32[2,1024,128]{2,1,0:T(8,128)S(1)}, f32[1,128,128]{2,1,0:T(8,128)S(1)}) custom-call(f32[8,128]{1,0:T(8,128)S(1)} %get-tuple-element.51.refs_0_, ...), custom_call_target="tpu_custom_call", output_to_operand_aliasing={{3}: (9, {}), {4}: (10, {})} | custom-call | flops 4000000000 | bytes 2629632 | tf_op jit(solution)/shard_map/pallas_call | solution.py:353
  34.9 2.7 %shard_map.109 = (bf16[2,1024,512]{2,1,0:T(8,128)(2,1)S(1)}, bf16[2,1024,256]{2,1,0:T(8,128)(2,1)S(1)}, f32[512,128]{1,0:T(8,128)S(1)}, f32[512,128]{1,0:T(8,128...) custom-call(f32[8,128]{1,0:T(8,128)S(1)} %get-tuple-element.51.refs_, ...), custom_call_target="tpu_custom_call", output_to_operand_aliasing={{4}: (6, {}), {5}: (7, {})} | custom-call | flops 2000000000 | bytes 2154496 | tf_op jit(solution)/shard_map/pallas_call | solution.py:353
  37.6 1.5 %collective-permute-done.16.other_ref = f32[512,128]{1,0:T(8,128)S(1)} collective-permute-done((f32[512,128]{1,0:T(8,128)S(1)}, f32[512,128]{1,0:T(8,128)S(1)}, u32[]{:S(2)}, u32[]{:S(2)}) %collective-permute-start.16) | collective-permute-done | bytes 262176 | tf_op jit(solution)/shard_map/ppermute | solution.py:522
  40.1 1.6 %collective-permute-start.17 = (bf16[640,128]{1,0:T(8,128)(2,1)S(1)}, bf16[640,128]{1,0:T(8,128)(2,1)S(1)}, u32[]{:S(2)}, u32[]{:S(2)}) collective-permute-start(bf16[640,128]{1,0:T(8,128)(2,1)S(1)} %get-tuple-element.65.refs_2_), channel_id=1, source_target_pairs={{0,4},{1,3},{4,8},{5,1},{8,12},{9,5},{12,14},{13,9},{14,10},{15,13... | collective-permute-start | bytes 491528 | tf_op jit(solution)/shard_map/ppermute | solution.py:539
  43.2 2.6 %collective-permute-done.17.refs_2_ = bf16[640,128]{1,0:T(8,128)(2,1)S(1)} collective-permute-done((bf16[640,128]{1,0:T(8,128)(2,1)S(1)}, bf16[640,128]{1,0:T(8,128)(2,1)S(1)}, u32[]{:S(2)}, u32[]{:S(2)}) %collective-permute-start.17) | collective-permute-done | bytes 163872 | tf_op jit(solution)/shard_map/ppermute | solution.py:539
  45.8 2.5 %collective-permute-start.18 = (bf16[640,128]{1,0:T(8,128)(2,1)S(1)}, bf16[640,128]{1,0:T(8,128)(2,1)S(1)}, u32[]{:S(2)}, u32[]{:S(2)}) collective-permute-start(bf16[640,128]{1,0:T(8,128)(2,1)S(1)} %collective-permute-done.17.refs_2_), channel_id=1, source_target_pairs={{0,4},{1,3},{4,8},{5,1},{8,12},{9,5},{12,14},{13,9},{14,10},{15,13... | collective-permute-start | bytes 491528 | tf_op jit(solution)/shard_map/ppermute | solution.py:543
  49.5 1.5 %shard_map.115 = (f32[2,1024,128]{2,1,0:T(8,128)S(1)}, f32[1,128,128]{2,1,0:T(8,128)S(1)}) custom-call(f32[8,128]{1,0:T(8,128)S(1)} %get-tuple-element.51.refs_0_, f32[8,128]{1,0:T(8,128)S(1)} %collective-permute-done.refs_0_.refs_1_, bf16[640,128]{1,0:T(8,128)(2,1)S(1)} %collective-permute-done.17.refs_2_, ...), custom_call_target="tpu_custom_call", output_to_operand_aliasing={{0}: (6, {}), {1}: (7, {})} | custom-call | flops 1000000000 | bytes 4595712 | tf_op jit(solution)/shard_map/pallas_call | solution.py:353
  50.9 1.6 %collective-permute-done.18.refs_2_ = bf16[640,128]{1,0:T(8,128)(2,1)S(1)} collective-permute-done((bf16[640,128]{1,0:T(8,128)(2,1)S(1)}, bf16[640,128]{1,0:T(8,128)(2,1)S(1)}, u32[]{:S(2)}, u32[]{:S(2)}) %collective-permute-start.18) | collective-permute-done | bytes 163872 | tf_op jit(solution)/shard_map/ppermute | solution.py:543
  52.5 2.4 %collective-permute-start.19 = (bf16[640,128]{1,0:T(8,128)(2,1)S(1)}, bf16[640,128]{1,0:T(8,128)(2,1)S(1)}, u32[]{:S(2)}, u32[]{:S(2)}) collective-permute-start(bf16[640,128]{1,0:T(8,128)(2,1)S(1)} %collective-permute-done.18.refs_2_), channel_id=1, source_target_pairs={{0,4},{1,3},{4,8},{5,1},{8,12},{9,5},{12,14},{13,9},{14,10},{15,13... | collective-permute-start | bytes 491528 | tf_op jit(solution)/shard_map/ppermute | solution.py:543
  56.4 1.5 %shard_map.118 = (f32[2,1024,128]{2,1,0:T(8,128)S(1)}, f32[1,128,128]{2,1,0:T(8,128)S(1)}) custom-call(f32[8,128]{1,0:T(8,128)S(1)} %get-tuple-element.51.refs_0_, f32[8,128]{1,0:T(8,128)S(1)} %collective-permute-done.refs_0_.refs_1_, bf16[640,128]{1,0:T(8,128)(2,1)S(1)} %collective-permute-done.18.refs_2_, ...), custom_call_target="tpu_custom_call", output_to_operand_aliasing={{0}: (6, {}), {1}: (7, {})} | custom-call | flops 1000000000 | bytes 4595712 | tf_op jit(solution)/shard_map/pallas_call | solution.py:353
  58.8 2.0 %collective-permute-start.20 = (bf16[640,128]{1,0:T(8,128)(2,1)S(1)}, bf16[640,128]{1,0:T(8,128)(2,1)S(1)}, u32[]{:S(2)}, u32[]{:S(2)}) collective-permute-start(bf16[640,128]{1,0:T(8,128)(2,1)S(1)} %collective-permute-done.19.refs_2_), channel_id=1, source_target_pairs={{0,4},{1,3},{4,8},{5,1},{8,12},{9,5},{12,14},{13,9},{14,10},{15,13... | collective-permute-start | bytes 491528 | tf_op jit(solution)/shard_map/ppermute | solution.py:543
  62.1 1.5 %shard_map.120 = (f32[2,1024,128]{2,1,0:T(8,128)S(1)}, f32[1,128,128]{2,1,0:T(8,128)S(1)}) custom-call(f32[8,128]{1,0:T(8,128)S(1)} %get-tuple-element.51.refs_0_, f32[8,128]{1,0:T(8,128)S(1)} %collective-permute-done.refs_0_.refs_1_, bf16[640,128]{1,0:T(8,128)(2,1)S(1)} %collective-permute-done.19.refs_2_, ...), custom_call_target="tpu_custom_call", output_to_operand_aliasing={{0}: (6, {}), {1}: (7, {})} | custom-call | flops 1000000000 | bytes 4595712 | tf_op jit(solution)/shard_map/pallas_call | solution.py:353
  64.1 1.8 %shard_map.121 = (f32[512,128]{1,0:T(8,128)S(1)}, f32[512,128]{1,0:T(8,128)S(1)}, f32[2,1024,128]{2,1,0:T(8,128)S(1)}, f32[1,128,128]{2,1,0:T(8,128)S(1)}) custom-call(f32[8,128]{1,0:T(8,128)S(1)} %get-tuple-element.51.refs_0_, f32[8,128]{1,0:T(8,128)S(1)} %collective-permute-done.refs_0_.refs_1_, ...), custom_call_target="tpu_custom_call", output_to_operand_aliasing={{2}: (5, {}), {3}: (6, {})} | custom-call | flops 1000000000 | bytes 4431872 | tf_op jit(solution)/shard_map/pallas_call | solution.py:353
  66.0 1.5 %collective-permute-done.24.other_ref = f32[512,128]{1,0:T(8,128)S(1)} collective-permute-done((f32[512,128]{1,0:T(8,128)S(1)}, f32[512,128]{1,0:T(8,128)S(1)}, u32[]{:S(2)}, u32[]{:S(2)}) %collective-permute-start.24) | collective-permute-done | bytes 262176 | tf_op jit(solution)/shard_map/ppermute | solution.py:553
  (55 shorter events, 18.0 us)
Async XLA Ops:
  0.6 9.0 %collective-permute-start.10 = (bf16[64,1024]{1,0:T(8,128)(2,1)}, bf16[64,1024]{1,0:T(8,128)(2,1)S(1)}, u32[]{:S(2)}, u32[]{:S(2)}) collective-permute-start(bf16[64,1024]{1,0:T(8,128)(2,1)} %coords_ref.1), channel_id=1, source_target_pairs={{0,2},{1,5},{4,0},{5,9},{8,4},{9,13},{12,8},{13,15},{14,12},{15,11... | collective-permute-start | bytes 393224 | tf_op jit(solution)/shard_map/ppermute | solution.py:409
  3.6 6.9 %collective-permute-start.2 = (bf16[64,1024]{1,0:T(8,128)(2,1)}, bf16[64,1024]{1,0:T(8,128)(2,1)S(1)}, u32[]{:S(2)}, u32[]{:S(2)}) collective-permute-start(bf16[64,1024]{1,0:T(8,128)(2,1)} %coords_ref.1), channel_id=1, source_target_pairs={{0,4},{1,3},{4,8},{5,1},{8,12},{9,5},{12,14},{13,9},{14,10},{15,13... | collective-permute-start | bytes 393224 | tf_op jit(solution)/shard_map/ppermute | solution.py:409
  3.8 7.9 %collective-permute-start.1 = (bf16[64,1024]{1,0:T(8,128)(2,1)}, bf16[64,1024]{1,0:T(8,128)(2,1)S(1)}, u32[]{:S(2)}, u32[]{:S(2)}) collective-permute-start(bf16[64,1024]{1,0:T(8,128)(2,1)} %coords_ref.1), channel_id=1, source_target_pairs={{0,1},{1,0},{2,3},{3,2},{4,5},{5,4},{6,7},{7,6},{8,9},{9,8},{10,11... | collective-permute-start | bytes 393224 | tf_op jit(solution)/shard_map/ppermute | solution.py:408
  6.1 2.4 %collective-permute-start = (f32[8,128]{1,0:T(8,128)}, f32[8,128]{1,0:T(8,128)S(1)}, u32[]{:S(2)}, u32[]{:S(2)}) collective-permute-start(f32[8,128]{1,0:T(8,128)} %get-tuple-element.49), channel_id=1, source_target_pairs={{0,1},{1,0},{2,3},{3,2},{4,5},{5,4},{6,7},{7,6},{8,9},{9,8},{10,11... | collective-permute-start | bytes 12296 | tf_op jit(solution)/shard_map/ppermute | solution.py:421
  6.6 8.1 %collective-permute-start.13 = (bf16[704,128]{1,0:T(8,128)(2,1)}, bf16[704,128]{1,0:T(8,128)(2,1)S(1)}, u32[]{:S(2)}, u32[]{:S(2)}) collective-permute-start(bf16[704,128]{1,0:T(8,128)(2,1)} %get-tuple-element.52), channel_id=1, source_target_pairs={{0,2},{1,5},{4,0},{5,9},{8,4},{9,13},{12,8},{13,15},{14,12},{15,11... | collective-permute-start | bytes 540680 | tf_op jit(solution)/shard_map/ppermute | solution.py:503
  8.5 7.3 %collective-permute-start.6 = (bf16[704,128]{1,0:T(8,128)(2,1)}, bf16[704,128]{1,0:T(8,128)(2,1)S(1)}, u32[]{:S(2)}, u32[]{:S(2)}) collective-permute-start(bf16[704,128]{1,0:T(8,128)(2,1)} %get-tuple-element.52), channel_id=1, source_target_pairs={{0,4},{1,3},{4,8},{5,1},{8,12},{9,5},{12,14},{13,9},{14,10},{15,13... | collective-permute-start | bytes 540680 | tf_op jit(solution)/shard_map/ppermute | solution.py:503
  9.6 10.6 %collective-permute-start.11 = (bf16[64,1024]{1,0:T(8,128)(2,1)S(1)}, bf16[64,1024]{1,0:T(8,128)(2,1)S(1)}, u32[]{:S(2)}, u32[]{:S(2)}) collective-permute-start(bf16[64,1024]{1,0:T(8,128)(2,1)S(1)} %collective-permute-done.10.refs_3_), channel_id=1, source_target_pairs={{0,2},{1,5},{4,0},{5,9},{8,4},{9,13},{12,8},{13,15},{14,12},{15,11... | collective-permute-start | bytes 393224 | tf_op jit(solution)/shard_map/ppermute | solution.py:513
  10.6 10.8 %collective-permute-start.3 = (bf16[64,1024]{1,0:T(8,128)(2,1)S(1)}, bf16[64,1024]{1,0:T(8,128)(2,1)S(1)}, u32[]{:S(2)}, u32[]{:S(2)}) collective-permute-start(bf16[64,1024]{1,0:T(8,128)(2,1)S(1)} %collective-permute-done.2.refs_2_), channel_id=1, source_target_pairs={{0,4},{1,3},{4,8},{5,1},{8,12},{9,5},{12,14},{13,9},{14,10},{15,13... | collective-permute-start | bytes 393224 | tf_op jit(solution)/shard_map/ppermute | solution.py:513
  14.7 7.6 %collective-permute-start.14 = (bf16[704,128]{1,0:T(8,128)(2,1)S(1)}, bf16[704,128]{1,0:T(8,128)(2,1)S(1)}, u32[]{:S(2)}, u32[]{:S(2)}) collective-permute-start(bf16[704,128]{1,0:T(8,128)(2,1)S(1)} %collective-permute-done.13.refs_5_.refs_7_), channel_id=1, source_target_pairs={{0,2},{1,5},{4,0},{5,9},{8,4},{9,13},{12,8},{13,15},{14,12},{15,11... | collective-permute-start | bytes 540680 | tf_op jit(solution)/shard_map/ppermute | solution.py:514
  15.8 7.5 %collective-permute-start.7 = (bf16[704,128]{1,0:T(8,128)(2,1)S(1)}, bf16[704,128]{1,0:T(8,128)(2,1)S(1)}, u32[]{:S(2)}, u32[]{:S(2)}) collective-permute-start(bf16[704,128]{1,0:T(8,128)(2,1)S(1)} %collective-permute-done.6.refs_4_.refs_6_), channel_id=1, source_target_pairs={{0,4},{1,3},{4,8},{5,1},{8,12},{9,5},{12,14},{13,9},{14,10},{15,13... | collective-permute-start | bytes 540680 | tf_op jit(solution)/shard_map/ppermute | solution.py:514
  20.2 10.8 %collective-permute-start.12 = (bf16[64,1024]{1,0:T(8,128)(2,1)S(1)}, bf16[64,1024]{1,0:T(8,128)(2,1)S(1)}, u32[]{:S(2)}, u32[]{:S(2)}) collective-permute-start(bf16[64,1024]{1,0:T(8,128)(2,1)S(1)} %collective-permute-done.11.refs_3_), channel_id=1, source_target_pairs={{0,2},{1,5},{4,0},{5,9},{8,4},{9,13},{12,8},{13,15},{14,12},{15,11... | collective-permute-start | bytes 393224 | tf_op jit(solution)/shard_map/ppermute | solution.py:513
  21.3 6.4 %collective-permute-start.4 = (bf16[64,1024]{1,0:T(8,128)(2,1)S(1)}, bf16[64,1024]{1,0:T(8,128)(2,1)S(1)}, u32[]{:S(2)}, u32[]{:S(2)}) collective-permute-start(bf16[64,1024]{1,0:T(8,128)(2,1)S(1)} %collective-permute-done.3.refs_2_), channel_id=1, source_target_pairs={{0,4},{1,3},{4,8},{5,1},{8,12},{9,5},{12,14},{13,9},{14,10},{15,13... | collective-permute-start | bytes 393224 | tf_op jit(solution)/shard_map/ppermute | solution.py:513
  22.3 8.7 %collective-permute-start.15 = (bf16[704,128]{1,0:T(8,128)(2,1)S(1)}, bf16[704,128]{1,0:T(8,128)(2,1)S(1)}, u32[]{:S(2)}, u32[]{:S(2)}) collective-permute-start(bf16[704,128]{1,0:T(8,128)(2,1)S(1)} %collective-permute-done.14.refs_5_.refs_7_), channel_id=1, source_target_pairs={{0,2},{1,5},{4,0},{5,9},{8,4},{9,13},{12,8},{13,15},{14,12},{15,11... | collective-permute-start | bytes 540680 | tf_op jit(solution)/shard_map/ppermute | solution.py:514
  23.4 6.0 %collective-permute-start.8 = (bf16[704,128]{1,0:T(8,128)(2,1)S(1)}, bf16[704,128]{1,0:T(8,128)(2,1)S(1)}, u32[]{:S(2)}, u32[]{:S(2)}) collective-permute-start(bf16[704,128]{1,0:T(8,128)(2,1)S(1)} %collective-permute-done.7.refs_4_.refs_6_), channel_id=1, source_target_pairs={{0,4},{1,3},{4,8},{5,1},{8,12},{9,5},{12,14},{13,9},{14,10},{15,13... | collective-permute-start | bytes 540680 | tf_op jit(solution)/shard_map/ppermute | solution.py:514
  27.7 6.7 %collective-permute-start.5 = (bf16[64,1024]{1,0:T(8,128)(2,1)S(1)}, bf16[64,1024]{1,0:T(8,128)(2,1)S(1)}, u32[]{:S(2)}, u32[]{:S(2)}) collective-permute-start(bf16[64,1024]{1,0:T(8,128)(2,1)S(1)} %collective-permute-done.4.refs_2_), channel_id=1, source_target_pairs={{0,4},{1,3},{4,8},{5,1},{8,12},{9,5},{12,14},{13,9},{14,10},{15,13... | collective-permute-start | bytes 393224 | tf_op jit(solution)/shard_map/ppermute | solution.py:513
  29.4 5.5 %collective-permute-start.9 = (bf16[704,128]{1,0:T(8,128)(2,1)S(1)}, bf16[704,128]{1,0:T(8,128)(2,1)S(1)}, u32[]{:S(2)}, u32[]{:S(2)}) collective-permute-start(bf16[704,128]{1,0:T(8,128)(2,1)S(1)} %collective-permute-done.8.refs_4_.refs_6_), channel_id=1, source_target_pairs={{0,4},{1,3},{4,8},{5,1},{8,12},{9,5},{12,14},{13,9},{14,10},{15,13... | collective-permute-start | bytes 540680 | tf_op jit(solution)/shard_map/ppermute | solution.py:514
  37.6 1.6 %collective-permute-start.16 = (f32[512,128]{1,0:T(8,128)S(1)}, f32[512,128]{1,0:T(8,128)S(1)}, u32[]{:S(2)}, u32[]{:S(2)}) collective-permute-start(f32[512,128]{1,0:T(8,128)S(1)} %get-tuple-element.63), channel_id=1, source_target_pairs={{0,1},{1,0},{2,3},{3,2},{4,5},{5,4},{6,7},{7,6},{8,9},{9,8},{10,11... | collective-permute-start | bytes 786440 | tf_op jit(solution)/shard_map/ppermute | solution.py:522
  40.1 5.8 %collective-permute-start.17 = (bf16[640,128]{1,0:T(8,128)(2,1)S(1)}, bf16[640,128]{1,0:T(8,128)(2,1)S(1)}, u32[]{:S(2)}, u32[]{:S(2)}) collective-permute-start(bf16[640,128]{1,0:T(8,128)(2,1)S(1)} %get-tuple-element.65.refs_2_), channel_id=1, source_target_pairs={{0,4},{1,3},{4,8},{5,1},{8,12},{9,5},{12,14},{13,9},{14,10},{15,13... | collective-permute-start | bytes 491528 | tf_op jit(solution)/shard_map/ppermute | solution.py:539
  42.8 6.6 %collective-permute-start.21 = (bf16[640,128]{1,0:T(8,128)(2,1)S(1)}, bf16[640,128]{1,0:T(8,128)(2,1)S(1)}, u32[]{:S(2)}, u32[]{:S(2)}) collective-permute-start(bf16[640,128]{1,0:T(8,128)(2,1)S(1)} %shard_map.112), channel_id=1, source_target_pairs={{0,2},{1,5},{4,0},{5,9},{8,4},{9,13},{12,8},{13,15},{14,12},{15,11... | collective-permute-start | bytes 491528 | tf_op jit(solution)/shard_map/ppermute | solution.py:541
  45.8 6.7 %collective-permute-start.18 = (bf16[640,128]{1,0:T(8,128)(2,1)S(1)}, bf16[640,128]{1,0:T(8,128)(2,1)S(1)}, u32[]{:S(2)}, u32[]{:S(2)}) collective-permute-start(bf16[640,128]{1,0:T(8,128)(2,1)S(1)} %collective-permute-done.17.refs_2_), channel_id=1, source_target_pairs={{0,4},{1,3},{4,8},{5,1},{8,12},{9,5},{12,14},{13,9},{14,10},{15,13... | collective-permute-start | bytes 491528 | tf_op jit(solution)/shard_map/ppermute | solution.py:543
  49.4 6.8 %collective-permute-start.22 = (bf16[640,128]{1,0:T(8,128)(2,1)S(1)}, bf16[640,128]{1,0:T(8,128)(2,1)S(1)}, u32[]{:S(2)}, u32[]{:S(2)}) collective-permute-start(bf16[640,128]{1,0:T(8,128)(2,1)S(1)} %shard_map.114.refs_3_), channel_id=1, source_target_pairs={{0,2},{1,5},{4,0},{5,9},{8,4},{9,13},{12,8},{13,15},{14,12},{15,11... | collective-permute-start | bytes 491528 | tf_op jit(solution)/shard_map/ppermute | solution.py:548
  52.5 6.3 %collective-permute-start.19 = (bf16[640,128]{1,0:T(8,128)(2,1)S(1)}, bf16[640,128]{1,0:T(8,128)(2,1)S(1)}, u32[]{:S(2)}, u32[]{:S(2)}) collective-permute-start(bf16[640,128]{1,0:T(8,128)(2,1)S(1)} %collective-permute-done.18.refs_2_), channel_id=1, source_target_pairs={{0,4},{1,3},{4,8},{5,1},{8,12},{9,5},{12,14},{13,9},{14,10},{15,13... | collective-permute-start | bytes 491528 | tf_op jit(solution)/shard_map/ppermute | solution.py:543
  56.2 6.0 %collective-permute-start.23 = (bf16[640,128]{1,0:T(8,128)(2,1)S(1)}, bf16[640,128]{1,0:T(8,128)(2,1)S(1)}, u32[]{:S(2)}, u32[]{:S(2)}) collective-permute-start(bf16[640,128]{1,0:T(8,128)(2,1)S(1)} %shard_map.117.refs_3_), channel_id=1, source_target_pairs={{0,2},{1,5},{4,0},{5,9},{8,4},{9,13},{12,8},{13,15},{14,12},{15,11... | collective-permute-start | bytes 491528 | tf_op jit(solution)/shard_map/ppermute | solution.py:548
  58.8 5.3 %collective-permute-start.20 = (bf16[640,128]{1,0:T(8,128)(2,1)S(1)}, bf16[640,128]{1,0:T(8,128)(2,1)S(1)}, u32[]{:S(2)}, u32[]{:S(2)}) collective-permute-start(bf16[640,128]{1,0:T(8,128)(2,1)S(1)} %collective-permute-done.19.refs_2_), channel_id=1, source_target_pairs={{0,4},{1,3},{4,8},{5,1},{8,12},{9,5},{12,14},{13,9},{14,10},{15,13... | collective-permute-start | bytes 491528 | tf_op jit(solution)/shard_map/ppermute | solution.py:543
  (6 other events, 19.4 us)

commit v12 on v11

--- a/solution.py
+++ b/solution.py
@@ -117,8 +117,8 @@
     node_ref,
     upper_ref,
     message_ref,
+    places_ref,
     local_ref,
-    table_ref,
 ):
     dim, local = coords_ref.shape
     half = local // LEAVES
@@ -137,8 +137,8 @@
     for block in range(local // LANES):
         local_ref[place : place + dim, :] = coords_ref[:, block * LANES : (block + 1) * LANES]
         place += dim
+    places_ref[...] = coords_ref[...]
     table = count_rows(near_ref, far_ref)
-    table_ref[...] = table
     local_ref[place : place + 16, :] = jnp.concatenate([table, table], axis=0).astype(bf16)
 
 
@@ -162,41 +162,43 @@
 
 
 def stage_kernel(stage, *refs):
-    ring, near_spots, far_spots, n_sub, dim, points, begins, first, last, mode = stage
+    ring, near_spots, far_spots, n_sub, dim, points, begins, first, last, near, far = stage
     refs = list(refs)
-    use, keep = mode == "use", mode == "keep"
     spots = sorted(set(near_spots) | set(far_spots))
-    makes = not use
-    table_refs = [refs.pop(0) for _ in range(1 if begins else CORES)]
+    makes_near, makes_far = near != "use", far != "use" and bool(far_spots)
+    adds = near != "only"
     if begins:
-        local_ref = refs.pop(0)
-        charge_refs = skeleton_refs = {spots[0]: local_ref}
+        local_refs = refs.pop(0), refs.pop(0)
+        charge_refs = skeleton_refs = {spots[0]: local_refs[0]}
     else:
-        place_refs = {spot: refs.pop(0) for spot in near_spots} if makes else {}
-        skeleton_refs = {spot: refs.pop(0) for spot in far_spots} if makes else {}
-        charge_refs = {spot: refs.pop(0) for spot in spots}
+        table_refs = refs.pop(0), refs.pop(0)
+        place_refs = {spot: refs.pop(0) for spot in near_spots} if makes_near else {}
+        skeleton_refs = {spot: refs.pop(0) for spot in far_spots} if makes_far else {}
+        charge_refs = {spot: refs.pop(0) for spot in spots} if adds else {}
     kept_refs = {}
     far_kept_ref = None
-    if use:
+    if near == "use":
         kept_refs = {spot: refs.pop(0) for spot in near_spots}
-        far_kept_ref = refs.pop(0) if far_spots else None
+    if far == "use" and far_spots:
+        far_kept_ref = refs.pop(0)
+    if (makes_near or makes_far) and not begins:
+        targets_ref = refs.pop(0)
+    if not first and adds:
+        refs.pop(0), refs.pop(0)
+    upper_points_ref = refs.pop(0) if last and makes_far else None
     if begins:
-        sibling_ref = refs.pop(0)
-    elif makes:
         targets_ref = refs.pop(0)
-    if not first:
-        refs.pop(0), refs.pop(0)
-    upper_points_ref = refs.pop(0) if last and makes else None
-    if begins:
-        targets_ref, table_ref = refs.pop(0), refs.pop(0)
-    if keep:
+        table_refs = refs.pop(0), refs.pop(0)
+    if near in ("keep", "only"):
         kept_refs = {spot: refs.pop(0) for spot in near_spots}
-        far_kept_ref = refs.pop(0) if far_spots else None
-    if last:
+    if far == "keep" and far_spots:
+        far_kept_ref = refs.pop(0)
+    if last and adds:
         half_refs = refs.pop(0), refs.pop(0)
-    total_ref, sums_ref, far_charges_ref, charges_ref = refs[:4]
-    if makes:
-        near_ref, far_ref = refs[4:]
+    if adds:
+        total_ref, sums_ref, far_charges_ref, charges_ref = (refs.pop(0) for _ in range(4))
+    near_ref = refs.pop(0) if makes_near else None
+    far_ref = refs.pop(0) if makes_far else None
 
     skeletons_at = points + LANES
     blocks = points // LANES
@@ -206,20 +208,22 @@
     def span_of(leaf):
         return slice(leaf * points, (leaf + 1) * points)
 
-    def points_of(spot, leaf):
-        if not begins:
-            return place_refs[spot][:, span_of(leaf)]
+    def local_points(ref, leaf):
         begin = skeletons_at + dim + leaf * blocks * dim
         rows = [begin + block * dim for block in range(blocks)]
-        return jnp.concatenate([local_ref[row : row + dim, :] for row in rows], axis=1)
+        return jnp.concatenate([ref[row : row + dim, :] for row in rows], axis=1)
+
+    def points_of(spot, leaf):
+        if begins:
+            return local_points(local_refs[0], leaf)
+        return place_refs[spot][:, span_of(leaf)]
 
     if begins:
         begin = skeletons_at + dim + LEAVES * blocks * dim
-        table_ref[...] = local_ref[begin : begin + 16, :].astype(f32)[0:8]
-        table_refs = [table_ref] + table_refs
-        for leaf in range(LEAVES):
-            targets_ref[0, span_of(leaf), :] = target_rows(points_of(0, leaf))
-            targets_ref[1, span_of(leaf), :] = target_rows(sibling_ref[:, span_of(leaf)])
+        for core, ref in enumerate(local_refs):
+            table_refs[core][...] = ref[begin : begin + 16, :].astype(f32)[0:8]
+            for leaf in range(LEAVES):
+                targets_ref[core, span_of(leaf), :] = target_rows(local_points(ref, leaf))
     if first:
         total_ref[...] = jnp.zeros_like(total_ref)
         sums_ref[...] = jnp.zeros_like(sums_ref)
@@ -231,8 +235,8 @@
     def picked(table, entry):
         return jnp.sum(jnp.where(lane == entry, table, 0.0), axis=1, keepdims=True)
 
-    def values(core, sources_ref, kept_ref):
-        if use:
+    def values(makes, core, sources_ref, kept_ref):
+        if not makes:
             return kept_ref[...]
         made = kernel_values(targets_ref[core], sources_ref[...])
         if kept_ref is not None:
@@ -252,14 +256,17 @@
         else:
             second = jnp.full((1, 1), float(leaf), f32)
         times = named[0] * (1.0 - second) + named[1] * second
-        if makes:
+        if makes_near:
             low, high = (points_of(spot, which) for which in range(LEAVES))
             chosen = low * (1.0 - second).astype(bf16) + high * second.astype(bf16)
             put_sources(near_ref.at[at], chosen)
+        kept = kept_refs[spot].at[turn] if kept_refs else None
+        kernel = values(makes_near, core, near_ref.at[at] if makes_near else None, kept)
+        if not adds:
+            return None
         half = jnp.where(lane[0:1] < LANES // LEAVES, 1.0 - second, second).astype(bf16)
         charges_ref[at] = charge_refs[spot][0:points, :] * half
-        kept = kept_refs[spot].at[turn] if kept_refs else None
-        added = matmul(values(core, near_ref.at[at] if makes else None, kept), charges_ref[at])
+        added = matmul(kernel, charges_ref[at])
         return [times[own : own + 1] * added[span_of(own)] for own in range(LEAVES)]
 
     weights = []
@@ -268,22 +275,23 @@
         rows = charge_refs[spot][points : points + LANES, :].astype(f32)
         weights.append((jnp.where(low_half, rows, swapped(rows)), devices[spot]))
         sums_ref[devices[spot] // BRANCH] += rows
-        if makes:
+        if makes_far:
             skeletons.append(skeleton_refs[spot][skeletons_at : skeletons_at + dim, :])
-    if last:
+    if last and adds:
         for sub in range(n_sub):
             rows = sums_ref[sub]
             weights.append((jnp.where(low_half, swapped(rows), rows), len(ring) * CORES + sub))
-            if makes:
+            if makes_far:
                 skeletons.append(upper_points_ref[:, sub * LANES : (sub + 1) * LANES])
-    if far_spots and makes:
+    if makes_far:
         put_sources(far_ref, jnp.concatenate(skeletons, axis=1))
 
     def far_part(core):
         table = table_of(core)
         kernel = values(
+            makes_far,
             core,
-            far_ref if makes else None,
+            far_ref if makes_far else None,
             None if far_kept_ref is None else far_kept_ref.at[core],
         )
         added = []
@@ -311,12 +319,13 @@
 
         def step(core, carry):
             parts = [near_part(core, spot, core, None) for spot in near_spots]
-            add(core, parts + ([far_part(core)] if far_spots else []))
+            if adds:
+                add(core, parts + ([far_part(core)] if far_spots else []))
             return carry
 
         lax.fori_loop(0, CORES, step, 0)
 
-    if last:
+    if last and adds:
         for core, ref in enumerate(half_refs):
             both = [total_ref[core, span_of(leaf), :] for leaf in range(LEAVES)]
             both = [total + swapped(total) for total in both]
@@ -405,20 +414,21 @@
         return jax.ShapeDtypeStruct(extent, dtype)
 
     maps = [leaf_interp, node_interp, upper_interp]
-    sibling_coords = to_sibling(coords)
-    coords_next = one_way(coords), other_way(coords)
-    message, own, table = call(
+    message, places, own = call(
         message_kernel,
         [near_lists, far_lists, coords, charges, node_points] + maps,
         [
             shape(points + LANES + dim, LANES),
+            shape(dim, local),
             shape(points + LANES + dim + LEAVES * points // LANES * dim + 16, LANES),
-            shape(8, LANES, dtype=f32),
         ],
         streamed=range(2, 8),
         vmem_mib=60,
     )
-    sibling_table = to_sibling(table)
+    sibling_own = to_sibling(own)
+    sent = one_way(message), other_way(message)
+    places = gated(places, sibling_own)
+    coords_next = one_way(places), other_way(places)
 
     total_shape = shape(CORES, local, LANES, dtype=f32)
     sums_shape = shape(n_sub, LANES, LANES, dtype=f32)
@@ -429,61 +439,58 @@
     kept_bytes = 2 * points * (steps * local + CORES * LEAVES * (chips + n_sub) * LANES)
     keeping = kept_bytes <= KEPT_MIB * 2**20
 
-    def stage(near_spots, far_spots, given, carried, last, mode, begins=False):
-        first = not carried
-        makes = mode != "use"
+    def stage(near_spots, far_spots, given, carried, last, near, far, begins=False):
+        adds = near != "only"
+        first = not carried and adds
+        makes_near, makes_far = near != "use", far != "use" and bool(far_spots)
         spots = sorted(set(near_spots) | set(far_spots))
         if begins:
-            args = [sibling_table, own, sibling_coords]
+            args = [own, sibling_own]
         else:
             args = list(given["tables"])
-            if makes:
-                args += [given["places"][spot] for spot in near_spots]
-                args += [given["skeletons"][spot] for spot in far_spots]
-            args += [given["charges"][spot] for spot in spots]
-            if makes:
-                args += [given["targets"]]
-            else:
-                args += [given["near"][spot] for spot in near_spots]
-                args += [given["far"][far_spots]] if far_spots else []
+            args += [given["places"][spot] for spot in near_spots] if makes_near else []
+            args += [given["skeletons"][spot] for spot in far_spots] if makes_far else []
+            args += [given["charges"][spot] for spot in spots] if adds else []
+        args += [given["near"][spot] for spot in near_spots] if near == "use" else []
+        args += [given["far"][far_spots]] if far == "use" and far_spots else []
+        args += [given["targets"]] if (makes_near or makes_far) and not begins else []
         carried_at = len(args)
         args += carried
-        args += [upper_points] if last and makes else []
+        args += [upper_points] if last and makes_far else []
         far_width = max(LANES, LANES * (len(far_spots) + (n_sub if last else 0)))
-        scratch = [
-            pltpu.VMEM((LEAVES, far_width, LANES), bf16),
-            pltpu.VMEM((len(near_spots), points, LANES), bf16),
-        ]
-        if makes:
+        scratch = []
+        if adds:
             scratch += [
-                pltpu.VMEM((len(near_spots), LANES, points), bf16),
-                pltpu.VMEM((LANES, far_width), bf16),
+                pltpu.VMEM((LEAVES, far_width, LANES), bf16),
+                pltpu.VMEM((len(near_spots), points, LANES), bf16),
             ]
+        scratch += [pltpu.VMEM((len(near_spots), LANES, points), bf16)] if makes_near else []
+        scratch += [pltpu.VMEM((LANES, far_width), bf16)] if makes_far else []
         names, outs = [], []
         if begins:
-            names += ["targets", "table"]
-            outs += [targets_shape, shape(8, LANES, dtype=f32)]
-        if mode == "keep":
+            names += ["targets", "mine", "other"]
+            outs += [targets_shape] + [shape(8, LANES, dtype=f32)] * CORES
+        if near in ("keep", "only"):
             names += [("near", spot) for spot in near_spots]
             outs += [shape(LEAVES + 1 if first else CORES, local, points) for _ in near_spots]
-            names += [("far", far_spots)] if far_spots else []
-            outs += [shape(CORES, local, far_width)] if far_spots else []
-        if last:
+        if far == "keep" and far_spots:
+            names += [("far", far_spots)]
+            outs += [shape(CORES, local, far_width)]
+        if last and adds:
             names += ["mine", "other"]
             outs += [half_shape, half_shape]
         aliases = {carried_at + k: len(outs) + k for k in range(len(carried))}
-        names += ["total", "sums"]
-        outs += [total_shape, sums_shape]
-        static = (
-            ring, near_spots, far_spots, n_sub, dim, points, begins, first, last, mode
-        )
+        if adds:
+            names += ["total", "sums"]
+            outs += [total_shape, sums_shape]
+        static = (ring, near_spots, far_spots, n_sub, dim, points, begins, first, last, near, far)
         results = call(
             functools.partial(stage_kernel, static),
             args,
             outs,
             scratch=scratch,
             aliases=aliases,
-            flops=len(near_spots) * (2 if makes else 1) * 10**9,
+            flops=len(near_spots) * (2 if makes_near else 1) * 10**9,
         )
         return dict(zip(names, results))
 
@@ -491,7 +498,7 @@
         return (spot - 1, spot) if spot % 2 == 0 and spot > 0 else (spot,)
 
     mode = "keep" if keeping else "make"
-    given = {"near": {}, "far": {}, "places": {0: coords}, "skeletons": {0: message}}
+    given = {"near": {}, "far": {}, "places": {0: places}, "skeletons": {0: message}}
     given["charges"] = given["skeletons"]
 
     def keep_results(results):
@@ -500,22 +507,28 @@
                 given[name[0]][name[1]] = value
         return [results["total"], results["sums"]]
 
-    sent = one_way(message), other_way(message)
-    results = stage((0,), (0,), given, [], False, mode, begins=True)
-    given["targets"], given["tables"] = results["targets"], [results["table"], sibling_table]
+    results = stage((0,), (0,), given, [], False, mode, mode, begins=True)
+    given["targets"], given["tables"] = results["targets"], [results["mine"], results["other"]]
     carried = keep_results(results)
     for hop in range(1, chips // 2):
         final = hop == chips // 2 - 1
         spots = (2 * hop - 1, 2 * hop)
+        coords_next = [gated(part, carried[1]) for part in coords_next]
+        sent = [gated(part, carried[1]) for part in sent]
         for at, spot in enumerate(spots):
             given["places"][spot] = coords_next[at]
             given["skeletons"][spot] = sent[at]
         coords_next = one_way(coords_next[0]), None if final else other_way(coords_next[1])
         sent = one_way(sent[0]), None if final else other_way(sent[1])
-        carried = keep_results(stage(spots, spots, given, carried, False, mode))
+        carried = keep_results(stage(spots, spots, given, carried, False, mode, mode))
     across = (chips - 1,)
     given["places"][across[0]], given["skeletons"][across[0]] = coords_next[0], sent[0]
-    results = stage(across, across, given, carried, True, mode)
+    near = mode
+    if keeping:
+        near = "use"
+        results = stage(across, (), given, [], False, "only", "use")
+        given["near"][across[0]] = results[("near", across[0])]
+    results = stage(across, across, given, carried, True, near, mode)
     keep_results(results)
     first, message, again = call(
         joined_kernel,
@@ -532,7 +545,7 @@
         given["charges"][spot] = message
         last = spot == chips - 1
         far_spots = () if spot % 2 == 1 and not last else far_spots_of(spot)
-        results = stage((spot,), far_spots, given, carried, last, mode)
+        results = stage((spot,), far_spots, given, carried, last, mode, mode)
         carried = [results["total"], results["sums"]]
         return results
 

time: 68.5 us -> 68.9 us (level)
  starting transfers between devices: 27.5 us -> 25.2 us
  waiting for transfers between devices: 9.59 us -> 11.7 us
    ppermute x2, waiting for transfers between devices: 0.01 us -> 1.64 us  [on_device(): sent = (one_way(message), other_way(message))]
    ppermute x4 -> x3, starting transfers between devices: 3.65 us -> 2.48 us  [the longest x2 2.03 us: on_device(): coords_next = (one_way(places), other_way(places))]
    ppermute x3, waiting for transfers between devices: 0.01 us -> 0.83 us  [on_device(): one_way(coords_next[0])]
    pallas_call x16 -> x17, Pallas kernels: 29.4 us -> 30 us  [call(): pl.pallas_call(body, grid=(1,), out_shape=out_shapes, in_specs=specs, out...]
  transfers between devices with their start and end apart: 25 -> 24, of which waited for: 9 -> 11; matrix products, arithmetic and copies ran while one was open for 0% -> 0% of each run, Pallas kernels for 34% -> 32%
where the time goes in v12:
time: 68.9 us; the launch traced here: 68.8 us
  Pallas kernels  30 us (44%)
  starting transfers between devices  25.2 us (37%)
  waiting for transfers between devices  11.7 us (17%)
  local copies, waits for them, and re-layouts  0.99 us (1%)
  between operations  0.89 us (1%)
    pallas_call x17, Pallas kernels, call(): pl.pallas_call(body, grid=(1,), out_shape=out_shapes, in_specs=specs, out...  30 us
    ppermute x3, starting transfers between devices, on_device(): one_next = one_way(one)  6.95 us
    ppermute x5, starting transfers between devices, on_device(): sent = (one_way(sent[0]), None if final else other_way(sent[1]))  5.42 us
    ppermute x3, starting transfers between devices, on_device(): one_way(coords_next[0])  3.8 us
    ppermute x3, waiting for transfers between devices, on_device(): one_next = one_way(one)  3.42 us
    ppermute x2, waiting for transfers between devices, on_device(): to_sibling(results['other'])  3.04 us
    ppermute x2, starting transfers between devices, on_device(): sent = (one_way(message), other_way(message))  2.63 us
    ppermute x1, waiting for transfers between devices, on_device(): one = one_way(message)  2.25 us
  transfers between devices with their start and end apart: 24, of which 11 were waited for; matrix products, arithmetic and copies ran while one was open for 0% of the time, Pallas kernels for 32%

profile of v12, /device:TPU:0, one launch (start us, length us, event | category | flops | bytes accessed | tf_op | source)
XLA Modules:
  0.0 68.8 jit_solution(12000990934630375464)
XLA Ops:
  0.6 2.4 %shard_map.104 = (bf16[704,128]{1,0:T(8,128)(2,1)}, bf16[64,1024]{1,0:T(8,128)(2,1)}, bf16[1232,128]{1,0:T(8,128)(2,1)}) custom-call(s32[2,16]{1,0:T(2,128)} %near_ref.1, s32[2,32]{1,0:T(2,128)} %far_ref.1, bf16[64,1024]{1,0:T(8,128)(2,1)} %coords_ref.1, bf16[64,1024]{1,0:T(8,128)(2,1)} %charges_ref.1, bf16[64,128]{1,0:T(8,128)(2,1)} %points_ref.1, ...), custom_call_target="tpu_custom_call" | custom-call | bytes 639360 | tf_op jit(solution)/shard_map/pallas_call | solution.py:362
  3.4 2.5 %collective-permute-start.5 = (bf16[704,128]{1,0:T(8,128)(2,1)}, bf16[704,128]{1,0:T(8,128)(2,1)S(1)}, u32[]{:S(2)}, u32[]{:S(2)}) collective-permute-start(bf16[704,128]{1,0:T(8,128)(2,1)} %get-tuple-element.52), channel_id=1, source_target_pairs={{0,2},{1,5},{4,0},{5,9},{8,4},{9,13},{12,8},{13,15},{14,12},{15,11... | collective-permute-start | bytes 540680 | tf_op jit(solution)/shard_map/ppermute | solution.py:429
  6.1 1.9 %collective-permute-start.4 = (bf16[64,1024]{1,0:T(8,128)(2,1)}, bf16[64,1024]{1,0:T(8,128)(2,1)S(1)}, u32[]{:S(2)}, u32[]{:S(2)}) collective-permute-start(bf16[64,1024]{1,0:T(8,128)(2,1)} %shard_map.107), channel_id=1, source_target_pairs={{0,2},{1,5},{4,0},{5,9},{8,4},{9,13},{12,8},{13,15},{14,12},{15,11... | collective-permute-start | bytes 393224 | tf_op jit(solution)/shard_map/ppermute | solution.py:431
  9.1 2.1 %shard_map.105 = (bf16[2,1024,128]{2,1,0:T(8,128)(2,1)S(1)}, f32[8,128]{1,0:T(8,128)S(1)}, f32[8,128]{1,0:T(8,128)S(1)}, bf16[3,1024,512]{2,1,0:T(8,128)(2,1)S(1...) custom-call(bf16[1232,128]{1,0:T(8,128)(2,1)S(1)} %copy-done.4, ...), custom_call_target="tpu_custom_call" | custom-call | flops 2000000000 | bytes 630784 | tf_op jit(solution)/shard_map/pallas_call | solution.py:362
  11.2 1.6 %collective-permute-done.1.message_ref = bf16[704,128]{1,0:T(8,128)(2,1)S(1)} collective-permute-done((bf16[704,128]{1,0:T(8,128)(2,1)}, bf16[704,128]{1,0:T(8,128)(2,1)S(1)}, u32[]{:S(2)}, u32[]{:S(2)}) %collective-permute-start.1) | collective-permute-done | bytes 180256 | tf_op jit(solution)/shard_map/ppermute | solution.py:429
  16.9 3.4 %shard_map.111 = (bf16[2,1024,512]{2,1,0:T(8,128)(2,1)S(1)}, bf16[2,1024,512]{2,1,0:T(8,128)(2,1)S(1)}, bf16[2,1024,256]{2,1,0:T(8,128)(2,1)S(1)}, f32[2,1024,128]{2,1,0:T(8,128)S(1)}, f32[1,128,128]{2,1,0:T(8,128)S(1)}) custom-call(f32[8,128]{1,0:T(8,128)S(1)} %get-tuple-element.50.refs_0_, ...), custom_call_target="tpu_custom_call", output_to_operand_aliasing={{3}: (9, {}), {4}: (10, {})} | custom-call | flops 4000000000 | bytes 2629632 | tf_op jit(solution)/shard_map/pallas_call | solution.py:362
  22.4 1.3 %collective-permute-start.11 = (bf16[64,1024]{1,0:T(8,128)(2,1)S(1)}, bf16[64,1024]{1,0:T(8,128)(2,1)S(1)}, u32[]{:S(2)}, u32[]{:S(2)}) collective-permute-start(bf16[64,1024]{1,0:T(8,128)(2,1)S(1)} %shard_map.113.refs_2_), channel_id=1, source_target_pairs={{0,4},{1,3},{4,8},{5,1},{8,12},{9,5},{12,14},{13,9},{14,10},{15,13... | collective-permute-start | bytes 393224 | tf_op jit(solution)/shard_map/ppermute | solution.py:521
  24.4 3.4 %shard_map.116 = (bf16[2,1024,512]{2,1,0:T(8,128)(2,1)S(1)}, bf16[2,1024,512]{2,1,0:T(8,128)(2,1)S(1)}, bf16[2,1024,256]{2,1,0:T(8,128)(2,1)S(1)}, f32[2,1024,128]{2,1,0:T(8,128)S(1)}, f32[1,128,128]{2,1,0:T(8,128)S(1)}) custom-call(f32[8,128]{1,0:T(8,128)S(1)} %get-tuple-element.50.refs_0_, ...), custom_call_target="tpu_custom_call", output_to_operand_aliasing={{3}: (9, {}), {4}: (10, {})} | custom-call | flops 4000000000 | bytes 2629632 | tf_op jit(solution)/shard_map/pallas_call | solution.py:362
  27.9 1.3 %collective-permute-start.10 = (bf16[704,128]{1,0:T(8,128)(2,1)S(1)}, bf16[704,128]{1,0:T(8,128)(2,1)S(1)}, u32[]{:S(2)}, u32[]{:S(2)}) collective-permute-start(bf16[704,128]{1,0:T(8,128)(2,1)S(1)} %shard_map.117.refs_4_.refs_6_), channel_id=1, source_target_pairs={{0,4},{1,3},{4,8},{5,1},{8,12},{9,5},{12,14},{13,9},{14,10},{15,13... | collective-permute-start | bytes 540680 | tf_op jit(solution)/shard_map/ppermute | solution.py:522
  29.8 1.4 %collective-permute-start.12 = (bf16[64,1024]{1,0:T(8,128)(2,1)S(1)}, bf16[64,1024]{1,0:T(8,128)(2,1)S(1)}, u32[]{:S(2)}, u32[]{:S(2)}) collective-permute-start(bf16[64,1024]{1,0:T(8,128)(2,1)S(1)} %shard_map.118.refs_2_), channel_id=1, source_target_pairs={{0,4},{1,3},{4,8},{5,1},{8,12},{9,5},{12,14},{13,9},{14,10},{15,13... | collective-permute-start | bytes 393224 | tf_op jit(solution)/shard_map/ppermute | solution.py:521
  31.2 3.4 %shard_map.122 = (bf16[2,1024,512]{2,1,0:T(8,128)(2,1)S(1)}, bf16[2,1024,512]{2,1,0:T(8,128)(2,1)S(1)}, bf16[2,1024,256]{2,1,0:T(8,128)(2,1)S(1)}, f32[2,1024,128]{2,1,0:T(8,128)S(1)}, f32[1,128,128]{2,1,0:T(8,128)S(1)}) custom-call(f32[8,128]{1,0:T(8,128)S(1)} %get-tuple-element.50.refs_0_, ...), custom_call_target="tpu_custom_call", output_to_operand_aliasing={{3}: (9, {}), {4}: (10, {})} | custom-call | flops 4000000000 | bytes 2629632 | tf_op jit(solution)/shard_map/pallas_call | solution.py:362
  36.0 2.1 %shard_map.123 = (bf16[2,1024,256]{2,1,0:T(8,128)(2,1)S(1)}, f32[512,128]{1,0:T(8,128)S(1)}, f32[512,128]{1,0:T(8,128)S(1)}, f32[2,1024,128]{2,1,0:T(8,128)S(1)}, f32[1,128,128]{2,1,0:T(8,128)S(1)}) custom-call(f32[8,128]{1,0:T(8,128)S(1)} %get-tuple-element.50.refs_0_, ...), custom_call_target="tpu_custom_call", output_to_operand_aliasing={{3}: (6, {}), {4}: (7, {})} | custom-call | flops 1000000000 | bytes 4120576 | tf_op jit(solution)/shard_map/pallas_call | solution.py:362
  38.2 1.5 %collective-permute-done.15.other_ref = f32[512,128]{1,0:T(8,128)S(1)} collective-permute-done((f32[512,128]{1,0:T(8,128)S(1)}, f32[512,128]{1,0:T(8,128)S(1)}, u32[]{:S(2)}, u32[]{:S(2)}) %collective-permute-start.15) | collective-permute-done | bytes 262176 | tf_op jit(solution)/shard_map/ppermute | solution.py:535
  40.6 1.4 %collective-permute-start.16 = (bf16[640,128]{1,0:T(8,128)(2,1)S(1)}, bf16[640,128]{1,0:T(8,128)(2,1)S(1)}, u32[]{:S(2)}, u32[]{:S(2)}) collective-permute-start(bf16[640,128]{1,0:T(8,128)(2,1)S(1)} %get-tuple-element.66.refs_2_), channel_id=1, source_target_pairs={{0,4},{1,3},{4,8},{5,1},{8,12},{9,5},{12,14},{13,9},{14,10},{15,13... | collective-permute-start | bytes 491528 | tf_op jit(solution)/shard_map/ppermute | solution.py:552
  43.7 2.3 %collective-permute-done.16.refs_2_ = bf16[640,128]{1,0:T(8,128)(2,1)S(1)} collective-permute-done((bf16[640,128]{1,0:T(8,128)(2,1)S(1)}, bf16[640,128]{1,0:T(8,128)(2,1)S(1)}, u32[]{:S(2)}, u32[]{:S(2)}) %collective-permute-start.16) | collective-permute-done | bytes 163872 | tf_op jit(solution)/shard_map/ppermute | solution.py:552
  46.0 2.5 %collective-permute-start.17 = (bf16[640,128]{1,0:T(8,128)(2,1)S(1)}, bf16[640,128]{1,0:T(8,128)(2,1)S(1)}, u32[]{:S(2)}, u32[]{:S(2)}) collective-permute-start(bf16[640,128]{1,0:T(8,128)(2,1)S(1)} %collective-permute-done.16.refs_2_), channel_id=1, source_target_pairs={{0,4},{1,3},{4,8},{5,1},{8,12},{9,5},{12,14},{13,9},{14,10},{15,13... | collective-permute-start | bytes 491528 | tf_op jit(solution)/shard_map/ppermute | solution.py:556
  49.7 1.5 %shard_map.129 = (f32[2,1024,128]{2,1,0:T(8,128)S(1)}, f32[1,128,128]{2,1,0:T(8,128)S(1)}) custom-call(f32[8,128]{1,0:T(8,128)S(1)} %get-tuple-element.50.refs_0_, f32[8,128]{1,0:T(8,128)S(1)} %get-tuple-element.51.refs_1_, bf16[640,128]{1,0:T(8,128)(2,1)S(1)} %collective-permute-done.16.refs_2_, ...), custom_call_target="tpu_custom_call", output_to_operand_aliasing={{0}: (6, {}), {1}: (7, {})} | custom-call | flops 1000000000 | bytes 4595712 | tf_op jit(solution)/shard_map/pallas_call | solution.py:362
  51.1 1.7 %collective-permute-done.17.refs_2_ = bf16[640,128]{1,0:T(8,128)(2,1)S(1)} collective-permute-done((bf16[640,128]{1,0:T(8,128)(2,1)S(1)}, bf16[640,128]{1,0:T(8,128)(2,1)S(1)}, u32[]{:S(2)}, u32[]{:S(2)}) %collective-permute-start.17) | collective-permute-done | bytes 163872 | tf_op jit(solution)/shard_map/ppermute | solution.py:556
  52.8 2.5 %collective-permute-start.18 = (bf16[640,128]{1,0:T(8,128)(2,1)S(1)}, bf16[640,128]{1,0:T(8,128)(2,1)S(1)}, u32[]{:S(2)}, u32[]{:S(2)}) collective-permute-start(bf16[640,128]{1,0:T(8,128)(2,1)S(1)} %collective-permute-done.17.refs_2_), channel_id=1, source_target_pairs={{0,4},{1,3},{4,8},{5,1},{8,12},{9,5},{12,14},{13,9},{14,10},{15,13... | collective-permute-start | bytes 491528 | tf_op jit(solution)/shard_map/ppermute | solution.py:556
  56.6 1.5 %shard_map.132 = (f32[2,1024,128]{2,1,0:T(8,128)S(1)}, f32[1,128,128]{2,1,0:T(8,128)S(1)}) custom-call(f32[8,128]{1,0:T(8,128)S(1)} %get-tuple-element.50.refs_0_, f32[8,128]{1,0:T(8,128)S(1)} %get-tuple-element.51.refs_1_, bf16[640,128]{1,0:T(8,128)(2,1)S(1)} %collective-permute-done.17.refs_2_, ...), custom_call_target="tpu_custom_call", output_to_operand_aliasing={{0}: (6, {}), {1}: (7, {})} | custom-call | flops 1000000000 | bytes 4595712 | tf_op jit(solution)/shard_map/pallas_call | solution.py:362
  59.3 2.0 %collective-permute-start.19 = (bf16[640,128]{1,0:T(8,128)(2,1)S(1)}, bf16[640,128]{1,0:T(8,128)(2,1)S(1)}, u32[]{:S(2)}, u32[]{:S(2)}) collective-permute-start(bf16[640,128]{1,0:T(8,128)(2,1)S(1)} %collective-permute-done.18.refs_2_), channel_id=1, source_target_pairs={{0,4},{1,3},{4,8},{5,1},{8,12},{9,5},{12,14},{13,9},{14,10},{15,13... | collective-permute-start | bytes 491528 | tf_op jit(solution)/shard_map/ppermute | solution.py:556
  62.6 1.5 %shard_map.134 = (f32[2,1024,128]{2,1,0:T(8,128)S(1)}, f32[1,128,128]{2,1,0:T(8,128)S(1)}) custom-call(f32[8,128]{1,0:T(8,128)S(1)} %get-tuple-element.50.refs_0_, f32[8,128]{1,0:T(8,128)S(1)} %get-tuple-element.51.refs_1_, bf16[640,128]{1,0:T(8,128)(2,1)S(1)} %collective-permute-done.18.refs_2_, ...), custom_call_target="tpu_custom_call", output_to_operand_aliasing={{0}: (6, {}), {1}: (7, {})} | custom-call | flops 1000000000 | bytes 4595712 | tf_op jit(solution)/shard_map/pallas_call | solution.py:362
  64.6 1.8 %shard_map.135 = (f32[512,128]{1,0:T(8,128)S(1)}, f32[512,128]{1,0:T(8,128)S(1)}, f32[2,1024,128]{2,1,0:T(8,128)S(1)}, f32[1,128,128]{2,1,0:T(8,128)S(1)}) custom-call(f32[8,128]{1,0:T(8,128)S(1)} %get-tuple-element.50.refs_0_, f32[8,128]{1,0:T(8,128)S(1)} %get-tuple-element.51.refs_1_, ...), custom_call_target="tpu_custom_call", output_to_operand_aliasing={{2}: (5, {}), {3}: (6, {})} | custom-call | flops 1000000000 | bytes 4431872 | tf_op jit(solution)/shard_map/pallas_call | solution.py:362
  66.5 1.5 %collective-permute-done.23.other_ref = f32[512,128]{1,0:T(8,128)S(1)} collective-permute-done((f32[512,128]{1,0:T(8,128)S(1)}, f32[512,128]{1,0:T(8,128)S(1)}, u32[]{:S(2)}, u32[]{:S(2)}) %collective-permute-start.23) | collective-permute-done | bytes 262176 | tf_op jit(solution)/shard_map/ppermute | solution.py:566
  (67 shorter events, 19.5 us)
Async XLA Ops:
  3.0 3.1 %collective-permute-start = (bf16[1232,128]{1,0:T(8,128)(2,1)}, bf16[1232,128]{1,0:T(8,128)(2,1)S(1)}, u32[]{:S(2)}, u32[]{:S(2)}) collective-permute-start(bf16[1232,128]{1,0:T(8,128)(2,1)} %get-tuple-element.49.refs_0_), channel_id=1, source_target_pairs={{0,1},{1,0},{2,3},{3,2},{4,5},{5,4},{6,7},{7,6},{8,9},{9,8},{10,11... | collective-permute-start | bytes 946184 | tf_op jit(solution)/shard_map/ppermute | solution.py:428
  3.4 10.2 %collective-permute-start.5 = (bf16[704,128]{1,0:T(8,128)(2,1)}, bf16[704,128]{1,0:T(8,128)(2,1)S(1)}, u32[]{:S(2)}, u32[]{:S(2)}) collective-permute-start(bf16[704,128]{1,0:T(8,128)(2,1)} %get-tuple-element.52), channel_id=1, source_target_pairs={{0,2},{1,5},{4,0},{5,9},{8,4},{9,13},{12,8},{13,15},{14,12},{15,11... | collective-permute-start | bytes 540680 | tf_op jit(solution)/shard_map/ppermute | solution.py:429
  6.0 6.8 %collective-permute-start.1 = (bf16[704,128]{1,0:T(8,128)(2,1)}, bf16[704,128]{1,0:T(8,128)(2,1)S(1)}, u32[]{:S(2)}, u32[]{:S(2)}) collective-permute-start(bf16[704,128]{1,0:T(8,128)(2,1)} %get-tuple-element.52), channel_id=1, source_target_pairs={{0,4},{1,3},{4,8},{5,1},{8,12},{9,5},{12,14},{13,9},{14,10},{15,13... | collective-permute-start | bytes 540680 | tf_op jit(solution)/shard_map/ppermute | solution.py:429
  6.1 9.9 %collective-permute-start.4 = (bf16[64,1024]{1,0:T(8,128)(2,1)}, bf16[64,1024]{1,0:T(8,128)(2,1)S(1)}, u32[]{:S(2)}, u32[]{:S(2)}) collective-permute-start(bf16[64,1024]{1,0:T(8,128)(2,1)} %shard_map.107), channel_id=1, source_target_pairs={{0,2},{1,5},{4,0},{5,9},{8,4},{9,13},{12,8},{13,15},{14,12},{15,11... | collective-permute-start | bytes 393224 | tf_op jit(solution)/shard_map/ppermute | solution.py:431
  8.0 6.8 %collective-permute-start.3 = (bf16[64,1024]{1,0:T(8,128)(2,1)}, bf16[64,1024]{1,0:T(8,128)(2,1)S(1)}, u32[]{:S(2)}, u32[]{:S(2)}) collective-permute-start(bf16[64,1024]{1,0:T(8,128)(2,1)} %shard_map.107), channel_id=1, source_target_pairs={{0,4},{1,3},{4,8},{5,1},{8,12},{9,5},{12,14},{13,9},{14,10},{15,13... | collective-permute-start | bytes 393224 | tf_op jit(solution)/shard_map/ppermute | solution.py:431
  12.8 7.5 %collective-permute-start.2 = (bf16[704,128]{1,0:T(8,128)(2,1)S(1)}, bf16[704,128]{1,0:T(8,128)(2,1)S(1)}, u32[]{:S(2)}, u32[]{:S(2)}) collective-permute-start(bf16[704,128]{1,0:T(8,128)(2,1)S(1)} %shard_map.106.refs_4_.refs_6_), channel_id=1, source_target_pairs={{0,4},{1,3},{4,8},{5,1},{8,12},{9,5},{12,14},{13,9},{14,10},{15,13... | collective-permute-start | bytes 540680 | tf_op jit(solution)/shard_map/ppermute | solution.py:522
  13.6 7.9 %collective-permute-start.9 = (bf16[704,128]{1,0:T(8,128)(2,1)S(1)}, bf16[704,128]{1,0:T(8,128)(2,1)S(1)}, u32[]{:S(2)}, u32[]{:S(2)}) collective-permute-start(bf16[704,128]{1,0:T(8,128)(2,1)S(1)} %shard_map.110.refs_5_.refs_7_), channel_id=1, source_target_pairs={{0,2},{1,5},{4,0},{5,9},{8,4},{9,13},{12,8},{13,15},{14,12},{15,11... | collective-permute-start | bytes 540680 | tf_op jit(solution)/shard_map/ppermute | solution.py:522
  14.8 7.6 %collective-permute-start.7 = (bf16[64,1024]{1,0:T(8,128)(2,1)S(1)}, bf16[64,1024]{1,0:T(8,128)(2,1)S(1)}, u32[]{:S(2)}, u32[]{:S(2)}) collective-permute-start(bf16[64,1024]{1,0:T(8,128)(2,1)S(1)} %shard_map.108.refs_2_), channel_id=1, source_target_pairs={{0,4},{1,3},{4,8},{5,1},{8,12},{9,5},{12,14},{13,9},{14,10},{15,13... | collective-permute-start | bytes 393224 | tf_op jit(solution)/shard_map/ppermute | solution.py:521
  16.0 7.7 %collective-permute-start.8 = (bf16[64,1024]{1,0:T(8,128)(2,1)S(1)}, bf16[64,1024]{1,0:T(8,128)(2,1)S(1)}, u32[]{:S(2)}, u32[]{:S(2)}) collective-permute-start(bf16[64,1024]{1,0:T(8,128)(2,1)S(1)} %shard_map.109.refs_3_), channel_id=1, source_target_pairs={{0,2},{1,5},{4,0},{5,9},{8,4},{9,13},{12,8},{13,15},{14,12},{15,11... | collective-permute-start | bytes 393224 | tf_op jit(solution)/shard_map/ppermute | solution.py:521
  20.3 7.6 %collective-permute-start.6 = (bf16[704,128]{1,0:T(8,128)(2,1)S(1)}, bf16[704,128]{1,0:T(8,128)(2,1)S(1)}, u32[]{:S(2)}, u32[]{:S(2)}) collective-permute-start(bf16[704,128]{1,0:T(8,128)(2,1)S(1)} %shard_map.112.refs_4_.refs_6_), channel_id=1, source_target_pairs={{0,4},{1,3},{4,8},{5,1},{8,12},{9,5},{12,14},{13,9},{14,10},{15,13... | collective-permute-start | bytes 540680 | tf_op jit(solution)/shard_map/ppermute | solution.py:522
  21.5 7.7 %collective-permute-start.14 = (bf16[704,128]{1,0:T(8,128)(2,1)S(1)}, bf16[704,128]{1,0:T(8,128)(2,1)S(1)}, u32[]{:S(2)}, u32[]{:S(2)}) collective-permute-start(bf16[704,128]{1,0:T(8,128)(2,1)S(1)} %shard_map.115.refs_5_.refs_7_), channel_id=1, source_target_pairs={{0,2},{1,5},{4,0},{5,9},{8,4},{9,13},{12,8},{13,15},{14,12},{15,11... | collective-permute-start | bytes 540680 | tf_op jit(solution)/shard_map/ppermute | solution.py:522
  22.4 7.4 %collective-permute-start.11 = (bf16[64,1024]{1,0:T(8,128)(2,1)S(1)}, bf16[64,1024]{1,0:T(8,128)(2,1)S(1)}, u32[]{:S(2)}, u32[]{:S(2)}) collective-permute-start(bf16[64,1024]{1,0:T(8,128)(2,1)S(1)} %shard_map.113.refs_2_), channel_id=1, source_target_pairs={{0,4},{1,3},{4,8},{5,1},{8,12},{9,5},{12,14},{13,9},{14,10},{15,13... | collective-permute-start | bytes 393224 | tf_op jit(solution)/shard_map/ppermute | solution.py:521
  23.7 7.5 %collective-permute-start.13 = (bf16[64,1024]{1,0:T(8,128)(2,1)S(1)}, bf16[64,1024]{1,0:T(8,128)(2,1)S(1)}, u32[]{:S(2)}, u32[]{:S(2)}) collective-permute-start(bf16[64,1024]{1,0:T(8,128)(2,1)S(1)} %shard_map.114.refs_3_), channel_id=1, source_target_pairs={{0,2},{1,5},{4,0},{5,9},{8,4},{9,13},{12,8},{13,15},{14,12},{15,11... | collective-permute-start | bytes 393224 | tf_op jit(solution)/shard_map/ppermute | solution.py:521
  27.9 8.1 %collective-permute-start.10 = (bf16[704,128]{1,0:T(8,128)(2,1)S(1)}, bf16[704,128]{1,0:T(8,128)(2,1)S(1)}, u32[]{:S(2)}, u32[]{:S(2)}) collective-permute-start(bf16[704,128]{1,0:T(8,128)(2,1)S(1)} %shard_map.117.refs_4_.refs_6_), channel_id=1, source_target_pairs={{0,4},{1,3},{4,8},{5,1},{8,12},{9,5},{12,14},{13,9},{14,10},{15,13... | collective-permute-start | bytes 540680 | tf_op jit(solution)/shard_map/ppermute | solution.py:522
  29.8 5.0 %collective-permute-start.12 = (bf16[64,1024]{1,0:T(8,128)(2,1)S(1)}, bf16[64,1024]{1,0:T(8,128)(2,1)S(1)}, u32[]{:S(2)}, u32[]{:S(2)}) collective-permute-start(bf16[64,1024]{1,0:T(8,128)(2,1)S(1)} %shard_map.118.refs_2_), channel_id=1, source_target_pairs={{0,4},{1,3},{4,8},{5,1},{8,12},{9,5},{12,14},{13,9},{14,10},{15,13... | collective-permute-start | bytes 393224 | tf_op jit(solution)/shard_map/ppermute | solution.py:521
  38.1 1.6 %collective-permute-start.15 = (f32[512,128]{1,0:T(8,128)S(1)}, f32[512,128]{1,0:T(8,128)S(1)}, u32[]{:S(2)}, u32[]{:S(2)}) collective-permute-start(f32[512,128]{1,0:T(8,128)S(1)} %get-tuple-element.64), channel_id=1, source_target_pairs={{0,1},{1,0},{2,3},{3,2},{4,5},{5,4},{6,7},{7,6},{8,9},{9,8},{10,11... | collective-permute-start | bytes 786440 | tf_op jit(solution)/shard_map/ppermute | solution.py:535
  40.6 5.4 %collective-permute-start.16 = (bf16[640,128]{1,0:T(8,128)(2,1)S(1)}, bf16[640,128]{1,0:T(8,128)(2,1)S(1)}, u32[]{:S(2)}, u32[]{:S(2)}) collective-permute-start(bf16[640,128]{1,0:T(8,128)(2,1)S(1)} %get-tuple-element.66.refs_2_), channel_id=1, source_target_pairs={{0,4},{1,3},{4,8},{5,1},{8,12},{9,5},{12,14},{13,9},{14,10},{15,13... | collective-permute-start | bytes 491528 | tf_op jit(solution)/shard_map/ppermute | solution.py:552
  43.1 6.5 %collective-permute-start.20 = (bf16[640,128]{1,0:T(8,128)(2,1)S(1)}, bf16[640,128]{1,0:T(8,128)(2,1)S(1)}, u32[]{:S(2)}, u32[]{:S(2)}) collective-permute-start(bf16[640,128]{1,0:T(8,128)(2,1)S(1)} %shard_map.126), channel_id=1, source_target_pairs={{0,2},{1,5},{4,0},{5,9},{8,4},{9,13},{12,8},{13,15},{14,12},{15,11... | collective-permute-start | bytes 491528 | tf_op jit(solution)/shard_map/ppermute | solution.py:554
  46.0 6.8 %collective-permute-start.17 = (bf16[640,128]{1,0:T(8,128)(2,1)S(1)}, bf16[640,128]{1,0:T(8,128)(2,1)S(1)}, u32[]{:S(2)}, u32[]{:S(2)}) collective-permute-start(bf16[640,128]{1,0:T(8,128)(2,1)S(1)} %collective-permute-done.16.refs_2_), channel_id=1, source_target_pairs={{0,4},{1,3},{4,8},{5,1},{8,12},{9,5},{12,14},{13,9},{14,10},{15,13... | collective-permute-start | bytes 491528 | tf_op jit(solution)/shard_map/ppermute | solution.py:556
  49.6 7.0 %collective-permute-start.21 = (bf16[640,128]{1,0:T(8,128)(2,1)S(1)}, bf16[640,128]{1,0:T(8,128)(2,1)S(1)}, u32[]{:S(2)}, u32[]{:S(2)}) collective-permute-start(bf16[640,128]{1,0:T(8,128)(2,1)S(1)} %shard_map.128.refs_3_), channel_id=1, source_target_pairs={{0,2},{1,5},{4,0},{5,9},{8,4},{9,13},{12,8},{13,15},{14,12},{15,11... | collective-permute-start | bytes 491528 | tf_op jit(solution)/shard_map/ppermute | solution.py:561
  52.8 6.4 %collective-permute-start.18 = (bf16[640,128]{1,0:T(8,128)(2,1)S(1)}, bf16[640,128]{1,0:T(8,128)(2,1)S(1)}, u32[]{:S(2)}, u32[]{:S(2)}) collective-permute-start(bf16[640,128]{1,0:T(8,128)(2,1)S(1)} %collective-permute-done.17.refs_2_), channel_id=1, source_target_pairs={{0,4},{1,3},{4,8},{5,1},{8,12},{9,5},{12,14},{13,9},{14,10},{15,13... | collective-permute-start | bytes 491528 | tf_op jit(solution)/shard_map/ppermute | solution.py:556
  56.6 6.1 %collective-permute-start.22 = (bf16[640,128]{1,0:T(8,128)(2,1)S(1)}, bf16[640,128]{1,0:T(8,128)(2,1)S(1)}, u32[]{:S(2)}, u32[]{:S(2)}) collective-permute-start(bf16[640,128]{1,0:T(8,128)(2,1)S(1)} %shard_map.131.refs_3_), channel_id=1, source_target_pairs={{0,2},{1,5},{4,0},{5,9},{8,4},{9,13},{12,8},{13,15},{14,12},{15,11... | collective-permute-start | bytes 491528 | tf_op jit(solution)/shard_map/ppermute | solution.py:561
  59.3 5.3 %collective-permute-start.19 = (bf16[640,128]{1,0:T(8,128)(2,1)S(1)}, bf16[640,128]{1,0:T(8,128)(2,1)S(1)}, u32[]{:S(2)}, u32[]{:S(2)}) collective-permute-start(bf16[640,128]{1,0:T(8,128)(2,1)S(1)} %collective-permute-done.18.refs_2_), channel_id=1, source_target_pairs={{0,4},{1,3},{4,8},{5,1},{8,12},{9,5},{12,14},{13,9},{14,10},{15,13... | collective-permute-start | bytes 491528 | tf_op jit(solution)/shard_map/ppermute | solution.py:556
  66.4 1.6 %collective-permute-start.23 = (f32[512,128]{1,0:T(8,128)S(1)}, f32[512,128]{1,0:T(8,128)S(1)}, u32[]{:S(2)}, u32[]{:S(2)}) collective-permute-start(f32[512,128]{1,0:T(8,128)S(1)} %get-tuple-element.95), channel_id=1, source_target_pairs={{0,1},{1,0},{2,3},{3,2},{4,5},{5,4},{6,7},{7,6},{8,9},{9,8},{10,11... | collective-permute-start | bytes 786440 | tf_op jit(solution)/shard_map/ppermute | solution.py:566
  (5 other events, 13.6 us)

commit v13 on v12

--- a/solution.py
+++ b/solution.py
@@ -91,13 +91,18 @@
     return table
 
 
+def place_on(ring):
+    chip = lax.axis_index("leaf") // CORES
+    place = jnp.int32(0)
+    for at, other in enumerate(ring):
+        place = jnp.where(chip == other, at, place)
+    return place
+
+
 def device_of(ring, spot):
     chips = len(ring)
-    me = lax.axis_index("leaf")
-    core = me % CORES
-    place = jnp.int32(0)
-    for at, chip in enumerate(ring):
-        place = jnp.where(me // CORES == chip, at, place)
+    core = lax.axis_index("leaf") % CORES
+    place = place_on(ring)
     hop = (spot + 1) // 2
     step = hop if spot % 2 == 0 else -hop
     met = (place + step * (1 - 2 * core) + chips) % chips
@@ -117,7 +122,6 @@
     node_ref,
     upper_ref,
     message_ref,
-    places_ref,
     local_ref,
 ):
     dim, local = coords_ref.shape
@@ -137,7 +141,6 @@
     for block in range(local // LANES):
         local_ref[place : place + dim, :] = coords_ref[:, block * LANES : (block + 1) * LANES]
         place += dim
-    places_ref[...] = coords_ref[...]
     table = count_rows(near_ref, far_ref)
     local_ref[place : place + 16, :] = jnp.concatenate([table, table], axis=0).astype(bf16)
 
@@ -162,7 +165,7 @@
 
 
 def stage_kernel(stage, *refs):
-    ring, near_spots, far_spots, n_sub, dim, points, begins, first, last, near, far = stage
+    ring, near_spots, blocks_at, far_spots, n_sub, dim, points, begins, first, last, near, far = stage
     refs = list(refs)
     spots = sorted(set(near_spots) | set(far_spots))
     makes_near, makes_far = near != "use", far != "use" and bool(far_spots)
@@ -172,7 +175,9 @@
         charge_refs = skeleton_refs = {spots[0]: local_refs[0]}
     else:
         table_refs = refs.pop(0), refs.pop(0)
-        place_refs = {spot: refs.pop(0) for spot in near_spots} if makes_near else {}
+        place_refs = {}
+        for spot, indices in zip(near_spots, blocks_at):
+            place_refs[spot] = [refs.pop(0).at[index] for index in indices]
         skeleton_refs = {spot: refs.pop(0) for spot in far_spots} if makes_far else {}
         charge_refs = {spot: refs.pop(0) for spot in spots} if adds else {}
     kept_refs = {}
@@ -216,7 +221,14 @@
     def points_of(spot, leaf):
         if begins:
             return local_points(local_refs[0], leaf)
-        return place_refs[spot][:, span_of(leaf)]
+        found = [ref[:, span_of(leaf)] for ref in place_refs[spot]]
+        if len(found) == 1:
+            return found[0]
+        hop = (spot + 1) // 2
+        first_to_even = (place_on(ring) + hop) % 2 == 1
+        chosen = jnp.where(first_to_even == (spot % 2 == 0), 1.0, 0.0).astype(f32)
+        chosen = jnp.full((1, 1), chosen, f32)
+        return found[0] * chosen.astype(bf16) + found[1] * (1.0 - chosen).astype(bf16)
 
     if begins:
         begin = skeletons_at + dim + LEAVES * blocks * dim
@@ -414,12 +426,21 @@
         return jax.ShapeDtypeStruct(extent, dtype)
 
     maps = [leaf_interp, node_interp, upper_interp]
-    message, places, own = call(
+    def swap(turn):
+        pairs = []
+        for place, chip in enumerate(ring):
+            for core in range(CORES):
+                step = 1 if (place + core + turn) % 2 == 0 else -1
+                pairs.append((chip * CORES + core, ring[(place + step) % chips] * CORES + core))
+        return functools.partial(lax.ppermute, axis_name="leaf", perm=pairs)
+
+    mine = coords[None]
+    partner = swap(0)(mine)
+    message, own = call(
         message_kernel,
         [near_lists, far_lists, coords, charges, node_points] + maps,
         [
             shape(points + LANES + dim, LANES),
-            shape(dim, local),
             shape(points + LANES + dim + LEAVES * points // LANES * dim + 16, LANES),
         ],
         streamed=range(2, 8),
@@ -427,8 +448,7 @@
     )
     sibling_own = to_sibling(own)
     sent = one_way(message), other_way(message)
-    places = gated(places, sibling_own)
-    coords_next = one_way(places), other_way(places)
+    pair = swap(1)(jnp.concatenate([mine, partner], axis=0))
 
     total_shape = shape(CORES, local, LANES, dtype=f32)
     sums_shape = shape(n_sub, LANES, LANES, dtype=f32)
@@ -441,6 +461,7 @@
 
     def stage(near_spots, far_spots, given, carried, last, near, far, begins=False):
         adds = near != "only"
+        blocks_at = ((),) * len(near_spots)
         first = not carried and adds
         makes_near, makes_far = near != "use", far != "use" and bool(far_spots)
         spots = sorted(set(near_spots) | set(far_spots))
@@ -448,7 +469,9 @@
             args = [own, sibling_own]
         else:
             args = list(given["tables"])
-            args += [given["places"][spot] for spot in near_spots] if makes_near else []
+            if makes_near:
+                blocks_at = tuple(tuple(at for _, at in given["places"][spot]) for spot in near_spots)
+                args += [block for spot in near_spots for block, _ in given["places"][spot]]
             args += [given["skeletons"][spot] for spot in far_spots] if makes_far else []
             args += [given["charges"][spot] for spot in spots] if adds else []
         args += [given["near"][spot] for spot in near_spots] if near == "use" else []
@@ -483,7 +506,8 @@
         if adds:
             names += ["total", "sums"]
             outs += [total_shape, sums_shape]
-        static = (ring, near_spots, far_spots, n_sub, dim, points, begins, first, last, near, far)
+        static = (ring, near_spots, blocks_at, far_spots, n_sub, dim, points)
+        static += (begins, first, last, near, far)
         results = call(
             functools.partial(stage_kernel, static),
             args,
@@ -498,7 +522,7 @@
         return (spot - 1, spot) if spot % 2 == 0 and spot > 0 else (spot,)
 
     mode = "keep" if keeping else "make"
-    given = {"near": {}, "far": {}, "places": {0: places}, "skeletons": {0: message}}
+    given = {"near": {}, "far": {}, "places": {0: [(mine, 0)]}, "skeletons": {0: message}}
     given["charges"] = given["skeletons"]
 
     def keep_results(results):
@@ -510,19 +534,24 @@
     results = stage((0,), (0,), given, [], False, mode, mode, begins=True)
     given["targets"], given["tables"] = results["targets"], [results["mine"], results["other"]]
     carried = keep_results(results)
+    arrivals = [(partner, 0), (pair, 0), (pair, 1)]
     for hop in range(1, chips // 2):
         final = hop == chips // 2 - 1
         spots = (2 * hop - 1, 2 * hop)
-        coords_next = [gated(part, carried[1]) for part in coords_next]
         sent = [gated(part, carried[1]) for part in sent]
+        if not final:
+            pair = gated(pair, carried[1])
+            arrivals[-2:] = [(pair, 0), (pair, 1)]
         for at, spot in enumerate(spots):
-            given["places"][spot] = coords_next[at]
+            given["places"][spot] = arrivals[2 * hop - 2 : 2 * hop]
             given["skeletons"][spot] = sent[at]
-        coords_next = one_way(coords_next[0]), None if final else other_way(coords_next[1])
         sent = one_way(sent[0]), None if final else other_way(sent[1])
+        if not final:
+            pair = swap(hop + 1)(pair)
+            arrivals += [(pair, 0), (pair, 1)]
         carried = keep_results(stage(spots, spots, given, carried, False, mode, mode))
     across = (chips - 1,)
-    given["places"][across[0]], given["skeletons"][across[0]] = coords_next[0], sent[0]
+    given["places"][across[0]], given["skeletons"][across[0]] = arrivals[-1:], sent[0]
     near = mode
     if keeping:
         near = "use"

time: 68.9 us -> 74.4 us (1.080)
  waiting for transfers between devices: 11.7 us -> 17.5 us
  starting transfers between devices: 25.2 us -> 24 us
  other arithmetic: 0 us -> 0.93 us
    ppermute x7 -> x4, waiting for transfers between devices: 0.84 us -> 4.21 us  [the longest x2 3.4 us: on_device(): pair = swap(hop + 1)(pair)]
    ppermute x1, starting transfers between devices: 1.43 us -> 3.02 us  [on_device(): one = one_way(message)]
    ppermute x2, waiting for transfers between devices: 1.64 us -> 3.16 us  [on_device(): sent = (one_way(message), other_way(message))]
    ppermute x3, waiting for transfers between devices: 3.42 us -> 2.03 us  [on_device(): one_next = one_way(one)]
    ppermute x7 -> x4, starting transfers between devices: 7.44 us -> 6.32 us  [the longest x1 3.09 us: on_device(): partner = swap(0)(mine)]
    concatenate x0 -> x1, other arithmetic: none -> 0.93 us  [on_device(): pair = swap(1)(jnp.concatenate([mine, partner], axis=0))]
    ppermute x1, waiting for transfers between devices: 2.25 us -> 3.07 us  [on_device(): one = one_way(message)]
    ppermute x5, waiting for transfers between devices: 0.01 us -> 0.82 us  [on_device(): sent = (one_way(sent[0]), None if final else other_way(sent[1]))]
  transfers between devices with their start and end apart: 24 -> 21, of which waited for: 11 -> 13; matrix products, arithmetic and copies ran while one was open for 0% -> 1% of each run, Pallas kernels for 32% -> 33%
where the time goes in v13:
time: 74.4 us; the launch traced here: 74.3 us
  Pallas kernels  30 us (40%)
  starting transfers between devices  24 us (32%)
  waiting for transfers between devices  17.5 us (24%)
  local copies, waits for them, and re-layouts  0.99 us (1%)
  other arithmetic  0.93 us (1%)
  between operations  0.87 us (1%)
    pallas_call x17, Pallas kernels, call(): pl.pallas_call(body, grid=(1,), out_shape=out_shapes, in_specs=specs, out...  30 us
    ppermute x3, starting transfers between devices, on_device(): one_next = one_way(one)  6.51 us
    ppermute x5, starting transfers between devices, on_device(): sent = (one_way(sent[0]), None if final else other_way(sent[1]))  5.53 us
    ppermute x2, waiting for transfers between devices, on_device(): pair = swap(hop + 1)(pair)  3.4 us
    ppermute x2, waiting for transfers between devices, on_device(): sent = (one_way(message), other_way(message))  3.16 us
    ppermute x1, starting transfers between devices, on_device(): partner = swap(0)(mine)  3.09 us
    ppermute x1, waiting for transfers between devices, on_device(): one = one_way(message)  3.07 us
    ppermute x2, waiting for transfers between devices, on_device(): to_sibling(results['other'])  3.04 us
  transfers between devices with their start and end apart: 21, of which 13 were waited for; matrix products, arithmetic and copies ran while one was open for 1% of the time, Pallas kernels for 33%

profile of v13, /device:TPU:0, one launch (start us, length us, event | category | flops | bytes accessed | tf_op | source)
XLA Modules:
  0.0 74.3 jit_solution(4363489892501706811)
XLA Ops:
  0.6 3.1 %collective-permute-start.3 = (bf16[1,64,1024]{2,1,0:T(8,128)(2,1)}, bf16[1,64,1024]{2,1,0:T(8,128)(2,1)S(1)}, u32[]{:S(2)}, u32[]{:S(2)}) collective-permute-start(bf16[1,64,1024]{2,1,0:T(8,128)(2,1)} %bitcast.1), channel_id=1, source_target_pairs={{0,4},{1,3},{4,0},{5,9},{8,12},{9,5},{12,8},{13,15},{14,10},{15,13... | collective-permute-start | bytes 393224 | tf_op jit(solution)/shard_map/ppermute | solution.py:438
  3.7 2.3 %shard_map.104 = (bf16[704,128]{1,0:T(8,128)(2,1)}, bf16[1232,128]{1,0:T(8,128)(2,1)}) custom-call(s32[2,16]{1,0:T(2,128)} %near_ref.1, s32[2,32]{1,0:T(2,128)} %far_ref.1, bf16[64,1024]{1,0:T(8,128)(2,1)} %coords_ref.1, bf16[64,1024]{1,0:T(8,128)(2,1)} %charges_ref.1, bf16[64,128]{1,0:T(8,128)(2,1)} %points_ref.1, bf16[1024,128]{1,0:T(8,128)(2,1)} %leaf_ref.3, ...), custom_call_target="tpu_custom_call" | custom-call | bytes 639360 | tf_op jit(solution)/shard_map/pallas_call | solution.py:374
  7.8 2.0 %collective-permute-start.4 = (bf16[2,64,1024]{2,1,0:T(8,128)(2,1)S(1)}, bf16[2,64,1024]{2,1,0:T(8,128)(2,1)S(1)}, u32[]{:S(2)}, u32[]{:S(2)}) collective-permute-start(bf16[2,64,1024]{2,1,0:T(8,128)(2,1)S(1)} %pad_maximum_fusion), channel_id=1, source_target_pairs={{0,2},{1,5},{4,8},{5,1},{8,4},{9,13},{12,14},{13,9},{14,12},{15,11... | collective-permute-start | bytes 786440 | tf_op jit(solution)/shard_map/ppermute | solution.py:451
  9.9 2.0 %collective-permute-start.1 = (bf16[704,128]{1,0:T(8,128)(2,1)}, bf16[704,128]{1,0:T(8,128)(2,1)S(1)}, u32[]{:S(2)}, u32[]{:S(2)}) collective-permute-start(bf16[704,128]{1,0:T(8,128)(2,1)} %get-tuple-element.51), channel_id=1, source_target_pairs={{0,4},{1,3},{4,8},{5,1},{8,12},{9,5},{12,14},{13,9},{14,10},{15,13... | collective-permute-start | bytes 540680 | tf_op jit(solution)/shard_map/ppermute | solution.py:450
  12.8 2.1 %shard_map.105 = (bf16[2,1024,128]{2,1,0:T(8,128)(2,1)S(1)}, f32[8,128]{1,0:T(8,128)S(1)}, f32[8,128]{1,0:T(8,128)S(1)}, bf16[3,1024,512]{2,1,0:T(8,128)(2,1)S(1...) custom-call(bf16[1232,128]{1,0:T(8,128)(2,1)S(1)} %copy-done.4, ...), custom_call_target="tpu_custom_call" | custom-call | flops 2000000000 | bytes 630784 | tf_op jit(solution)/shard_map/pallas_call | solution.py:374
  14.9 3.2 %collective-permute-done.1.message_ref = bf16[704,128]{1,0:T(8,128)(2,1)S(1)} collective-permute-done((bf16[704,128]{1,0:T(8,128)(2,1)}, bf16[704,128]{1,0:T(8,128)(2,1)S(1)}, u32[]{:S(2)}, u32[]{:S(2)}) %collective-permute-start.1) | collective-permute-done | bytes 180256 | tf_op jit(solution)/shard_map/ppermute | solution.py:450
  21.3 3.4 %shard_map.109 = (bf16[2,1024,512]{2,1,0:T(8,128)(2,1)S(1)}, bf16[2,1024,512]{2,1,0:T(8,128)(2,1)S(1)}, bf16[2,1024,256]{2,1,0:T(8,128)(2,1)S(1)}, f32[2,1024,128]{2,1,0:T(8,128)S(1)}, f32[1,128,128]{2,1,0:T(8,128)S(1)}) custom-call(f32[8,128]{1,0:T(8,128)S(1)} %get-tuple-element.49.refs_0_, ...), custom_call_target="tpu_custom_call", output_to_operand_aliasing={{3}: (11, {}), {4}: (12, {})} | custom-call | flops 4000000000 | bytes 3153920 | tf_op jit(solution)/shard_map/pallas_call | solution.py:374
  27.6 2.0 %collective-permute-done.7.message_ref = bf16[2,64,1024]{2,1,0:T(8,128)(2,1)S(1)} collective-permute-done((bf16[2,64,1024]{2,1,0:T(8,128)(2,1)S(1)}, bf16[2,64,1024]{2,1,0:T(8,128)(2,1)S(1)}, u32[]{:S(2)}, u32[]{:S(2)}) %collective-permute-start.7) | collective-permute-done | bytes 262176 | tf_op jit(solution)/shard_map/ppermute | solution.py:550
  29.6 3.4 %shard_map.113 = (bf16[2,1024,512]{2,1,0:T(8,128)(2,1)S(1)}, bf16[2,1024,512]{2,1,0:T(8,128)(2,1)S(1)}, bf16[2,1024,256]{2,1,0:T(8,128)(2,1)S(1)}, f32[2,1024,128]{2,1,0:T(8,128)S(1)}, f32[1,128,128]{2,1,0:T(8,128)S(1)}) custom-call(f32[8,128]{1,0:T(8,128)S(1)} %get-tuple-element.49.refs_0_, ...), custom_call_target="tpu_custom_call", output_to_operand_aliasing={{3}: (11, {}), {4}: (12, {})} | custom-call | flops 4000000000 | bytes 3416064 | tf_op jit(solution)/shard_map/pallas_call | solution.py:374
  33.0 1.5 %collective-permute-start.9 = (bf16[704,128]{1,0:T(8,128)(2,1)S(1)}, bf16[704,128]{1,0:T(8,128)(2,1)S(1)}, u32[]{:S(2)}, u32[]{:S(2)}) collective-permute-start(bf16[704,128]{1,0:T(8,128)(2,1)S(1)} %shard_map.114.refs_6_.refs_8_), channel_id=1, source_target_pairs={{0,4},{1,3},{4,8},{5,1},{8,12},{9,5},{12,14},{13,9},{14,10},{15,13... | collective-permute-start | bytes 540680 | tf_op jit(solution)/shard_map/ppermute | solution.py:548
  35.9 3.4 %shard_map.117 = (bf16[2,1024,512]{2,1,0:T(8,128)(2,1)S(1)}, bf16[2,1024,512]{2,1,0:T(8,128)(2,1)S(1)}, bf16[2,1024,256]{2,1,0:T(8,128)(2,1)S(1)}, f32[2,1024,128]{2,1,0:T(8,128)S(1)}, f32[1,128,128]{2,1,0:T(8,128)S(1)}) custom-call(f32[8,128]{1,0:T(8,128)S(1)} %get-tuple-element.49.refs_0_, ...), custom_call_target="tpu_custom_call", output_to_operand_aliasing={{3}: (11, {}), {4}: (12, {})} | custom-call | flops 4000000000 | bytes 3416064 | tf_op jit(solution)/shard_map/pallas_call | solution.py:374
  40.5 2.1 %shard_map.118 = (bf16[2,1024,256]{2,1,0:T(8,128)(2,1)S(1)}, f32[512,128]{1,0:T(8,128)S(1)}, f32[512,128]{1,0:T(8,128)S(1)}, f32[2,1024,128]{2,1,0:T(8,128)S(1)}, f32[1,128,128]{2,1,0:T(8,128)S(1)}) custom-call(f32[8,128]{1,0:T(8,128)S(1)} %get-tuple-element.49.refs_0_, ...), custom_call_target="tpu_custom_call", output_to_operand_aliasing={{3}: (6, {}), {4}: (7, {})} | custom-call | flops 1000000000 | bytes 4120576 | tf_op jit(solution)/shard_map/pallas_call | solution.py:374
  42.7 1.5 %collective-permute-done.12.other_ref = f32[512,128]{1,0:T(8,128)S(1)} collective-permute-done((f32[512,128]{1,0:T(8,128)S(1)}, f32[512,128]{1,0:T(8,128)S(1)}, u32[]{:S(2)}, u32[]{:S(2)}) %collective-permute-start.12) | collective-permute-done | bytes 262176 | tf_op jit(solution)/shard_map/ppermute | solution.py:564
  45.1 3.0 %collective-permute-start.13 = (bf16[640,128]{1,0:T(8,128)(2,1)S(1)}, bf16[640,128]{1,0:T(8,128)(2,1)S(1)}, u32[]{:S(2)}, u32[]{:S(2)}) collective-permute-start(bf16[640,128]{1,0:T(8,128)(2,1)S(1)} %get-tuple-element.64.refs_2_), channel_id=1, source_target_pairs={{0,4},{1,3},{4,8},{5,1},{8,12},{9,5},{12,14},{13,9},{14,10},{15,13... | collective-permute-start | bytes 491528 | tf_op jit(solution)/shard_map/ppermute | solution.py:581
  49.3 3.1 %collective-permute-done.13.refs_2_ = bf16[640,128]{1,0:T(8,128)(2,1)S(1)} collective-permute-done((bf16[640,128]{1,0:T(8,128)(2,1)S(1)}, bf16[640,128]{1,0:T(8,128)(2,1)S(1)}, u32[]{:S(2)}, u32[]{:S(2)}) %collective-permute-start.13) | collective-permute-done | bytes 163872 | tf_op jit(solution)/shard_map/ppermute | solution.py:581
  52.4 2.5 %collective-permute-start.14 = (bf16[640,128]{1,0:T(8,128)(2,1)S(1)}, bf16[640,128]{1,0:T(8,128)(2,1)S(1)}, u32[]{:S(2)}, u32[]{:S(2)}) collective-permute-start(bf16[640,128]{1,0:T(8,128)(2,1)S(1)} %collective-permute-done.13.refs_2_), channel_id=1, source_target_pairs={{0,4},{1,3},{4,8},{5,1},{8,12},{9,5},{12,14},{13,9},{14,10},{15,13... | collective-permute-start | bytes 491528 | tf_op jit(solution)/shard_map/ppermute | solution.py:585
  56.1 1.5 %shard_map.124 = (f32[2,1024,128]{2,1,0:T(8,128)S(1)}, f32[1,128,128]{2,1,0:T(8,128)S(1)}) custom-call(f32[8,128]{1,0:T(8,128)S(1)} %get-tuple-element.49.refs_0_, f32[8,128]{1,0:T(8,128)S(1)} %get-tuple-element.50.refs_1_, bf16[640,128]{1,0:T(8,128)(2,1)S(1)} %collective-permute-done.13.refs_2_, ...), custom_call_target="tpu_custom_call", output_to_operand_aliasing={{0}: (6, {}), {1}: (7, {})} | custom-call | flops 1000000000 | bytes 4595712 | tf_op jit(solution)/shard_map/pallas_call | solution.py:374
  57.5 1.5 %collective-permute-done.14.refs_2_ = bf16[640,128]{1,0:T(8,128)(2,1)S(1)} collective-permute-done((bf16[640,128]{1,0:T(8,128)(2,1)S(1)}, bf16[640,128]{1,0:T(8,128)(2,1)S(1)}, u32[]{:S(2)}, u32[]{:S(2)}) %collective-permute-start.14) | collective-permute-done | bytes 163872 | tf_op jit(solution)/shard_map/ppermute | solution.py:585
  59.0 2.2 %collective-permute-start.15 = (bf16[640,128]{1,0:T(8,128)(2,1)S(1)}, bf16[640,128]{1,0:T(8,128)(2,1)S(1)}, u32[]{:S(2)}, u32[]{:S(2)}) collective-permute-start(bf16[640,128]{1,0:T(8,128)(2,1)S(1)} %collective-permute-done.14.refs_2_), channel_id=1, source_target_pairs={{0,4},{1,3},{4,8},{5,1},{8,12},{9,5},{12,14},{13,9},{14,10},{15,13... | collective-permute-start | bytes 491528 | tf_op jit(solution)/shard_map/ppermute | solution.py:585
  62.9 1.5 %shard_map.127 = (f32[2,1024,128]{2,1,0:T(8,128)S(1)}, f32[1,128,128]{2,1,0:T(8,128)S(1)}) custom-call(f32[8,128]{1,0:T(8,128)S(1)} %get-tuple-element.49.refs_0_, f32[8,128]{1,0:T(8,128)S(1)} %get-tuple-element.50.refs_1_, bf16[640,128]{1,0:T(8,128)(2,1)S(1)} %collective-permute-done.14.refs_2_, ...), custom_call_target="tpu_custom_call", output_to_operand_aliasing={{0}: (6, {}), {1}: (7, {})} | custom-call | flops 1000000000 | bytes 4595712 | tf_op jit(solution)/shard_map/pallas_call | solution.py:374
  64.8 1.8 %collective-permute-start.16 = (bf16[640,128]{1,0:T(8,128)(2,1)S(1)}, bf16[640,128]{1,0:T(8,128)(2,1)S(1)}, u32[]{:S(2)}, u32[]{:S(2)}) collective-permute-start(bf16[640,128]{1,0:T(8,128)(2,1)S(1)} %collective-permute-done.15.refs_2_), channel_id=1, source_target_pairs={{0,4},{1,3},{4,8},{5,1},{8,12},{9,5},{12,14},{13,9},{14,10},{15,13... | collective-permute-start | bytes 491528 | tf_op jit(solution)/shard_map/ppermute | solution.py:585
  68.4 1.5 %shard_map.129 = (f32[2,1024,128]{2,1,0:T(8,128)S(1)}, f32[1,128,128]{2,1,0:T(8,128)S(1)}) custom-call(f32[8,128]{1,0:T(8,128)S(1)} %get-tuple-element.49.refs_0_, f32[8,128]{1,0:T(8,128)S(1)} %get-tuple-element.50.refs_1_, bf16[640,128]{1,0:T(8,128)(2,1)S(1)} %collective-permute-done.15.refs_2_, ...), custom_call_target="tpu_custom_call", output_to_operand_aliasing={{0}: (6, {}), {1}: (7, {})} | custom-call | flops 1000000000 | bytes 4595712 | tf_op jit(solution)/shard_map/pallas_call | solution.py:374
  70.1 1.8 %shard_map.130 = (f32[512,128]{1,0:T(8,128)S(1)}, f32[512,128]{1,0:T(8,128)S(1)}, f32[2,1024,128]{2,1,0:T(8,128)S(1)}, f32[1,128,128]{2,1,0:T(8,128)S(1)}) custom-call(f32[8,128]{1,0:T(8,128)S(1)} %get-tuple-element.49.refs_0_, f32[8,128]{1,0:T(8,128)S(1)} %get-tuple-element.50.refs_1_, ...), custom_call_target="tpu_custom_call", output_to_operand_aliasing={{2}: (5, {}), {3}: (6, {})} | custom-call | flops 1000000000 | bytes 4431872 | tf_op jit(solution)/shard_map/pallas_call | solution.py:374
  72.0 1.5 %collective-permute-done.20.other_ref = f32[512,128]{1,0:T(8,128)S(1)} collective-permute-done((f32[512,128]{1,0:T(8,128)S(1)}, f32[512,128]{1,0:T(8,128)S(1)}, u32[]{:S(2)}, u32[]{:S(2)}) %collective-permute-start.20) | collective-permute-done | bytes 262176 | tf_op jit(solution)/shard_map/ppermute | solution.py:595
  (57 shorter events, 19.7 us)
Async XLA Ops:
  0.6 6.2 %collective-permute-start.3 = (bf16[1,64,1024]{2,1,0:T(8,128)(2,1)}, bf16[1,64,1024]{2,1,0:T(8,128)(2,1)S(1)}, u32[]{:S(2)}, u32[]{:S(2)}) collective-permute-start(bf16[1,64,1024]{2,1,0:T(8,128)(2,1)} %bitcast.1), channel_id=1, source_target_pairs={{0,4},{1,3},{4,0},{5,9},{8,12},{9,5},{12,8},{13,15},{14,10},{15,13... | collective-permute-start | bytes 393224 | tf_op jit(solution)/shard_map/ppermute | solution.py:438
  6.1 5.8 %collective-permute-start = (bf16[1232,128]{1,0:T(8,128)(2,1)}, bf16[1232,128]{1,0:T(8,128)(2,1)S(1)}, u32[]{:S(2)}, u32[]{:S(2)}) collective-permute-start(bf16[1232,128]{1,0:T(8,128)(2,1)} %get-tuple-element.48.refs_0_), channel_id=1, source_target_pairs={{0,1},{1,0},{2,3},{3,2},{4,5},{5,4},{6,7},{7,6},{8,9},{9,8},{10,11... | collective-permute-start | bytes 946184 | tf_op jit(solution)/shard_map/ppermute | solution.py:449
  7.8 12.3 %collective-permute-start.4 = (bf16[2,64,1024]{2,1,0:T(8,128)(2,1)S(1)}, bf16[2,64,1024]{2,1,0:T(8,128)(2,1)S(1)}, u32[]{:S(2)}, u32[]{:S(2)}) collective-permute-start(bf16[2,64,1024]{2,1,0:T(8,128)(2,1)S(1)} %pad_maximum_fusion), channel_id=1, source_target_pairs={{0,2},{1,5},{4,8},{5,1},{8,4},{9,13},{12,14},{13,9},{14,12},{15,11... | collective-permute-start | bytes 786440 | tf_op jit(solution)/shard_map/ppermute | solution.py:451
  9.8 9.0 %collective-permute-start.5 = (bf16[704,128]{1,0:T(8,128)(2,1)}, bf16[704,128]{1,0:T(8,128)(2,1)S(1)}, u32[]{:S(2)}, u32[]{:S(2)}) collective-permute-start(bf16[704,128]{1,0:T(8,128)(2,1)} %get-tuple-element.51), channel_id=1, source_target_pairs={{0,2},{1,5},{4,0},{5,9},{8,4},{9,13},{12,8},{13,15},{14,12},{15,11... | collective-permute-start | bytes 540680 | tf_op jit(solution)/shard_map/ppermute | solution.py:450
  9.9 8.2 %collective-permute-start.1 = (bf16[704,128]{1,0:T(8,128)(2,1)}, bf16[704,128]{1,0:T(8,128)(2,1)S(1)}, u32[]{:S(2)}, u32[]{:S(2)}) collective-permute-start(bf16[704,128]{1,0:T(8,128)(2,1)} %get-tuple-element.51), channel_id=1, source_target_pairs={{0,4},{1,3},{4,8},{5,1},{8,12},{9,5},{12,14},{13,9},{14,10},{15,13... | collective-permute-start | bytes 540680 | tf_op jit(solution)/shard_map/ppermute | solution.py:450
  18.1 7.5 %collective-permute-start.2 = (bf16[704,128]{1,0:T(8,128)(2,1)S(1)}, bf16[704,128]{1,0:T(8,128)(2,1)S(1)}, u32[]{:S(2)}, u32[]{:S(2)}) collective-permute-start(bf16[704,128]{1,0:T(8,128)(2,1)S(1)} %shard_map.106.refs_6_.refs_8_), channel_id=1, source_target_pairs={{0,4},{1,3},{4,8},{5,1},{8,12},{9,5},{12,14},{13,9},{14,10},{15,13... | collective-permute-start | bytes 540680 | tf_op jit(solution)/shard_map/ppermute | solution.py:548
  18.9 7.4 %collective-permute-start.8 = (bf16[704,128]{1,0:T(8,128)(2,1)S(1)}, bf16[704,128]{1,0:T(8,128)(2,1)S(1)}, u32[]{:S(2)}, u32[]{:S(2)}) collective-permute-start(bf16[704,128]{1,0:T(8,128)(2,1)S(1)} %shard_map.108.refs_7_.refs_9_), channel_id=1, source_target_pairs={{0,2},{1,5},{4,0},{5,9},{8,4},{9,13},{12,8},{13,15},{14,12},{15,11... | collective-permute-start | bytes 540680 | tf_op jit(solution)/shard_map/ppermute | solution.py:548
  20.1 9.4 %collective-permute-start.7 = (bf16[2,64,1024]{2,1,0:T(8,128)(2,1)S(1)}, bf16[2,64,1024]{2,1,0:T(8,128)(2,1)S(1)}, u32[]{:S(2)}, u32[]{:S(2)}) collective-permute-start(bf16[2,64,1024]{2,1,0:T(8,128)(2,1)S(1)} %shard_map.107.refs_3_.refs_5_.refs_2_.refs_4_), channel_id=1, source_target_pairs={{0,4},{1,3},{4,0},{5,9},{8,12},{9,5},{12,8},{13,15},{14,10},{15,13... | collective-permute-start | bytes 786440 | tf_op jit(solution)/shard_map/ppermute | solution.py:550
  25.6 7.4 %collective-permute-start.6 = (bf16[704,128]{1,0:T(8,128)(2,1)S(1)}, bf16[704,128]{1,0:T(8,128)(2,1)S(1)}, u32[]{:S(2)}, u32[]{:S(2)}) collective-permute-start(bf16[704,128]{1,0:T(8,128)(2,1)S(1)} %shard_map.110.refs_6_.refs_8_), channel_id=1, source_target_pairs={{0,4},{1,3},{4,8},{5,1},{8,12},{9,5},{12,14},{13,9},{14,10},{15,13... | collective-permute-start | bytes 540680 | tf_op jit(solution)/shard_map/ppermute | solution.py:548
  26.2 8.2 %collective-permute-start.11 = (bf16[704,128]{1,0:T(8,128)(2,1)S(1)}, bf16[704,128]{1,0:T(8,128)(2,1)S(1)}, u32[]{:S(2)}, u32[]{:S(2)}) collective-permute-start(bf16[704,128]{1,0:T(8,128)(2,1)S(1)} %shard_map.112.refs_7_.refs_9_), channel_id=1, source_target_pairs={{0,2},{1,5},{4,0},{5,9},{8,4},{9,13},{12,8},{13,15},{14,12},{15,11... | collective-permute-start | bytes 540680 | tf_op jit(solution)/shard_map/ppermute | solution.py:548
  29.5 6.4 %collective-permute-start.10 = (bf16[2,64,1024]{2,1,0:T(8,128)(2,1)S(1)}, bf16[2,64,1024]{2,1,0:T(8,128)(2,1)S(1)}, u32[]{:S(2)}, u32[]{:S(2)}) collective-permute-start(bf16[2,64,1024]{2,1,0:T(8,128)(2,1)S(1)} %shard_map.111.refs_3_.refs_5_.refs_2_.refs_4_), channel_id=1, source_target_pairs={{0,2},{1,5},{4,8},{5,1},{8,4},{9,13},{12,14},{13,9},{14,12},{15,11... | collective-permute-start | bytes 786440 | tf_op jit(solution)/shard_map/ppermute | solution.py:550
  33.0 7.5 %collective-permute-start.9 = (bf16[704,128]{1,0:T(8,128)(2,1)S(1)}, bf16[704,128]{1,0:T(8,128)(2,1)S(1)}, u32[]{:S(2)}, u32[]{:S(2)}) collective-permute-start(bf16[704,128]{1,0:T(8,128)(2,1)S(1)} %shard_map.114.refs_6_.refs_8_), channel_id=1, source_target_pairs={{0,4},{1,3},{4,8},{5,1},{8,12},{9,5},{12,14},{13,9},{14,10},{15,13... | collective-permute-start | bytes 540680 | tf_op jit(solution)/shard_map/ppermute | solution.py:548
  40.5 3.8 %copy-start = (bf16[1024,128]{1,0:T(8,128)(2,1)S(1)}, bf16[1024,128]{1,0:T(8,128)(2,1)}, u32[]{:S(2)}) copy-start(bf16[1024,128]{1,0:T(8,128)(2,1)} %leaf_ref.3) | copy-start | bytes 786436
  40.5 3.8 %copy-start.1 = (bf16[256,128]{1,0:T(8,128)(2,1)S(1)}, bf16[256,128]{1,0:T(8,128)(2,1)}, u32[]{:S(2)}) copy-start(bf16[256,128]{1,0:T(8,128)(2,1)} %node_ref.3) | copy-start | bytes 196612
  40.5 3.8 %copy-start.2 = (bf16[128,128]{1,0:T(8,128)(2,1)S(1)}, bf16[128,128]{1,0:T(8,128)(2,1)}, u32[]{:S(2)}) copy-start(bf16[128,128]{1,0:T(8,128)(2,1)} %upper_ref.3) | copy-start | bytes 98308
  42.6 1.6 %collective-permute-start.12 = (f32[512,128]{1,0:T(8,128)S(1)}, f32[512,128]{1,0:T(8,128)S(1)}, u32[]{:S(2)}, u32[]{:S(2)}) collective-permute-start(f32[512,128]{1,0:T(8,128)S(1)} %get-tuple-element.62), channel_id=1, source_target_pairs={{0,1},{1,0},{2,3},{3,2},{4,5},{5,4},{6,7},{7,6},{8,9},{9,8},{10,11... | collective-permute-start | bytes 786440 | tf_op jit(solution)/shard_map/ppermute | solution.py:564
  45.1 7.3 %collective-permute-start.13 = (bf16[640,128]{1,0:T(8,128)(2,1)S(1)}, bf16[640,128]{1,0:T(8,128)(2,1)S(1)}, u32[]{:S(2)}, u32[]{:S(2)}) collective-permute-start(bf16[640,128]{1,0:T(8,128)(2,1)S(1)} %get-tuple-element.64.refs_2_), channel_id=1, source_target_pairs={{0,4},{1,3},{4,8},{5,1},{8,12},{9,5},{12,14},{13,9},{14,10},{15,13... | collective-permute-start | bytes 491528 | tf_op jit(solution)/shard_map/ppermute | solution.py:581
  49.3 6.7 %collective-permute-start.17 = (bf16[640,128]{1,0:T(8,128)(2,1)S(1)}, bf16[640,128]{1,0:T(8,128)(2,1)S(1)}, u32[]{:S(2)}, u32[]{:S(2)}) collective-permute-start(bf16[640,128]{1,0:T(8,128)(2,1)S(1)} %shard_map.121), channel_id=1, source_target_pairs={{0,2},{1,5},{4,0},{5,9},{8,4},{9,13},{12,8},{13,15},{14,12},{15,11... | collective-permute-start | bytes 491528 | tf_op jit(solution)/shard_map/ppermute | solution.py:583
  52.4 6.6 %collective-permute-start.14 = (bf16[640,128]{1,0:T(8,128)(2,1)S(1)}, bf16[640,128]{1,0:T(8,128)(2,1)S(1)}, u32[]{:S(2)}, u32[]{:S(2)}) collective-permute-start(bf16[640,128]{1,0:T(8,128)(2,1)S(1)} %collective-permute-done.13.refs_2_), channel_id=1, source_target_pairs={{0,4},{1,3},{4,8},{5,1},{8,12},{9,5},{12,14},{13,9},{14,10},{15,13... | collective-permute-start | bytes 491528 | tf_op jit(solution)/shard_map/ppermute | solution.py:585
  56.0 6.6 %collective-permute-start.18 = (bf16[640,128]{1,0:T(8,128)(2,1)S(1)}, bf16[640,128]{1,0:T(8,128)(2,1)S(1)}, u32[]{:S(2)}, u32[]{:S(2)}) collective-permute-start(bf16[640,128]{1,0:T(8,128)(2,1)S(1)} %shard_map.123.refs_3_), channel_id=1, source_target_pairs={{0,2},{1,5},{4,0},{5,9},{8,4},{9,13},{12,8},{13,15},{14,12},{15,11... | collective-permute-start | bytes 491528 | tf_op jit(solution)/shard_map/ppermute | solution.py:590
  59.0 5.8 %collective-permute-start.15 = (bf16[640,128]{1,0:T(8,128)(2,1)S(1)}, bf16[640,128]{1,0:T(8,128)(2,1)S(1)}, u32[]{:S(2)}, u32[]{:S(2)}) collective-permute-start(bf16[640,128]{1,0:T(8,128)(2,1)S(1)} %collective-permute-done.14.refs_2_), channel_id=1, source_target_pairs={{0,4},{1,3},{4,8},{5,1},{8,12},{9,5},{12,14},{13,9},{14,10},{15,13... | collective-permute-start | bytes 491528 | tf_op jit(solution)/shard_map/ppermute | solution.py:585
  62.6 5.8 %collective-permute-start.19 = (bf16[640,128]{1,0:T(8,128)(2,1)S(1)}, bf16[640,128]{1,0:T(8,128)(2,1)S(1)}, u32[]{:S(2)}, u32[]{:S(2)}) collective-permute-start(bf16[640,128]{1,0:T(8,128)(2,1)S(1)} %shard_map.126.refs_3_), channel_id=1, source_target_pairs={{0,2},{1,5},{4,0},{5,9},{8,4},{9,13},{12,8},{13,15},{14,12},{15,11... | collective-permute-start | bytes 491528 | tf_op jit(solution)/shard_map/ppermute | solution.py:590
  64.8 5.3 %collective-permute-start.16 = (bf16[640,128]{1,0:T(8,128)(2,1)S(1)}, bf16[640,128]{1,0:T(8,128)(2,1)S(1)}, u32[]{:S(2)}, u32[]{:S(2)}) collective-permute-start(bf16[640,128]{1,0:T(8,128)(2,1)S(1)} %collective-permute-done.15.refs_2_), channel_id=1, source_target_pairs={{0,4},{1,3},{4,8},{5,1},{8,12},{9,5},{12,14},{13,9},{14,10},{15,13... | collective-permute-start | bytes 491528 | tf_op jit(solution)/shard_map/ppermute | solution.py:585
  71.9 1.6 %collective-permute-start.20 = (f32[512,128]{1,0:T(8,128)S(1)}, f32[512,128]{1,0:T(8,128)S(1)}, u32[]{:S(2)}, u32[]{:S(2)}) collective-permute-start(f32[512,128]{1,0:T(8,128)S(1)} %get-tuple-element.93), channel_id=1, source_target_pairs={{0,1},{1,0},{2,3},{3,2},{4,5},{5,4},{6,7},{7,6},{8,9},{9,8},{10,11... | collective-permute-start | bytes 786440 | tf_op jit(solution)/shard_map/ppermute | solution.py:595
  (2 other events, 2.1 us)

commit v14 on v11

--- a/solution.py
+++ b/solution.py
@@ -225,8 +225,7 @@
         sums_ref[...] = jnp.zeros_like(sums_ref)
 
     def table_of(core):
-        mine, other = (ref[...] for ref in table_refs)
-        return jnp.where(core == 0, mine, other)
+        return table_refs[core][...]
 
     def picked(table, entry):
         return jnp.sum(jnp.where(lane == entry, table, 0.0), axis=1, keepdims=True)
@@ -242,7 +241,7 @@
     devices = {spot: device_of(ring, spot) for spot in spots}
 
     def near_part(turn, spot, core, leaf):
-        at = near_spots.index(spot)
+        at = core * len(near_spots) + near_spots.index(spot)
         table = table_of(core)
         named = [
             picked(table, devices[spot] * LEAVES + which)[0:LEAVES] for which in range(LEAVES)
@@ -292,8 +291,8 @@
                 scaled = block * picked(table, node)[LEAVES + own : LEAVES + own + 1]
                 high = scaled.astype(bf16).astype(f32)
                 rows = slice(position * LANES, (position + 1) * LANES)
-                far_charges_ref[own, rows, :] = jnp.where(low_half, high, scaled - high).astype(bf16)
-            added.append(matmul(kernel[span_of(own)], far_charges_ref[own]))
+                far_charges_ref[core * LEAVES + own, rows, :] = jnp.where(low_half, high, scaled - high).astype(bf16)
+            added.append(matmul(kernel[span_of(own)], far_charges_ref[core * LEAVES + own]))
         return added
 
     def add(core, parts):
@@ -309,12 +308,9 @@
         add(1, [near_part(LEAVES, 0, 1, None), far_part(1)])
     else:
 
-        def step(core, carry):
+        for core in range(CORES):
             parts = [near_part(core, spot, core, None) for spot in near_spots]
             add(core, parts + ([far_part(core)] if far_spots else []))
-            return carry
-
-        lax.fori_loop(0, CORES, step, 0)
 
     if last:
         for core, ref in enumerate(half_refs):
@@ -451,12 +447,12 @@
         args += [upper_points] if last and makes else []
         far_width = max(LANES, LANES * (len(far_spots) + (n_sub if last else 0)))
         scratch = [
-            pltpu.VMEM((LEAVES, far_width, LANES), bf16),
-            pltpu.VMEM((len(near_spots), points, LANES), bf16),
+            pltpu.VMEM((CORES * LEAVES, far_width, LANES), bf16),
+            pltpu.VMEM((CORES * len(near_spots), points, LANES), bf16),
         ]
         if makes:
             scratch += [
-                pltpu.VMEM((len(near_spots), LANES, points), bf16),
+                pltpu.VMEM((CORES * len(near_spots), LANES, points), bf16),
                 pltpu.VMEM((LANES, far_width), bf16),
             ]
         names, outs = [], []

time: 68.5 us -> 66.8 us (0.975)
  Pallas kernels: 29.4 us -> 25.5 us
  waiting for transfers between devices: 9.59 us -> 12.2 us
    pallas_call x16, Pallas kernels: 29.4 us -> 25.5 us  [call(): pl.pallas_call(body, grid=(1,), out_shape=out_shapes, in_specs=specs, out...]
    ppermute x3, waiting for transfers between devices: 3.05 us -> 4.95 us  [on_device(): one_next = one_way(one)]
  transfers between devices with their start and end apart: 25 -> 25, of which waited for: 9 -> 10; matrix products, arithmetic and copies ran while one was open for 0% -> 0% of each run, Pallas kernels for 34% -> 31%
where the time goes in v14:
time: 66.8 us; the launch traced here: 66.6 us
  starting transfers between devices  27.1 us (41%)
  Pallas kernels  25.5 us (38%)
  waiting for transfers between devices  12.2 us (18%)
  local copies, waits for them, and re-layouts  0.98 us (1%)
  between operations  0.84 us (1%)
    pallas_call x16, Pallas kernels, call(): pl.pallas_call(body, grid=(1,), out_shape=out_shapes, in_specs=specs, out...  25.5 us
    ppermute x3, starting transfers between devices, on_device(): one_next = one_way(one)  6.83 us
    ppermute x5, starting transfers between devices, on_device(): sent = (one_way(sent[0]), None if final else other_way(sent[1]))  5.6 us
    ppermute x3, waiting for transfers between devices, on_device(): one_next = one_way(one)  4.95 us
    ppermute x3, starting transfers between devices, on_device(): one_way(coords_next[0])  3.65 us
    ppermute x2, starting transfers between devices, on_device(): coords_next = (one_way(coords), other_way(coords))  3.14 us
    ppermute x2, waiting for transfers between devices, on_device(): to_sibling(results['other'])  3.04 us
    ppermute x2, starting transfers between devices, on_device(): sent = (one_way(message), other_way(message))  2.99 us
  transfers between devices with their start and end apart: 25, of which 10 were waited for; matrix products, arithmetic and copies ran while one was open for 0% of the time, Pallas kernels for 31%

profile of v14, /device:TPU:0, one launch (start us, length us, event | category | flops | bytes accessed | tf_op | source)
XLA Modules:
  0.0 66.6 jit_solution(11590769246697985945)
XLA Ops:
  0.6 3.0 %collective-permute-start.10 = (bf16[64,1024]{1,0:T(8,128)(2,1)}, bf16[64,1024]{1,0:T(8,128)(2,1)S(1)}, u32[]{:S(2)}, u32[]{:S(2)}) collective-permute-start(bf16[64,1024]{1,0:T(8,128)(2,1)} %coords_ref.1), channel_id=1, source_target_pairs={{0,2},{1,5},{4,0},{5,9},{8,4},{9,13},{12,8},{13,15},{14,12},{15,11... | collective-permute-start | bytes 393224 | tf_op jit(solution)/shard_map/ppermute | solution.py:405
  3.8 2.3 %shard_map.104 = (bf16[704,128]{1,0:T(8,128)(2,1)}, bf16[1232,128]{1,0:T(8,128)(2,1)}, f32[8,128]{1,0:T(8,128)}) custom-call(s32[2,16]{1,0:T(2,128)} %near_ref.1, s32[2,32]{1,0:T(2,128)} %far_ref.1, bf16[64,1024]{1,0:T(8,128)(2,1)} %coords_ref.1, bf16[64,1024]{1,0:T(8,128)(2,1)} %charges_ref.1, bf16[64,128]{1,0:T(8,128)(2,1)} %points_ref.1, ...), custom_call_target="tpu_custom_call" | custom-call | bytes 639360 | tf_op jit(solution)/shard_map/pallas_call | solution.py:349
  6.6 1.9 %collective-permute-start.13 = (bf16[704,128]{1,0:T(8,128)(2,1)}, bf16[704,128]{1,0:T(8,128)(2,1)S(1)}, u32[]{:S(2)}, u32[]{:S(2)}) collective-permute-start(bf16[704,128]{1,0:T(8,128)(2,1)} %get-tuple-element.52), channel_id=1, source_target_pairs={{0,2},{1,5},{4,0},{5,9},{8,4},{9,13},{12,8},{13,15},{14,12},{15,11... | collective-permute-start | bytes 540680 | tf_op jit(solution)/shard_map/ppermute | solution.py:499
  12.6 2.1 %shard_map.105 = (bf16[2,1024,128]{2,1,0:T(8,128)(2,1)S(1)}, f32[8,128]{1,0:T(8,128)S(1)}, bf16[3,1024,512]{2,1,0:T(8,128)(2,1)S(1)}, bf16[2,1024,128]{2,1,0:T(8...) custom-call(f32[8,128]{1,0:T(8,128)S(1)} %collective-permute-done.refs_0_.refs_1_, ...), custom_call_target="tpu_custom_call" | custom-call | flops 2000000000 | bytes 450560 | tf_op jit(solution)/shard_map/pallas_call | solution.py:349
  14.7 1.1 %collective-permute-start.14 = (bf16[704,128]{1,0:T(8,128)(2,1)S(1)}, bf16[704,128]{1,0:T(8,128)(2,1)S(1)}, u32[]{:S(2)}, u32[]{:S(2)}) collective-permute-start(bf16[704,128]{1,0:T(8,128)(2,1)S(1)} %collective-permute-done.13.refs_5_.refs_7_), channel_id=1, source_target_pairs={{0,2},{1,5},{4,0},{5,9},{8,4},{9,13},{12,8},{13,15},{14,12},{15,11... | collective-permute-start | bytes 540680 | tf_op jit(solution)/shard_map/ppermute | solution.py:510
  16.8 3.1 %shard_map.106 = (bf16[2,1024,512]{2,1,0:T(8,128)(2,1)S(1)}, bf16[2,1024,512]{2,1,0:T(8,128)(2,1)S(1)}, bf16[2,1024,256]{2,1,0:T(8,128)(2,1)S(1)}, f32[2,1024,128]{2,1,0:T(8,128)S(1)}, f32[1,128,128]{2,1,0:T(8,128)S(1)}) custom-call(f32[8,128]{1,0:T(8,128)S(1)} %get-tuple-element.51.refs_0_, ...), custom_call_target="tpu_custom_call", output_to_operand_aliasing={{3}: (9, {}), {4}: (10, {})} | custom-call | flops 4000000000 | bytes 2629632 | tf_op jit(solution)/shard_map/pallas_call | solution.py:349
  24.0 3.1 %shard_map.107 = (bf16[2,1024,512]{2,1,0:T(8,128)(2,1)S(1)}, bf16[2,1024,512]{2,1,0:T(8,128)(2,1)S(1)}, bf16[2,1024,256]{2,1,0:T(8,128)(2,1)S(1)}, f32[2,1024,128]{2,1,0:T(8,128)S(1)}, f32[1,128,128]{2,1,0:T(8,128)S(1)}) custom-call(f32[8,128]{1,0:T(8,128)S(1)} %get-tuple-element.51.refs_0_, ...), custom_call_target="tpu_custom_call", output_to_operand_aliasing={{3}: (9, {}), {4}: (10, {})} | custom-call | flops 4000000000 | bytes 2629632 | tf_op jit(solution)/shard_map/pallas_call | solution.py:349
  27.1 1.6 %collective-permute-start.5 = (bf16[64,1024]{1,0:T(8,128)(2,1)S(1)}, bf16[64,1024]{1,0:T(8,128)(2,1)S(1)}, u32[]{:S(2)}, u32[]{:S(2)}) collective-permute-start(bf16[64,1024]{1,0:T(8,128)(2,1)S(1)} %collective-permute-done.4.refs_2_), channel_id=1, source_target_pairs={{0,4},{1,3},{4,8},{5,1},{8,12},{9,5},{12,14},{13,9},{14,10},{15,13... | collective-permute-start | bytes 393224 | tf_op jit(solution)/shard_map/ppermute | solution.py:509
  28.8 1.5 %collective-permute-start.9 = (bf16[704,128]{1,0:T(8,128)(2,1)S(1)}, bf16[704,128]{1,0:T(8,128)(2,1)S(1)}, u32[]{:S(2)}, u32[]{:S(2)}) collective-permute-start(bf16[704,128]{1,0:T(8,128)(2,1)S(1)} %collective-permute-done.8.refs_4_.refs_6_), channel_id=1, source_target_pairs={{0,4},{1,3},{4,8},{5,1},{8,12},{9,5},{12,14},{13,9},{14,10},{15,13... | collective-permute-start | bytes 540680 | tf_op jit(solution)/shard_map/ppermute | solution.py:510
  30.3 3.1 %shard_map.108 = (bf16[2,1024,512]{2,1,0:T(8,128)(2,1)S(1)}, bf16[2,1024,512]{2,1,0:T(8,128)(2,1)S(1)}, bf16[2,1024,256]{2,1,0:T(8,128)(2,1)S(1)}, f32[2,1024,128]{2,1,0:T(8,128)S(1)}, f32[1,128,128]{2,1,0:T(8,128)S(1)}) custom-call(f32[8,128]{1,0:T(8,128)S(1)} %get-tuple-element.51.refs_0_, ...), custom_call_target="tpu_custom_call", output_to_operand_aliasing={{3}: (9, {}), {4}: (10, {})} | custom-call | flops 4000000000 | bytes 2629632 | tf_op jit(solution)/shard_map/pallas_call | solution.py:349
  34.3 2.1 %shard_map.109 = (bf16[2,1024,512]{2,1,0:T(8,128)(2,1)S(1)}, bf16[2,1024,256]{2,1,0:T(8,128)(2,1)S(1)}, f32[512,128]{1,0:T(8,128)S(1)}, f32[512,128]{1,0:T(8,128...) custom-call(f32[8,128]{1,0:T(8,128)S(1)} %get-tuple-element.51.refs_, ...), custom_call_target="tpu_custom_call", output_to_operand_aliasing={{4}: (6, {}), {5}: (7, {})} | custom-call | flops 2000000000 | bytes 2154496 | tf_op jit(solution)/shard_map/pallas_call | solution.py:349
  36.4 1.5 %collective-permute-done.16.other_ref = f32[512,128]{1,0:T(8,128)S(1)} collective-permute-done((f32[512,128]{1,0:T(8,128)S(1)}, f32[512,128]{1,0:T(8,128)S(1)}, u32[]{:S(2)}, u32[]{:S(2)}) %collective-permute-start.16) | collective-permute-done | bytes 262176 | tf_op jit(solution)/shard_map/ppermute | solution.py:518
  38.8 1.5 %collective-permute-start.17 = (bf16[640,128]{1,0:T(8,128)(2,1)S(1)}, bf16[640,128]{1,0:T(8,128)(2,1)S(1)}, u32[]{:S(2)}, u32[]{:S(2)}) collective-permute-start(bf16[640,128]{1,0:T(8,128)(2,1)S(1)} %get-tuple-element.65.refs_2_), channel_id=1, source_target_pairs={{0,4},{1,3},{4,8},{5,1},{8,12},{9,5},{12,14},{13,9},{14,10},{15,13... | collective-permute-start | bytes 491528 | tf_op jit(solution)/shard_map/ppermute | solution.py:535
  42.0 2.4 %collective-permute-done.17.refs_2_ = bf16[640,128]{1,0:T(8,128)(2,1)S(1)} collective-permute-done((bf16[640,128]{1,0:T(8,128)(2,1)S(1)}, bf16[640,128]{1,0:T(8,128)(2,1)S(1)}, u32[]{:S(2)}, u32[]{:S(2)}) %collective-permute-start.17) | collective-permute-done | bytes 163872 | tf_op jit(solution)/shard_map/ppermute | solution.py:535
  44.4 2.5 %collective-permute-start.18 = (bf16[640,128]{1,0:T(8,128)(2,1)S(1)}, bf16[640,128]{1,0:T(8,128)(2,1)S(1)}, u32[]{:S(2)}, u32[]{:S(2)}) collective-permute-start(bf16[640,128]{1,0:T(8,128)(2,1)S(1)} %collective-permute-done.17.refs_2_), channel_id=1, source_target_pairs={{0,4},{1,3},{4,8},{5,1},{8,12},{9,5},{12,14},{13,9},{14,10},{15,13... | collective-permute-start | bytes 491528 | tf_op jit(solution)/shard_map/ppermute | solution.py:539
  47.8 1.1 %shard_map.115 = (f32[2,1024,128]{2,1,0:T(8,128)S(1)}, f32[1,128,128]{2,1,0:T(8,128)S(1)}) custom-call(f32[8,128]{1,0:T(8,128)S(1)} %get-tuple-element.51.refs_0_, f32[8,128]{1,0:T(8,128)S(1)} %collective-permute-done.refs_0_.refs_1_, bf16[640,128]{1,0:T(8,128)(2,1)S(1)} %collective-permute-done.17.refs_2_, ...), custom_call_target="tpu_custom_call", output_to_operand_aliasing={{0}: (6, {}), {1}: (7, {})} | custom-call | flops 1000000000 | bytes 4595712 | tf_op jit(solution)/shard_map/pallas_call | solution.py:349
  49.0 2.2 %collective-permute-done.18.refs_2_ = bf16[640,128]{1,0:T(8,128)(2,1)S(1)} collective-permute-done((bf16[640,128]{1,0:T(8,128)(2,1)S(1)}, bf16[640,128]{1,0:T(8,128)(2,1)S(1)}, u32[]{:S(2)}, u32[]{:S(2)}) %collective-permute-start.18) | collective-permute-done | bytes 163872 | tf_op jit(solution)/shard_map/ppermute | solution.py:539
  51.2 2.5 %collective-permute-start.19 = (bf16[640,128]{1,0:T(8,128)(2,1)S(1)}, bf16[640,128]{1,0:T(8,128)(2,1)S(1)}, u32[]{:S(2)}, u32[]{:S(2)}) collective-permute-start(bf16[640,128]{1,0:T(8,128)(2,1)S(1)} %collective-permute-done.18.refs_2_), channel_id=1, source_target_pairs={{0,4},{1,3},{4,8},{5,1},{8,12},{9,5},{12,14},{13,9},{14,10},{15,13... | collective-permute-start | bytes 491528 | tf_op jit(solution)/shard_map/ppermute | solution.py:539
  54.8 1.2 %shard_map.118 = (f32[2,1024,128]{2,1,0:T(8,128)S(1)}, f32[1,128,128]{2,1,0:T(8,128)S(1)}) custom-call(f32[8,128]{1,0:T(8,128)S(1)} %get-tuple-element.51.refs_0_, f32[8,128]{1,0:T(8,128)S(1)} %collective-permute-done.refs_0_.refs_1_, bf16[640,128]{1,0:T(8,128)(2,1)S(1)} %collective-permute-done.18.refs_2_, ...), custom_call_target="tpu_custom_call", output_to_operand_aliasing={{0}: (6, {}), {1}: (7, {})} | custom-call | flops 1000000000 | bytes 4595712 | tf_op jit(solution)/shard_map/pallas_call | solution.py:349
  56.0 1.8 %collective-permute-done.19.refs_2_ = bf16[640,128]{1,0:T(8,128)(2,1)S(1)} collective-permute-done((bf16[640,128]{1,0:T(8,128)(2,1)S(1)}, bf16[640,128]{1,0:T(8,128)(2,1)S(1)}, u32[]{:S(2)}, u32[]{:S(2)}) %collective-permute-start.19) | collective-permute-done | bytes 163872 | tf_op jit(solution)/shard_map/ppermute | solution.py:539
  57.7 1.9 %collective-permute-start.20 = (bf16[640,128]{1,0:T(8,128)(2,1)S(1)}, bf16[640,128]{1,0:T(8,128)(2,1)S(1)}, u32[]{:S(2)}, u32[]{:S(2)}) collective-permute-start(bf16[640,128]{1,0:T(8,128)(2,1)S(1)} %collective-permute-done.19.refs_2_), channel_id=1, source_target_pairs={{0,4},{1,3},{4,8},{5,1},{8,12},{9,5},{12,14},{13,9},{14,10},{15,13... | collective-permute-start | bytes 491528 | tf_op jit(solution)/shard_map/ppermute | solution.py:539
  60.9 1.2 %shard_map.120 = (f32[2,1024,128]{2,1,0:T(8,128)S(1)}, f32[1,128,128]{2,1,0:T(8,128)S(1)}) custom-call(f32[8,128]{1,0:T(8,128)S(1)} %get-tuple-element.51.refs_0_, f32[8,128]{1,0:T(8,128)S(1)} %collective-permute-done.refs_0_.refs_1_, bf16[640,128]{1,0:T(8,128)(2,1)S(1)} %collective-permute-done.19.refs_2_, ...), custom_call_target="tpu_custom_call", output_to_operand_aliasing={{0}: (6, {}), {1}: (7, {})} | custom-call | flops 1000000000 | bytes 4595712 | tf_op jit(solution)/shard_map/pallas_call | solution.py:349
  63.1 1.2 %shard_map.121 = (f32[512,128]{1,0:T(8,128)S(1)}, f32[512,128]{1,0:T(8,128)S(1)}, f32[2,1024,128]{2,1,0:T(8,128)S(1)}, f32[1,128,128]{2,1,0:T(8,128)S(1)}) custom-call(f32[8,128]{1,0:T(8,128)S(1)} %get-tuple-element.51.refs_0_, f32[8,128]{1,0:T(8,128)S(1)} %collective-permute-done.refs_0_.refs_1_, ...), custom_call_target="tpu_custom_call", output_to_operand_aliasing={{2}: (5, {}), {3}: (6, {})} | custom-call | flops 1000000000 | bytes 4431872 | tf_op jit(solution)/shard_map/pallas_call | solution.py:349
  64.3 1.5 %collective-permute-done.24.other_ref = f32[512,128]{1,0:T(8,128)S(1)} collective-permute-done((f32[512,128]{1,0:T(8,128)S(1)}, f32[512,128]{1,0:T(8,128)S(1)}, u32[]{:S(2)}, u32[]{:S(2)}) %collective-permute-start.24) | collective-permute-done | bytes 262176 | tf_op jit(solution)/shard_map/ppermute | solution.py:549
  (55 shorter events, 18.5 us)
Async XLA Ops:
  0.6 9.0 %collective-permute-start.10 = (bf16[64,1024]{1,0:T(8,128)(2,1)}, bf16[64,1024]{1,0:T(8,128)(2,1)S(1)}, u32[]{:S(2)}, u32[]{:S(2)}) collective-permute-start(bf16[64,1024]{1,0:T(8,128)(2,1)} %coords_ref.1), channel_id=1, source_target_pairs={{0,2},{1,5},{4,0},{5,9},{8,4},{9,13},{12,8},{13,15},{14,12},{15,11... | collective-permute-start | bytes 393224 | tf_op jit(solution)/shard_map/ppermute | solution.py:405
  3.6 6.9 %collective-permute-start.2 = (bf16[64,1024]{1,0:T(8,128)(2,1)}, bf16[64,1024]{1,0:T(8,128)(2,1)S(1)}, u32[]{:S(2)}, u32[]{:S(2)}) collective-permute-start(bf16[64,1024]{1,0:T(8,128)(2,1)} %coords_ref.1), channel_id=1, source_target_pairs={{0,4},{1,3},{4,8},{5,1},{8,12},{9,5},{12,14},{13,9},{14,10},{15,13... | collective-permute-start | bytes 393224 | tf_op jit(solution)/shard_map/ppermute | solution.py:405
  3.8 7.9 %collective-permute-start.1 = (bf16[64,1024]{1,0:T(8,128)(2,1)}, bf16[64,1024]{1,0:T(8,128)(2,1)S(1)}, u32[]{:S(2)}, u32[]{:S(2)}) collective-permute-start(bf16[64,1024]{1,0:T(8,128)(2,1)} %coords_ref.1), channel_id=1, source_target_pairs={{0,1},{1,0},{2,3},{3,2},{4,5},{5,4},{6,7},{7,6},{8,9},{9,8},{10,11... | collective-permute-start | bytes 393224 | tf_op jit(solution)/shard_map/ppermute | solution.py:404
  6.1 2.4 %collective-permute-start = (f32[8,128]{1,0:T(8,128)}, f32[8,128]{1,0:T(8,128)S(1)}, u32[]{:S(2)}, u32[]{:S(2)}) collective-permute-start(f32[8,128]{1,0:T(8,128)} %get-tuple-element.49), channel_id=1, source_target_pairs={{0,1},{1,0},{2,3},{3,2},{4,5},{5,4},{6,7},{7,6},{8,9},{9,8},{10,11... | collective-permute-start | bytes 12296 | tf_op jit(solution)/shard_map/ppermute | solution.py:417
  6.6 8.1 %collective-permute-start.13 = (bf16[704,128]{1,0:T(8,128)(2,1)}, bf16[704,128]{1,0:T(8,128)(2,1)S(1)}, u32[]{:S(2)}, u32[]{:S(2)}) collective-permute-start(bf16[704,128]{1,0:T(8,128)(2,1)} %get-tuple-element.52), channel_id=1, source_target_pairs={{0,2},{1,5},{4,0},{5,9},{8,4},{9,13},{12,8},{13,15},{14,12},{15,11... | collective-permute-start | bytes 540680 | tf_op jit(solution)/shard_map/ppermute | solution.py:499
  8.5 7.3 %collective-permute-start.6 = (bf16[704,128]{1,0:T(8,128)(2,1)}, bf16[704,128]{1,0:T(8,128)(2,1)S(1)}, u32[]{:S(2)}, u32[]{:S(2)}) collective-permute-start(bf16[704,128]{1,0:T(8,128)(2,1)} %get-tuple-element.52), channel_id=1, source_target_pairs={{0,4},{1,3},{4,8},{5,1},{8,12},{9,5},{12,14},{13,9},{14,10},{15,13... | collective-permute-start | bytes 540680 | tf_op jit(solution)/shard_map/ppermute | solution.py:499
  9.6 10.2 %collective-permute-start.11 = (bf16[64,1024]{1,0:T(8,128)(2,1)S(1)}, bf16[64,1024]{1,0:T(8,128)(2,1)S(1)}, u32[]{:S(2)}, u32[]{:S(2)}) collective-permute-start(bf16[64,1024]{1,0:T(8,128)(2,1)S(1)} %collective-permute-done.10.refs_3_), channel_id=1, source_target_pairs={{0,2},{1,5},{4,0},{5,9},{8,4},{9,13},{12,8},{13,15},{14,12},{15,11... | collective-permute-start | bytes 393224 | tf_op jit(solution)/shard_map/ppermute | solution.py:509
  10.6 10.4 %collective-permute-start.3 = (bf16[64,1024]{1,0:T(8,128)(2,1)S(1)}, bf16[64,1024]{1,0:T(8,128)(2,1)S(1)}, u32[]{:S(2)}, u32[]{:S(2)}) collective-permute-start(bf16[64,1024]{1,0:T(8,128)(2,1)S(1)} %collective-permute-done.2.refs_2_), channel_id=1, source_target_pairs={{0,4},{1,3},{4,8},{5,1},{8,12},{9,5},{12,14},{13,9},{14,10},{15,13... | collective-permute-start | bytes 393224 | tf_op jit(solution)/shard_map/ppermute | solution.py:509
  14.7 7.2 %collective-permute-start.14 = (bf16[704,128]{1,0:T(8,128)(2,1)S(1)}, bf16[704,128]{1,0:T(8,128)(2,1)S(1)}, u32[]{:S(2)}, u32[]{:S(2)}) collective-permute-start(bf16[704,128]{1,0:T(8,128)(2,1)S(1)} %collective-permute-done.13.refs_5_.refs_7_), channel_id=1, source_target_pairs={{0,2},{1,5},{4,0},{5,9},{8,4},{9,13},{12,8},{13,15},{14,12},{15,11... | collective-permute-start | bytes 540680 | tf_op jit(solution)/shard_map/ppermute | solution.py:510
  15.8 7.2 %collective-permute-start.7 = (bf16[704,128]{1,0:T(8,128)(2,1)S(1)}, bf16[704,128]{1,0:T(8,128)(2,1)S(1)}, u32[]{:S(2)}, u32[]{:S(2)}) collective-permute-start(bf16[704,128]{1,0:T(8,128)(2,1)S(1)} %collective-permute-done.6.refs_4_.refs_6_), channel_id=1, source_target_pairs={{0,4},{1,3},{4,8},{5,1},{8,12},{9,5},{12,14},{13,9},{14,10},{15,13... | collective-permute-start | bytes 540680 | tf_op jit(solution)/shard_map/ppermute | solution.py:510
  19.9 10.4 %collective-permute-start.12 = (bf16[64,1024]{1,0:T(8,128)(2,1)S(1)}, bf16[64,1024]{1,0:T(8,128)(2,1)S(1)}, u32[]{:S(2)}, u32[]{:S(2)}) collective-permute-start(bf16[64,1024]{1,0:T(8,128)(2,1)S(1)} %collective-permute-done.11.refs_3_), channel_id=1, source_target_pairs={{0,2},{1,5},{4,0},{5,9},{8,4},{9,13},{12,8},{13,15},{14,12},{15,11... | collective-permute-start | bytes 393224 | tf_op jit(solution)/shard_map/ppermute | solution.py:509
  21.0 6.1 %collective-permute-start.4 = (bf16[64,1024]{1,0:T(8,128)(2,1)S(1)}, bf16[64,1024]{1,0:T(8,128)(2,1)S(1)}, u32[]{:S(2)}, u32[]{:S(2)}) collective-permute-start(bf16[64,1024]{1,0:T(8,128)(2,1)S(1)} %collective-permute-done.3.refs_2_), channel_id=1, source_target_pairs={{0,4},{1,3},{4,8},{5,1},{8,12},{9,5},{12,14},{13,9},{14,10},{15,13... | collective-permute-start | bytes 393224 | tf_op jit(solution)/shard_map/ppermute | solution.py:509
  21.9 8.3 %collective-permute-start.15 = (bf16[704,128]{1,0:T(8,128)(2,1)S(1)}, bf16[704,128]{1,0:T(8,128)(2,1)S(1)}, u32[]{:S(2)}, u32[]{:S(2)}) collective-permute-start(bf16[704,128]{1,0:T(8,128)(2,1)S(1)} %collective-permute-done.14.refs_5_.refs_7_), channel_id=1, source_target_pairs={{0,2},{1,5},{4,0},{5,9},{8,4},{9,13},{12,8},{13,15},{14,12},{15,11... | collective-permute-start | bytes 540680 | tf_op jit(solution)/shard_map/ppermute | solution.py:510
  23.1 5.7 %collective-permute-start.8 = (bf16[704,128]{1,0:T(8,128)(2,1)S(1)}, bf16[704,128]{1,0:T(8,128)(2,1)S(1)}, u32[]{:S(2)}, u32[]{:S(2)}) collective-permute-start(bf16[704,128]{1,0:T(8,128)(2,1)S(1)} %collective-permute-done.7.refs_4_.refs_6_), channel_id=1, source_target_pairs={{0,4},{1,3},{4,8},{5,1},{8,12},{9,5},{12,14},{13,9},{14,10},{15,13... | collective-permute-start | bytes 540680 | tf_op jit(solution)/shard_map/ppermute | solution.py:510
  27.1 6.3 %collective-permute-start.5 = (bf16[64,1024]{1,0:T(8,128)(2,1)S(1)}, bf16[64,1024]{1,0:T(8,128)(2,1)S(1)}, u32[]{:S(2)}, u32[]{:S(2)}) collective-permute-start(bf16[64,1024]{1,0:T(8,128)(2,1)S(1)} %collective-permute-done.4.refs_2_), channel_id=1, source_target_pairs={{0,4},{1,3},{4,8},{5,1},{8,12},{9,5},{12,14},{13,9},{14,10},{15,13... | collective-permute-start | bytes 393224 | tf_op jit(solution)/shard_map/ppermute | solution.py:509
  28.8 5.5 %collective-permute-start.9 = (bf16[704,128]{1,0:T(8,128)(2,1)S(1)}, bf16[704,128]{1,0:T(8,128)(2,1)S(1)}, u32[]{:S(2)}, u32[]{:S(2)}) collective-permute-start(bf16[704,128]{1,0:T(8,128)(2,1)S(1)} %collective-permute-done.8.refs_4_.refs_6_), channel_id=1, source_target_pairs={{0,4},{1,3},{4,8},{5,1},{8,12},{9,5},{12,14},{13,9},{14,10},{15,13... | collective-permute-start | bytes 540680 | tf_op jit(solution)/shard_map/ppermute | solution.py:510
  36.3 1.6 %collective-permute-start.16 = (f32[512,128]{1,0:T(8,128)S(1)}, f32[512,128]{1,0:T(8,128)S(1)}, u32[]{:S(2)}, u32[]{:S(2)}) collective-permute-start(f32[512,128]{1,0:T(8,128)S(1)} %get-tuple-element.63), channel_id=1, source_target_pairs={{0,1},{1,0},{2,3},{3,2},{4,5},{5,4},{6,7},{7,6},{8,9},{9,8},{10,11... | collective-permute-start | bytes 786440 | tf_op jit(solution)/shard_map/ppermute | solution.py:518
  38.8 5.6 %collective-permute-start.17 = (bf16[640,128]{1,0:T(8,128)(2,1)S(1)}, bf16[640,128]{1,0:T(8,128)(2,1)S(1)}, u32[]{:S(2)}, u32[]{:S(2)}) collective-permute-start(bf16[640,128]{1,0:T(8,128)(2,1)S(1)} %get-tuple-element.65.refs_2_), channel_id=1, source_target_pairs={{0,4},{1,3},{4,8},{5,1},{8,12},{9,5},{12,14},{13,9},{14,10},{15,13... | collective-permute-start | bytes 491528 | tf_op jit(solution)/shard_map/ppermute | solution.py:535
  41.4 6.3 %collective-permute-start.21 = (bf16[640,128]{1,0:T(8,128)(2,1)S(1)}, bf16[640,128]{1,0:T(8,128)(2,1)S(1)}, u32[]{:S(2)}, u32[]{:S(2)}) collective-permute-start(bf16[640,128]{1,0:T(8,128)(2,1)S(1)} %shard_map.112), channel_id=1, source_target_pairs={{0,2},{1,5},{4,0},{5,9},{8,4},{9,13},{12,8},{13,15},{14,12},{15,11... | collective-permute-start | bytes 491528 | tf_op jit(solution)/shard_map/ppermute | solution.py:537
  44.4 6.7 %collective-permute-start.18 = (bf16[640,128]{1,0:T(8,128)(2,1)S(1)}, bf16[640,128]{1,0:T(8,128)(2,1)S(1)}, u32[]{:S(2)}, u32[]{:S(2)}) collective-permute-start(bf16[640,128]{1,0:T(8,128)(2,1)S(1)} %collective-permute-done.17.refs_2_), channel_id=1, source_target_pairs={{0,4},{1,3},{4,8},{5,1},{8,12},{9,5},{12,14},{13,9},{14,10},{15,13... | collective-permute-start | bytes 491528 | tf_op jit(solution)/shard_map/ppermute | solution.py:539
  47.8 7.0 %collective-permute-start.22 = (bf16[640,128]{1,0:T(8,128)(2,1)S(1)}, bf16[640,128]{1,0:T(8,128)(2,1)S(1)}, u32[]{:S(2)}, u32[]{:S(2)}) collective-permute-start(bf16[640,128]{1,0:T(8,128)(2,1)S(1)} %shard_map.114.refs_3_), channel_id=1, source_target_pairs={{0,2},{1,5},{4,0},{5,9},{8,4},{9,13},{12,8},{13,15},{14,12},{15,11... | collective-permute-start | bytes 491528 | tf_op jit(solution)/shard_map/ppermute | solution.py:544
  51.2 6.6 %collective-permute-start.19 = (bf16[640,128]{1,0:T(8,128)(2,1)S(1)}, bf16[640,128]{1,0:T(8,128)(2,1)S(1)}, u32[]{:S(2)}, u32[]{:S(2)}) collective-permute-start(bf16[640,128]{1,0:T(8,128)(2,1)S(1)} %collective-permute-done.18.refs_2_), channel_id=1, source_target_pairs={{0,4},{1,3},{4,8},{5,1},{8,12},{9,5},{12,14},{13,9},{14,10},{15,13... | collective-permute-start | bytes 491528 | tf_op jit(solution)/shard_map/ppermute | solution.py:539
  54.8 6.1 %collective-permute-start.23 = (bf16[640,128]{1,0:T(8,128)(2,1)S(1)}, bf16[640,128]{1,0:T(8,128)(2,1)S(1)}, u32[]{:S(2)}, u32[]{:S(2)}) collective-permute-start(bf16[640,128]{1,0:T(8,128)(2,1)S(1)} %shard_map.117.refs_3_), channel_id=1, source_target_pairs={{0,2},{1,5},{4,0},{5,9},{8,4},{9,13},{12,8},{13,15},{14,12},{15,11... | collective-permute-start | bytes 491528 | tf_op jit(solution)/shard_map/ppermute | solution.py:544
  57.7 5.3 %collective-permute-start.20 = (bf16[640,128]{1,0:T(8,128)(2,1)S(1)}, bf16[640,128]{1,0:T(8,128)(2,1)S(1)}, u32[]{:S(2)}, u32[]{:S(2)}) collective-permute-start(bf16[640,128]{1,0:T(8,128)(2,1)S(1)} %collective-permute-done.19.refs_2_), channel_id=1, source_target_pairs={{0,4},{1,3},{4,8},{5,1},{8,12},{9,5},{12,14},{13,9},{14,10},{15,13... | collective-permute-start | bytes 491528 | tf_op jit(solution)/shard_map/ppermute | solution.py:539
  (6 other events, 17.6 us)

commit v15 on v14

--- a/solution.py
+++ b/solution.py
@@ -142,17 +142,15 @@
     local_ref[place : place + 16, :] = jnp.concatenate([table, table], axis=0).astype(bf16)
 
 
-def joined_kernel(mine_ref, other_ref, leaf_ref, node_ref, upper_ref, out_ref, *message_refs):
+def joined_kernel(mine_ref, other_ref, leaf_ref, node_ref, upper_ref, out_ref, message_ref):
     half = mine_ref.shape[0]
     columns = LANES // LEAVES
     result = mine_ref[...] + other_ref[...]
+    message_ref[0:half, :] = result.astype(bf16)
     flat = result.T.astype(bf16)
     charges = [flat[0:columns], flat[columns:]]
     out_ref[...] = jnp.concatenate(charges, axis=1)
-    rows = skeleton_rows(charges, leaf_ref, node_ref, upper_ref)
-    for message_ref in message_refs:
-        message_ref[0:half, :] = result.astype(bf16)
-        message_ref[half : half + LANES, :] = rows
+    message_ref[half : half + LANES, :] = skeleton_rows(charges, leaf_ref, node_ref, upper_ref)
 
 
 def added_kernel(mine_ref, other_ref, out_ref):
@@ -241,7 +239,7 @@
     devices = {spot: device_of(ring, spot) for spot in spots}
 
     def near_part(turn, spot, core, leaf):
-        at = core * len(near_spots) + near_spots.index(spot)
+        at = turn if first else core * len(near_spots) + near_spots.index(spot)
         table = table_of(core)
         named = [
             picked(table, devices[spot] * LEAVES + which)[0:LEAVES] for which in range(LEAVES)
@@ -317,22 +315,6 @@
             both = [total_ref[core, span_of(leaf), :] for leaf in range(LEAVES)]
             both = [total + swapped(total) for total in both]
             ref[...] = jnp.where(in_low_half(both[0].shape), both[0], both[1])
-
-
-def gate_kernel(message_ref, after_ref, out_ref):
-    pass
-
-
-def gated(message, after):
-    anywhere = pl.BlockSpec(memory_space=pl.ANY)
-    return pl.pallas_call(
-        gate_kernel,
-        out_shape=jax.ShapeDtypeStruct(message.shape, message.dtype),
-        in_specs=[anywhere] * 2,
-        out_specs=anywhere,
-        input_output_aliases={0: 0},
-        compiler_params=pltpu.CompilerParams(vmem_limit_bytes=2**20),
-    )(message, after)
 
 
 def call(body, args, out_shapes, streamed=(), scratch=(), aliases={}, flops=0, vmem_mib=16):
@@ -448,11 +430,11 @@
         far_width = max(LANES, LANES * (len(far_spots) + (n_sub if last else 0)))
         scratch = [
             pltpu.VMEM((CORES * LEAVES, far_width, LANES), bf16),
-            pltpu.VMEM((CORES * len(near_spots), points, LANES), bf16),
+            pltpu.VMEM((LEAVES + 1 if first else CORES * len(near_spots), points, LANES), bf16),
         ]
         if makes:
             scratch += [
-                pltpu.VMEM((CORES * len(near_spots), LANES, points), bf16),
+                pltpu.VMEM((LEAVES + 1 if first else CORES * len(near_spots), LANES, points), bf16),
                 pltpu.VMEM((LANES, far_width), bf16),
             ]
         names, outs = [], []
@@ -483,9 +465,6 @@
         )
         return dict(zip(names, results))
 
-    def far_spots_of(spot):
-        return (spot - 1, spot) if spot % 2 == 0 and spot > 0 else (spot,)
-
     mode = "keep" if keeping else "make"
     given = {"near": {}, "far": {}, "places": {0: coords}, "skeletons": {0: message}}
     given["charges"] = given["skeletons"]
@@ -513,38 +492,26 @@
     given["places"][across[0]], given["skeletons"][across[0]] = coords_next[0], sent[0]
     results = stage(across, across, given, carried, True, mode)
     keep_results(results)
-    first, message, again = call(
+    first, message = call(
         joined_kernel,
         [results["mine"], to_sibling(results["other"])] + maps,
-        [shape(columns, local)] + [shape(points + LANES, LANES)] * 2,
+        [shape(columns, local), shape(points + LANES, LANES)],
     )
 
     mode = "use" if keeping else "make"
-    given["charges"] = {}
-    carried = []
-
-    def arrived(spot, message):
-        nonlocal carried
-        given["charges"][spot] = message
-        last = spot == chips - 1
-        far_spots = () if spot % 2 == 1 and not last else far_spots_of(spot)
-        results = stage((spot,), far_spots, given, carried, last, mode)
+    given["charges"] = {0: message}
+    sent = one_way(message), other_way(message)
+    results = stage((0,), (0,), given, [], False, mode)
+    carried = [results["total"], results["sums"]]
+    for hop in range(1, chips // 2):
+        spots = (2 * hop - 1, 2 * hop)
+        for at, spot in enumerate(spots):
+            given["charges"][spot] = sent[at]
+        sent = one_way(sent[0]), None if hop == chips // 2 - 1 else other_way(sent[1])
+        results = stage(spots, spots, given, carried, False, mode)
         carried = [results["total"], results["sums"]]
-        return results
-
-    one = one_way(message)
-    arrived(0, message)
-    other = other_way(gated(again, carried[1]))
-    for hop in range(1, chips // 2):
-        one_next = one_way(one)
-        arrived(2 * hop - 1, one)
-        other_next = None
-        if hop < chips // 2 - 1:
-            other = gated(other, carried[1])
-            other_next = other_way(other)
-        arrived(2 * hop, other)
-        one, other = one_next, other_next
-    results = arrived(chips - 1, one)
+    given["charges"][across[0]] = sent[0]
+    results = stage(across, across, given, carried, True, mode)
     (second,) = call(
         added_kernel, [results["mine"], to_sibling(results["other"])], [shape(columns, local)]
     )

time: 66.8 us -> 68.3 us (1.022)
  waiting for transfers between devices: 12.2 us -> 18.7 us
  starting transfers between devices: 27.1 us -> 22.9 us
  Pallas kernels: 25.5 us -> 24.7 us
    ppermute x7 -> x5, starting transfers between devices: 8.96 us -> 2.72 us  [the longest x2 1.73 us: on_device(): other_way(sent[1])]
    ppermute x2 -> x4, waiting for transfers between devices: 0.01 us -> 3.6 us  [on_device(): sent = (one_way(message), other_way(message))]
    ppermute x7 -> x5, waiting for transfers between devices: 8.19 us -> 11.2 us  [the longest x3 8.5 us: on_device(): one_way(sent[0])]
    ppermute x2 -> x4, starting transfers between devices: 2.99 us -> 5.02 us  [on_device(): sent = (one_way(message), other_way(message))]
    pallas_call x16 -> x13, Pallas kernels: 25.5 us -> 24.7 us  [call(): pl.pallas_call(body, grid=(1,), out_shape=out_shapes, in_specs=specs, out...]
  transfers between devices with their start and end apart: 25 -> 25, of which waited for: 10 -> 8; matrix products, arithmetic and copies ran while one was open for 0% -> 0% of each run, Pallas kernels for 31% -> 29%
where the time goes in v15:
time: 68.3 us; the launch traced here: 68.1 us
  Pallas kernels  24.7 us (36%)
  starting transfers between devices  22.9 us (34%)
  waiting for transfers between devices  18.7 us (27%)
  local copies, waits for them, and re-layouts  0.98 us (1%)
  between operations  0.78 us (1%)
    pallas_call x13, Pallas kernels, call(): pl.pallas_call(body, grid=(1,), out_shape=out_shapes, in_specs=specs, out...  24.7 us
    ppermute x3, waiting for transfers between devices, on_device(): one_way(sent[0])  8.5 us
    ppermute x5, starting transfers between devices, on_device(): sent = (one_way(sent[0]), None if final else other_way(sent[1]))  5.66 us
    ppermute x4, starting transfers between devices, on_device(): sent = (one_way(message), other_way(message))  5.02 us
    ppermute x3, starting transfers between devices, on_device(): one_way(coords_next[0])  3.69 us
    ppermute x4, waiting for transfers between devices, on_device(): sent = (one_way(message), other_way(message))  3.6 us
    ppermute x2, starting transfers between devices, on_device(): coords_next = (one_way(coords), other_way(coords))  3.14 us
    ppermute x2, waiting for transfers between devices, on_device(): to_sibling(results['other'])  3.04 us
  transfers between devices with their start and end apart: 25, of which 8 were waited for; matrix products, arithmetic and copies ran while one was open for 0% of the time, Pallas kernels for 29%

profile of v15, /device:TPU:0, one launch (start us, length us, event | category | flops | bytes accessed | tf_op | source)
XLA Modules:
  0.0 68.1 jit_solution(7385136041023850144)
XLA Ops:
  0.6 3.0 %collective-permute-start.10 = (bf16[64,1024]{1,0:T(8,128)(2,1)}, bf16[64,1024]{1,0:T(8,128)(2,1)S(1)}, u32[]{:S(2)}, u32[]{:S(2)}) collective-permute-start(bf16[64,1024]{1,0:T(8,128)(2,1)} %coords_ref.1), channel_id=1, source_target_pairs={{0,2},{1,5},{4,0},{5,9},{8,4},{9,13},{12,8},{13,15},{14,12},{15,11... | collective-permute-start | bytes 393224 | tf_op jit(solution)/shard_map/ppermute | solution.py:387
  3.8 2.3 %shard_map.104 = (bf16[704,128]{1,0:T(8,128)(2,1)}, bf16[1232,128]{1,0:T(8,128)(2,1)}, f32[8,128]{1,0:T(8,128)}) custom-call(s32[2,16]{1,0:T(2,128)} %near_ref.1, s32[2,32]{1,0:T(2,128)} %far_ref.1, bf16[64,1024]{1,0:T(8,128)(2,1)} %coords_ref.1, bf16[64,1024]{1,0:T(8,128)(2,1)} %charges_ref.1, bf16[64,128]{1,0:T(8,128)(2,1)} %points_ref.1, ...), custom_call_target="tpu_custom_call" | custom-call | bytes 639360 | tf_op jit(solution)/shard_map/pallas_call | solution.py:331
  6.6 1.9 %collective-permute-start.13 = (bf16[704,128]{1,0:T(8,128)(2,1)}, bf16[704,128]{1,0:T(8,128)(2,1)S(1)}, u32[]{:S(2)}, u32[]{:S(2)}) collective-permute-start(bf16[704,128]{1,0:T(8,128)(2,1)} %get-tuple-element.45), channel_id=1, source_target_pairs={{0,2},{1,5},{4,0},{5,9},{8,4},{9,13},{12,8},{13,15},{14,12},{15,11... | collective-permute-start | bytes 540680 | tf_op jit(solution)/shard_map/ppermute | solution.py:478
  12.6 2.1 %shard_map.105 = (bf16[2,1024,128]{2,1,0:T(8,128)(2,1)S(1)}, f32[8,128]{1,0:T(8,128)S(1)}, bf16[3,1024,512]{2,1,0:T(8,128)(2,1)S(1)}, bf16[2,1024,128]{2,1,0:T(8...) custom-call(f32[8,128]{1,0:T(8,128)S(1)} %collective-permute-done.refs_0_.refs_1_, ...), custom_call_target="tpu_custom_call" | custom-call | flops 2000000000 | bytes 450560 | tf_op jit(solution)/shard_map/pallas_call | solution.py:331
  16.8 3.1 %shard_map.106 = (bf16[2,1024,512]{2,1,0:T(8,128)(2,1)S(1)}, bf16[2,1024,512]{2,1,0:T(8,128)(2,1)S(1)}, bf16[2,1024,256]{2,1,0:T(8,128)(2,1)S(1)}, f32[2,1024,128]{2,1,0:T(8,128)S(1)}, f32[1,128,128]{2,1,0:T(8,128)S(1)}) custom-call(f32[8,128]{1,0:T(8,128)S(1)} %get-tuple-element.44.refs_0_, ...), custom_call_target="tpu_custom_call", output_to_operand_aliasing={{3}: (9, {}), {4}: (10, {})} | custom-call | flops 4000000000 | bytes 2629632 | tf_op jit(solution)/shard_map/pallas_call | solution.py:331
  19.9 1.1 %collective-permute-start.12 = (bf16[64,1024]{1,0:T(8,128)(2,1)S(1)}, bf16[64,1024]{1,0:T(8,128)(2,1)S(1)}, u32[]{:S(2)}, u32[]{:S(2)}) collective-permute-start(bf16[64,1024]{1,0:T(8,128)(2,1)S(1)} %collective-permute-done.11.refs_3_), channel_id=1, source_target_pairs={{0,2},{1,5},{4,0},{5,9},{8,4},{9,13},{12,8},{13,15},{14,12},{15,11... | collective-permute-start | bytes 393224 | tf_op jit(solution)/shard_map/ppermute | solution.py:488
  24.0 3.1 %shard_map.107 = (bf16[2,1024,512]{2,1,0:T(8,128)(2,1)S(1)}, bf16[2,1024,512]{2,1,0:T(8,128)(2,1)S(1)}, bf16[2,1024,256]{2,1,0:T(8,128)(2,1)S(1)}, f32[2,1024,128]{2,1,0:T(8,128)S(1)}, f32[1,128,128]{2,1,0:T(8,128)S(1)}) custom-call(f32[8,128]{1,0:T(8,128)S(1)} %get-tuple-element.44.refs_0_, ...), custom_call_target="tpu_custom_call", output_to_operand_aliasing={{3}: (9, {}), {4}: (10, {})} | custom-call | flops 4000000000 | bytes 2629632 | tf_op jit(solution)/shard_map/pallas_call | solution.py:331
  27.1 1.6 %collective-permute-start.5 = (bf16[64,1024]{1,0:T(8,128)(2,1)S(1)}, bf16[64,1024]{1,0:T(8,128)(2,1)S(1)}, u32[]{:S(2)}, u32[]{:S(2)}) collective-permute-start(bf16[64,1024]{1,0:T(8,128)(2,1)S(1)} %collective-permute-done.4.refs_2_), channel_id=1, source_target_pairs={{0,4},{1,3},{4,8},{5,1},{8,12},{9,5},{12,14},{13,9},{14,10},{15,13... | collective-permute-start | bytes 393224 | tf_op jit(solution)/shard_map/ppermute | solution.py:488
  28.8 1.6 %collective-permute-start.9 = (bf16[704,128]{1,0:T(8,128)(2,1)S(1)}, bf16[704,128]{1,0:T(8,128)(2,1)S(1)}, u32[]{:S(2)}, u32[]{:S(2)}) collective-permute-start(bf16[704,128]{1,0:T(8,128)(2,1)S(1)} %collective-permute-done.8.refs_4_.refs_6_), channel_id=1, source_target_pairs={{0,4},{1,3},{4,8},{5,1},{8,12},{9,5},{12,14},{13,9},{14,10},{15,13... | collective-permute-start | bytes 540680 | tf_op jit(solution)/shard_map/ppermute | solution.py:489
  30.4 3.1 %shard_map.108 = (bf16[2,1024,512]{2,1,0:T(8,128)(2,1)S(1)}, bf16[2,1024,512]{2,1,0:T(8,128)(2,1)S(1)}, bf16[2,1024,256]{2,1,0:T(8,128)(2,1)S(1)}, f32[2,1024,128]{2,1,0:T(8,128)S(1)}, f32[1,128,128]{2,1,0:T(8,128)S(1)}) custom-call(f32[8,128]{1,0:T(8,128)S(1)} %get-tuple-element.44.refs_0_, ...), custom_call_target="tpu_custom_call", output_to_operand_aliasing={{3}: (9, {}), {4}: (10, {})} | custom-call | flops 4000000000 | bytes 2629632 | tf_op jit(solution)/shard_map/pallas_call | solution.py:331
  34.3 2.1 %shard_map.109 = (bf16[2,1024,512]{2,1,0:T(8,128)(2,1)S(1)}, bf16[2,1024,256]{2,1,0:T(8,128)(2,1)S(1)}, f32[512,128]{1,0:T(8,128)S(1)}, f32[512,128]{1,0:T(8,128...) custom-call(f32[8,128]{1,0:T(8,128)S(1)} %get-tuple-element.44.refs_, ...), custom_call_target="tpu_custom_call", output_to_operand_aliasing={{4}: (6, {}), {5}: (7, {})} | custom-call | flops 2000000000 | bytes 2154496 | tf_op jit(solution)/shard_map/pallas_call | solution.py:331
  36.4 1.5 %collective-permute-done.16.other_ref = f32[512,128]{1,0:T(8,128)S(1)} collective-permute-done((f32[512,128]{1,0:T(8,128)S(1)}, f32[512,128]{1,0:T(8,128)S(1)}, u32[]{:S(2)}, u32[]{:S(2)}) %collective-permute-start.16) | collective-permute-done | bytes 262176 | tf_op jit(solution)/shard_map/ppermute | solution.py:497
  38.9 1.6 %collective-permute-start.21 = (bf16[640,128]{1,0:T(8,128)(2,1)S(1)}, bf16[640,128]{1,0:T(8,128)(2,1)S(1)}, u32[]{:S(2)}, u32[]{:S(2)}) collective-permute-start(bf16[640,128]{1,0:T(8,128)(2,1)S(1)} %get-tuple-element.58.refs_2_), channel_id=1, source_target_pairs={{0,2},{1,5},{4,0},{5,9},{8,4},{9,13},{12,8},{13,15},{14,12},{15,11... | collective-permute-start | bytes 491528 | tf_op jit(solution)/shard_map/ppermute | solution.py:503
  42.0 3.6 %collective-permute-done.21.refs_3_ = bf16[640,128]{1,0:T(8,128)(2,1)S(1)} collective-permute-done((bf16[640,128]{1,0:T(8,128)(2,1)S(1)}, bf16[640,128]{1,0:T(8,128)(2,1)S(1)}, u32[]{:S(2)}, u32[]{:S(2)}) %collective-permute-start.21) | collective-permute-done | bytes 163872 | tf_op jit(solution)/shard_map/ppermute | solution.py:503
  45.6 1.3 %collective-permute-start.22 = (bf16[640,128]{1,0:T(8,128)(2,1)S(1)}, bf16[640,128]{1,0:T(8,128)(2,1)S(1)}, u32[]{:S(2)}, u32[]{:S(2)}) collective-permute-start(bf16[640,128]{1,0:T(8,128)(2,1)S(1)} %collective-permute-done.21.refs_3_), channel_id=1, source_target_pairs={{0,2},{1,5},{4,0},{5,9},{8,4},{9,13},{12,8},{13,15},{14,12},{15,11... | collective-permute-start | bytes 491528 | tf_op jit(solution)/shard_map/ppermute | solution.py:510
  47.6 1.7 %shard_map.112 = (f32[2,1024,128]{2,1,0:T(8,128)S(1)}, f32[1,128,128]{2,1,0:T(8,128)S(1)}) custom-call(f32[8,128]{1,0:T(8,128)S(1)} %get-tuple-element.44.refs_0_, f32[8,128]{1,0:T(8,128)S(1)} %collective-permute-done.refs_0_.refs_1_, bf16[640,128]{1,0:T(8,128)(2,1)S(1)} %collective-permute-done.17.refs_2_, ...), custom_call_target="tpu_custom_call", output_to_operand_aliasing={{0}: (7, {}), {1}: (8, {})} | custom-call | flops 2000000000 | bytes 6692864 | tf_op jit(solution)/shard_map/pallas_call | solution.py:331
  49.3 2.7 %collective-permute-done.22.refs_3_ = bf16[640,128]{1,0:T(8,128)(2,1)S(1)} collective-permute-done((bf16[640,128]{1,0:T(8,128)(2,1)S(1)}, bf16[640,128]{1,0:T(8,128)(2,1)S(1)}, u32[]{:S(2)}, u32[]{:S(2)}) %collective-permute-start.22) | collective-permute-done | bytes 163872 | tf_op jit(solution)/shard_map/ppermute | solution.py:510
  52.5 1.4 %collective-permute-done.18.refs_2_ = bf16[640,128]{1,0:T(8,128)(2,1)S(1)} collective-permute-done((bf16[640,128]{1,0:T(8,128)(2,1)S(1)}, bf16[640,128]{1,0:T(8,128)(2,1)S(1)}, u32[]{:S(2)}, u32[]{:S(2)}) %collective-permute-start.18) | collective-permute-done | bytes 163872 | tf_op jit(solution)/shard_map/ppermute | solution.py:510
  54.0 1.7 %shard_map.113 = (f32[2,1024,128]{2,1,0:T(8,128)S(1)}, f32[1,128,128]{2,1,0:T(8,128)S(1)}) custom-call(f32[8,128]{1,0:T(8,128)S(1)} %get-tuple-element.44.refs_0_, f32[8,128]{1,0:T(8,128)S(1)} %collective-permute-done.refs_0_.refs_1_, bf16[640,128]{1,0:T(8,128)(2,1)S(1)} %collective-permute-done.18.refs_2_, ...), custom_call_target="tpu_custom_call", output_to_operand_aliasing={{0}: (7, {}), {1}: (8, {})} | custom-call | flops 2000000000 | bytes 6692864 | tf_op jit(solution)/shard_map/pallas_call | solution.py:331
  55.7 3.5 %collective-permute-done.19.refs_2_ = bf16[640,128]{1,0:T(8,128)(2,1)S(1)} collective-permute-done((bf16[640,128]{1,0:T(8,128)(2,1)S(1)}, bf16[640,128]{1,0:T(8,128)(2,1)S(1)}, u32[]{:S(2)}, u32[]{:S(2)}) %collective-permute-start.19) | collective-permute-done | bytes 163872 | tf_op jit(solution)/shard_map/ppermute | solution.py:510
  59.3 1.7 %shard_map.114 = (f32[2,1024,128]{2,1,0:T(8,128)S(1)}, f32[1,128,128]{2,1,0:T(8,128)S(1)}) custom-call(f32[8,128]{1,0:T(8,128)S(1)} %get-tuple-element.44.refs_0_, f32[8,128]{1,0:T(8,128)S(1)} %collective-permute-done.refs_0_.refs_1_, bf16[640,128]{1,0:T(8,128)(2,1)S(1)} %collective-permute-done.19.refs_2_, ...), custom_call_target="tpu_custom_call", output_to_operand_aliasing={{0}: (7, {}), {1}: (8, {})} | custom-call | flops 2000000000 | bytes 6692864 | tf_op jit(solution)/shard_map/pallas_call | solution.py:331
  61.0 3.5 %collective-permute-done.20.refs_2_ = bf16[640,128]{1,0:T(8,128)(2,1)S(1)} collective-permute-done((bf16[640,128]{1,0:T(8,128)(2,1)S(1)}, bf16[640,128]{1,0:T(8,128)(2,1)S(1)}, u32[]{:S(2)}, u32[]{:S(2)}) %collective-permute-start.20) | collective-permute-done | bytes 163872 | tf_op jit(solution)/shard_map/ppermute | solution.py:510
  64.5 1.2 %shard_map.115 = (f32[512,128]{1,0:T(8,128)S(1)}, f32[512,128]{1,0:T(8,128)S(1)}, f32[2,1024,128]{2,1,0:T(8,128)S(1)}, f32[1,128,128]{2,1,0:T(8,128)S(1)}) custom-call(f32[8,128]{1,0:T(8,128)S(1)} %get-tuple-element.44.refs_0_, f32[8,128]{1,0:T(8,128)S(1)} %collective-permute-done.refs_0_.refs_1_, ...), custom_call_target="tpu_custom_call", output_to_operand_aliasing={{2}: (5, {}), {3}: (6, {})} | custom-call | flops 1000000000 | bytes 4431872 | tf_op jit(solution)/shard_map/pallas_call | solution.py:331
  65.8 1.5 %collective-permute-done.24.other_ref = f32[512,128]{1,0:T(8,128)S(1)} collective-permute-done((f32[512,128]{1,0:T(8,128)S(1)}, f32[512,128]{1,0:T(8,128)S(1)}, u32[]{:S(2)}, u32[]{:S(2)}) %collective-permute-start.24) | collective-permute-done | bytes 262176 | tf_op jit(solution)/shard_map/ppermute | solution.py:516
  (49 shorter events, 15.5 us)
Async XLA Ops:
  0.6 9.0 %collective-permute-start.10 = (bf16[64,1024]{1,0:T(8,128)(2,1)}, bf16[64,1024]{1,0:T(8,128)(2,1)S(1)}, u32[]{:S(2)}, u32[]{:S(2)}) collective-permute-start(bf16[64,1024]{1,0:T(8,128)(2,1)} %coords_ref.1), channel_id=1, source_target_pairs={{0,2},{1,5},{4,0},{5,9},{8,4},{9,13},{12,8},{13,15},{14,12},{15,11... | collective-permute-start | bytes 393224 | tf_op jit(solution)/shard_map/ppermute | solution.py:387
  3.6 6.9 %collective-permute-start.2 = (bf16[64,1024]{1,0:T(8,128)(2,1)}, bf16[64,1024]{1,0:T(8,128)(2,1)S(1)}, u32[]{:S(2)}, u32[]{:S(2)}) collective-permute-start(bf16[64,1024]{1,0:T(8,128)(2,1)} %coords_ref.1), channel_id=1, source_target_pairs={{0,4},{1,3},{4,8},{5,1},{8,12},{9,5},{12,14},{13,9},{14,10},{15,13... | collective-permute-start | bytes 393224 | tf_op jit(solution)/shard_map/ppermute | solution.py:387
  3.8 7.9 %collective-permute-start.1 = (bf16[64,1024]{1,0:T(8,128)(2,1)}, bf16[64,1024]{1,0:T(8,128)(2,1)S(1)}, u32[]{:S(2)}, u32[]{:S(2)}) collective-permute-start(bf16[64,1024]{1,0:T(8,128)(2,1)} %coords_ref.1), channel_id=1, source_target_pairs={{0,1},{1,0},{2,3},{3,2},{4,5},{5,4},{6,7},{7,6},{8,9},{9,8},{10,11... | collective-permute-start | bytes 393224 | tf_op jit(solution)/shard_map/ppermute | solution.py:386
  6.1 2.4 %collective-permute-start = (f32[8,128]{1,0:T(8,128)}, f32[8,128]{1,0:T(8,128)S(1)}, u32[]{:S(2)}, u32[]{:S(2)}) collective-permute-start(f32[8,128]{1,0:T(8,128)} %get-tuple-element.42), channel_id=1, source_target_pairs={{0,1},{1,0},{2,3},{3,2},{4,5},{5,4},{6,7},{7,6},{8,9},{9,8},{10,11... | collective-permute-start | bytes 12296 | tf_op jit(solution)/shard_map/ppermute | solution.py:399
  6.6 8.1 %collective-permute-start.13 = (bf16[704,128]{1,0:T(8,128)(2,1)}, bf16[704,128]{1,0:T(8,128)(2,1)S(1)}, u32[]{:S(2)}, u32[]{:S(2)}) collective-permute-start(bf16[704,128]{1,0:T(8,128)(2,1)} %get-tuple-element.45), channel_id=1, source_target_pairs={{0,2},{1,5},{4,0},{5,9},{8,4},{9,13},{12,8},{13,15},{14,12},{15,11... | collective-permute-start | bytes 540680 | tf_op jit(solution)/shard_map/ppermute | solution.py:478
  8.5 7.3 %collective-permute-start.6 = (bf16[704,128]{1,0:T(8,128)(2,1)}, bf16[704,128]{1,0:T(8,128)(2,1)S(1)}, u32[]{:S(2)}, u32[]{:S(2)}) collective-permute-start(bf16[704,128]{1,0:T(8,128)(2,1)} %get-tuple-element.45), channel_id=1, source_target_pairs={{0,4},{1,3},{4,8},{5,1},{8,12},{9,5},{12,14},{13,9},{14,10},{15,13... | collective-permute-start | bytes 540680 | tf_op jit(solution)/shard_map/ppermute | solution.py:478
  9.6 10.3 %collective-permute-start.11 = (bf16[64,1024]{1,0:T(8,128)(2,1)S(1)}, bf16[64,1024]{1,0:T(8,128)(2,1)S(1)}, u32[]{:S(2)}, u32[]{:S(2)}) collective-permute-start(bf16[64,1024]{1,0:T(8,128)(2,1)S(1)} %collective-permute-done.10.refs_3_), channel_id=1, source_target_pairs={{0,2},{1,5},{4,0},{5,9},{8,4},{9,13},{12,8},{13,15},{14,12},{15,11... | collective-permute-start | bytes 393224 | tf_op jit(solution)/shard_map/ppermute | solution.py:488
  10.6 10.4 %collective-permute-start.3 = (bf16[64,1024]{1,0:T(8,128)(2,1)S(1)}, bf16[64,1024]{1,0:T(8,128)(2,1)S(1)}, u32[]{:S(2)}, u32[]{:S(2)}) collective-permute-start(bf16[64,1024]{1,0:T(8,128)(2,1)S(1)} %collective-permute-done.2.refs_2_), channel_id=1, source_target_pairs={{0,4},{1,3},{4,8},{5,1},{8,12},{9,5},{12,14},{13,9},{14,10},{15,13... | collective-permute-start | bytes 393224 | tf_op jit(solution)/shard_map/ppermute | solution.py:488
  14.7 7.2 %collective-permute-start.14 = (bf16[704,128]{1,0:T(8,128)(2,1)S(1)}, bf16[704,128]{1,0:T(8,128)(2,1)S(1)}, u32[]{:S(2)}, u32[]{:S(2)}) collective-permute-start(bf16[704,128]{1,0:T(8,128)(2,1)S(1)} %collective-permute-done.13.refs_5_.refs_7_), channel_id=1, source_target_pairs={{0,2},{1,5},{4,0},{5,9},{8,4},{9,13},{12,8},{13,15},{14,12},{15,11... | collective-permute-start | bytes 540680 | tf_op jit(solution)/shard_map/ppermute | solution.py:489
  15.8 7.2 %collective-permute-start.7 = (bf16[704,128]{1,0:T(8,128)(2,1)S(1)}, bf16[704,128]{1,0:T(8,128)(2,1)S(1)}, u32[]{:S(2)}, u32[]{:S(2)}) collective-permute-start(bf16[704,128]{1,0:T(8,128)(2,1)S(1)} %collective-permute-done.6.refs_4_.refs_6_), channel_id=1, source_target_pairs={{0,4},{1,3},{4,8},{5,1},{8,12},{9,5},{12,14},{13,9},{14,10},{15,13... | collective-permute-start | bytes 540680 | tf_op jit(solution)/shard_map/ppermute | solution.py:489
  19.9 10.4 %collective-permute-start.12 = (bf16[64,1024]{1,0:T(8,128)(2,1)S(1)}, bf16[64,1024]{1,0:T(8,128)(2,1)S(1)}, u32[]{:S(2)}, u32[]{:S(2)}) collective-permute-start(bf16[64,1024]{1,0:T(8,128)(2,1)S(1)} %collective-permute-done.11.refs_3_), channel_id=1, source_target_pairs={{0,2},{1,5},{4,0},{5,9},{8,4},{9,13},{12,8},{13,15},{14,12},{15,11... | collective-permute-start | bytes 393224 | tf_op jit(solution)/shard_map/ppermute | solution.py:488
  21.0 6.1 %collective-permute-start.4 = (bf16[64,1024]{1,0:T(8,128)(2,1)S(1)}, bf16[64,1024]{1,0:T(8,128)(2,1)S(1)}, u32[]{:S(2)}, u32[]{:S(2)}) collective-permute-start(bf16[64,1024]{1,0:T(8,128)(2,1)S(1)} %collective-permute-done.3.refs_2_), channel_id=1, source_target_pairs={{0,4},{1,3},{4,8},{5,1},{8,12},{9,5},{12,14},{13,9},{14,10},{15,13... | collective-permute-start | bytes 393224 | tf_op jit(solution)/shard_map/ppermute | solution.py:488
  22.0 8.4 %collective-permute-start.15 = (bf16[704,128]{1,0:T(8,128)(2,1)S(1)}, bf16[704,128]{1,0:T(8,128)(2,1)S(1)}, u32[]{:S(2)}, u32[]{:S(2)}) collective-permute-start(bf16[704,128]{1,0:T(8,128)(2,1)S(1)} %collective-permute-done.14.refs_5_.refs_7_), channel_id=1, source_target_pairs={{0,2},{1,5},{4,0},{5,9},{8,4},{9,13},{12,8},{13,15},{14,12},{15,11... | collective-permute-start | bytes 540680 | tf_op jit(solution)/shard_map/ppermute | solution.py:489
  23.1 5.7 %collective-permute-start.8 = (bf16[704,128]{1,0:T(8,128)(2,1)S(1)}, bf16[704,128]{1,0:T(8,128)(2,1)S(1)}, u32[]{:S(2)}, u32[]{:S(2)}) collective-permute-start(bf16[704,128]{1,0:T(8,128)(2,1)S(1)} %collective-permute-done.7.refs_4_.refs_6_), channel_id=1, source_target_pairs={{0,4},{1,3},{4,8},{5,1},{8,12},{9,5},{12,14},{13,9},{14,10},{15,13... | collective-permute-start | bytes 540680 | tf_op jit(solution)/shard_map/ppermute | solution.py:489
  27.1 6.4 %collective-permute-start.5 = (bf16[64,1024]{1,0:T(8,128)(2,1)S(1)}, bf16[64,1024]{1,0:T(8,128)(2,1)S(1)}, u32[]{:S(2)}, u32[]{:S(2)}) collective-permute-start(bf16[64,1024]{1,0:T(8,128)(2,1)S(1)} %collective-permute-done.4.refs_2_), channel_id=1, source_target_pairs={{0,4},{1,3},{4,8},{5,1},{8,12},{9,5},{12,14},{13,9},{14,10},{15,13... | collective-permute-start | bytes 393224 | tf_op jit(solution)/shard_map/ppermute | solution.py:488
  28.8 5.5 %collective-permute-start.9 = (bf16[704,128]{1,0:T(8,128)(2,1)S(1)}, bf16[704,128]{1,0:T(8,128)(2,1)S(1)}, u32[]{:S(2)}, u32[]{:S(2)}) collective-permute-start(bf16[704,128]{1,0:T(8,128)(2,1)S(1)} %collective-permute-done.8.refs_4_.refs_6_), channel_id=1, source_target_pairs={{0,4},{1,3},{4,8},{5,1},{8,12},{9,5},{12,14},{13,9},{14,10},{15,13... | collective-permute-start | bytes 540680 | tf_op jit(solution)/shard_map/ppermute | solution.py:489
  36.4 1.6 %collective-permute-start.16 = (f32[512,128]{1,0:T(8,128)S(1)}, f32[512,128]{1,0:T(8,128)S(1)}, u32[]{:S(2)}, u32[]{:S(2)}) collective-permute-start(f32[512,128]{1,0:T(8,128)S(1)} %get-tuple-element.56), channel_id=1, source_target_pairs={{0,1},{1,0},{2,3},{3,2},{4,5},{5,4},{6,7},{7,6},{8,9},{9,8},{10,11... | collective-permute-start | bytes 786440 | tf_op jit(solution)/shard_map/ppermute | solution.py:497
  38.9 6.7 %collective-permute-start.21 = (bf16[640,128]{1,0:T(8,128)(2,1)S(1)}, bf16[640,128]{1,0:T(8,128)(2,1)S(1)}, u32[]{:S(2)}, u32[]{:S(2)}) collective-permute-start(bf16[640,128]{1,0:T(8,128)(2,1)S(1)} %get-tuple-element.58.refs_2_), channel_id=1, source_target_pairs={{0,2},{1,5},{4,0},{5,9},{8,4},{9,13},{12,8},{13,15},{14,12},{15,11... | collective-permute-start | bytes 491528 | tf_op jit(solution)/shard_map/ppermute | solution.py:503
  40.4 6.4 %collective-permute-start.17 = (bf16[640,128]{1,0:T(8,128)(2,1)S(1)}, bf16[640,128]{1,0:T(8,128)(2,1)S(1)}, u32[]{:S(2)}, u32[]{:S(2)}) collective-permute-start(bf16[640,128]{1,0:T(8,128)(2,1)S(1)} %get-tuple-element.58.refs_2_), channel_id=1, source_target_pairs={{0,4},{1,3},{4,8},{5,1},{8,12},{9,5},{12,14},{13,9},{14,10},{15,13... | collective-permute-start | bytes 491528 | tf_op jit(solution)/shard_map/ppermute | solution.py:503
  45.6 6.4 %collective-permute-start.22 = (bf16[640,128]{1,0:T(8,128)(2,1)S(1)}, bf16[640,128]{1,0:T(8,128)(2,1)S(1)}, u32[]{:S(2)}, u32[]{:S(2)}) collective-permute-start(bf16[640,128]{1,0:T(8,128)(2,1)S(1)} %collective-permute-done.21.refs_3_), channel_id=1, source_target_pairs={{0,2},{1,5},{4,0},{5,9},{8,4},{9,13},{12,8},{13,15},{14,12},{15,11... | collective-permute-start | bytes 491528 | tf_op jit(solution)/shard_map/ppermute | solution.py:510
  46.9 7.0 %collective-permute-start.18 = (bf16[640,128]{1,0:T(8,128)(2,1)S(1)}, bf16[640,128]{1,0:T(8,128)(2,1)S(1)}, u32[]{:S(2)}, u32[]{:S(2)}) collective-permute-start(bf16[640,128]{1,0:T(8,128)(2,1)S(1)} %collective-permute-done.17.refs_2_), channel_id=1, source_target_pairs={{0,4},{1,3},{4,8},{5,1},{8,12},{9,5},{12,14},{13,9},{14,10},{15,13... | collective-permute-start | bytes 491528 | tf_op jit(solution)/shard_map/ppermute | solution.py:510
  52.0 7.4 %collective-permute-start.23 = (bf16[640,128]{1,0:T(8,128)(2,1)S(1)}, bf16[640,128]{1,0:T(8,128)(2,1)S(1)}, u32[]{:S(2)}, u32[]{:S(2)}) collective-permute-start(bf16[640,128]{1,0:T(8,128)(2,1)S(1)} %collective-permute-done.22.refs_3_), channel_id=1, source_target_pairs={{0,2},{1,5},{4,0},{5,9},{8,4},{9,13},{12,8},{13,15},{14,12},{15,11... | collective-permute-start | bytes 491528 | tf_op jit(solution)/shard_map/ppermute | solution.py:510
  53.9 5.3 %collective-permute-start.19 = (bf16[640,128]{1,0:T(8,128)(2,1)S(1)}, bf16[640,128]{1,0:T(8,128)(2,1)S(1)}, u32[]{:S(2)}, u32[]{:S(2)}) collective-permute-start(bf16[640,128]{1,0:T(8,128)(2,1)S(1)} %collective-permute-done.18.refs_2_), channel_id=1, source_target_pairs={{0,4},{1,3},{4,8},{5,1},{8,12},{9,5},{12,14},{13,9},{14,10},{15,13... | collective-permute-start | bytes 491528 | tf_op jit(solution)/shard_map/ppermute | solution.py:510
  59.2 5.3 %collective-permute-start.20 = (bf16[640,128]{1,0:T(8,128)(2,1)S(1)}, bf16[640,128]{1,0:T(8,128)(2,1)S(1)}, u32[]{:S(2)}, u32[]{:S(2)}) collective-permute-start(bf16[640,128]{1,0:T(8,128)(2,1)S(1)} %collective-permute-done.19.refs_2_), channel_id=1, source_target_pairs={{0,4},{1,3},{4,8},{5,1},{8,12},{9,5},{12,14},{13,9},{14,10},{15,13... | collective-permute-start | bytes 491528 | tf_op jit(solution)/shard_map/ppermute | solution.py:510
  (6 other events, 17.6 us)

commit v16 on v14

--- a/solution.py
+++ b/solution.py
@@ -240,8 +240,8 @@
 
     devices = {spot: device_of(ring, spot) for spot in spots}
 
-    def near_part(turn, spot, core, leaf):
-        at = core * len(near_spots) + near_spots.index(spot)
+    def near_values(turn, spot, core, leaf):
+        at = turn if first else core * len(near_spots) + near_spots.index(spot)
         table = table_of(core)
         named = [
             picked(table, devices[spot] * LEAVES + which)[0:LEAVES] for which in range(LEAVES)
@@ -258,7 +258,10 @@
         half = jnp.where(lane[0:1] < LANES // LEAVES, 1.0 - second, second).astype(bf16)
         charges_ref[at] = charge_refs[spot][0:points, :] * half
         kept = kept_refs[spot].at[turn] if kept_refs else None
-        added = matmul(values(core, near_ref.at[at] if makes else None, kept), charges_ref[at])
+        return values(core, near_ref.at[at] if makes else None, kept), at, times
+
+    def near_product(core, kernel, at, times):
+        added = matmul(kernel, charges_ref[at])
         return [times[own : own + 1] * added[span_of(own)] for own in range(LEAVES)]
 
     weights = []
@@ -278,22 +281,24 @@
     if far_spots and makes:
         put_sources(far_ref, jnp.concatenate(skeletons, axis=1))
 
-    def far_part(core):
+    def far_values(core):
         table = table_of(core)
-        kernel = values(
-            core,
-            far_ref if makes else None,
-            None if far_kept_ref is None else far_kept_ref.at[core],
-        )
-        added = []
         for own in range(LEAVES):
             for position, (block, node) in enumerate(weights):
                 scaled = block * picked(table, node)[LEAVES + own : LEAVES + own + 1]
                 high = scaled.astype(bf16).astype(f32)
                 rows = slice(position * LANES, (position + 1) * LANES)
-                far_charges_ref[core * LEAVES + own, rows, :] = jnp.where(low_half, high, scaled - high).astype(bf16)
-            added.append(matmul(kernel[span_of(own)], far_charges_ref[core * LEAVES + own]))
-        return added
+                far_charges_ref[core * LEAVES + own, rows, :] = jnp.where(
+                    low_half, high, scaled - high
+                ).astype(bf16)
+        kept = None if far_kept_ref is None else far_kept_ref.at[core]
+        return (values(core, far_ref if makes else None, kept),)
+
+    def far_product(core, kernel):
+        return [
+            matmul(kernel[span_of(own)], far_charges_ref[core * LEAVES + own])
+            for own in range(LEAVES)
+        ]
 
     def add(core, parts):
         for own in range(LEAVES):
@@ -302,15 +307,28 @@
                 total = total + part[own]
             total_ref[core, span_of(own), :] = total
 
-    if first:
-        for leaf in range(LEAVES):
-            add(0, [near_part(leaf, 0, 0, leaf)])
-        add(1, [near_part(LEAVES, 0, 1, None), far_part(1)])
-    else:
-
-        for core in range(CORES):
-            parts = [near_part(core, spot, core, None) for spot in near_spots]
-            add(core, parts + ([far_part(core)] if far_spots else []))
+    work = []
+    for core in range(CORES):
+        if first and core == 0:
+            wanted = [(leaf, 0, leaf) for leaf in range(LEAVES)]
+        elif first:
+            wanted = [(LEAVES, 0, None)]
+        else:
+            wanted = [(core, spot, None) for spot in near_spots]
+        for turn, spot, leaf in wanted:
+            work.append((core, functools.partial(near_values, turn, spot, core, leaf), near_product))
+        if far_spots and not (first and core == 0):
+            work.append((core, functools.partial(far_values, core), far_product))
+    parts = [[] for _ in range(CORES)]
+    waiting = None
+    for step in work + [None]:
+        found = step[1]() if step else None
+        if waiting:
+            core, product, ready = waiting
+            parts[core].append(product(core, *ready))
+            if not step or step[0] != core:
+                add(core, parts[core])
+        waiting = (step[0], step[2], found) if step else None
 
     if last:
         for core, ref in enumerate(half_refs):
@@ -448,11 +466,11 @@
         far_width = max(LANES, LANES * (len(far_spots) + (n_sub if last else 0)))
         scratch = [
             pltpu.VMEM((CORES * LEAVES, far_width, LANES), bf16),
-            pltpu.VMEM((CORES * len(near_spots), points, LANES), bf16),
+            pltpu.VMEM((LEAVES + 1 if first else CORES * len(near_spots), points, LANES), bf16),
         ]
         if makes:
             scratch += [
-                pltpu.VMEM((CORES * len(near_spots), LANES, points), bf16),
+                pltpu.VMEM((LEAVES + 1 if first else CORES * len(near_spots), LANES, points), bf16),
                 pltpu.VMEM((LANES, far_width), bf16),
             ]
         names, outs = [], []

time: 66.8 us -> 66.9 us (level)
  transfers between devices with their start and end apart: 25 -> 25, of which waited for: 10 -> 9; matrix products, arithmetic and copies ran while one was open for 0% -> 0% of each run, Pallas kernels for 31% -> 31%
where the time goes in v16:
time: 66.9 us; the launch traced here: 66.7 us
  starting transfers between devices  27.1 us (41%)
  Pallas kernels  25.6 us (38%)
  waiting for transfers between devices  12.3 us (18%)
  local copies, waits for them, and re-layouts  0.98 us (1%)
  between operations  0.83 us (1%)
    pallas_call x16, Pallas kernels, call(): pl.pallas_call(body, grid=(1,), out_shape=out_shapes, in_specs=specs, out...  25.6 us
    ppermute x3, starting transfers between devices, on_device(): one_next = one_way(one)  6.77 us
    ppermute x5, starting transfers between devices, on_device(): sent = (one_way(sent[0]), None if final else other_way(sent[1]))  5.64 us
    ppermute x3, waiting for transfers between devices, on_device(): one_next = one_way(one)  4.97 us
    ppermute x3, starting transfers between devices, on_device(): one_way(coords_next[0])  3.73 us
    ppermute x2, starting transfers between devices, on_device(): coords_next = (one_way(coords), other_way(coords))  3.14 us
    ppermute x2, waiting for transfers between devices, on_device(): to_sibling(results['other'])  3.04 us
    ppermute x2, starting transfers between devices, on_device(): sent = (one_way(message), other_way(message))  2.99 us
  transfers between devices with their start and end apart: 25, of which 9 were waited for; matrix products, arithmetic and copies ran while one was open for 0% of the time, Pallas kernels for 31%

profile of v16, /device:TPU:0, one launch (start us, length us, event | category | flops | bytes accessed | tf_op | source)
XLA Modules:
  0.0 66.7 jit_solution(6330351073889154210)
XLA Ops:
  0.6 3.0 %collective-permute-start.10 = (bf16[64,1024]{1,0:T(8,128)(2,1)}, bf16[64,1024]{1,0:T(8,128)(2,1)S(1)}, u32[]{:S(2)}, u32[]{:S(2)}) collective-permute-start(bf16[64,1024]{1,0:T(8,128)(2,1)} %coords_ref.1), channel_id=1, source_target_pairs={{0,2},{1,5},{4,0},{5,9},{8,4},{9,13},{12,8},{13,15},{14,12},{15,11... | collective-permute-start | bytes 393224 | tf_op jit(solution)/shard_map/ppermute | solution.py:423
  3.8 2.3 %shard_map.104 = (bf16[704,128]{1,0:T(8,128)(2,1)}, bf16[1232,128]{1,0:T(8,128)(2,1)}, f32[8,128]{1,0:T(8,128)}) custom-call(s32[2,16]{1,0:T(2,128)} %near_ref.1, s32[2,32]{1,0:T(2,128)} %far_ref.1, bf16[64,1024]{1,0:T(8,128)(2,1)} %coords_ref.1, bf16[64,1024]{1,0:T(8,128)(2,1)} %charges_ref.1, bf16[64,128]{1,0:T(8,128)(2,1)} %points_ref.1, ...), custom_call_target="tpu_custom_call" | custom-call | bytes 639360 | tf_op jit(solution)/shard_map/pallas_call | solution.py:367
  6.6 1.9 %collective-permute-start.13 = (bf16[704,128]{1,0:T(8,128)(2,1)}, bf16[704,128]{1,0:T(8,128)(2,1)S(1)}, u32[]{:S(2)}, u32[]{:S(2)}) collective-permute-start(bf16[704,128]{1,0:T(8,128)(2,1)} %get-tuple-element.52), channel_id=1, source_target_pairs={{0,2},{1,5},{4,0},{5,9},{8,4},{9,13},{12,8},{13,15},{14,12},{15,11... | collective-permute-start | bytes 540680 | tf_op jit(solution)/shard_map/ppermute | solution.py:517
  12.6 2.1 %shard_map.105 = (bf16[2,1024,128]{2,1,0:T(8,128)(2,1)S(1)}, f32[8,128]{1,0:T(8,128)S(1)}, bf16[3,1024,512]{2,1,0:T(8,128)(2,1)S(1)}, bf16[2,1024,128]{2,1,0:T(8...) custom-call(f32[8,128]{1,0:T(8,128)S(1)} %collective-permute-done.refs_0_.refs_1_, ...), custom_call_target="tpu_custom_call" | custom-call | flops 2000000000 | bytes 450560 | tf_op jit(solution)/shard_map/pallas_call | solution.py:367
  16.9 3.1 %shard_map.106 = (bf16[2,1024,512]{2,1,0:T(8,128)(2,1)S(1)}, bf16[2,1024,512]{2,1,0:T(8,128)(2,1)S(1)}, bf16[2,1024,256]{2,1,0:T(8,128)(2,1)S(1)}, f32[2,1024,128]{2,1,0:T(8,128)S(1)}, f32[1,128,128]{2,1,0:T(8,128)S(1)}) custom-call(f32[8,128]{1,0:T(8,128)S(1)} %get-tuple-element.51.refs_0_, ...), custom_call_target="tpu_custom_call", output_to_operand_aliasing={{3}: (9, {}), {4}: (10, {})} | custom-call | flops 4000000000 | bytes 2629632 | tf_op jit(solution)/shard_map/pallas_call | solution.py:367
  24.0 3.0 %shard_map.107 = (bf16[2,1024,512]{2,1,0:T(8,128)(2,1)S(1)}, bf16[2,1024,512]{2,1,0:T(8,128)(2,1)S(1)}, bf16[2,1024,256]{2,1,0:T(8,128)(2,1)S(1)}, f32[2,1024,128]{2,1,0:T(8,128)S(1)}, f32[1,128,128]{2,1,0:T(8,128)S(1)}) custom-call(f32[8,128]{1,0:T(8,128)S(1)} %get-tuple-element.51.refs_0_, ...), custom_call_target="tpu_custom_call", output_to_operand_aliasing={{3}: (9, {}), {4}: (10, {})} | custom-call | flops 4000000000 | bytes 2629632 | tf_op jit(solution)/shard_map/pallas_call | solution.py:367
  27.1 1.6 %collective-permute-start.5 = (bf16[64,1024]{1,0:T(8,128)(2,1)S(1)}, bf16[64,1024]{1,0:T(8,128)(2,1)S(1)}, u32[]{:S(2)}, u32[]{:S(2)}) collective-permute-start(bf16[64,1024]{1,0:T(8,128)(2,1)S(1)} %collective-permute-done.4.refs_2_), channel_id=1, source_target_pairs={{0,4},{1,3},{4,8},{5,1},{8,12},{9,5},{12,14},{13,9},{14,10},{15,13... | collective-permute-start | bytes 393224 | tf_op jit(solution)/shard_map/ppermute | solution.py:527
  28.8 1.5 %collective-permute-start.9 = (bf16[704,128]{1,0:T(8,128)(2,1)S(1)}, bf16[704,128]{1,0:T(8,128)(2,1)S(1)}, u32[]{:S(2)}, u32[]{:S(2)}) collective-permute-start(bf16[704,128]{1,0:T(8,128)(2,1)S(1)} %collective-permute-done.8.refs_4_.refs_6_), channel_id=1, source_target_pairs={{0,4},{1,3},{4,8},{5,1},{8,12},{9,5},{12,14},{13,9},{14,10},{15,13... | collective-permute-start | bytes 540680 | tf_op jit(solution)/shard_map/ppermute | solution.py:528
  30.3 3.1 %shard_map.108 = (bf16[2,1024,512]{2,1,0:T(8,128)(2,1)S(1)}, bf16[2,1024,512]{2,1,0:T(8,128)(2,1)S(1)}, bf16[2,1024,256]{2,1,0:T(8,128)(2,1)S(1)}, f32[2,1024,128]{2,1,0:T(8,128)S(1)}, f32[1,128,128]{2,1,0:T(8,128)S(1)}) custom-call(f32[8,128]{1,0:T(8,128)S(1)} %get-tuple-element.51.refs_0_, ...), custom_call_target="tpu_custom_call", output_to_operand_aliasing={{3}: (9, {}), {4}: (10, {})} | custom-call | flops 4000000000 | bytes 2629632 | tf_op jit(solution)/shard_map/pallas_call | solution.py:367
  34.3 2.1 %shard_map.109 = (bf16[2,1024,512]{2,1,0:T(8,128)(2,1)S(1)}, bf16[2,1024,256]{2,1,0:T(8,128)(2,1)S(1)}, f32[512,128]{1,0:T(8,128)S(1)}, f32[512,128]{1,0:T(8,128...) custom-call(f32[8,128]{1,0:T(8,128)S(1)} %get-tuple-element.51.refs_, ...), custom_call_target="tpu_custom_call", output_to_operand_aliasing={{4}: (6, {}), {5}: (7, {})} | custom-call | flops 2000000000 | bytes 2154496 | tf_op jit(solution)/shard_map/pallas_call | solution.py:367
  36.5 1.5 %collective-permute-done.16.other_ref = f32[512,128]{1,0:T(8,128)S(1)} collective-permute-done((f32[512,128]{1,0:T(8,128)S(1)}, f32[512,128]{1,0:T(8,128)S(1)}, u32[]{:S(2)}, u32[]{:S(2)}) %collective-permute-start.16) | collective-permute-done | bytes 262176 | tf_op jit(solution)/shard_map/ppermute | solution.py:536
  38.9 1.5 %collective-permute-start.17 = (bf16[640,128]{1,0:T(8,128)(2,1)S(1)}, bf16[640,128]{1,0:T(8,128)(2,1)S(1)}, u32[]{:S(2)}, u32[]{:S(2)}) collective-permute-start(bf16[640,128]{1,0:T(8,128)(2,1)S(1)} %get-tuple-element.65.refs_2_), channel_id=1, source_target_pairs={{0,4},{1,3},{4,8},{5,1},{8,12},{9,5},{12,14},{13,9},{14,10},{15,13... | collective-permute-start | bytes 491528 | tf_op jit(solution)/shard_map/ppermute | solution.py:553
  40.4 1.1 %shard_map.111 = (f32[2,1024,128]{2,1,0:T(8,128)S(1)}, f32[1,128,128]{2,1,0:T(8,128)S(1)}) custom-call(f32[8,128]{1,0:T(8,128)S(1)} %get-tuple-element.51.refs_0_, f32[8,128]{1,0:T(8,128)S(1)} %collective-permute-done.refs_0_.refs_1_, bf16[640,128]{1,0:T(8,128)(2,1)S(1)} %get-tuple-element.65.refs_2_, bf16[3,1024,512]{2,1,0:T(8,128)(2,1)S(1)} %get-tuple-element.69.refs_3_, ...), custom_call_target="tpu_custom_call" | custom-call | flops 1000000000 | bytes 3842048 | tf_op jit(solution)/shard_map/pallas_call | solution.py:367
  42.1 2.5 %collective-permute-done.17.refs_2_ = bf16[640,128]{1,0:T(8,128)(2,1)S(1)} collective-permute-done((bf16[640,128]{1,0:T(8,128)(2,1)S(1)}, bf16[640,128]{1,0:T(8,128)(2,1)S(1)}, u32[]{:S(2)}, u32[]{:S(2)}) %collective-permute-start.17) | collective-permute-done | bytes 163872 | tf_op jit(solution)/shard_map/ppermute | solution.py:553
  44.5 2.5 %collective-permute-start.18 = (bf16[640,128]{1,0:T(8,128)(2,1)S(1)}, bf16[640,128]{1,0:T(8,128)(2,1)S(1)}, u32[]{:S(2)}, u32[]{:S(2)}) collective-permute-start(bf16[640,128]{1,0:T(8,128)(2,1)S(1)} %collective-permute-done.17.refs_2_), channel_id=1, source_target_pairs={{0,4},{1,3},{4,8},{5,1},{8,12},{9,5},{12,14},{13,9},{14,10},{15,13... | collective-permute-start | bytes 491528 | tf_op jit(solution)/shard_map/ppermute | solution.py:557
  47.9 1.1 %shard_map.115 = (f32[2,1024,128]{2,1,0:T(8,128)S(1)}, f32[1,128,128]{2,1,0:T(8,128)S(1)}) custom-call(f32[8,128]{1,0:T(8,128)S(1)} %get-tuple-element.51.refs_0_, f32[8,128]{1,0:T(8,128)S(1)} %collective-permute-done.refs_0_.refs_1_, bf16[640,128]{1,0:T(8,128)(2,1)S(1)} %collective-permute-done.17.refs_2_, ...), custom_call_target="tpu_custom_call", output_to_operand_aliasing={{0}: (6, {}), {1}: (7, {})} | custom-call | flops 1000000000 | bytes 4595712 | tf_op jit(solution)/shard_map/pallas_call | solution.py:367
  49.1 2.2 %collective-permute-done.18.refs_2_ = bf16[640,128]{1,0:T(8,128)(2,1)S(1)} collective-permute-done((bf16[640,128]{1,0:T(8,128)(2,1)S(1)}, bf16[640,128]{1,0:T(8,128)(2,1)S(1)}, u32[]{:S(2)}, u32[]{:S(2)}) %collective-permute-start.18) | collective-permute-done | bytes 163872 | tf_op jit(solution)/shard_map/ppermute | solution.py:557
  51.2 2.5 %collective-permute-start.19 = (bf16[640,128]{1,0:T(8,128)(2,1)S(1)}, bf16[640,128]{1,0:T(8,128)(2,1)S(1)}, u32[]{:S(2)}, u32[]{:S(2)}) collective-permute-start(bf16[640,128]{1,0:T(8,128)(2,1)S(1)} %collective-permute-done.18.refs_2_), channel_id=1, source_target_pairs={{0,4},{1,3},{4,8},{5,1},{8,12},{9,5},{12,14},{13,9},{14,10},{15,13... | collective-permute-start | bytes 491528 | tf_op jit(solution)/shard_map/ppermute | solution.py:557
  54.9 1.1 %shard_map.118 = (f32[2,1024,128]{2,1,0:T(8,128)S(1)}, f32[1,128,128]{2,1,0:T(8,128)S(1)}) custom-call(f32[8,128]{1,0:T(8,128)S(1)} %get-tuple-element.51.refs_0_, f32[8,128]{1,0:T(8,128)S(1)} %collective-permute-done.refs_0_.refs_1_, bf16[640,128]{1,0:T(8,128)(2,1)S(1)} %collective-permute-done.18.refs_2_, ...), custom_call_target="tpu_custom_call", output_to_operand_aliasing={{0}: (6, {}), {1}: (7, {})} | custom-call | flops 1000000000 | bytes 4595712 | tf_op jit(solution)/shard_map/pallas_call | solution.py:367
  56.0 1.8 %collective-permute-done.19.refs_2_ = bf16[640,128]{1,0:T(8,128)(2,1)S(1)} collective-permute-done((bf16[640,128]{1,0:T(8,128)(2,1)S(1)}, bf16[640,128]{1,0:T(8,128)(2,1)S(1)}, u32[]{:S(2)}, u32[]{:S(2)}) %collective-permute-start.19) | collective-permute-done | bytes 163872 | tf_op jit(solution)/shard_map/ppermute | solution.py:557
  57.8 1.8 %collective-permute-start.20 = (bf16[640,128]{1,0:T(8,128)(2,1)S(1)}, bf16[640,128]{1,0:T(8,128)(2,1)S(1)}, u32[]{:S(2)}, u32[]{:S(2)}) collective-permute-start(bf16[640,128]{1,0:T(8,128)(2,1)S(1)} %collective-permute-done.19.refs_2_), channel_id=1, source_target_pairs={{0,4},{1,3},{4,8},{5,1},{8,12},{9,5},{12,14},{13,9},{14,10},{15,13... | collective-permute-start | bytes 491528 | tf_op jit(solution)/shard_map/ppermute | solution.py:557
  61.0 1.1 %shard_map.120 = (f32[2,1024,128]{2,1,0:T(8,128)S(1)}, f32[1,128,128]{2,1,0:T(8,128)S(1)}) custom-call(f32[8,128]{1,0:T(8,128)S(1)} %get-tuple-element.51.refs_0_, f32[8,128]{1,0:T(8,128)S(1)} %collective-permute-done.refs_0_.refs_1_, bf16[640,128]{1,0:T(8,128)(2,1)S(1)} %collective-permute-done.19.refs_2_, ...), custom_call_target="tpu_custom_call", output_to_operand_aliasing={{0}: (6, {}), {1}: (7, {})} | custom-call | flops 1000000000 | bytes 4595712 | tf_op jit(solution)/shard_map/pallas_call | solution.py:367
  63.2 1.2 %shard_map.121 = (f32[512,128]{1,0:T(8,128)S(1)}, f32[512,128]{1,0:T(8,128)S(1)}, f32[2,1024,128]{2,1,0:T(8,128)S(1)}, f32[1,128,128]{2,1,0:T(8,128)S(1)}) custom-call(f32[8,128]{1,0:T(8,128)S(1)} %get-tuple-element.51.refs_0_, f32[8,128]{1,0:T(8,128)S(1)} %collective-permute-done.refs_0_.refs_1_, ...), custom_call_target="tpu_custom_call", output_to_operand_aliasing={{2}: (5, {}), {3}: (6, {})} | custom-call | flops 1000000000 | bytes 4431872 | tf_op jit(solution)/shard_map/pallas_call | solution.py:367
  64.4 1.5 %collective-permute-done.24.other_ref = f32[512,128]{1,0:T(8,128)S(1)} collective-permute-done((f32[512,128]{1,0:T(8,128)S(1)}, f32[512,128]{1,0:T(8,128)S(1)}, u32[]{:S(2)}, u32[]{:S(2)}) %collective-permute-start.24) | collective-permute-done | bytes 262176 | tf_op jit(solution)/shard_map/ppermute | solution.py:567
  (55 shorter events, 18.5 us)
Async XLA Ops:
  0.6 9.0 %collective-permute-start.10 = (bf16[64,1024]{1,0:T(8,128)(2,1)}, bf16[64,1024]{1,0:T(8,128)(2,1)S(1)}, u32[]{:S(2)}, u32[]{:S(2)}) collective-permute-start(bf16[64,1024]{1,0:T(8,128)(2,1)} %coords_ref.1), channel_id=1, source_target_pairs={{0,2},{1,5},{4,0},{5,9},{8,4},{9,13},{12,8},{13,15},{14,12},{15,11... | collective-permute-start | bytes 393224 | tf_op jit(solution)/shard_map/ppermute | solution.py:423
  3.6 6.9 %collective-permute-start.2 = (bf16[64,1024]{1,0:T(8,128)(2,1)}, bf16[64,1024]{1,0:T(8,128)(2,1)S(1)}, u32[]{:S(2)}, u32[]{:S(2)}) collective-permute-start(bf16[64,1024]{1,0:T(8,128)(2,1)} %coords_ref.1), channel_id=1, source_target_pairs={{0,4},{1,3},{4,8},{5,1},{8,12},{9,5},{12,14},{13,9},{14,10},{15,13... | collective-permute-start | bytes 393224 | tf_op jit(solution)/shard_map/ppermute | solution.py:423
  3.8 7.9 %collective-permute-start.1 = (bf16[64,1024]{1,0:T(8,128)(2,1)}, bf16[64,1024]{1,0:T(8,128)(2,1)S(1)}, u32[]{:S(2)}, u32[]{:S(2)}) collective-permute-start(bf16[64,1024]{1,0:T(8,128)(2,1)} %coords_ref.1), channel_id=1, source_target_pairs={{0,1},{1,0},{2,3},{3,2},{4,5},{5,4},{6,7},{7,6},{8,9},{9,8},{10,11... | collective-permute-start | bytes 393224 | tf_op jit(solution)/shard_map/ppermute | solution.py:422
  6.1 2.4 %collective-permute-start = (f32[8,128]{1,0:T(8,128)}, f32[8,128]{1,0:T(8,128)S(1)}, u32[]{:S(2)}, u32[]{:S(2)}) collective-permute-start(f32[8,128]{1,0:T(8,128)} %get-tuple-element.49), channel_id=1, source_target_pairs={{0,1},{1,0},{2,3},{3,2},{4,5},{5,4},{6,7},{7,6},{8,9},{9,8},{10,11... | collective-permute-start | bytes 12296 | tf_op jit(solution)/shard_map/ppermute | solution.py:435
  6.6 8.1 %collective-permute-start.13 = (bf16[704,128]{1,0:T(8,128)(2,1)}, bf16[704,128]{1,0:T(8,128)(2,1)S(1)}, u32[]{:S(2)}, u32[]{:S(2)}) collective-permute-start(bf16[704,128]{1,0:T(8,128)(2,1)} %get-tuple-element.52), channel_id=1, source_target_pairs={{0,2},{1,5},{4,0},{5,9},{8,4},{9,13},{12,8},{13,15},{14,12},{15,11... | collective-permute-start | bytes 540680 | tf_op jit(solution)/shard_map/ppermute | solution.py:517
  8.5 7.3 %collective-permute-start.6 = (bf16[704,128]{1,0:T(8,128)(2,1)}, bf16[704,128]{1,0:T(8,128)(2,1)S(1)}, u32[]{:S(2)}, u32[]{:S(2)}) collective-permute-start(bf16[704,128]{1,0:T(8,128)(2,1)} %get-tuple-element.52), channel_id=1, source_target_pairs={{0,4},{1,3},{4,8},{5,1},{8,12},{9,5},{12,14},{13,9},{14,10},{15,13... | collective-permute-start | bytes 540680 | tf_op jit(solution)/shard_map/ppermute | solution.py:517
  9.6 10.3 %collective-permute-start.11 = (bf16[64,1024]{1,0:T(8,128)(2,1)S(1)}, bf16[64,1024]{1,0:T(8,128)(2,1)S(1)}, u32[]{:S(2)}, u32[]{:S(2)}) collective-permute-start(bf16[64,1024]{1,0:T(8,128)(2,1)S(1)} %collective-permute-done.10.refs_3_), channel_id=1, source_target_pairs={{0,2},{1,5},{4,0},{5,9},{8,4},{9,13},{12,8},{13,15},{14,12},{15,11... | collective-permute-start | bytes 393224 | tf_op jit(solution)/shard_map/ppermute | solution.py:527
  10.6 10.4 %collective-permute-start.3 = (bf16[64,1024]{1,0:T(8,128)(2,1)S(1)}, bf16[64,1024]{1,0:T(8,128)(2,1)S(1)}, u32[]{:S(2)}, u32[]{:S(2)}) collective-permute-start(bf16[64,1024]{1,0:T(8,128)(2,1)S(1)} %collective-permute-done.2.refs_2_), channel_id=1, source_target_pairs={{0,4},{1,3},{4,8},{5,1},{8,12},{9,5},{12,14},{13,9},{14,10},{15,13... | collective-permute-start | bytes 393224 | tf_op jit(solution)/shard_map/ppermute | solution.py:527
  14.8 7.2 %collective-permute-start.14 = (bf16[704,128]{1,0:T(8,128)(2,1)S(1)}, bf16[704,128]{1,0:T(8,128)(2,1)S(1)}, u32[]{:S(2)}, u32[]{:S(2)}) collective-permute-start(bf16[704,128]{1,0:T(8,128)(2,1)S(1)} %collective-permute-done.13.refs_5_.refs_7_), channel_id=1, source_target_pairs={{0,2},{1,5},{4,0},{5,9},{8,4},{9,13},{12,8},{13,15},{14,12},{15,11... | collective-permute-start | bytes 540680 | tf_op jit(solution)/shard_map/ppermute | solution.py:528
  15.8 7.2 %collective-permute-start.7 = (bf16[704,128]{1,0:T(8,128)(2,1)S(1)}, bf16[704,128]{1,0:T(8,128)(2,1)S(1)}, u32[]{:S(2)}, u32[]{:S(2)}) collective-permute-start(bf16[704,128]{1,0:T(8,128)(2,1)S(1)} %collective-permute-done.6.refs_4_.refs_6_), channel_id=1, source_target_pairs={{0,4},{1,3},{4,8},{5,1},{8,12},{9,5},{12,14},{13,9},{14,10},{15,13... | collective-permute-start | bytes 540680 | tf_op jit(solution)/shard_map/ppermute | solution.py:528
  19.9 10.4 %collective-permute-start.12 = (bf16[64,1024]{1,0:T(8,128)(2,1)S(1)}, bf16[64,1024]{1,0:T(8,128)(2,1)S(1)}, u32[]{:S(2)}, u32[]{:S(2)}) collective-permute-start(bf16[64,1024]{1,0:T(8,128)(2,1)S(1)} %collective-permute-done.11.refs_3_), channel_id=1, source_target_pairs={{0,2},{1,5},{4,0},{5,9},{8,4},{9,13},{12,8},{13,15},{14,12},{15,11... | collective-permute-start | bytes 393224 | tf_op jit(solution)/shard_map/ppermute | solution.py:527
  21.0 6.1 %collective-permute-start.4 = (bf16[64,1024]{1,0:T(8,128)(2,1)S(1)}, bf16[64,1024]{1,0:T(8,128)(2,1)S(1)}, u32[]{:S(2)}, u32[]{:S(2)}) collective-permute-start(bf16[64,1024]{1,0:T(8,128)(2,1)S(1)} %collective-permute-done.3.refs_2_), channel_id=1, source_target_pairs={{0,4},{1,3},{4,8},{5,1},{8,12},{9,5},{12,14},{13,9},{14,10},{15,13... | collective-permute-start | bytes 393224 | tf_op jit(solution)/shard_map/ppermute | solution.py:527
  22.0 8.3 %collective-permute-start.15 = (bf16[704,128]{1,0:T(8,128)(2,1)S(1)}, bf16[704,128]{1,0:T(8,128)(2,1)S(1)}, u32[]{:S(2)}, u32[]{:S(2)}) collective-permute-start(bf16[704,128]{1,0:T(8,128)(2,1)S(1)} %collective-permute-done.14.refs_5_.refs_7_), channel_id=1, source_target_pairs={{0,2},{1,5},{4,0},{5,9},{8,4},{9,13},{12,8},{13,15},{14,12},{15,11... | collective-permute-start | bytes 540680 | tf_op jit(solution)/shard_map/ppermute | solution.py:528
  23.1 5.7 %collective-permute-start.8 = (bf16[704,128]{1,0:T(8,128)(2,1)S(1)}, bf16[704,128]{1,0:T(8,128)(2,1)S(1)}, u32[]{:S(2)}, u32[]{:S(2)}) collective-permute-start(bf16[704,128]{1,0:T(8,128)(2,1)S(1)} %collective-permute-done.7.refs_4_.refs_6_), channel_id=1, source_target_pairs={{0,4},{1,3},{4,8},{5,1},{8,12},{9,5},{12,14},{13,9},{14,10},{15,13... | collective-permute-start | bytes 540680 | tf_op jit(solution)/shard_map/ppermute | solution.py:528
  27.1 6.3 %collective-permute-start.5 = (bf16[64,1024]{1,0:T(8,128)(2,1)S(1)}, bf16[64,1024]{1,0:T(8,128)(2,1)S(1)}, u32[]{:S(2)}, u32[]{:S(2)}) collective-permute-start(bf16[64,1024]{1,0:T(8,128)(2,1)S(1)} %collective-permute-done.4.refs_2_), channel_id=1, source_target_pairs={{0,4},{1,3},{4,8},{5,1},{8,12},{9,5},{12,14},{13,9},{14,10},{15,13... | collective-permute-start | bytes 393224 | tf_op jit(solution)/shard_map/ppermute | solution.py:527
  28.8 5.5 %collective-permute-start.9 = (bf16[704,128]{1,0:T(8,128)(2,1)S(1)}, bf16[704,128]{1,0:T(8,128)(2,1)S(1)}, u32[]{:S(2)}, u32[]{:S(2)}) collective-permute-start(bf16[704,128]{1,0:T(8,128)(2,1)S(1)} %collective-permute-done.8.refs_4_.refs_6_), channel_id=1, source_target_pairs={{0,4},{1,3},{4,8},{5,1},{8,12},{9,5},{12,14},{13,9},{14,10},{15,13... | collective-permute-start | bytes 540680 | tf_op jit(solution)/shard_map/ppermute | solution.py:528
  36.4 1.6 %collective-permute-start.16 = (f32[512,128]{1,0:T(8,128)S(1)}, f32[512,128]{1,0:T(8,128)S(1)}, u32[]{:S(2)}, u32[]{:S(2)}) collective-permute-start(f32[512,128]{1,0:T(8,128)S(1)} %get-tuple-element.63), channel_id=1, source_target_pairs={{0,1},{1,0},{2,3},{3,2},{4,5},{5,4},{6,7},{7,6},{8,9},{9,8},{10,11... | collective-permute-start | bytes 786440 | tf_op jit(solution)/shard_map/ppermute | solution.py:536
  38.9 5.7 %collective-permute-start.17 = (bf16[640,128]{1,0:T(8,128)(2,1)S(1)}, bf16[640,128]{1,0:T(8,128)(2,1)S(1)}, u32[]{:S(2)}, u32[]{:S(2)}) collective-permute-start(bf16[640,128]{1,0:T(8,128)(2,1)S(1)} %get-tuple-element.65.refs_2_), channel_id=1, source_target_pairs={{0,4},{1,3},{4,8},{5,1},{8,12},{9,5},{12,14},{13,9},{14,10},{15,13... | collective-permute-start | bytes 491528 | tf_op jit(solution)/shard_map/ppermute | solution.py:553
  41.5 6.3 %collective-permute-start.21 = (bf16[640,128]{1,0:T(8,128)(2,1)S(1)}, bf16[640,128]{1,0:T(8,128)(2,1)S(1)}, u32[]{:S(2)}, u32[]{:S(2)}) collective-permute-start(bf16[640,128]{1,0:T(8,128)(2,1)S(1)} %shard_map.112), channel_id=1, source_target_pairs={{0,2},{1,5},{4,0},{5,9},{8,4},{9,13},{12,8},{13,15},{14,12},{15,11... | collective-permute-start | bytes 491528 | tf_op jit(solution)/shard_map/ppermute | solution.py:555
  44.5 6.7 %collective-permute-start.18 = (bf16[640,128]{1,0:T(8,128)(2,1)S(1)}, bf16[640,128]{1,0:T(8,128)(2,1)S(1)}, u32[]{:S(2)}, u32[]{:S(2)}) collective-permute-start(bf16[640,128]{1,0:T(8,128)(2,1)S(1)} %collective-permute-done.17.refs_2_), channel_id=1, source_target_pairs={{0,4},{1,3},{4,8},{5,1},{8,12},{9,5},{12,14},{13,9},{14,10},{15,13... | collective-permute-start | bytes 491528 | tf_op jit(solution)/shard_map/ppermute | solution.py:557
  47.9 7.0 %collective-permute-start.22 = (bf16[640,128]{1,0:T(8,128)(2,1)S(1)}, bf16[640,128]{1,0:T(8,128)(2,1)S(1)}, u32[]{:S(2)}, u32[]{:S(2)}) collective-permute-start(bf16[640,128]{1,0:T(8,128)(2,1)S(1)} %shard_map.114.refs_3_), channel_id=1, source_target_pairs={{0,2},{1,5},{4,0},{5,9},{8,4},{9,13},{12,8},{13,15},{14,12},{15,11... | collective-permute-start | bytes 491528 | tf_op jit(solution)/shard_map/ppermute | solution.py:562
  51.2 6.6 %collective-permute-start.19 = (bf16[640,128]{1,0:T(8,128)(2,1)S(1)}, bf16[640,128]{1,0:T(8,128)(2,1)S(1)}, u32[]{:S(2)}, u32[]{:S(2)}) collective-permute-start(bf16[640,128]{1,0:T(8,128)(2,1)S(1)} %collective-permute-done.18.refs_2_), channel_id=1, source_target_pairs={{0,4},{1,3},{4,8},{5,1},{8,12},{9,5},{12,14},{13,9},{14,10},{15,13... | collective-permute-start | bytes 491528 | tf_op jit(solution)/shard_map/ppermute | solution.py:557
  54.9 6.1 %collective-permute-start.23 = (bf16[640,128]{1,0:T(8,128)(2,1)S(1)}, bf16[640,128]{1,0:T(8,128)(2,1)S(1)}, u32[]{:S(2)}, u32[]{:S(2)}) collective-permute-start(bf16[640,128]{1,0:T(8,128)(2,1)S(1)} %shard_map.117.refs_3_), channel_id=1, source_target_pairs={{0,2},{1,5},{4,0},{5,9},{8,4},{9,13},{12,8},{13,15},{14,12},{15,11... | collective-permute-start | bytes 491528 | tf_op jit(solution)/shard_map/ppermute | solution.py:562
  57.8 5.3 %collective-permute-start.20 = (bf16[640,128]{1,0:T(8,128)(2,1)S(1)}, bf16[640,128]{1,0:T(8,128)(2,1)S(1)}, u32[]{:S(2)}, u32[]{:S(2)}) collective-permute-start(bf16[640,128]{1,0:T(8,128)(2,1)S(1)} %collective-permute-done.19.refs_2_), channel_id=1, source_target_pairs={{0,4},{1,3},{4,8},{5,1},{8,12},{9,5},{12,14},{13,9},{14,10},{15,13... | collective-permute-start | bytes 491528 | tf_op jit(solution)/shard_map/ppermute | solution.py:557
  (6 other events, 17.7 us)

commit v17 on v14

--- a/solution.py
+++ b/solution.py
@@ -162,23 +162,25 @@
 
 
 def stage_kernel(stage, *refs):
-    ring, near_spots, far_spots, n_sub, dim, points, begins, first, last, mode = stage
+    ring, near_spots, far_spots, n_sub, dim, points, begins, first, last, mode, near_given = stage
     refs = list(refs)
     use, keep = mode == "use", mode == "keep"
     spots = sorted(set(near_spots) | set(far_spots))
     makes = not use
+    makes_near = makes and not near_given
     table_refs = [refs.pop(0) for _ in range(1 if begins else CORES)]
     if begins:
         local_ref = refs.pop(0)
         charge_refs = skeleton_refs = {spots[0]: local_ref}
     else:
-        place_refs = {spot: refs.pop(0) for spot in near_spots} if makes else {}
+        place_refs = {spot: refs.pop(0) for spot in near_spots} if makes_near else {}
         skeleton_refs = {spot: refs.pop(0) for spot in far_spots} if makes else {}
         charge_refs = {spot: refs.pop(0) for spot in spots}
     kept_refs = {}
     far_kept_ref = None
+    if not makes_near:
+        kept_refs = {spot: refs.pop(0) for spot in near_spots}
     if use:
-        kept_refs = {spot: refs.pop(0) for spot in near_spots}
         far_kept_ref = refs.pop(0) if far_spots else None
     if begins:
         sibling_ref = refs.pop(0)
@@ -190,13 +192,14 @@
     if begins:
         targets_ref, table_ref = refs.pop(0), refs.pop(0)
     if keep:
-        kept_refs = {spot: refs.pop(0) for spot in near_spots}
+        if makes_near:
+            kept_refs = {spot: refs.pop(0) for spot in near_spots}
         far_kept_ref = refs.pop(0) if far_spots else None
     if last:
         half_refs = refs.pop(0), refs.pop(0)
     total_ref, sums_ref, far_charges_ref, charges_ref = refs[:4]
-    if makes:
-        near_ref, far_ref = refs[4:]
+    near_ref = refs[4] if makes_near else None
+    far_ref = refs[-1] if makes else None
 
     skeletons_at = points + LANES
     blocks = points // LANES
@@ -231,7 +234,7 @@
         return jnp.sum(jnp.where(lane == entry, table, 0.0), axis=1, keepdims=True)
 
     def values(core, sources_ref, kept_ref):
-        if use:
+        if sources_ref is None:
             return kept_ref[...]
         made = kernel_values(targets_ref[core], sources_ref[...])
         if kept_ref is not None:
@@ -251,14 +254,14 @@
         else:
             second = jnp.full((1, 1), float(leaf), f32)
         times = named[0] * (1.0 - second) + named[1] * second
-        if makes:
+        if makes_near:
             low, high = (points_of(spot, which) for which in range(LEAVES))
             chosen = low * (1.0 - second).astype(bf16) + high * second.astype(bf16)
             put_sources(near_ref.at[at], chosen)
         half = jnp.where(lane[0:1] < LANES // LEAVES, 1.0 - second, second).astype(bf16)
         charges_ref[at] = charge_refs[spot][0:points, :] * half
         kept = kept_refs[spot].at[turn] if kept_refs else None
-        added = matmul(values(core, near_ref.at[at] if makes else None, kept), charges_ref[at])
+        added = matmul(values(core, near_ref.at[at] if makes_near else None, kept), charges_ref[at])
         return [times[own : own + 1] * added[span_of(own)] for own in range(LEAVES)]
 
     weights = []
@@ -317,6 +320,19 @@
             both = [total_ref[core, span_of(leaf), :] for leaf in range(LEAVES)]
             both = [total + swapped(total) for total in both]
             ref[...] = jnp.where(in_low_half(both[0].shape), both[0], both[1])
+
+
+def near_values_kernel(ring, spot, points, mine_ref, other_ref, place_ref, targets_ref, kept_ref, near_ref):
+    lane = lax.broadcasted_iota(i32, (LEAVES, LANES), 1)
+    entry = device_of(ring, spot) * LEAVES + 1
+    for core, table_ref in enumerate((mine_ref, other_ref)):
+        named = jnp.where(lane == entry, table_ref[0:LEAVES, :], 0.0)
+        named = jnp.sum(jnp.sum(named, axis=1, keepdims=True), axis=0, keepdims=True)
+        second = jnp.where(named > 0.0, 1.0, 0.0)
+        low, high = place_ref[:, 0:points], place_ref[:, points:]
+        chosen = low * (1.0 - second).astype(bf16) + high * second.astype(bf16)
+        put_sources(near_ref.at[core], chosen)
+        kept_ref[core] = kernel_values(targets_ref[core], near_ref[core])
 
 
 def gate_kernel(message_ref, after_ref, out_ref):
@@ -425,7 +441,7 @@
     kept_bytes = 2 * points * (steps * local + CORES * LEAVES * (chips + n_sub) * LANES)
     keeping = kept_bytes <= KEPT_MIB * 2**20
 
-    def stage(near_spots, far_spots, given, carried, last, mode, begins=False):
+    def stage(near_spots, far_spots, given, carried, last, mode, begins=False, near_given=False):
         first = not carried
         makes = mode != "use"
         spots = sorted(set(near_spots) | set(far_spots))
@@ -434,13 +450,15 @@
         else:
             args = list(given["tables"])
             if makes:
-                args += [given["places"][spot] for spot in near_spots]
+                if not near_given:
+                    args += [given["places"][spot] for spot in near_spots]
                 args += [given["skeletons"][spot] for spot in far_spots]
             args += [given["charges"][spot] for spot in spots]
+            if near_given or not makes:
+                args += [given["near"][spot] for spot in near_spots]
             if makes:
                 args += [given["targets"]]
             else:
-                args += [given["near"][spot] for spot in near_spots]
                 args += [given["far"][far_spots]] if far_spots else []
         carried_at = len(args)
         args += carried
@@ -450,18 +468,18 @@
             pltpu.VMEM((CORES * LEAVES, far_width, LANES), bf16),
             pltpu.VMEM((CORES * len(near_spots), points, LANES), bf16),
         ]
+        if makes and not near_given:
+            scratch += [pltpu.VMEM((CORES * len(near_spots), LANES, points), bf16)]
         if makes:
-            scratch += [
-                pltpu.VMEM((CORES * len(near_spots), LANES, points), bf16),
-                pltpu.VMEM((LANES, far_width), bf16),
-            ]
+            scratch += [pltpu.VMEM((LANES, far_width), bf16)]
         names, outs = [], []
         if begins:
             names += ["targets", "table"]
             outs += [targets_shape, shape(8, LANES, dtype=f32)]
         if mode == "keep":
-            names += [("near", spot) for spot in near_spots]
-            outs += [shape(LEAVES + 1 if first else CORES, local, points) for _ in near_spots]
+            if not near_given:
+                names += [("near", spot) for spot in near_spots]
+                outs += [shape(LEAVES + 1 if first else CORES, local, points) for _ in near_spots]
             names += [("far", far_spots)] if far_spots else []
             outs += [shape(CORES, local, far_width)] if far_spots else []
         if last:
@@ -471,7 +489,7 @@
         names += ["total", "sums"]
         outs += [total_shape, sums_shape]
         static = (
-            ring, near_spots, far_spots, n_sub, dim, points, begins, first, last, mode
+            ring, near_spots, far_spots, n_sub, dim, points, begins, first, last, mode, near_given
         )
         results = call(
             functools.partial(stage_kernel, static),
@@ -511,7 +529,15 @@
         carried = keep_results(stage(spots, spots, given, carried, False, mode))
     across = (chips - 1,)
     given["places"][across[0]], given["skeletons"][across[0]] = coords_next[0], sent[0]
-    results = stage(across, across, given, carried, True, mode)
+    if keeping:
+        (given["near"][across[0]],) = call(
+            functools.partial(near_values_kernel, ring, across[0], points),
+            given["tables"] + [gated(coords_next[0], carried[1]), given["targets"]],
+            [shape(CORES, local, points)],
+            scratch=[pltpu.VMEM((CORES, LANES, points), bf16)],
+            flops=10**9,
+        )
+    results = stage(across, across, given, carried, True, mode, near_given=keeping)
     keep_results(results)
     first, message, again = call(
         joined_kernel,

time: 66.8 us -> 66.4 us (level)
  waiting for transfers between devices: 12.2 us -> 11.5 us
    ppermute x5, waiting for transfers between devices: 0.96 us -> 0.07 us  [on_device(): sent = (one_way(sent[0]), None if final else other_way(sent[1]))]
    pallas_call x16 -> x17, Pallas kernels: 25.5 us -> 25.8 us  [call(): pl.pallas_call(body, grid=(1,), out_shape=out_shapes, in_specs=specs, out...]
  transfers between devices with their start and end apart: 25 -> 25, of which waited for: 10 -> 9; matrix products, arithmetic and copies ran while one was open for 0% -> 0% of each run, Pallas kernels for 31% -> 32%
where the time goes in v17:
time: 66.4 us; the launch traced here: 66.2 us
  starting transfers between devices  27 us (41%)
  Pallas kernels  25.8 us (39%)
  waiting for transfers between devices  11.5 us (17%)
  local copies, waits for them, and re-layouts  0.99 us (1%)
  between operations  0.89 us (1%)
    pallas_call x17, Pallas kernels, call(): pl.pallas_call(body, grid=(1,), out_shape=out_shapes, in_specs=specs, out...  25.8 us
    ppermute x3, starting transfers between devices, on_device(): one_next = one_way(one)  6.75 us
    ppermute x5, starting transfers between devices, on_device(): sent = (one_way(sent[0]), None if final else other_way(sent[1]))  5.63 us
    ppermute x3, waiting for transfers between devices, on_device(): one_next = one_way(one)  5.02 us
    ppermute x3, starting transfers between devices, on_device(): one_way(coords_next[0])  3.67 us
    ppermute x2, starting transfers between devices, on_device(): coords_next = (one_way(coords), other_way(coords))  3.14 us
    ppermute x2, waiting for transfers between devices, on_device(): to_sibling(results['other'])  3.04 us
    ppermute x2, starting transfers between devices, on_device(): sent = (one_way(message), other_way(message))  2.99 us
  transfers between devices with their start and end apart: 25, of which 9 were waited for; matrix products, arithmetic and copies ran while one was open for 0% of the time, Pallas kernels for 32%

profile of v17, /device:TPU:0, one launch (start us, length us, event | category | flops | bytes accessed | tf_op | source)
XLA Modules:
  0.0 66.2 jit_solution(832614299301299789)
XLA Ops:
  0.6 3.0 %collective-permute-start.10 = (bf16[64,1024]{1,0:T(8,128)(2,1)}, bf16[64,1024]{1,0:T(8,128)(2,1)S(1)}, u32[]{:S(2)}, u32[]{:S(2)}) collective-permute-start(bf16[64,1024]{1,0:T(8,128)(2,1)} %coords_ref.1), channel_id=1, source_target_pairs={{0,2},{1,5},{4,0},{5,9},{8,4},{9,13},{12,8},{13,15},{14,12},{15,11... | collective-permute-start | bytes 393224 | tf_op jit(solution)/shard_map/ppermute | solution.py:421
  3.8 2.3 %shard_map.104 = (bf16[704,128]{1,0:T(8,128)(2,1)}, bf16[1232,128]{1,0:T(8,128)(2,1)}, f32[8,128]{1,0:T(8,128)}) custom-call(s32[2,16]{1,0:T(2,128)} %near_ref.1, s32[2,32]{1,0:T(2,128)} %far_ref.1, bf16[64,1024]{1,0:T(8,128)(2,1)} %coords_ref.1, bf16[64,1024]{1,0:T(8,128)(2,1)} %charges_ref.1, bf16[64,128]{1,0:T(8,128)(2,1)} %points_ref.1, ...), custom_call_target="tpu_custom_call" | custom-call | bytes 639360 | tf_op jit(solution)/shard_map/pallas_call | solution.py:365
  6.6 1.9 %collective-permute-start.13 = (bf16[704,128]{1,0:T(8,128)(2,1)}, bf16[704,128]{1,0:T(8,128)(2,1)S(1)}, u32[]{:S(2)}, u32[]{:S(2)}) collective-permute-start(bf16[704,128]{1,0:T(8,128)(2,1)} %get-tuple-element.51), channel_id=1, source_target_pairs={{0,2},{1,5},{4,0},{5,9},{8,4},{9,13},{12,8},{13,15},{14,12},{15,11... | collective-permute-start | bytes 540680 | tf_op jit(solution)/shard_map/ppermute | solution.py:517
  12.6 2.1 %shard_map.105 = (bf16[2,1024,128]{2,1,0:T(8,128)(2,1)S(1)}, f32[8,128]{1,0:T(8,128)S(1)}, bf16[3,1024,512]{2,1,0:T(8,128)(2,1)S(1)}, bf16[2,1024,128]{2,1,0:T(8...) custom-call(f32[8,128]{1,0:T(8,128)S(1)} %collective-permute-done.refs_0_.refs_1_.other_ref, ...), custom_call_target="tpu_custom_call" | custom-call | flops 2000000000 | bytes 450560 | tf_op jit(solution)/shard_map/pallas_call | solution.py:365
  14.7 1.1 %collective-permute-start.14 = (bf16[704,128]{1,0:T(8,128)(2,1)S(1)}, bf16[704,128]{1,0:T(8,128)(2,1)S(1)}, u32[]{:S(2)}, u32[]{:S(2)}) collective-permute-start(bf16[704,128]{1,0:T(8,128)(2,1)S(1)} %collective-permute-done.13.refs_5_.refs_7_), channel_id=1, source_target_pairs={{0,2},{1,5},{4,0},{5,9},{8,4},{9,13},{12,8},{13,15},{14,12},{15,11... | collective-permute-start | bytes 540680 | tf_op jit(solution)/shard_map/ppermute | solution.py:528
  16.8 3.1 %shard_map.106 = (bf16[2,1024,512]{2,1,0:T(8,128)(2,1)S(1)}, bf16[2,1024,512]{2,1,0:T(8,128)(2,1)S(1)}, bf16[2,1024,256]{2,1,0:T(8,128)(2,1)S(1)}, f32[2,1024,128]{2,1,0:T(8,128)S(1)}, f32[1,128,128]{2,1,0:T(8,128)S(1)}) custom-call(f32[8,128]{1,0:T(8,128)S(1)} %get-tuple-element.50.refs_0_.mine_ref, ...), custom_call_target="tpu_custom_call", output_to_operand_aliasing={{3}: (9, {}), {4}: (10, {})} | custom-call | flops 4000000000 | bytes 2629632 | tf_op jit(solution)/shard_map/pallas_call | solution.py:365
  24.0 3.1 %shard_map.107 = (bf16[2,1024,512]{2,1,0:T(8,128)(2,1)S(1)}, bf16[2,1024,512]{2,1,0:T(8,128)(2,1)S(1)}, bf16[2,1024,256]{2,1,0:T(8,128)(2,1)S(1)}, f32[2,1024,128]{2,1,0:T(8,128)S(1)}, f32[1,128,128]{2,1,0:T(8,128)S(1)}) custom-call(f32[8,128]{1,0:T(8,128)S(1)} %get-tuple-element.50.refs_0_.mine_ref, ...), custom_call_target="tpu_custom_call", output_to_operand_aliasing={{3}: (9, {}), {4}: (10, {})} | custom-call | flops 4000000000 | bytes 2629632 | tf_op jit(solution)/shard_map/pallas_call | solution.py:365
  27.1 1.6 %collective-permute-start.9 = (bf16[64,1024]{1,0:T(8,128)(2,1)S(1)}, bf16[64,1024]{1,0:T(8,128)(2,1)S(1)}, u32[]{:S(2)}, u32[]{:S(2)}) collective-permute-start(bf16[64,1024]{1,0:T(8,128)(2,1)S(1)} %collective-permute-done.8.refs_2_), channel_id=1, source_target_pairs={{0,4},{1,3},{4,8},{5,1},{8,12},{9,5},{12,14},{13,9},{14,10},{15,13... | collective-permute-start | bytes 393224 | tf_op jit(solution)/shard_map/ppermute | solution.py:527
  28.8 1.5 %collective-permute-start.5 = (bf16[704,128]{1,0:T(8,128)(2,1)S(1)}, bf16[704,128]{1,0:T(8,128)(2,1)S(1)}, u32[]{:S(2)}, u32[]{:S(2)}) collective-permute-start(bf16[704,128]{1,0:T(8,128)(2,1)S(1)} %collective-permute-done.4.refs_4_.refs_6_), channel_id=1, source_target_pairs={{0,4},{1,3},{4,8},{5,1},{8,12},{9,5},{12,14},{13,9},{14,10},{15,13... | collective-permute-start | bytes 540680 | tf_op jit(solution)/shard_map/ppermute | solution.py:528
  30.3 3.1 %shard_map.108 = (bf16[2,1024,512]{2,1,0:T(8,128)(2,1)S(1)}, bf16[2,1024,512]{2,1,0:T(8,128)(2,1)S(1)}, bf16[2,1024,256]{2,1,0:T(8,128)(2,1)S(1)}, f32[2,1024,128]{2,1,0:T(8,128)S(1)}, f32[1,128,128]{2,1,0:T(8,128)S(1)}) custom-call(f32[8,128]{1,0:T(8,128)S(1)} %get-tuple-element.50.refs_0_.mine_ref, ...), custom_call_target="tpu_custom_call", output_to_operand_aliasing={{3}: (9, {}), {4}: (10, {})} | custom-call | flops 4000000000 | bytes 2629632 | tf_op jit(solution)/shard_map/pallas_call | solution.py:365
  34.4 1.5 %shard_map.111 = (bf16[2,1024,256]{2,1,0:T(8,128)(2,1)S(1)}, f32[512,128]{1,0:T(8,128)S(1)}, f32[512,128]{1,0:T(8,128)S(1)}, f32[2,1024,128]{2,1,0:T(8,128)S(1)}, f32[1,128,128]{2,1,0:T(8,128)S(1)}) custom-call(f32[8,128]{1,0:T(8,128)S(1)} %get-tuple-element.50.refs_0_.mine_ref, ...), custom_call_target="tpu_custom_call", output_to_operand_aliasing={{3}: (6, {}), {4}: (7, {})} | custom-call | flops 2000000000 | bytes 4120576 | tf_op jit(solution)/shard_map/pallas_call | solution.py:365
  35.9 1.5 %collective-permute-done.16.other_ref = f32[512,128]{1,0:T(8,128)S(1)} collective-permute-done((f32[512,128]{1,0:T(8,128)S(1)}, f32[512,128]{1,0:T(8,128)S(1)}, u32[]{:S(2)}, u32[]{:S(2)}) %collective-permute-start.16) | collective-permute-done | bytes 262176 | tf_op jit(solution)/shard_map/ppermute | solution.py:544
  38.3 1.5 %collective-permute-start.17 = (bf16[640,128]{1,0:T(8,128)(2,1)S(1)}, bf16[640,128]{1,0:T(8,128)(2,1)S(1)}, u32[]{:S(2)}, u32[]{:S(2)}) collective-permute-start(bf16[640,128]{1,0:T(8,128)(2,1)S(1)} %get-tuple-element.64.refs_2_), channel_id=1, source_target_pairs={{0,4},{1,3},{4,8},{5,1},{8,12},{9,5},{12,14},{13,9},{14,10},{15,13... | collective-permute-start | bytes 491528 | tf_op jit(solution)/shard_map/ppermute | solution.py:561
  41.5 2.5 %collective-permute-done.17.refs_2_ = bf16[640,128]{1,0:T(8,128)(2,1)S(1)} collective-permute-done((bf16[640,128]{1,0:T(8,128)(2,1)S(1)}, bf16[640,128]{1,0:T(8,128)(2,1)S(1)}, u32[]{:S(2)}, u32[]{:S(2)}) %collective-permute-start.17) | collective-permute-done | bytes 163872 | tf_op jit(solution)/shard_map/ppermute | solution.py:561
  44.0 2.5 %collective-permute-start.18 = (bf16[640,128]{1,0:T(8,128)(2,1)S(1)}, bf16[640,128]{1,0:T(8,128)(2,1)S(1)}, u32[]{:S(2)}, u32[]{:S(2)}) collective-permute-start(bf16[640,128]{1,0:T(8,128)(2,1)S(1)} %collective-permute-done.17.refs_2_), channel_id=1, source_target_pairs={{0,4},{1,3},{4,8},{5,1},{8,12},{9,5},{12,14},{13,9},{14,10},{15,13... | collective-permute-start | bytes 491528 | tf_op jit(solution)/shard_map/ppermute | solution.py:565
  47.4 1.1 %shard_map.117 = (f32[2,1024,128]{2,1,0:T(8,128)S(1)}, f32[1,128,128]{2,1,0:T(8,128)S(1)}) custom-call(f32[8,128]{1,0:T(8,128)S(1)} %get-tuple-element.50.refs_0_.mine_ref, f32[8,128]{1,0:T(8,128)S(1)} %collective-permute-done.refs_0_.refs_1_.other_ref, ...), custom_call_target="tpu_custom_call", output_to_operand_aliasing={{0}: (6, {}), {1}: (7, {})} | custom-call | flops 1000000000 | bytes 4595712 | tf_op jit(solution)/shard_map/pallas_call | solution.py:365
  48.5 2.2 %collective-permute-done.18.refs_2_ = bf16[640,128]{1,0:T(8,128)(2,1)S(1)} collective-permute-done((bf16[640,128]{1,0:T(8,128)(2,1)S(1)}, bf16[640,128]{1,0:T(8,128)(2,1)S(1)}, u32[]{:S(2)}, u32[]{:S(2)}) %collective-permute-start.18) | collective-permute-done | bytes 163872 | tf_op jit(solution)/shard_map/ppermute | solution.py:565
  50.7 2.5 %collective-permute-start.19 = (bf16[640,128]{1,0:T(8,128)(2,1)S(1)}, bf16[640,128]{1,0:T(8,128)(2,1)S(1)}, u32[]{:S(2)}, u32[]{:S(2)}) collective-permute-start(bf16[640,128]{1,0:T(8,128)(2,1)S(1)} %collective-permute-done.18.refs_2_), channel_id=1, source_target_pairs={{0,4},{1,3},{4,8},{5,1},{8,12},{9,5},{12,14},{13,9},{14,10},{15,13... | collective-permute-start | bytes 491528 | tf_op jit(solution)/shard_map/ppermute | solution.py:565
  54.3 1.2 %shard_map.120 = (f32[2,1024,128]{2,1,0:T(8,128)S(1)}, f32[1,128,128]{2,1,0:T(8,128)S(1)}) custom-call(f32[8,128]{1,0:T(8,128)S(1)} %get-tuple-element.50.refs_0_.mine_ref, f32[8,128]{1,0:T(8,128)S(1)} %collective-permute-done.refs_0_.refs_1_.other_ref, ...), custom_call_target="tpu_custom_call", output_to_operand_aliasing={{0}: (6, {}), {1}: (7, {})} | custom-call | flops 1000000000 | bytes 4595712 | tf_op jit(solution)/shard_map/pallas_call | solution.py:365
  55.5 1.8 %collective-permute-done.19.refs_2_ = bf16[640,128]{1,0:T(8,128)(2,1)S(1)} collective-permute-done((bf16[640,128]{1,0:T(8,128)(2,1)S(1)}, bf16[640,128]{1,0:T(8,128)(2,1)S(1)}, u32[]{:S(2)}, u32[]{:S(2)}) %collective-permute-start.19) | collective-permute-done | bytes 163872 | tf_op jit(solution)/shard_map/ppermute | solution.py:565
  57.3 1.8 %collective-permute-start.20 = (bf16[640,128]{1,0:T(8,128)(2,1)S(1)}, bf16[640,128]{1,0:T(8,128)(2,1)S(1)}, u32[]{:S(2)}, u32[]{:S(2)}) collective-permute-start(bf16[640,128]{1,0:T(8,128)(2,1)S(1)} %collective-permute-done.19.refs_2_), channel_id=1, source_target_pairs={{0,4},{1,3},{4,8},{5,1},{8,12},{9,5},{12,14},{13,9},{14,10},{15,13... | collective-permute-start | bytes 491528 | tf_op jit(solution)/shard_map/ppermute | solution.py:565
  60.4 1.2 %shard_map.122 = (f32[2,1024,128]{2,1,0:T(8,128)S(1)}, f32[1,128,128]{2,1,0:T(8,128)S(1)}) custom-call(f32[8,128]{1,0:T(8,128)S(1)} %get-tuple-element.50.refs_0_.mine_ref, f32[8,128]{1,0:T(8,128)S(1)} %collective-permute-done.refs_0_.refs_1_.other_ref, ...), custom_call_target="tpu_custom_call", output_to_operand_aliasing={{0}: (6, {}), {1}: (7, {})} | custom-call | flops 1000000000 | bytes 4595712 | tf_op jit(solution)/shard_map/pallas_call | solution.py:365
  62.6 1.2 %shard_map.123 = (f32[512,128]{1,0:T(8,128)S(1)}, f32[512,128]{1,0:T(8,128)S(1)}, f32[2,1024,128]{2,1,0:T(8,128)S(1)}, f32[1,128,128]{2,1,0:T(8,128)S(1)}) custom-call(f32[8,128]{1,0:T(8,128)S(1)} %get-tuple-element.50.refs_0_.mine_ref, f32[8,128]{1,0:T(8,128)S(1)} %collective-permute-done.refs_0_.refs_1_.other_ref, ...), custom_call_target="tpu_custom_call", output_to_operand_aliasing={{2}: (5, {}), {3}: (6, {})} | custom-call | flops 1000000000 | bytes 4431872 | tf_op jit(solution)/shard_map/pallas_call | solution.py:365
  63.9 1.5 %collective-permute-done.24.other_ref = f32[512,128]{1,0:T(8,128)S(1)} collective-permute-done((f32[512,128]{1,0:T(8,128)S(1)}, f32[512,128]{1,0:T(8,128)S(1)}, u32[]{:S(2)}, u32[]{:S(2)}) %collective-permute-start.24) | collective-permute-done | bytes 262176 | tf_op jit(solution)/shard_map/ppermute | solution.py:575
  (57 shorter events, 18.5 us)
Async XLA Ops:
  0.6 9.0 %collective-permute-start.10 = (bf16[64,1024]{1,0:T(8,128)(2,1)}, bf16[64,1024]{1,0:T(8,128)(2,1)S(1)}, u32[]{:S(2)}, u32[]{:S(2)}) collective-permute-start(bf16[64,1024]{1,0:T(8,128)(2,1)} %coords_ref.1), channel_id=1, source_target_pairs={{0,2},{1,5},{4,0},{5,9},{8,4},{9,13},{12,8},{13,15},{14,12},{15,11... | collective-permute-start | bytes 393224 | tf_op jit(solution)/shard_map/ppermute | solution.py:421
  3.6 6.9 %collective-permute-start.6 = (bf16[64,1024]{1,0:T(8,128)(2,1)}, bf16[64,1024]{1,0:T(8,128)(2,1)S(1)}, u32[]{:S(2)}, u32[]{:S(2)}) collective-permute-start(bf16[64,1024]{1,0:T(8,128)(2,1)} %coords_ref.1), channel_id=1, source_target_pairs={{0,4},{1,3},{4,8},{5,1},{8,12},{9,5},{12,14},{13,9},{14,10},{15,13... | collective-permute-start | bytes 393224 | tf_op jit(solution)/shard_map/ppermute | solution.py:421
  3.8 7.9 %collective-permute-start.1 = (bf16[64,1024]{1,0:T(8,128)(2,1)}, bf16[64,1024]{1,0:T(8,128)(2,1)S(1)}, u32[]{:S(2)}, u32[]{:S(2)}) collective-permute-start(bf16[64,1024]{1,0:T(8,128)(2,1)} %coords_ref.1), channel_id=1, source_target_pairs={{0,1},{1,0},{2,3},{3,2},{4,5},{5,4},{6,7},{7,6},{8,9},{9,8},{10,11... | collective-permute-start | bytes 393224 | tf_op jit(solution)/shard_map/ppermute | solution.py:420
  6.1 2.4 %collective-permute-start = (f32[8,128]{1,0:T(8,128)}, f32[8,128]{1,0:T(8,128)S(1)}, u32[]{:S(2)}, u32[]{:S(2)}) collective-permute-start(f32[8,128]{1,0:T(8,128)} %get-tuple-element.48), channel_id=1, source_target_pairs={{0,1},{1,0},{2,3},{3,2},{4,5},{5,4},{6,7},{7,6},{8,9},{9,8},{10,11... | collective-permute-start | bytes 12296 | tf_op jit(solution)/shard_map/ppermute | solution.py:433
  6.6 8.1 %collective-permute-start.13 = (bf16[704,128]{1,0:T(8,128)(2,1)}, bf16[704,128]{1,0:T(8,128)(2,1)S(1)}, u32[]{:S(2)}, u32[]{:S(2)}) collective-permute-start(bf16[704,128]{1,0:T(8,128)(2,1)} %get-tuple-element.51), channel_id=1, source_target_pairs={{0,2},{1,5},{4,0},{5,9},{8,4},{9,13},{12,8},{13,15},{14,12},{15,11... | collective-permute-start | bytes 540680 | tf_op jit(solution)/shard_map/ppermute | solution.py:517
  8.5 7.3 %collective-permute-start.2 = (bf16[704,128]{1,0:T(8,128)(2,1)}, bf16[704,128]{1,0:T(8,128)(2,1)S(1)}, u32[]{:S(2)}, u32[]{:S(2)}) collective-permute-start(bf16[704,128]{1,0:T(8,128)(2,1)} %get-tuple-element.51), channel_id=1, source_target_pairs={{0,4},{1,3},{4,8},{5,1},{8,12},{9,5},{12,14},{13,9},{14,10},{15,13... | collective-permute-start | bytes 540680 | tf_op jit(solution)/shard_map/ppermute | solution.py:517
  9.6 10.2 %collective-permute-start.11 = (bf16[64,1024]{1,0:T(8,128)(2,1)S(1)}, bf16[64,1024]{1,0:T(8,128)(2,1)S(1)}, u32[]{:S(2)}, u32[]{:S(2)}) collective-permute-start(bf16[64,1024]{1,0:T(8,128)(2,1)S(1)} %collective-permute-done.10.refs_3_), channel_id=1, source_target_pairs={{0,2},{1,5},{4,0},{5,9},{8,4},{9,13},{12,8},{13,15},{14,12},{15,11... | collective-permute-start | bytes 393224 | tf_op jit(solution)/shard_map/ppermute | solution.py:527
  10.6 10.4 %collective-permute-start.7 = (bf16[64,1024]{1,0:T(8,128)(2,1)S(1)}, bf16[64,1024]{1,0:T(8,128)(2,1)S(1)}, u32[]{:S(2)}, u32[]{:S(2)}) collective-permute-start(bf16[64,1024]{1,0:T(8,128)(2,1)S(1)} %collective-permute-done.6.refs_2_), channel_id=1, source_target_pairs={{0,4},{1,3},{4,8},{5,1},{8,12},{9,5},{12,14},{13,9},{14,10},{15,13... | collective-permute-start | bytes 393224 | tf_op jit(solution)/shard_map/ppermute | solution.py:527
  14.7 7.3 %collective-permute-start.14 = (bf16[704,128]{1,0:T(8,128)(2,1)S(1)}, bf16[704,128]{1,0:T(8,128)(2,1)S(1)}, u32[]{:S(2)}, u32[]{:S(2)}) collective-permute-start(bf16[704,128]{1,0:T(8,128)(2,1)S(1)} %collective-permute-done.13.refs_5_.refs_7_), channel_id=1, source_target_pairs={{0,2},{1,5},{4,0},{5,9},{8,4},{9,13},{12,8},{13,15},{14,12},{15,11... | collective-permute-start | bytes 540680 | tf_op jit(solution)/shard_map/ppermute | solution.py:528
  15.8 7.2 %collective-permute-start.3 = (bf16[704,128]{1,0:T(8,128)(2,1)S(1)}, bf16[704,128]{1,0:T(8,128)(2,1)S(1)}, u32[]{:S(2)}, u32[]{:S(2)}) collective-permute-start(bf16[704,128]{1,0:T(8,128)(2,1)S(1)} %collective-permute-done.2.refs_4_.refs_6_), channel_id=1, source_target_pairs={{0,4},{1,3},{4,8},{5,1},{8,12},{9,5},{12,14},{13,9},{14,10},{15,13... | collective-permute-start | bytes 540680 | tf_op jit(solution)/shard_map/ppermute | solution.py:528
  19.9 10.4 %collective-permute-start.12 = (bf16[64,1024]{1,0:T(8,128)(2,1)S(1)}, bf16[64,1024]{1,0:T(8,128)(2,1)S(1)}, u32[]{:S(2)}, u32[]{:S(2)}) collective-permute-start(bf16[64,1024]{1,0:T(8,128)(2,1)S(1)} %collective-permute-done.11.refs_3_), channel_id=1, source_target_pairs={{0,2},{1,5},{4,0},{5,9},{8,4},{9,13},{12,8},{13,15},{14,12},{15,11... | collective-permute-start | bytes 393224 | tf_op jit(solution)/shard_map/ppermute | solution.py:527
  21.0 6.1 %collective-permute-start.8 = (bf16[64,1024]{1,0:T(8,128)(2,1)S(1)}, bf16[64,1024]{1,0:T(8,128)(2,1)S(1)}, u32[]{:S(2)}, u32[]{:S(2)}) collective-permute-start(bf16[64,1024]{1,0:T(8,128)(2,1)S(1)} %collective-permute-done.7.refs_2_), channel_id=1, source_target_pairs={{0,4},{1,3},{4,8},{5,1},{8,12},{9,5},{12,14},{13,9},{14,10},{15,13... | collective-permute-start | bytes 393224 | tf_op jit(solution)/shard_map/ppermute | solution.py:527
  22.0 8.4 %collective-permute-start.15 = (bf16[704,128]{1,0:T(8,128)(2,1)S(1)}, bf16[704,128]{1,0:T(8,128)(2,1)S(1)}, u32[]{:S(2)}, u32[]{:S(2)}) collective-permute-start(bf16[704,128]{1,0:T(8,128)(2,1)S(1)} %collective-permute-done.14.refs_5_.refs_7_), channel_id=1, source_target_pairs={{0,2},{1,5},{4,0},{5,9},{8,4},{9,13},{12,8},{13,15},{14,12},{15,11... | collective-permute-start | bytes 540680 | tf_op jit(solution)/shard_map/ppermute | solution.py:528
  23.1 5.7 %collective-permute-start.4 = (bf16[704,128]{1,0:T(8,128)(2,1)S(1)}, bf16[704,128]{1,0:T(8,128)(2,1)S(1)}, u32[]{:S(2)}, u32[]{:S(2)}) collective-permute-start(bf16[704,128]{1,0:T(8,128)(2,1)S(1)} %collective-permute-done.3.refs_4_.refs_6_), channel_id=1, source_target_pairs={{0,4},{1,3},{4,8},{5,1},{8,12},{9,5},{12,14},{13,9},{14,10},{15,13... | collective-permute-start | bytes 540680 | tf_op jit(solution)/shard_map/ppermute | solution.py:528
  27.1 6.3 %collective-permute-start.9 = (bf16[64,1024]{1,0:T(8,128)(2,1)S(1)}, bf16[64,1024]{1,0:T(8,128)(2,1)S(1)}, u32[]{:S(2)}, u32[]{:S(2)}) collective-permute-start(bf16[64,1024]{1,0:T(8,128)(2,1)S(1)} %collective-permute-done.8.refs_2_), channel_id=1, source_target_pairs={{0,4},{1,3},{4,8},{5,1},{8,12},{9,5},{12,14},{13,9},{14,10},{15,13... | collective-permute-start | bytes 393224 | tf_op jit(solution)/shard_map/ppermute | solution.py:527
  28.8 5.5 %collective-permute-start.5 = (bf16[704,128]{1,0:T(8,128)(2,1)S(1)}, bf16[704,128]{1,0:T(8,128)(2,1)S(1)}, u32[]{:S(2)}, u32[]{:S(2)}) collective-permute-start(bf16[704,128]{1,0:T(8,128)(2,1)S(1)} %collective-permute-done.4.refs_4_.refs_6_), channel_id=1, source_target_pairs={{0,4},{1,3},{4,8},{5,1},{8,12},{9,5},{12,14},{13,9},{14,10},{15,13... | collective-permute-start | bytes 540680 | tf_op jit(solution)/shard_map/ppermute | solution.py:528
  35.8 1.6 %collective-permute-start.16 = (f32[512,128]{1,0:T(8,128)S(1)}, f32[512,128]{1,0:T(8,128)S(1)}, u32[]{:S(2)}, u32[]{:S(2)}) collective-permute-start(f32[512,128]{1,0:T(8,128)S(1)} %get-tuple-element.62), channel_id=1, source_target_pairs={{0,1},{1,0},{2,3},{3,2},{4,5},{5,4},{6,7},{7,6},{8,9},{9,8},{10,11... | collective-permute-start | bytes 786440 | tf_op jit(solution)/shard_map/ppermute | solution.py:544
  38.3 5.7 %collective-permute-start.17 = (bf16[640,128]{1,0:T(8,128)(2,1)S(1)}, bf16[640,128]{1,0:T(8,128)(2,1)S(1)}, u32[]{:S(2)}, u32[]{:S(2)}) collective-permute-start(bf16[640,128]{1,0:T(8,128)(2,1)S(1)} %get-tuple-element.64.refs_2_), channel_id=1, source_target_pairs={{0,4},{1,3},{4,8},{5,1},{8,12},{9,5},{12,14},{13,9},{14,10},{15,13... | collective-permute-start | bytes 491528 | tf_op jit(solution)/shard_map/ppermute | solution.py:561
  41.0 6.3 %collective-permute-start.21 = (bf16[640,128]{1,0:T(8,128)(2,1)S(1)}, bf16[640,128]{1,0:T(8,128)(2,1)S(1)}, u32[]{:S(2)}, u32[]{:S(2)}) collective-permute-start(bf16[640,128]{1,0:T(8,128)(2,1)S(1)} %shard_map.114), channel_id=1, source_target_pairs={{0,2},{1,5},{4,0},{5,9},{8,4},{9,13},{12,8},{13,15},{14,12},{15,11... | collective-permute-start | bytes 491528 | tf_op jit(solution)/shard_map/ppermute | solution.py:563
  44.0 6.7 %collective-permute-start.18 = (bf16[640,128]{1,0:T(8,128)(2,1)S(1)}, bf16[640,128]{1,0:T(8,128)(2,1)S(1)}, u32[]{:S(2)}, u32[]{:S(2)}) collective-permute-start(bf16[640,128]{1,0:T(8,128)(2,1)S(1)} %collective-permute-done.17.refs_2_), channel_id=1, source_target_pairs={{0,4},{1,3},{4,8},{5,1},{8,12},{9,5},{12,14},{13,9},{14,10},{15,13... | collective-permute-start | bytes 491528 | tf_op jit(solution)/shard_map/ppermute | solution.py:565
  47.3 7.0 %collective-permute-start.22 = (bf16[640,128]{1,0:T(8,128)(2,1)S(1)}, bf16[640,128]{1,0:T(8,128)(2,1)S(1)}, u32[]{:S(2)}, u32[]{:S(2)}) collective-permute-start(bf16[640,128]{1,0:T(8,128)(2,1)S(1)} %shard_map.116.refs_3_), channel_id=1, source_target_pairs={{0,2},{1,5},{4,0},{5,9},{8,4},{9,13},{12,8},{13,15},{14,12},{15,11... | collective-permute-start | bytes 491528 | tf_op jit(solution)/shard_map/ppermute | solution.py:570
  50.7 6.6 %collective-permute-start.19 = (bf16[640,128]{1,0:T(8,128)(2,1)S(1)}, bf16[640,128]{1,0:T(8,128)(2,1)S(1)}, u32[]{:S(2)}, u32[]{:S(2)}) collective-permute-start(bf16[640,128]{1,0:T(8,128)(2,1)S(1)} %collective-permute-done.18.refs_2_), channel_id=1, source_target_pairs={{0,4},{1,3},{4,8},{5,1},{8,12},{9,5},{12,14},{13,9},{14,10},{15,13... | collective-permute-start | bytes 491528 | tf_op jit(solution)/shard_map/ppermute | solution.py:565
  54.3 6.1 %collective-permute-start.23 = (bf16[640,128]{1,0:T(8,128)(2,1)S(1)}, bf16[640,128]{1,0:T(8,128)(2,1)S(1)}, u32[]{:S(2)}, u32[]{:S(2)}) collective-permute-start(bf16[640,128]{1,0:T(8,128)(2,1)S(1)} %shard_map.119.refs_3_), channel_id=1, source_target_pairs={{0,2},{1,5},{4,0},{5,9},{8,4},{9,13},{12,8},{13,15},{14,12},{15,11... | collective-permute-start | bytes 491528 | tf_op jit(solution)/shard_map/ppermute | solution.py:570
  57.3 5.3 %collective-permute-start.20 = (bf16[640,128]{1,0:T(8,128)(2,1)S(1)}, bf16[640,128]{1,0:T(8,128)(2,1)S(1)}, u32[]{:S(2)}, u32[]{:S(2)}) collective-permute-start(bf16[640,128]{1,0:T(8,128)(2,1)S(1)} %collective-permute-done.19.refs_2_), channel_id=1, source_target_pairs={{0,4},{1,3},{4,8},{5,1},{8,12},{9,5},{12,14},{13,9},{14,10},{15,13... | collective-permute-start | bytes 491528 | tf_op jit(solution)/shard_map/ppermute | solution.py:565
  (6 other events, 12.8 us)

commit v18 on v17

--- a/solution.py
+++ b/solution.py
@@ -429,6 +429,7 @@
         ],
         streamed=range(2, 8),
         vmem_mib=60,
+        flops=25 * 10**8,
     )
     sibling_table = to_sibling(table)
 

time: 66.4 us -> 66.3 us (level)
    ppermute x3, starting transfers between devices: 3.67 us -> 4.41 us  [on_device(): one_way(coords_next[0])]
    ppermute x2, starting transfers between devices: 2.07 us -> 1.33 us  [on_device(): other_way(coords_next[1])]
  transfers between devices with their start and end apart: 25 -> 25, of which waited for: 9 -> 8; matrix products, arithmetic and copies ran while one was open for 0% -> 0% of each run, Pallas kernels for 32% -> 32%
where the time goes in v18:
time: 66.3 us; the launch traced here: 66.2 us
  starting transfers between devices  27 us (41%)
  Pallas kernels  25.8 us (39%)
  waiting for transfers between devices  11.5 us (17%)
  local copies, waits for them, and re-layouts  0.99 us (1%)
  between operations  0.89 us (1%)
    pallas_call x17, Pallas kernels, call(): pl.pallas_call(body, grid=(1,), out_shape=out_shapes, in_specs=specs, out...  25.8 us
    ppermute x3, starting transfers between devices, on_device(): one_next = one_way(one)  6.69 us
    ppermute x5, starting transfers between devices, on_device(): sent = (one_way(sent[0]), None if final else other_way(sent[1]))  5.71 us
    ppermute x3, waiting for transfers between devices, on_device(): one_next = one_way(one)  5.09 us
    ppermute x3, starting transfers between devices, on_device(): one_way(coords_next[0])  4.41 us
    ppermute x2, starting transfers between devices, on_device(): sent = (one_way(message), other_way(message))  3.23 us
    ppermute x2, waiting for transfers between devices, on_device(): to_sibling(results['other'])  3.04 us
    ppermute x2, starting transfers between devices, on_device(): coords_next = (one_way(coords), other_way(coords))  2.72 us
  transfers between devices with their start and end apart: 25, of which 8 were waited for; matrix products, arithmetic and copies ran while one was open for 0% of the time, Pallas kernels for 32%

profile of v18, /device:TPU:0, one launch (start us, length us, event | category | flops | bytes accessed | tf_op | source)
XLA Modules:
  0.0 66.2 jit_solution(7533488051380348965)
XLA Ops:
  1.1 2.6 %collective-permute-start.10 = (bf16[64,1024]{1,0:T(8,128)(2,1)}, bf16[64,1024]{1,0:T(8,128)(2,1)S(1)}, u32[]{:S(2)}, u32[]{:S(2)}) collective-permute-start(bf16[64,1024]{1,0:T(8,128)(2,1)} %coords_ref.1), channel_id=1, source_target_pairs={{0,2},{1,5},{4,0},{5,9},{8,4},{9,13},{12,8},{13,15},{14,12},{15,11... | collective-permute-start | bytes 393224 | tf_op jit(solution)/shard_map/ppermute | solution.py:421
  3.9 2.3 %shard_map.104 = (bf16[704,128]{1,0:T(8,128)(2,1)}, bf16[1232,128]{1,0:T(8,128)(2,1)}, f32[8,128]{1,0:T(8,128)}) custom-call(s32[2,16]{1,0:T(2,128)} %near_ref.1, s32[2,32]{1,0:T(2,128)} %far_ref.1, bf16[64,1024]{1,0:T(8,128)(2,1)} %coords_ref.1, bf16[64,1024]{1,0:T(8,128)(2,1)} %charges_ref.1, bf16[64,128]{1,0:T(8,128)(2,1)} %points_ref.1, ...), custom_call_target="tpu_custom_call" | custom-call | flops 2500000000 | bytes 639360 | tf_op jit(solution)/shard_map/pallas_call | solution.py:365
  6.3 1.9 %collective-permute-start.13 = (bf16[704,128]{1,0:T(8,128)(2,1)}, bf16[704,128]{1,0:T(8,128)(2,1)S(1)}, u32[]{:S(2)}, u32[]{:S(2)}) collective-permute-start(bf16[704,128]{1,0:T(8,128)(2,1)} %get-tuple-element.51), channel_id=1, source_target_pairs={{0,2},{1,5},{4,0},{5,9},{8,4},{9,13},{12,8},{13,15},{14,12},{15,11... | collective-permute-start | bytes 540680 | tf_op jit(solution)/shard_map/ppermute | solution.py:518
  8.1 1.4 %collective-permute-start.2 = (bf16[704,128]{1,0:T(8,128)(2,1)}, bf16[704,128]{1,0:T(8,128)(2,1)S(1)}, u32[]{:S(2)}, u32[]{:S(2)}) collective-permute-start(bf16[704,128]{1,0:T(8,128)(2,1)} %get-tuple-element.51), channel_id=1, source_target_pairs={{0,4},{1,3},{4,8},{5,1},{8,12},{9,5},{12,14},{13,9},{14,10},{15,13... | collective-permute-start | bytes 540680 | tf_op jit(solution)/shard_map/ppermute | solution.py:518
  10.2 1.4 %collective-permute-start.7 = (bf16[64,1024]{1,0:T(8,128)(2,1)S(1)}, bf16[64,1024]{1,0:T(8,128)(2,1)S(1)}, u32[]{:S(2)}, u32[]{:S(2)}) collective-permute-start(bf16[64,1024]{1,0:T(8,128)(2,1)S(1)} %collective-permute-done.6.refs_2_), channel_id=1, source_target_pairs={{0,4},{1,3},{4,8},{5,1},{8,12},{9,5},{12,14},{13,9},{14,10},{15,13... | collective-permute-start | bytes 393224 | tf_op jit(solution)/shard_map/ppermute | solution.py:528
  12.5 2.1 %shard_map.105 = (bf16[2,1024,128]{2,1,0:T(8,128)(2,1)S(1)}, f32[8,128]{1,0:T(8,128)S(1)}, bf16[3,1024,512]{2,1,0:T(8,128)(2,1)S(1)}, bf16[2,1024,128]{2,1,0:T(8...) custom-call(f32[8,128]{1,0:T(8,128)S(1)} %collective-permute-done.refs_0_.refs_1_.other_ref, ...), custom_call_target="tpu_custom_call" | custom-call | flops 2000000000 | bytes 450560 | tf_op jit(solution)/shard_map/pallas_call | solution.py:365
  15.3 1.4 %collective-permute-start.3 = (bf16[704,128]{1,0:T(8,128)(2,1)S(1)}, bf16[704,128]{1,0:T(8,128)(2,1)S(1)}, u32[]{:S(2)}, u32[]{:S(2)}) collective-permute-start(bf16[704,128]{1,0:T(8,128)(2,1)S(1)} %collective-permute-done.2.refs_4_.refs_6_), channel_id=1, source_target_pairs={{0,4},{1,3},{4,8},{5,1},{8,12},{9,5},{12,14},{13,9},{14,10},{15,13... | collective-permute-start | bytes 540680 | tf_op jit(solution)/shard_map/ppermute | solution.py:529
  16.7 3.1 %shard_map.106 = (bf16[2,1024,512]{2,1,0:T(8,128)(2,1)S(1)}, bf16[2,1024,512]{2,1,0:T(8,128)(2,1)S(1)}, bf16[2,1024,256]{2,1,0:T(8,128)(2,1)S(1)}, f32[2,1024,128]{2,1,0:T(8,128)S(1)}, f32[1,128,128]{2,1,0:T(8,128)S(1)}) custom-call(f32[8,128]{1,0:T(8,128)S(1)} %get-tuple-element.50.refs_0_.mine_ref, ...), custom_call_target="tpu_custom_call", output_to_operand_aliasing={{3}: (9, {}), {4}: (10, {})} | custom-call | flops 4000000000 | bytes 2629632 | tf_op jit(solution)/shard_map/pallas_call | solution.py:365
  20.5 1.4 %collective-permute-start.8 = (bf16[64,1024]{1,0:T(8,128)(2,1)S(1)}, bf16[64,1024]{1,0:T(8,128)(2,1)S(1)}, u32[]{:S(2)}, u32[]{:S(2)}) collective-permute-start(bf16[64,1024]{1,0:T(8,128)(2,1)S(1)} %collective-permute-done.7.refs_2_), channel_id=1, source_target_pairs={{0,4},{1,3},{4,8},{5,1},{8,12},{9,5},{12,14},{13,9},{14,10},{15,13... | collective-permute-start | bytes 393224 | tf_op jit(solution)/shard_map/ppermute | solution.py:528
  22.7 1.2 %collective-permute-start.4 = (bf16[704,128]{1,0:T(8,128)(2,1)S(1)}, bf16[704,128]{1,0:T(8,128)(2,1)S(1)}, u32[]{:S(2)}, u32[]{:S(2)}) collective-permute-start(bf16[704,128]{1,0:T(8,128)(2,1)S(1)} %collective-permute-done.3.refs_4_.refs_6_), channel_id=1, source_target_pairs={{0,4},{1,3},{4,8},{5,1},{8,12},{9,5},{12,14},{13,9},{14,10},{15,13... | collective-permute-start | bytes 540680 | tf_op jit(solution)/shard_map/ppermute | solution.py:529
  23.9 3.1 %shard_map.107 = (bf16[2,1024,512]{2,1,0:T(8,128)(2,1)S(1)}, bf16[2,1024,512]{2,1,0:T(8,128)(2,1)S(1)}, bf16[2,1024,256]{2,1,0:T(8,128)(2,1)S(1)}, f32[2,1024,128]{2,1,0:T(8,128)S(1)}, f32[1,128,128]{2,1,0:T(8,128)S(1)}) custom-call(f32[8,128]{1,0:T(8,128)S(1)} %get-tuple-element.50.refs_0_.mine_ref, ...), custom_call_target="tpu_custom_call", output_to_operand_aliasing={{3}: (9, {}), {4}: (10, {})} | custom-call | flops 4000000000 | bytes 2629632 | tf_op jit(solution)/shard_map/pallas_call | solution.py:365
  27.0 1.6 %collective-permute-start.9 = (bf16[64,1024]{1,0:T(8,128)(2,1)S(1)}, bf16[64,1024]{1,0:T(8,128)(2,1)S(1)}, u32[]{:S(2)}, u32[]{:S(2)}) collective-permute-start(bf16[64,1024]{1,0:T(8,128)(2,1)S(1)} %collective-permute-done.8.refs_2_), channel_id=1, source_target_pairs={{0,4},{1,3},{4,8},{5,1},{8,12},{9,5},{12,14},{13,9},{14,10},{15,13... | collective-permute-start | bytes 393224 | tf_op jit(solution)/shard_map/ppermute | solution.py:528
  28.7 1.6 %collective-permute-start.5 = (bf16[704,128]{1,0:T(8,128)(2,1)S(1)}, bf16[704,128]{1,0:T(8,128)(2,1)S(1)}, u32[]{:S(2)}, u32[]{:S(2)}) collective-permute-start(bf16[704,128]{1,0:T(8,128)(2,1)S(1)} %collective-permute-done.4.refs_4_.refs_6_), channel_id=1, source_target_pairs={{0,4},{1,3},{4,8},{5,1},{8,12},{9,5},{12,14},{13,9},{14,10},{15,13... | collective-permute-start | bytes 540680 | tf_op jit(solution)/shard_map/ppermute | solution.py:529
  30.3 3.1 %shard_map.108 = (bf16[2,1024,512]{2,1,0:T(8,128)(2,1)S(1)}, bf16[2,1024,512]{2,1,0:T(8,128)(2,1)S(1)}, bf16[2,1024,256]{2,1,0:T(8,128)(2,1)S(1)}, f32[2,1024,128]{2,1,0:T(8,128)S(1)}, f32[1,128,128]{2,1,0:T(8,128)S(1)}) custom-call(f32[8,128]{1,0:T(8,128)S(1)} %get-tuple-element.50.refs_0_.mine_ref, ...), custom_call_target="tpu_custom_call", output_to_operand_aliasing={{3}: (9, {}), {4}: (10, {})} | custom-call | flops 4000000000 | bytes 2629632 | tf_op jit(solution)/shard_map/pallas_call | solution.py:365
  34.3 1.5 %shard_map.111 = (bf16[2,1024,256]{2,1,0:T(8,128)(2,1)S(1)}, f32[512,128]{1,0:T(8,128)S(1)}, f32[512,128]{1,0:T(8,128)S(1)}, f32[2,1024,128]{2,1,0:T(8,128)S(1)}, f32[1,128,128]{2,1,0:T(8,128)S(1)}) custom-call(f32[8,128]{1,0:T(8,128)S(1)} %get-tuple-element.50.refs_0_.mine_ref, ...), custom_call_target="tpu_custom_call", output_to_operand_aliasing={{3}: (6, {}), {4}: (7, {})} | custom-call | flops 2000000000 | bytes 4120576 | tf_op jit(solution)/shard_map/pallas_call | solution.py:365
  35.9 1.5 %collective-permute-done.16.other_ref = f32[512,128]{1,0:T(8,128)S(1)} collective-permute-done((f32[512,128]{1,0:T(8,128)S(1)}, f32[512,128]{1,0:T(8,128)S(1)}, u32[]{:S(2)}, u32[]{:S(2)}) %collective-permute-start.16) | collective-permute-done | bytes 262176 | tf_op jit(solution)/shard_map/ppermute | solution.py:545
  38.3 1.5 %collective-permute-start.17 = (bf16[640,128]{1,0:T(8,128)(2,1)S(1)}, bf16[640,128]{1,0:T(8,128)(2,1)S(1)}, u32[]{:S(2)}, u32[]{:S(2)}) collective-permute-start(bf16[640,128]{1,0:T(8,128)(2,1)S(1)} %get-tuple-element.64.refs_2_), channel_id=1, source_target_pairs={{0,4},{1,3},{4,8},{5,1},{8,12},{9,5},{12,14},{13,9},{14,10},{15,13... | collective-permute-start | bytes 491528 | tf_op jit(solution)/shard_map/ppermute | solution.py:562
  41.5 2.5 %collective-permute-done.17.refs_2_ = bf16[640,128]{1,0:T(8,128)(2,1)S(1)} collective-permute-done((bf16[640,128]{1,0:T(8,128)(2,1)S(1)}, bf16[640,128]{1,0:T(8,128)(2,1)S(1)}, u32[]{:S(2)}, u32[]{:S(2)}) %collective-permute-start.17) | collective-permute-done | bytes 163872 | tf_op jit(solution)/shard_map/ppermute | solution.py:562
  44.0 2.4 %collective-permute-start.18 = (bf16[640,128]{1,0:T(8,128)(2,1)S(1)}, bf16[640,128]{1,0:T(8,128)(2,1)S(1)}, u32[]{:S(2)}, u32[]{:S(2)}) collective-permute-start(bf16[640,128]{1,0:T(8,128)(2,1)S(1)} %collective-permute-done.17.refs_2_), channel_id=1, source_target_pairs={{0,4},{1,3},{4,8},{5,1},{8,12},{9,5},{12,14},{13,9},{14,10},{15,13... | collective-permute-start | bytes 491528 | tf_op jit(solution)/shard_map/ppermute | solution.py:566
  48.5 2.2 %collective-permute-done.18.refs_2_ = bf16[640,128]{1,0:T(8,128)(2,1)S(1)} collective-permute-done((bf16[640,128]{1,0:T(8,128)(2,1)S(1)}, bf16[640,128]{1,0:T(8,128)(2,1)S(1)}, u32[]{:S(2)}, u32[]{:S(2)}) %collective-permute-start.18) | collective-permute-done | bytes 163872 | tf_op jit(solution)/shard_map/ppermute | solution.py:566
  50.6 2.5 %collective-permute-start.19 = (bf16[640,128]{1,0:T(8,128)(2,1)S(1)}, bf16[640,128]{1,0:T(8,128)(2,1)S(1)}, u32[]{:S(2)}, u32[]{:S(2)}) collective-permute-start(bf16[640,128]{1,0:T(8,128)(2,1)S(1)} %collective-permute-done.18.refs_2_), channel_id=1, source_target_pairs={{0,4},{1,3},{4,8},{5,1},{8,12},{9,5},{12,14},{13,9},{14,10},{15,13... | collective-permute-start | bytes 491528 | tf_op jit(solution)/shard_map/ppermute | solution.py:566
  55.4 1.8 %collective-permute-done.19.refs_2_ = bf16[640,128]{1,0:T(8,128)(2,1)S(1)} collective-permute-done((bf16[640,128]{1,0:T(8,128)(2,1)S(1)}, bf16[640,128]{1,0:T(8,128)(2,1)S(1)}, u32[]{:S(2)}, u32[]{:S(2)}) %collective-permute-start.19) | collective-permute-done | bytes 163872 | tf_op jit(solution)/shard_map/ppermute | solution.py:566
  57.3 1.8 %collective-permute-start.20 = (bf16[640,128]{1,0:T(8,128)(2,1)S(1)}, bf16[640,128]{1,0:T(8,128)(2,1)S(1)}, u32[]{:S(2)}, u32[]{:S(2)}) collective-permute-start(bf16[640,128]{1,0:T(8,128)(2,1)S(1)} %collective-permute-done.19.refs_2_), channel_id=1, source_target_pairs={{0,4},{1,3},{4,8},{5,1},{8,12},{9,5},{12,14},{13,9},{14,10},{15,13... | collective-permute-start | bytes 491528 | tf_op jit(solution)/shard_map/ppermute | solution.py:566
  63.9 1.5 %collective-permute-done.24.other_ref = f32[512,128]{1,0:T(8,128)S(1)} collective-permute-done((f32[512,128]{1,0:T(8,128)S(1)}, f32[512,128]{1,0:T(8,128)S(1)}, u32[]{:S(2)}, u32[]{:S(2)}) %collective-permute-start.24) | collective-permute-done | bytes 262176 | tf_op jit(solution)/shard_map/ppermute | solution.py:576
  (57 shorter events, 17.9 us)
Async XLA Ops:
  0.6 10.9 %collective-permute-start.1 = (bf16[64,1024]{1,0:T(8,128)(2,1)}, bf16[64,1024]{1,0:T(8,128)(2,1)S(1)}, u32[]{:S(2)}, u32[]{:S(2)}) collective-permute-start(bf16[64,1024]{1,0:T(8,128)(2,1)} %coords_ref.1), channel_id=1, source_target_pairs={{0,1},{1,0},{2,3},{3,2},{4,5},{5,4},{6,7},{7,6},{8,9},{9,8},{10,11... | collective-permute-start | bytes 393224 | tf_op jit(solution)/shard_map/ppermute | solution.py:420
  1.1 8.4 %collective-permute-start.10 = (bf16[64,1024]{1,0:T(8,128)(2,1)}, bf16[64,1024]{1,0:T(8,128)(2,1)S(1)}, u32[]{:S(2)}, u32[]{:S(2)}) collective-permute-start(bf16[64,1024]{1,0:T(8,128)(2,1)} %coords_ref.1), channel_id=1, source_target_pairs={{0,2},{1,5},{4,0},{5,9},{8,4},{9,13},{12,8},{13,15},{14,12},{15,11... | collective-permute-start | bytes 393224 | tf_op jit(solution)/shard_map/ppermute | solution.py:421
  3.7 6.4 %collective-permute-start.6 = (bf16[64,1024]{1,0:T(8,128)(2,1)}, bf16[64,1024]{1,0:T(8,128)(2,1)S(1)}, u32[]{:S(2)}, u32[]{:S(2)}) collective-permute-start(bf16[64,1024]{1,0:T(8,128)(2,1)} %coords_ref.1), channel_id=1, source_target_pairs={{0,4},{1,3},{4,8},{5,1},{8,12},{9,5},{12,14},{13,9},{14,10},{15,13... | collective-permute-start | bytes 393224 | tf_op jit(solution)/shard_map/ppermute | solution.py:421
  6.2 1.9 %collective-permute-start = (f32[8,128]{1,0:T(8,128)}, f32[8,128]{1,0:T(8,128)S(1)}, u32[]{:S(2)}, u32[]{:S(2)}) collective-permute-start(f32[8,128]{1,0:T(8,128)} %get-tuple-element.48), channel_id=1, source_target_pairs={{0,1},{1,0},{2,3},{3,2},{4,5},{5,4},{6,7},{7,6},{8,9},{9,8},{10,11... | collective-permute-start | bytes 12296 | tf_op jit(solution)/shard_map/ppermute | solution.py:434
  6.3 8.3 %collective-permute-start.13 = (bf16[704,128]{1,0:T(8,128)(2,1)}, bf16[704,128]{1,0:T(8,128)(2,1)S(1)}, u32[]{:S(2)}, u32[]{:S(2)}) collective-permute-start(bf16[704,128]{1,0:T(8,128)(2,1)} %get-tuple-element.51), channel_id=1, source_target_pairs={{0,2},{1,5},{4,0},{5,9},{8,4},{9,13},{12,8},{13,15},{14,12},{15,11... | collective-permute-start | bytes 540680 | tf_op jit(solution)/shard_map/ppermute | solution.py:518
  8.1 7.2 %collective-permute-start.2 = (bf16[704,128]{1,0:T(8,128)(2,1)}, bf16[704,128]{1,0:T(8,128)(2,1)S(1)}, u32[]{:S(2)}, u32[]{:S(2)}) collective-permute-start(bf16[704,128]{1,0:T(8,128)(2,1)} %get-tuple-element.51), channel_id=1, source_target_pairs={{0,4},{1,3},{4,8},{5,1},{8,12},{9,5},{12,14},{13,9},{14,10},{15,13... | collective-permute-start | bytes 540680 | tf_op jit(solution)/shard_map/ppermute | solution.py:518
  9.5 10.3 %collective-permute-start.11 = (bf16[64,1024]{1,0:T(8,128)(2,1)S(1)}, bf16[64,1024]{1,0:T(8,128)(2,1)S(1)}, u32[]{:S(2)}, u32[]{:S(2)}) collective-permute-start(bf16[64,1024]{1,0:T(8,128)(2,1)S(1)} %collective-permute-done.10.refs_3_), channel_id=1, source_target_pairs={{0,2},{1,5},{4,0},{5,9},{8,4},{9,13},{12,8},{13,15},{14,12},{15,11... | collective-permute-start | bytes 393224 | tf_op jit(solution)/shard_map/ppermute | solution.py:528
  10.2 10.3 %collective-permute-start.7 = (bf16[64,1024]{1,0:T(8,128)(2,1)S(1)}, bf16[64,1024]{1,0:T(8,128)(2,1)S(1)}, u32[]{:S(2)}, u32[]{:S(2)}) collective-permute-start(bf16[64,1024]{1,0:T(8,128)(2,1)S(1)} %collective-permute-done.6.refs_2_), channel_id=1, source_target_pairs={{0,4},{1,3},{4,8},{5,1},{8,12},{9,5},{12,14},{13,9},{14,10},{15,13... | collective-permute-start | bytes 393224 | tf_op jit(solution)/shard_map/ppermute | solution.py:528
  14.6 7.3 %collective-permute-start.14 = (bf16[704,128]{1,0:T(8,128)(2,1)S(1)}, bf16[704,128]{1,0:T(8,128)(2,1)S(1)}, u32[]{:S(2)}, u32[]{:S(2)}) collective-permute-start(bf16[704,128]{1,0:T(8,128)(2,1)S(1)} %collective-permute-done.13.refs_5_.refs_7_), channel_id=1, source_target_pairs={{0,2},{1,5},{4,0},{5,9},{8,4},{9,13},{12,8},{13,15},{14,12},{15,11... | collective-permute-start | bytes 540680 | tf_op jit(solution)/shard_map/ppermute | solution.py:529
  15.3 7.4 %collective-permute-start.3 = (bf16[704,128]{1,0:T(8,128)(2,1)S(1)}, bf16[704,128]{1,0:T(8,128)(2,1)S(1)}, u32[]{:S(2)}, u32[]{:S(2)}) collective-permute-start(bf16[704,128]{1,0:T(8,128)(2,1)S(1)} %collective-permute-done.2.refs_4_.refs_6_), channel_id=1, source_target_pairs={{0,4},{1,3},{4,8},{5,1},{8,12},{9,5},{12,14},{13,9},{14,10},{15,13... | collective-permute-start | bytes 540680 | tf_op jit(solution)/shard_map/ppermute | solution.py:529
  19.8 10.4 %collective-permute-start.12 = (bf16[64,1024]{1,0:T(8,128)(2,1)S(1)}, bf16[64,1024]{1,0:T(8,128)(2,1)S(1)}, u32[]{:S(2)}, u32[]{:S(2)}) collective-permute-start(bf16[64,1024]{1,0:T(8,128)(2,1)S(1)} %collective-permute-done.11.refs_3_), channel_id=1, source_target_pairs={{0,2},{1,5},{4,0},{5,9},{8,4},{9,13},{12,8},{13,15},{14,12},{15,11... | collective-permute-start | bytes 393224 | tf_op jit(solution)/shard_map/ppermute | solution.py:528
  20.5 6.5 %collective-permute-start.8 = (bf16[64,1024]{1,0:T(8,128)(2,1)S(1)}, bf16[64,1024]{1,0:T(8,128)(2,1)S(1)}, u32[]{:S(2)}, u32[]{:S(2)}) collective-permute-start(bf16[64,1024]{1,0:T(8,128)(2,1)S(1)} %collective-permute-done.7.refs_2_), channel_id=1, source_target_pairs={{0,4},{1,3},{4,8},{5,1},{8,12},{9,5},{12,14},{13,9},{14,10},{15,13... | collective-permute-start | bytes 393224 | tf_op jit(solution)/shard_map/ppermute | solution.py:528
  21.9 8.4 %collective-permute-start.15 = (bf16[704,128]{1,0:T(8,128)(2,1)S(1)}, bf16[704,128]{1,0:T(8,128)(2,1)S(1)}, u32[]{:S(2)}, u32[]{:S(2)}) collective-permute-start(bf16[704,128]{1,0:T(8,128)(2,1)S(1)} %collective-permute-done.14.refs_5_.refs_7_), channel_id=1, source_target_pairs={{0,2},{1,5},{4,0},{5,9},{8,4},{9,13},{12,8},{13,15},{14,12},{15,11... | collective-permute-start | bytes 540680 | tf_op jit(solution)/shard_map/ppermute | solution.py:529
  22.7 6.0 %collective-permute-start.4 = (bf16[704,128]{1,0:T(8,128)(2,1)S(1)}, bf16[704,128]{1,0:T(8,128)(2,1)S(1)}, u32[]{:S(2)}, u32[]{:S(2)}) collective-permute-start(bf16[704,128]{1,0:T(8,128)(2,1)S(1)} %collective-permute-done.3.refs_4_.refs_6_), channel_id=1, source_target_pairs={{0,4},{1,3},{4,8},{5,1},{8,12},{9,5},{12,14},{13,9},{14,10},{15,13... | collective-permute-start | bytes 540680 | tf_op jit(solution)/shard_map/ppermute | solution.py:529
  27.0 6.3 %collective-permute-start.9 = (bf16[64,1024]{1,0:T(8,128)(2,1)S(1)}, bf16[64,1024]{1,0:T(8,128)(2,1)S(1)}, u32[]{:S(2)}, u32[]{:S(2)}) collective-permute-start(bf16[64,1024]{1,0:T(8,128)(2,1)S(1)} %collective-permute-done.8.refs_2_), channel_id=1, source_target_pairs={{0,4},{1,3},{4,8},{5,1},{8,12},{9,5},{12,14},{13,9},{14,10},{15,13... | collective-permute-start | bytes 393224 | tf_op jit(solution)/shard_map/ppermute | solution.py:528
  28.7 5.6 %collective-permute-start.5 = (bf16[704,128]{1,0:T(8,128)(2,1)S(1)}, bf16[704,128]{1,0:T(8,128)(2,1)S(1)}, u32[]{:S(2)}, u32[]{:S(2)}) collective-permute-start(bf16[704,128]{1,0:T(8,128)(2,1)S(1)} %collective-permute-done.4.refs_4_.refs_6_), channel_id=1, source_target_pairs={{0,4},{1,3},{4,8},{5,1},{8,12},{9,5},{12,14},{13,9},{14,10},{15,13... | collective-permute-start | bytes 540680 | tf_op jit(solution)/shard_map/ppermute | solution.py:529
  38.3 5.7 %collective-permute-start.17 = (bf16[640,128]{1,0:T(8,128)(2,1)S(1)}, bf16[640,128]{1,0:T(8,128)(2,1)S(1)}, u32[]{:S(2)}, u32[]{:S(2)}) collective-permute-start(bf16[640,128]{1,0:T(8,128)(2,1)S(1)} %get-tuple-element.64.refs_2_), channel_id=1, source_target_pairs={{0,4},{1,3},{4,8},{5,1},{8,12},{9,5},{12,14},{13,9},{14,10},{15,13... | collective-permute-start | bytes 491528 | tf_op jit(solution)/shard_map/ppermute | solution.py:562
  40.9 6.3 %collective-permute-start.21 = (bf16[640,128]{1,0:T(8,128)(2,1)S(1)}, bf16[640,128]{1,0:T(8,128)(2,1)S(1)}, u32[]{:S(2)}, u32[]{:S(2)}) collective-permute-start(bf16[640,128]{1,0:T(8,128)(2,1)S(1)} %shard_map.114), channel_id=1, source_target_pairs={{0,2},{1,5},{4,0},{5,9},{8,4},{9,13},{12,8},{13,15},{14,12},{15,11... | collective-permute-start | bytes 491528 | tf_op jit(solution)/shard_map/ppermute | solution.py:564
  44.0 6.7 %collective-permute-start.18 = (bf16[640,128]{1,0:T(8,128)(2,1)S(1)}, bf16[640,128]{1,0:T(8,128)(2,1)S(1)}, u32[]{:S(2)}, u32[]{:S(2)}) collective-permute-start(bf16[640,128]{1,0:T(8,128)(2,1)S(1)} %collective-permute-done.17.refs_2_), channel_id=1, source_target_pairs={{0,4},{1,3},{4,8},{5,1},{8,12},{9,5},{12,14},{13,9},{14,10},{15,13... | collective-permute-start | bytes 491528 | tf_op jit(solution)/shard_map/ppermute | solution.py:566
  47.2 7.0 %collective-permute-start.22 = (bf16[640,128]{1,0:T(8,128)(2,1)S(1)}, bf16[640,128]{1,0:T(8,128)(2,1)S(1)}, u32[]{:S(2)}, u32[]{:S(2)}) collective-permute-start(bf16[640,128]{1,0:T(8,128)(2,1)S(1)} %shard_map.116.refs_3_), channel_id=1, source_target_pairs={{0,2},{1,5},{4,0},{5,9},{8,4},{9,13},{12,8},{13,15},{14,12},{15,11... | collective-permute-start | bytes 491528 | tf_op jit(solution)/shard_map/ppermute | solution.py:571
  50.6 6.6 %collective-permute-start.19 = (bf16[640,128]{1,0:T(8,128)(2,1)S(1)}, bf16[640,128]{1,0:T(8,128)(2,1)S(1)}, u32[]{:S(2)}, u32[]{:S(2)}) collective-permute-start(bf16[640,128]{1,0:T(8,128)(2,1)S(1)} %collective-permute-done.18.refs_2_), channel_id=1, source_target_pairs={{0,4},{1,3},{4,8},{5,1},{8,12},{9,5},{12,14},{13,9},{14,10},{15,13... | collective-permute-start | bytes 491528 | tf_op jit(solution)/shard_map/ppermute | solution.py:566
  54.2 6.1 %collective-permute-start.23 = (bf16[640,128]{1,0:T(8,128)(2,1)S(1)}, bf16[640,128]{1,0:T(8,128)(2,1)S(1)}, u32[]{:S(2)}, u32[]{:S(2)}) collective-permute-start(bf16[640,128]{1,0:T(8,128)(2,1)S(1)} %shard_map.119.refs_3_), channel_id=1, source_target_pairs={{0,2},{1,5},{4,0},{5,9},{8,4},{9,13},{12,8},{13,15},{14,12},{15,11... | collective-permute-start | bytes 491528 | tf_op jit(solution)/shard_map/ppermute | solution.py:571
  57.3 5.3 %collective-permute-start.20 = (bf16[640,128]{1,0:T(8,128)(2,1)S(1)}, bf16[640,128]{1,0:T(8,128)(2,1)S(1)}, u32[]{:S(2)}, u32[]{:S(2)}) collective-permute-start(bf16[640,128]{1,0:T(8,128)(2,1)S(1)} %collective-permute-done.19.refs_2_), channel_id=1, source_target_pairs={{0,4},{1,3},{4,8},{5,1},{8,12},{9,5},{12,14},{13,9},{14,10},{15,13... | collective-permute-start | bytes 491528 | tf_op jit(solution)/shard_map/ppermute | solution.py:566
  63.8 1.6 %collective-permute-start.24 = (f32[512,128]{1,0:T(8,128)S(1)}, f32[512,128]{1,0:T(8,128)S(1)}, u32[]{:S(2)}, u32[]{:S(2)}) collective-permute-start(f32[512,128]{1,0:T(8,128)S(1)} %get-tuple-element.93), channel_id=1, source_target_pairs={{0,1},{1,0},{2,3},{3,2},{4,5},{5,4},{6,7},{7,6},{8,9},{9,8},{10,11... | collective-permute-start | bytes 786440 | tf_op jit(solution)/shard_map/ppermute | solution.py:576
  (6 other events, 12.8 us)

commit v19 on v18

--- a/solution.py
+++ b/solution.py
@@ -124,7 +124,7 @@
     half = local // LEAVES
     charges = [charges_ref[:, 0:half], charges_ref[:, half:]]
     sent = [
-        jnp.concatenate(charges, axis=0).astype(f32).T.astype(bf16),
+        jnp.concatenate(charges, axis=0).T,
         skeleton_rows(charges, leaf_ref, node_ref, upper_ref),
         points_ref[...],
     ]

time: 66.3 us -> 66.3 us (level)
  no operation moved by 1% of the time
where the time goes in v19:
time: 66.3 us; the launch traced here: 66.2 us
  starting transfers between devices  27 us (41%)
  Pallas kernels  25.8 us (39%)
  waiting for transfers between devices  11.5 us (17%)
  local copies, waits for them, and re-layouts  0.99 us (1%)
  between operations  0.89 us (1%)
    pallas_call x17, Pallas kernels, call(): pl.pallas_call(body, grid=(1,), out_shape=out_shapes, in_specs=specs, out...  25.8 us
    ppermute x3, starting transfers between devices, on_device(): one_next = one_way(one)  6.69 us
    ppermute x5, starting transfers between devices, on_device(): sent = (one_way(sent[0]), None if final else other_way(sent[1]))  5.71 us
    ppermute x3, waiting for transfers between devices, on_device(): one_next = one_way(one)  5.09 us
    ppermute x3, starting transfers between devices, on_device(): one_way(coords_next[0])  4.41 us
    ppermute x2, starting transfers between devices, on_device(): sent = (one_way(message), other_way(message))  3.23 us
    ppermute x2, waiting for transfers between devices, on_device(): to_sibling(results['other'])  3.04 us
    ppermute x2, starting transfers between devices, on_device(): coords_next = (one_way(coords), other_way(coords))  2.72 us
  transfers between devices with their start and end apart: 25, of which 8 were waited for; matrix products, arithmetic and copies ran while one was open for 0% of the time, Pallas kernels for 32%

profile of v19, /device:TPU:0, one launch (start us, length us, event | category | flops | bytes accessed | tf_op | source)
XLA Modules:
  0.0 66.2 jit_solution(14148531179841564863)
XLA Ops:
  1.1 2.6 %collective-permute-start.10 = (bf16[64,1024]{1,0:T(8,128)(2,1)}, bf16[64,1024]{1,0:T(8,128)(2,1)S(1)}, u32[]{:S(2)}, u32[]{:S(2)}) collective-permute-start(bf16[64,1024]{1,0:T(8,128)(2,1)} %coords_ref.1), channel_id=1, source_target_pairs={{0,2},{1,5},{4,0},{5,9},{8,4},{9,13},{12,8},{13,15},{14,12},{15,11... | collective-permute-start | bytes 393224 | tf_op jit(solution)/shard_map/ppermute | solution.py:421
  3.9 2.3 %shard_map.104 = (bf16[704,128]{1,0:T(8,128)(2,1)}, bf16[1232,128]{1,0:T(8,128)(2,1)}, f32[8,128]{1,0:T(8,128)}) custom-call(s32[2,16]{1,0:T(2,128)} %near_ref.1, s32[2,32]{1,0:T(2,128)} %far_ref.1, bf16[64,1024]{1,0:T(8,128)(2,1)} %coords_ref.1, bf16[64,1024]{1,0:T(8,128)(2,1)} %charges_ref.1, bf16[64,128]{1,0:T(8,128)(2,1)} %points_ref.1, ...), custom_call_target="tpu_custom_call" | custom-call | flops 2500000000 | bytes 639360 | tf_op jit(solution)/shard_map/pallas_call | solution.py:365
  6.3 1.9 %collective-permute-start.13 = (bf16[704,128]{1,0:T(8,128)(2,1)}, bf16[704,128]{1,0:T(8,128)(2,1)S(1)}, u32[]{:S(2)}, u32[]{:S(2)}) collective-permute-start(bf16[704,128]{1,0:T(8,128)(2,1)} %get-tuple-element.51), channel_id=1, source_target_pairs={{0,2},{1,5},{4,0},{5,9},{8,4},{9,13},{12,8},{13,15},{14,12},{15,11... | collective-permute-start | bytes 540680 | tf_op jit(solution)/shard_map/ppermute | solution.py:518
  8.1 1.4 %collective-permute-start.2 = (bf16[704,128]{1,0:T(8,128)(2,1)}, bf16[704,128]{1,0:T(8,128)(2,1)S(1)}, u32[]{:S(2)}, u32[]{:S(2)}) collective-permute-start(bf16[704,128]{1,0:T(8,128)(2,1)} %get-tuple-element.51), channel_id=1, source_target_pairs={{0,4},{1,3},{4,8},{5,1},{8,12},{9,5},{12,14},{13,9},{14,10},{15,13... | collective-permute-start | bytes 540680 | tf_op jit(solution)/shard_map/ppermute | solution.py:518
  10.2 1.4 %collective-permute-start.7 = (bf16[64,1024]{1,0:T(8,128)(2,1)S(1)}, bf16[64,1024]{1,0:T(8,128)(2,1)S(1)}, u32[]{:S(2)}, u32[]{:S(2)}) collective-permute-start(bf16[64,1024]{1,0:T(8,128)(2,1)S(1)} %collective-permute-done.6.refs_2_), channel_id=1, source_target_pairs={{0,4},{1,3},{4,8},{5,1},{8,12},{9,5},{12,14},{13,9},{14,10},{15,13... | collective-permute-start | bytes 393224 | tf_op jit(solution)/shard_map/ppermute | solution.py:528
  12.5 2.1 %shard_map.105 = (bf16[2,1024,128]{2,1,0:T(8,128)(2,1)S(1)}, f32[8,128]{1,0:T(8,128)S(1)}, bf16[3,1024,512]{2,1,0:T(8,128)(2,1)S(1)}, bf16[2,1024,128]{2,1,0:T(8...) custom-call(f32[8,128]{1,0:T(8,128)S(1)} %collective-permute-done.refs_0_.refs_1_.other_ref, ...), custom_call_target="tpu_custom_call" | custom-call | flops 2000000000 | bytes 450560 | tf_op jit(solution)/shard_map/pallas_call | solution.py:365
  15.3 1.4 %collective-permute-start.3 = (bf16[704,128]{1,0:T(8,128)(2,1)S(1)}, bf16[704,128]{1,0:T(8,128)(2,1)S(1)}, u32[]{:S(2)}, u32[]{:S(2)}) collective-permute-start(bf16[704,128]{1,0:T(8,128)(2,1)S(1)} %collective-permute-done.2.refs_4_.refs_6_), channel_id=1, source_target_pairs={{0,4},{1,3},{4,8},{5,1},{8,12},{9,5},{12,14},{13,9},{14,10},{15,13... | collective-permute-start | bytes 540680 | tf_op jit(solution)/shard_map/ppermute | solution.py:529
  16.7 3.1 %shard_map.106 = (bf16[2,1024,512]{2,1,0:T(8,128)(2,1)S(1)}, bf16[2,1024,512]{2,1,0:T(8,128)(2,1)S(1)}, bf16[2,1024,256]{2,1,0:T(8,128)(2,1)S(1)}, f32[2,1024,128]{2,1,0:T(8,128)S(1)}, f32[1,128,128]{2,1,0:T(8,128)S(1)}) custom-call(f32[8,128]{1,0:T(8,128)S(1)} %get-tuple-element.50.refs_0_.mine_ref, ...), custom_call_target="tpu_custom_call", output_to_operand_aliasing={{3}: (9, {}), {4}: (10, {})} | custom-call | flops 4000000000 | bytes 2629632 | tf_op jit(solution)/shard_map/pallas_call | solution.py:365
  20.5 1.4 %collective-permute-start.8 = (bf16[64,1024]{1,0:T(8,128)(2,1)S(1)}, bf16[64,1024]{1,0:T(8,128)(2,1)S(1)}, u32[]{:S(2)}, u32[]{:S(2)}) collective-permute-start(bf16[64,1024]{1,0:T(8,128)(2,1)S(1)} %collective-permute-done.7.refs_2_), channel_id=1, source_target_pairs={{0,4},{1,3},{4,8},{5,1},{8,12},{9,5},{12,14},{13,9},{14,10},{15,13... | collective-permute-start | bytes 393224 | tf_op jit(solution)/shard_map/ppermute | solution.py:528
  22.7 1.2 %collective-permute-start.4 = (bf16[704,128]{1,0:T(8,128)(2,1)S(1)}, bf16[704,128]{1,0:T(8,128)(2,1)S(1)}, u32[]{:S(2)}, u32[]{:S(2)}) collective-permute-start(bf16[704,128]{1,0:T(8,128)(2,1)S(1)} %collective-permute-done.3.refs_4_.refs_6_), channel_id=1, source_target_pairs={{0,4},{1,3},{4,8},{5,1},{8,12},{9,5},{12,14},{13,9},{14,10},{15,13... | collective-permute-start | bytes 540680 | tf_op jit(solution)/shard_map/ppermute | solution.py:529
  23.9 3.1 %shard_map.107 = (bf16[2,1024,512]{2,1,0:T(8,128)(2,1)S(1)}, bf16[2,1024,512]{2,1,0:T(8,128)(2,1)S(1)}, bf16[2,1024,256]{2,1,0:T(8,128)(2,1)S(1)}, f32[2,1024,128]{2,1,0:T(8,128)S(1)}, f32[1,128,128]{2,1,0:T(8,128)S(1)}) custom-call(f32[8,128]{1,0:T(8,128)S(1)} %get-tuple-element.50.refs_0_.mine_ref, ...), custom_call_target="tpu_custom_call", output_to_operand_aliasing={{3}: (9, {}), {4}: (10, {})} | custom-call | flops 4000000000 | bytes 2629632 | tf_op jit(solution)/shard_map/pallas_call | solution.py:365
  27.0 1.6 %collective-permute-start.9 = (bf16[64,1024]{1,0:T(8,128)(2,1)S(1)}, bf16[64,1024]{1,0:T(8,128)(2,1)S(1)}, u32[]{:S(2)}, u32[]{:S(2)}) collective-permute-start(bf16[64,1024]{1,0:T(8,128)(2,1)S(1)} %collective-permute-done.8.refs_2_), channel_id=1, source_target_pairs={{0,4},{1,3},{4,8},{5,1},{8,12},{9,5},{12,14},{13,9},{14,10},{15,13... | collective-permute-start | bytes 393224 | tf_op jit(solution)/shard_map/ppermute | solution.py:528
  28.7 1.6 %collective-permute-start.5 = (bf16[704,128]{1,0:T(8,128)(2,1)S(1)}, bf16[704,128]{1,0:T(8,128)(2,1)S(1)}, u32[]{:S(2)}, u32[]{:S(2)}) collective-permute-start(bf16[704,128]{1,0:T(8,128)(2,1)S(1)} %collective-permute-done.4.refs_4_.refs_6_), channel_id=1, source_target_pairs={{0,4},{1,3},{4,8},{5,1},{8,12},{9,5},{12,14},{13,9},{14,10},{15,13... | collective-permute-start | bytes 540680 | tf_op jit(solution)/shard_map/ppermute | solution.py:529
  30.3 3.1 %shard_map.108 = (bf16[2,1024,512]{2,1,0:T(8,128)(2,1)S(1)}, bf16[2,1024,512]{2,1,0:T(8,128)(2,1)S(1)}, bf16[2,1024,256]{2,1,0:T(8,128)(2,1)S(1)}, f32[2,1024,128]{2,1,0:T(8,128)S(1)}, f32[1,128,128]{2,1,0:T(8,128)S(1)}) custom-call(f32[8,128]{1,0:T(8,128)S(1)} %get-tuple-element.50.refs_0_.mine_ref, ...), custom_call_target="tpu_custom_call", output_to_operand_aliasing={{3}: (9, {}), {4}: (10, {})} | custom-call | flops 4000000000 | bytes 2629632 | tf_op jit(solution)/shard_map/pallas_call | solution.py:365
  34.3 1.5 %shard_map.111 = (bf16[2,1024,256]{2,1,0:T(8,128)(2,1)S(1)}, f32[512,128]{1,0:T(8,128)S(1)}, f32[512,128]{1,0:T(8,128)S(1)}, f32[2,1024,128]{2,1,0:T(8,128)S(1)}, f32[1,128,128]{2,1,0:T(8,128)S(1)}) custom-call(f32[8,128]{1,0:T(8,128)S(1)} %get-tuple-element.50.refs_0_.mine_ref, ...), custom_call_target="tpu_custom_call", output_to_operand_aliasing={{3}: (6, {}), {4}: (7, {})} | custom-call | flops 2000000000 | bytes 4120576 | tf_op jit(solution)/shard_map/pallas_call | solution.py:365
  35.9 1.5 %collective-permute-done.16.other_ref = f32[512,128]{1,0:T(8,128)S(1)} collective-permute-done((f32[512,128]{1,0:T(8,128)S(1)}, f32[512,128]{1,0:T(8,128)S(1)}, u32[]{:S(2)}, u32[]{:S(2)}) %collective-permute-start.16) | collective-permute-done | bytes 262176 | tf_op jit(solution)/shard_map/ppermute | solution.py:545
  38.3 1.5 %collective-permute-start.17 = (bf16[640,128]{1,0:T(8,128)(2,1)S(1)}, bf16[640,128]{1,0:T(8,128)(2,1)S(1)}, u32[]{:S(2)}, u32[]{:S(2)}) collective-permute-start(bf16[640,128]{1,0:T(8,128)(2,1)S(1)} %get-tuple-element.64.refs_2_), channel_id=1, source_target_pairs={{0,4},{1,3},{4,8},{5,1},{8,12},{9,5},{12,14},{13,9},{14,10},{15,13... | collective-permute-start | bytes 491528 | tf_op jit(solution)/shard_map/ppermute | solution.py:562
  41.5 2.5 %collective-permute-done.17.refs_2_ = bf16[640,128]{1,0:T(8,128)(2,1)S(1)} collective-permute-done((bf16[640,128]{1,0:T(8,128)(2,1)S(1)}, bf16[640,128]{1,0:T(8,128)(2,1)S(1)}, u32[]{:S(2)}, u32[]{:S(2)}) %collective-permute-start.17) | collective-permute-done | bytes 163872 | tf_op jit(solution)/shard_map/ppermute | solution.py:562
  44.0 2.4 %collective-permute-start.18 = (bf16[640,128]{1,0:T(8,128)(2,1)S(1)}, bf16[640,128]{1,0:T(8,128)(2,1)S(1)}, u32[]{:S(2)}, u32[]{:S(2)}) collective-permute-start(bf16[640,128]{1,0:T(8,128)(2,1)S(1)} %collective-permute-done.17.refs_2_), channel_id=1, source_target_pairs={{0,4},{1,3},{4,8},{5,1},{8,12},{9,5},{12,14},{13,9},{14,10},{15,13... | collective-permute-start | bytes 491528 | tf_op jit(solution)/shard_map/ppermute | solution.py:566
  48.5 2.2 %collective-permute-done.18.refs_2_ = bf16[640,128]{1,0:T(8,128)(2,1)S(1)} collective-permute-done((bf16[640,128]{1,0:T(8,128)(2,1)S(1)}, bf16[640,128]{1,0:T(8,128)(2,1)S(1)}, u32[]{:S(2)}, u32[]{:S(2)}) %collective-permute-start.18) | collective-permute-done | bytes 163872 | tf_op jit(solution)/shard_map/ppermute | solution.py:566
  50.6 2.5 %collective-permute-start.19 = (bf16[640,128]{1,0:T(8,128)(2,1)S(1)}, bf16[640,128]{1,0:T(8,128)(2,1)S(1)}, u32[]{:S(2)}, u32[]{:S(2)}) collective-permute-start(bf16[640,128]{1,0:T(8,128)(2,1)S(1)} %collective-permute-done.18.refs_2_), channel_id=1, source_target_pairs={{0,4},{1,3},{4,8},{5,1},{8,12},{9,5},{12,14},{13,9},{14,10},{15,13... | collective-permute-start | bytes 491528 | tf_op jit(solution)/shard_map/ppermute | solution.py:566
  55.4 1.8 %collective-permute-done.19.refs_2_ = bf16[640,128]{1,0:T(8,128)(2,1)S(1)} collective-permute-done((bf16[640,128]{1,0:T(8,128)(2,1)S(1)}, bf16[640,128]{1,0:T(8,128)(2,1)S(1)}, u32[]{:S(2)}, u32[]{:S(2)}) %collective-permute-start.19) | collective-permute-done | bytes 163872 | tf_op jit(solution)/shard_map/ppermute | solution.py:566
  57.3 1.8 %collective-permute-start.20 = (bf16[640,128]{1,0:T(8,128)(2,1)S(1)}, bf16[640,128]{1,0:T(8,128)(2,1)S(1)}, u32[]{:S(2)}, u32[]{:S(2)}) collective-permute-start(bf16[640,128]{1,0:T(8,128)(2,1)S(1)} %collective-permute-done.19.refs_2_), channel_id=1, source_target_pairs={{0,4},{1,3},{4,8},{5,1},{8,12},{9,5},{12,14},{13,9},{14,10},{15,13... | collective-permute-start | bytes 491528 | tf_op jit(solution)/shard_map/ppermute | solution.py:566
  63.9 1.5 %collective-permute-done.24.other_ref = f32[512,128]{1,0:T(8,128)S(1)} collective-permute-done((f32[512,128]{1,0:T(8,128)S(1)}, f32[512,128]{1,0:T(8,128)S(1)}, u32[]{:S(2)}, u32[]{:S(2)}) %collective-permute-start.24) | collective-permute-done | bytes 262176 | tf_op jit(solution)/shard_map/ppermute | solution.py:576
  (57 shorter events, 17.9 us)
Async XLA Ops:
  0.6 10.9 %collective-permute-start.1 = (bf16[64,1024]{1,0:T(8,128)(2,1)}, bf16[64,1024]{1,0:T(8,128)(2,1)S(1)}, u32[]{:S(2)}, u32[]{:S(2)}) collective-permute-start(bf16[64,1024]{1,0:T(8,128)(2,1)} %coords_ref.1), channel_id=1, source_target_pairs={{0,1},{1,0},{2,3},{3,2},{4,5},{5,4},{6,7},{7,6},{8,9},{9,8},{10,11... | collective-permute-start | bytes 393224 | tf_op jit(solution)/shard_map/ppermute | solution.py:420
  1.1 8.4 %collective-permute-start.10 = (bf16[64,1024]{1,0:T(8,128)(2,1)}, bf16[64,1024]{1,0:T(8,128)(2,1)S(1)}, u32[]{:S(2)}, u32[]{:S(2)}) collective-permute-start(bf16[64,1024]{1,0:T(8,128)(2,1)} %coords_ref.1), channel_id=1, source_target_pairs={{0,2},{1,5},{4,0},{5,9},{8,4},{9,13},{12,8},{13,15},{14,12},{15,11... | collective-permute-start | bytes 393224 | tf_op jit(solution)/shard_map/ppermute | solution.py:421
  3.7 6.4 %collective-permute-start.6 = (bf16[64,1024]{1,0:T(8,128)(2,1)}, bf16[64,1024]{1,0:T(8,128)(2,1)S(1)}, u32[]{:S(2)}, u32[]{:S(2)}) collective-permute-start(bf16[64,1024]{1,0:T(8,128)(2,1)} %coords_ref.1), channel_id=1, source_target_pairs={{0,4},{1,3},{4,8},{5,1},{8,12},{9,5},{12,14},{13,9},{14,10},{15,13... | collective-permute-start | bytes 393224 | tf_op jit(solution)/shard_map/ppermute | solution.py:421
  6.2 1.9 %collective-permute-start = (f32[8,128]{1,0:T(8,128)}, f32[8,128]{1,0:T(8,128)S(1)}, u32[]{:S(2)}, u32[]{:S(2)}) collective-permute-start(f32[8,128]{1,0:T(8,128)} %get-tuple-element.48), channel_id=1, source_target_pairs={{0,1},{1,0},{2,3},{3,2},{4,5},{5,4},{6,7},{7,6},{8,9},{9,8},{10,11... | collective-permute-start | bytes 12296 | tf_op jit(solution)/shard_map/ppermute | solution.py:434
  6.3 8.3 %collective-permute-start.13 = (bf16[704,128]{1,0:T(8,128)(2,1)}, bf16[704,128]{1,0:T(8,128)(2,1)S(1)}, u32[]{:S(2)}, u32[]{:S(2)}) collective-permute-start(bf16[704,128]{1,0:T(8,128)(2,1)} %get-tuple-element.51), channel_id=1, source_target_pairs={{0,2},{1,5},{4,0},{5,9},{8,4},{9,13},{12,8},{13,15},{14,12},{15,11... | collective-permute-start | bytes 540680 | tf_op jit(solution)/shard_map/ppermute | solution.py:518
  8.1 7.2 %collective-permute-start.2 = (bf16[704,128]{1,0:T(8,128)(2,1)}, bf16[704,128]{1,0:T(8,128)(2,1)S(1)}, u32[]{:S(2)}, u32[]{:S(2)}) collective-permute-start(bf16[704,128]{1,0:T(8,128)(2,1)} %get-tuple-element.51), channel_id=1, source_target_pairs={{0,4},{1,3},{4,8},{5,1},{8,12},{9,5},{12,14},{13,9},{14,10},{15,13... | collective-permute-start | bytes 540680 | tf_op jit(solution)/shard_map/ppermute | solution.py:518
  9.5 10.3 %collective-permute-start.11 = (bf16[64,1024]{1,0:T(8,128)(2,1)S(1)}, bf16[64,1024]{1,0:T(8,128)(2,1)S(1)}, u32[]{:S(2)}, u32[]{:S(2)}) collective-permute-start(bf16[64,1024]{1,0:T(8,128)(2,1)S(1)} %collective-permute-done.10.refs_3_), channel_id=1, source_target_pairs={{0,2},{1,5},{4,0},{5,9},{8,4},{9,13},{12,8},{13,15},{14,12},{15,11... | collective-permute-start | bytes 393224 | tf_op jit(solution)/shard_map/ppermute | solution.py:528
  10.2 10.3 %collective-permute-start.7 = (bf16[64,1024]{1,0:T(8,128)(2,1)S(1)}, bf16[64,1024]{1,0:T(8,128)(2,1)S(1)}, u32[]{:S(2)}, u32[]{:S(2)}) collective-permute-start(bf16[64,1024]{1,0:T(8,128)(2,1)S(1)} %collective-permute-done.6.refs_2_), channel_id=1, source_target_pairs={{0,4},{1,3},{4,8},{5,1},{8,12},{9,5},{12,14},{13,9},{14,10},{15,13... | collective-permute-start | bytes 393224 | tf_op jit(solution)/shard_map/ppermute | solution.py:528
  14.6 7.3 %collective-permute-start.14 = (bf16[704,128]{1,0:T(8,128)(2,1)S(1)}, bf16[704,128]{1,0:T(8,128)(2,1)S(1)}, u32[]{:S(2)}, u32[]{:S(2)}) collective-permute-start(bf16[704,128]{1,0:T(8,128)(2,1)S(1)} %collective-permute-done.13.refs_5_.refs_7_), channel_id=1, source_target_pairs={{0,2},{1,5},{4,0},{5,9},{8,4},{9,13},{12,8},{13,15},{14,12},{15,11... | collective-permute-start | bytes 540680 | tf_op jit(solution)/shard_map/ppermute | solution.py:529
  15.3 7.4 %collective-permute-start.3 = (bf16[704,128]{1,0:T(8,128)(2,1)S(1)}, bf16[704,128]{1,0:T(8,128)(2,1)S(1)}, u32[]{:S(2)}, u32[]{:S(2)}) collective-permute-start(bf16[704,128]{1,0:T(8,128)(2,1)S(1)} %collective-permute-done.2.refs_4_.refs_6_), channel_id=1, source_target_pairs={{0,4},{1,3},{4,8},{5,1},{8,12},{9,5},{12,14},{13,9},{14,10},{15,13... | collective-permute-start | bytes 540680 | tf_op jit(solution)/shard_map/ppermute | solution.py:529
  19.8 10.4 %collective-permute-start.12 = (bf16[64,1024]{1,0:T(8,128)(2,1)S(1)}, bf16[64,1024]{1,0:T(8,128)(2,1)S(1)}, u32[]{:S(2)}, u32[]{:S(2)}) collective-permute-start(bf16[64,1024]{1,0:T(8,128)(2,1)S(1)} %collective-permute-done.11.refs_3_), channel_id=1, source_target_pairs={{0,2},{1,5},{4,0},{5,9},{8,4},{9,13},{12,8},{13,15},{14,12},{15,11... | collective-permute-start | bytes 393224 | tf_op jit(solution)/shard_map/ppermute | solution.py:528
  20.5 6.5 %collective-permute-start.8 = (bf16[64,1024]{1,0:T(8,128)(2,1)S(1)}, bf16[64,1024]{1,0:T(8,128)(2,1)S(1)}, u32[]{:S(2)}, u32[]{:S(2)}) collective-permute-start(bf16[64,1024]{1,0:T(8,128)(2,1)S(1)} %collective-permute-done.7.refs_2_), channel_id=1, source_target_pairs={{0,4},{1,3},{4,8},{5,1},{8,12},{9,5},{12,14},{13,9},{14,10},{15,13... | collective-permute-start | bytes 393224 | tf_op jit(solution)/shard_map/ppermute | solution.py:528
  21.9 8.4 %collective-permute-start.15 = (bf16[704,128]{1,0:T(8,128)(2,1)S(1)}, bf16[704,128]{1,0:T(8,128)(2,1)S(1)}, u32[]{:S(2)}, u32[]{:S(2)}) collective-permute-start(bf16[704,128]{1,0:T(8,128)(2,1)S(1)} %collective-permute-done.14.refs_5_.refs_7_), channel_id=1, source_target_pairs={{0,2},{1,5},{4,0},{5,9},{8,4},{9,13},{12,8},{13,15},{14,12},{15,11... | collective-permute-start | bytes 540680 | tf_op jit(solution)/shard_map/ppermute | solution.py:529
  22.7 6.0 %collective-permute-start.4 = (bf16[704,128]{1,0:T(8,128)(2,1)S(1)}, bf16[704,128]{1,0:T(8,128)(2,1)S(1)}, u32[]{:S(2)}, u32[]{:S(2)}) collective-permute-start(bf16[704,128]{1,0:T(8,128)(2,1)S(1)} %collective-permute-done.3.refs_4_.refs_6_), channel_id=1, source_target_pairs={{0,4},{1,3},{4,8},{5,1},{8,12},{9,5},{12,14},{13,9},{14,10},{15,13... | collective-permute-start | bytes 540680 | tf_op jit(solution)/shard_map/ppermute | solution.py:529
  27.0 6.3 %collective-permute-start.9 = (bf16[64,1024]{1,0:T(8,128)(2,1)S(1)}, bf16[64,1024]{1,0:T(8,128)(2,1)S(1)}, u32[]{:S(2)}, u32[]{:S(2)}) collective-permute-start(bf16[64,1024]{1,0:T(8,128)(2,1)S(1)} %collective-permute-done.8.refs_2_), channel_id=1, source_target_pairs={{0,4},{1,3},{4,8},{5,1},{8,12},{9,5},{12,14},{13,9},{14,10},{15,13... | collective-permute-start | bytes 393224 | tf_op jit(solution)/shard_map/ppermute | solution.py:528
  28.7 5.6 %collective-permute-start.5 = (bf16[704,128]{1,0:T(8,128)(2,1)S(1)}, bf16[704,128]{1,0:T(8,128)(2,1)S(1)}, u32[]{:S(2)}, u32[]{:S(2)}) collective-permute-start(bf16[704,128]{1,0:T(8,128)(2,1)S(1)} %collective-permute-done.4.refs_4_.refs_6_), channel_id=1, source_target_pairs={{0,4},{1,3},{4,8},{5,1},{8,12},{9,5},{12,14},{13,9},{14,10},{15,13... | collective-permute-start | bytes 540680 | tf_op jit(solution)/shard_map/ppermute | solution.py:529
  38.3 5.7 %collective-permute-start.17 = (bf16[640,128]{1,0:T(8,128)(2,1)S(1)}, bf16[640,128]{1,0:T(8,128)(2,1)S(1)}, u32[]{:S(2)}, u32[]{:S(2)}) collective-permute-start(bf16[640,128]{1,0:T(8,128)(2,1)S(1)} %get-tuple-element.64.refs_2_), channel_id=1, source_target_pairs={{0,4},{1,3},{4,8},{5,1},{8,12},{9,5},{12,14},{13,9},{14,10},{15,13... | collective-permute-start | bytes 491528 | tf_op jit(solution)/shard_map/ppermute | solution.py:562
  40.9 6.3 %collective-permute-start.21 = (bf16[640,128]{1,0:T(8,128)(2,1)S(1)}, bf16[640,128]{1,0:T(8,128)(2,1)S(1)}, u32[]{:S(2)}, u32[]{:S(2)}) collective-permute-start(bf16[640,128]{1,0:T(8,128)(2,1)S(1)} %shard_map.114), channel_id=1, source_target_pairs={{0,2},{1,5},{4,0},{5,9},{8,4},{9,13},{12,8},{13,15},{14,12},{15,11... | collective-permute-start | bytes 491528 | tf_op jit(solution)/shard_map/ppermute | solution.py:564
  44.0 6.7 %collective-permute-start.18 = (bf16[640,128]{1,0:T(8,128)(2,1)S(1)}, bf16[640,128]{1,0:T(8,128)(2,1)S(1)}, u32[]{:S(2)}, u32[]{:S(2)}) collective-permute-start(bf16[640,128]{1,0:T(8,128)(2,1)S(1)} %collective-permute-done.17.refs_2_), channel_id=1, source_target_pairs={{0,4},{1,3},{4,8},{5,1},{8,12},{9,5},{12,14},{13,9},{14,10},{15,13... | collective-permute-start | bytes 491528 | tf_op jit(solution)/shard_map/ppermute | solution.py:566
  47.2 7.0 %collective-permute-start.22 = (bf16[640,128]{1,0:T(8,128)(2,1)S(1)}, bf16[640,128]{1,0:T(8,128)(2,1)S(1)}, u32[]{:S(2)}, u32[]{:S(2)}) collective-permute-start(bf16[640,128]{1,0:T(8,128)(2,1)S(1)} %shard_map.116.refs_3_), channel_id=1, source_target_pairs={{0,2},{1,5},{4,0},{5,9},{8,4},{9,13},{12,8},{13,15},{14,12},{15,11... | collective-permute-start | bytes 491528 | tf_op jit(solution)/shard_map/ppermute | solution.py:571
  50.6 6.6 %collective-permute-start.19 = (bf16[640,128]{1,0:T(8,128)(2,1)S(1)}, bf16[640,128]{1,0:T(8,128)(2,1)S(1)}, u32[]{:S(2)}, u32[]{:S(2)}) collective-permute-start(bf16[640,128]{1,0:T(8,128)(2,1)S(1)} %collective-permute-done.18.refs_2_), channel_id=1, source_target_pairs={{0,4},{1,3},{4,8},{5,1},{8,12},{9,5},{12,14},{13,9},{14,10},{15,13... | collective-permute-start | bytes 491528 | tf_op jit(solution)/shard_map/ppermute | solution.py:566
  54.2 6.1 %collective-permute-start.23 = (bf16[640,128]{1,0:T(8,128)(2,1)S(1)}, bf16[640,128]{1,0:T(8,128)(2,1)S(1)}, u32[]{:S(2)}, u32[]{:S(2)}) collective-permute-start(bf16[640,128]{1,0:T(8,128)(2,1)S(1)} %shard_map.119.refs_3_), channel_id=1, source_target_pairs={{0,2},{1,5},{4,0},{5,9},{8,4},{9,13},{12,8},{13,15},{14,12},{15,11... | collective-permute-start | bytes 491528 | tf_op jit(solution)/shard_map/ppermute | solution.py:571
  57.3 5.3 %collective-permute-start.20 = (bf16[640,128]{1,0:T(8,128)(2,1)S(1)}, bf16[640,128]{1,0:T(8,128)(2,1)S(1)}, u32[]{:S(2)}, u32[]{:S(2)}) collective-permute-start(bf16[640,128]{1,0:T(8,128)(2,1)S(1)} %collective-permute-done.19.refs_2_), channel_id=1, source_target_pairs={{0,4},{1,3},{4,8},{5,1},{8,12},{9,5},{12,14},{13,9},{14,10},{15,13... | collective-permute-start | bytes 491528 | tf_op jit(solution)/shard_map/ppermute | solution.py:566
  63.8 1.6 %collective-permute-start.24 = (f32[512,128]{1,0:T(8,128)S(1)}, f32[512,128]{1,0:T(8,128)S(1)}, u32[]{:S(2)}, u32[]{:S(2)}) collective-permute-start(f32[512,128]{1,0:T(8,128)S(1)} %get-tuple-element.93), channel_id=1, source_target_pairs={{0,1},{1,0},{2,3},{3,2},{4,5},{5,4},{6,7},{7,6},{8,9},{9,8},{10,11... | collective-permute-start | bytes 786440 | tf_op jit(solution)/shard_map/ppermute | solution.py:576
  (6 other events, 12.8 us)
